TPU v7x, 256 devices: a whole 4x4x8 slice. The times are simulated.
256 devices in a mesh: px: 32 (over x, y, core), py: 8 (over z).
Axes of the slice: x: 4, y: 4, z: 8, core: 2. Of those that a mesh axis runs over, the one named last changes fastest.
Arguments:
- v_block: float32 [32, 32, 8, 2, 2048], P(None, 'px', 'py'), may hold values from -64 to 64
- edge_leaves: int32 [32, 8, 4, 2], replicated, may hold values from 0 to 15, as said below
- self_blocks: bfloat16 [32, 8, 2, 16, 128, 128], P('px', 'py'), may hold values from -0.375 to 0.375
- side_blocks: bfloat16 [32, 8, 4, 2, 256, 256], P('px', 'py'), may hold values from -0.25 to 0.25
- compress: bfloat16 [32, 8, 2, 2048, 256], P('px', 'py'), may hold values from -0.09375 to 0.09375
- expand: bfloat16 [32, 8, 2, 256, 2048], P('px', 'py'), may hold values from -0.25 to 0.25
- factors: bfloat16 [32, 8, 8, 2, 2, 256, 256], P('px', 'py'), may hold values from -0.1875 to 0.1875
Outputs:
- y_field: float32 [32, 32, 8, 2, 2048], P(None, 'px', 'py')
- new_basis: float32 [64, 32, 8, 2, 2048], P(None, 'px', 'py')
Inputs may be any that keep to these rules, and one draw needn't show every extreme that they name: `edge_leaves`: for each patch the 8 listed leaves are distinct.
All inputs are finite; a program needn't handle non-finite values.
Results may differ from a plain program's by a relative error of at most 0.03.
Values may be sent and summed in bfloat16 or wider, within the bound.
No kernel may reach another device: no remote copies, remote signals or barrier semaphores. Data moves between devices by JAX's collectives and lax.ppermute only.
A program may use at most 64 MiB of HBM per device.

v0:
```python
import functools

import jax
import jax.numpy as jnp
from jax import lax
from jax.experimental import pallas as pl
from jax.experimental.pallas import tpu as pltpu
from jax.sharding import PartitionSpec as P

F32 = jnp.float32
BF16 = jnp.bfloat16
NT = (((1,), (1,)), ((), ()))
VM = pl.BlockSpec(memory_space=pltpu.VMEM)
SM = pl.BlockSpec(memory_space=pltpu.SMEM)


def call(kernel, outs, args, flops, smem=0, limit=24):
    size = sum(a.size * a.dtype.itemsize for a in args)
    return pl.pallas_call(
        kernel,
        out_shape=[jax.ShapeDtypeStruct(s, d) for s, d in outs],
        in_specs=[SM] * smem + [VM] * (len(args) - smem),
        out_specs=[VM] * len(outs),
        cost_estimate=pl.CostEstimate(flops=flops, bytes_accessed=size, transcendentals=0),
        compiler_params=pltpu.CompilerParams(vmem_limit_bytes=limit * 2**20),
    )(*args)


def mul(x, gr, gi):
    h = x.shape[0] // 2
    re, im = x[:h], x[h:]
    first = jnp.dot(x, gr, preferred_element_type=F32)
    second = jnp.dot(jnp.concatenate([-im, re], 0), gi, preferred_element_type=F32)
    return first + second


def adj(x, gr, gi):
    h = x.shape[0] // 2
    re, im = x[:h], x[h:]
    first = lax.dot_general(x, gr, NT, preferred_element_type=F32)
    second = lax.dot_general(jnp.concatenate([im, -re], 0), gi, NT, preferred_element_type=F32)
    return first + second


def leaf_at(at, leaf):
    return pl.ds(pl.multiple_of(at * leaf, leaf), leaf)


def split(x):
    high = x.astype(BF16)
    return high, (x - high.astype(F32)).astype(BF16)


def piece(ref, info, side, leaf):
    return jnp.concatenate(
        [ref[:, leaf_at(info[2 * side + e], leaf)] for e in range(2)], 1
    )


def head_kernel(leaf, info, v_ref, c_ref, vb_ref, m_ref, pb_ref, pc_ref, pd_ref):
    cols = vb_ref.shape[0] // 2
    leaves = vb_ref.shape[1] // leaf
    per = 2 * leaves
    for at in range(leaves):
        for part in range(2):
            rows = v_ref[pl.ds(2 * at + part, cols, stride=per), :]
            vb_ref[part * cols : (part + 1) * cols, at * leaf : (at + 1) * leaf] = rows.astype(BF16)
    vb = vb_ref[...]
    m_ref[: 2 * cols] = mul(vb, c_ref[0], c_ref[1]).astype(BF16)
    m_ref[2 * cols :] = piece(vb_ref, info, info[8], leaf)
    pb_ref[...] = piece(vb_ref, info, info[9], leaf)
    pc_ref[...] = piece(vb_ref, info, info[10], leaf)
    pd_ref[...] = piece(vb_ref, info, info[11], leaf)


def own_kernel(level, adjoint, s_ref, f_ref, o_ref):
    rows = o_ref.shape[0]
    product = adj if adjoint else mul
    o_ref[...] = product(s_ref[:rows], f_ref[level, 0, 0], f_ref[level, 0, 1])


def up_kernel(level, own_ref, r_ref, f_ref, *rest):
    rows = own_ref.shape[0]
    o_ref = rest[-1]
    state = own_ref[...] + mul(r_ref[:rows], f_ref[level, 1, 0], f_ref[level, 1, 1])
    o_ref[:rows] = state.astype(BF16)
    if len(rest) > 1:
        o_ref[rows:] = rest[0][...]


def leaves_kernel(leaf, adjoint, x_ref, b_ref, o_ref):
    product = adj if adjoint else mul
    for at in range(b_ref.shape[1]):
        cut = slice(at * leaf, (at + 1) * leaf)
        o_ref[:, cut] = product(x_ref[:, cut], b_ref[0, at], b_ref[1, at])


def sides_kernel(leaf, info, near_ref, ra_ref, rb_ref, rc_ref, rd_ref, b_ref, o_ref):
    rows = near_ref.shape[0]
    o_ref[...] = near_ref[...]
    for at, ref in enumerate((ra_ref, rb_ref, rc_ref, rd_ref)):
        side = info[8 + at]
        x = ref[ref.shape[0] - rows :]
        term = mul(x, b_ref[side, 0], b_ref[side, 1])
        for e in range(2):
            o_ref[:, leaf_at(info[2 * side + e], leaf)] += term[:, e * leaf : (e + 1) * leaf]


def field_kernel(leaf, level, own_ref, r_ref, f_ref, near_ref, e_ref, y_ref, yb_ref, g_ref, m_ref):
    rows = own_ref.shape[0]
    cols = rows // 2
    leaves = yb_ref.shape[1] // leaf
    state = own_ref[...] + mul(r_ref[:rows], f_ref[level, 1, 0], f_ref[level, 1, 1])
    y = near_ref[...] + mul(state.astype(BF16), e_ref[0], e_ref[1])
    yb = y.astype(BF16)
    yb_ref[...] = yb
    g = adj(yb, e_ref[0], e_ref[1]).astype(BF16)
    g_ref[...] = g
    m_ref[...] = adj(g, f_ref[level, 1, 0], f_ref[level, 1, 1]).astype(BF16)
    for at in range(leaves):
        for part in range(2):
            y_ref[pl.ds(2 * at + part, cols, stride=2 * leaves), :] = y[
                part * cols : (part + 1) * cols, at * leaf : (at + 1) * leaf
            ]


def terms_kernel(leaf, info, yb_ref, b_ref, *outs):
    for at, o_ref in enumerate(outs):
        side = info[8 + at]
        x = piece(yb_ref, info, side, leaf)
        o_ref[...] = adj(x, b_ref[side, 0], b_ref[side, 1]).astype(BF16)


def down_kernel(level, own_ref, r_ref, f_ref, *rest):
    rows = own_ref.shape[0]
    g_ref, m_ref = rest[-2:]
    g = (own_ref[...] + r_ref[:rows].astype(F32)).astype(BF16)
    g_ref[...] = g
    m_ref[:rows] = adj(g, f_ref[level, 1, 0], f_ref[level, 1, 1]).astype(BF16)
    if len(rest) > 2:
        m_ref[rows:] = rest[0][...]


def close_kernel(
    leaf, info, near_ref, own_ref, ra_ref, rb_ref, rc_ref, rd_ref, c_ref, v_ref, x_ref, p_ref
):
    rows = own_ref.shape[0]
    cols = rows // 2
    unknowns = near_ref.shape[1]
    leaves = unknowns // leaf
    g = (own_ref[...] + ra_ref[:rows].astype(F32)).astype(BF16)
    x_ref[:rows] = near_ref[...] + adj(g, c_ref[0], c_ref[1])
    for at, ref in enumerate((ra_ref, rb_ref, rc_ref, rd_ref)):
        side = info[8 + at]
        low = ref.shape[0] - rows
        for e in range(2):
            x_ref[:rows, leaf_at(info[2 * side + e], leaf)] += ref[
                low:, e * leaf : (e + 1) * leaf
            ].astype(F32)
    for at in range(leaves):
        for part in range(2):
            x_ref[rows + part * cols : rows + (part + 1) * cols, at * leaf : (at + 1) * leaf] = (
                v_ref[pl.ds(2 * at + part, cols, stride=2 * leaves), :]
            )
    high, low = split(x_ref[...])
    cross = lax.dot_general(high, low, NT, preferred_element_type=F32)
    s = lax.dot_general(high, high, NT, preferred_element_type=F32) + cross + cross.T

    def block(i, j):
        return s[i * cols : (i + 1) * cols, j * cols : (j + 1) * cols]

    below = lax.broadcasted_iota(jnp.int32, (cols, cols), 0) >= lax.broadcasted_iota(
        jnp.int32, (cols, cols), 1
    )
    zz = jnp.where(below, block(0, 0) + block(1, 1), block(1, 0) - block(0, 1))
    vv = jnp.where(below, block(2, 2) + block(3, 3), block(3, 2) - block(2, 3))
    p_ref[...] = jnp.concatenate(
        [zz, vv, block(0, 2) + block(1, 3), block(1, 2) - block(0, 3)], 1
    )


def exact_dot(a, b, dims=(((1,), (0,)), ((), ()))):
    return lax.dot_general(a, b, dims, preferred_element_type=F32, precision=lax.Precision.HIGHEST)


def real_form(re, im):
    return jnp.concatenate(
        [jnp.concatenate([re, im], 1), jnp.concatenate([-im, re], 1)], 0
    )


def inverse_factor(gram):
    size = gram.shape[0]
    eye = (
        lax.broadcasted_iota(jnp.int32, (size, size), 0)
        == lax.broadcasted_iota(jnp.int32, (size, size), 1)
    ).astype(F32)
    wide = jnp.concatenate([gram, eye], 1)
    blocks = [wide[8 * j : 8 * j + 8] for j in range(size // 8)]
    width = wide.shape[1]
    sub = lax.broadcasted_iota(jnp.int32, (8, width), 0)
    done = [jnp.zeros((8, width), F32) for _ in blocks]

    def lanes(b, k):
        return jnp.broadcast_to(b[:, k : k + 1], (8, width))

    def row(b, r):
        return jnp.broadcast_to(b[r : r + 1, :], (8, width))

    for k in range(0, size, 2):
        j0, r = divmod(k, 8)
        cols_a = [lanes(b, k) for b in blocks[j0:]]
        cols_b = [lanes(b, k + 1) for b in blocks[j0:]]
        a, b, c = row(cols_a[0], r), row(cols_b[0], r), row(cols_b[0], r + 1)
        row_a, row_b = row(blocks[j0], r), row(blocks[j0], r + 1)
        a_inv = 1.0 / a
        l = b * a_inv
        d = c - b * l
        d_inv = 1.0 / d
        row_b = row_b - l * row_a
        done[j0] = jnp.where(sub == r, row_a * lax.rsqrt(a), done[j0])
        done[j0] = jnp.where(sub == r + 1, row_b * lax.rsqrt(d), done[j0])
        scaled_a, scaled_b = row_a * a_inv, row_b * d_inv
        for i, j in enumerate(range(j0, len(blocks))):
            ca, cb = cols_a[i], cols_b[i] - l * cols_a[i]
            step = ca * scaled_a + cb * scaled_b
            if j == j0:
                step = jnp.where(sub > r + 1, step, 0.0)
            blocks[j] = blocks[j] - step
    return jnp.concatenate(done, 0)[:, size:]


def finish_kernel(leaf, total, pa_ref, pb_ref, x_ref, o_ref):
    p = (pa_ref[...] + pb_ref[...]) * (1.0 / total)
    cols = p.shape[0]
    lower = lax.broadcasted_iota(jnp.int32, (cols, cols), 0)
    upper = lax.broadcasted_iota(jnp.int32, (cols, cols), 1)
    eye = (lower == upper).astype(F32)

    def turned(a):
        return exact_dot(a, eye, (((0,), (0,)), ((), ())))

    def hermitian(t):
        strict = jnp.where(lower > upper, t, 0.0)
        above = jnp.where(lower < upper, t, 0.0)
        re = jnp.where(lower >= upper, t, 0.0) + turned(strict)
        return real_form(re, above - turned(above))

    zz = hermitian(p[:, :cols])
    vv = hermitian(p[:, cols : 2 * cols])
    h = real_form(p[:, 2 * cols : 3 * cols], p[:, 3 * cols :])
    nt = (((1,), (1,)), ((), ()))
    middle = exact_dot(h, vv) - 2.0 * h
    gram = zz + exact_dot(middle, h, nt)
    inverse = inverse_factor(gram)
    w = exact_dot(inverse, h)
    l1, l2 = inverse[:, :cols], inverse[:, cols:]
    w1, w2 = w[:, :cols], w[:, cols:]
    mix = jnp.concatenate(
        [
            jnp.concatenate([l1, -l2, -w1, w2], 1),
            jnp.concatenate([l2, l1, -w2, -w1], 1),
        ],
        0,
    )
    mix_high, mix_low = split(mix)
    high, low = split(x_ref[...])
    out = (
        jnp.dot(mix_high, high, preferred_element_type=F32)
        + jnp.dot(mix_high, low, preferred_element_type=F32)
        + jnp.dot(mix_low, high, preferred_element_type=F32)
    )
    rows = 2 * cols
    leaves = x_ref.shape[1] // leaf
    for at in range(leaves):
        for part in range(2):
            o_ref[pl.ds(2 * at + part, rows, stride=2 * leaves), :] = out[
                part * rows : (part + 1) * rows, at * leaf : (at + 1) * leaf
            ]


def per_device(v_block, edge_leaves, self_blocks, side_blocks, compress, expand, factors):
    cols = v_block.shape[0]
    unknowns = v_block.shape[4]
    leaves = self_blocks.shape[3]
    leaf = self_blocks.shape[4]
    levels = factors.shape[2]
    rank = compress.shape[4]
    rows = 2 * cols
    row_count = lax.axis_size("px")
    col_count = lax.axis_size("py")
    row_bits = row_count.bit_length() - 1
    total = 2 * unknowns * row_count * col_count
    row_at = lax.axis_index("px")
    col_at = lax.axis_index("py")
    selfs = self_blocks.reshape(self_blocks.shape[2:])
    sides = side_blocks.reshape(side_blocks.shape[2:])
    squeeze = compress.reshape(compress.shape[2:])
    spread = expand.reshape(expand.shape[2:])
    sections = factors.reshape(factors.shape[2:])
    own_leaves = lax.dynamic_slice(edge_leaves, (row_at, col_at, 0, 0), (1, 1, 4, 2)).reshape(8)
    odd_row, odd_col = row_at % 2, col_at % 2
    order = jnp.stack([1 - odd_row, odd_row, 3 - odd_col, 2 + odd_col]).astype(jnp.int32)
    info = jnp.concatenate([own_leaves, order])
    tall = v_block.reshape(cols, 2, leaves, leaf).transpose(0, 2, 1, 3).reshape(-1, leaf)

    def partner(x, level):
        if level < row_bits:
            return lax.ppermute(x, "px", [(i, i ^ 1 << level) for i in range(row_count)])
        bit = level - row_bits
        return lax.ppermute(x, "py", [(i, i ^ 1 << bit) for i in range(col_count)])

    def beyond(x, axis, count):
        pairs = [(i, i + 1) for i in range(1, count - 1, 2)]
        return lax.ppermute(x, axis, pairs + [(j, i) for i, j in pairs])

    small = ((rows, rank), BF16)
    double = ((2 * rows, rank), BF16)
    wide = ((rows, rank), F32)
    step_flops = 8 * cols * rank * rank
    patch_flops = 8 * cols * rank * unknowns
    leaf_flops = 8 * cols * leaf * unknowns

    half, sent, piece_b, piece_c, piece_d = call(
        functools.partial(head_kernel, leaf),
        [((rows, unknowns), BF16), double, small, small, small],
        [info, tall, squeeze],
        patch_flops,
        smem=1,
    )
    (near,) = call(
        functools.partial(leaves_kernel, leaf, False),
        [((rows, unknowns), F32)],
        [half, selfs],
        leaf_flops,
    )
    got = {}
    for level in range(levels):
        arrived = partner(sent, level)
        (own,) = call(
            functools.partial(own_kernel, level, False), [wide], [sent, sections], step_flops
        )
        if level == 0:
            got["a"] = arrived
        if level == 1:
            got["b"] = beyond(piece_b, "px", row_count)
        if level == 2:
            got["d"] = beyond(piece_d, "py", col_count)
        if level == row_bits:
            got["c"] = arrived
            (near,) = call(
                functools.partial(sides_kernel, leaf),
                [((rows, unknowns), F32)],
                [info, near, got["a"], got["b"], got["c"], got["d"], sides],
                4 * step_flops,
                smem=1,
            )
        if level < levels - 1:
            extra = [piece_c] if level == row_bits - 1 else []
            (sent,) = call(
                functools.partial(up_kernel, level),
                [double if extra else small],
                [own, arrived, sections] + extra,
                step_flops,
            )
    y, yb, g, message = call(
        functools.partial(field_kernel, leaf, levels - 1),
        [((rows * leaves, leaf), F32), ((rows, unknowns), BF16), small, small],
        [own, arrived, sections, near, spread],
        2 * patch_flops,
    )
    terms = call(
        functools.partial(terms_kernel, leaf), [small] * 4, [info, yb, sides], 4 * step_flops, smem=1
    )
    (z_near,) = call(
        functools.partial(leaves_kernel, leaf, True),
        [((rows, unknowns), F32)],
        [yb, selfs],
        leaf_flops,
    )
    for level in range(levels - 1, -1, -1):
        arrived = partner(message, level)
        (own,) = call(functools.partial(own_kernel, level, True), [wide], [g, sections], step_flops)
        if level == levels - 1:
            got["b"] = beyond(terms[1], "px", row_count)
        if level == levels - 2:
            got["d"] = beyond(terms[3], "py", col_count)
        if level == row_bits:
            got["c"] = arrived
        if level > 0:
            extra = [terms[0]] if level == 1 else [terms[2]] if level == row_bits + 1 else []
            g, message = call(
                functools.partial(down_kernel, level - 1),
                [small, double if extra else small],
                [own, arrived, sections] + extra,
                step_flops,
            )
    stacked, part = call(
        functools.partial(close_kernel, leaf),
        [((2 * rows, unknowns), F32), ((cols, 4 * cols), F32)],
        [info, z_near, own, arrived, got["b"], got["c"], got["d"], squeeze, tall],
        patch_flops,
        smem=1,
    )
    for level in range(levels):
        other = partner(part, level)
        if level < levels - 1:
            part = part + other
    (basis,) = call(
        functools.partial(finish_kernel, leaf, total),
        [((2 * rows * leaves, leaf), F32)],
        [part, other, stacked],
        8 * rows * rows * unknowns,
    )

    def patch_form(a, count):
        a = a.reshape(count, leaves, 2, leaf).transpose(0, 2, 1, 3)
        return a.reshape(count, 1, 1, 2, unknowns)

    return patch_form(y, cols), patch_form(basis, rows)


def solution(mesh):
    in_specs = (
        P(None, "px", "py", None, None),
        P(),
        P("px", "py", None, None, None, None),
        P("px", "py", None, None, None, None),
        P("px", "py", None, None, None),
        P("px", "py", None, None, None),
        P("px", "py", None, None, None, None, None),
    )
    out_specs = (P(None, "px", "py", None, None), P(None, "px", "py", None, None))
    return jax.shard_map(
        per_device, mesh=mesh, in_specs=in_specs, out_specs=out_specs, check_vma=False
    )
```

profile of v0, /device:TPU:8, one launch (start us, length us, event | category | flops | bytes accessed | tf_op | source)
XLA Modules:
  0.0 147.5 jit_solution(1828222953523291911)
XLA Ops:
  1.8 1.6 %copy-done.3 = bf16[1,1,2,2048,256]{4,3,2,1,0:T(8,128)(2,1)S(1)} copy-done((bf16[1,1,2,2048,256]{4,3,2,1,0:T(8,128)(2,1)S(1)}, bf16[1,1,2,2048,256]{4,3,2,1,0:T(8,128)(2,1)}, u32[]{:S(2)}) %copy-start.3) | copy-done | bytes 2097176
  4.4 1.2 shard_map.86
  5.7 2.2 %copy-done.1 = bf16[1,1,8,2,2,256,256]{6,5,4,3,2,1,0:T(8,128)(2,1)S(1)} copy-done((bf16[1,1,8,2,2,256,256]{6,5,4,3,2,1,0:T(8,128)(2,1)S(1)}, bf16[1,1,8,2,2,256,256]{6,5,4,3,2,1,0:T(8,128)(2,1)}, u32[]{:S(2)}) %copy-start.1) | copy-done | bytes 4194328
  8.1 2.0 %copy-done.2 = bf16[1,1,8,2,2,256,256]{6,5,4,3,2,1,0:T(8,128)(2,1)S(1)} copy-done((bf16[1,1,8,2,2,256,256]{6,5,4,3,2,1,0:T(8,128)(2,1)S(1)}, bf16[1,1,8,2,2,256,256]{6,5,4,3,2,1,0:T(8,128)(2,1)}, u32[]{:S(2)}) %copy-start.2) | copy-done | bytes 4194328
  10.3 2.3 %collective-permute-start.1 = (bf16[64,256]{1,0:T(8,128)(2,1)S(1)}, bf16[64,256]{1,0:T(8,128)(2,1)S(1)}, u32[]{:S(2)}, u32[]{:S(2)}) collective-permute-start(bf16[64,256]{1,0:T(8,128)(2,1)S(1)} %shard_map.88.s_ref), channel_id=1, source_target_pairs={{0,16},{8,24},{16,0},{24,8},{32,48},{40,56},{48,32},{56,40},{64,80... | collective-permute-start | bytes 98312 | tf_op jit(solution)/shard_map/ppermute | solution.py:309
  12.7 1.9 %collective-permute-done.1.r_ref = bf16[64,256]{1,0:T(8,128)(2,1)S(1)} collective-permute-done((bf16[64,256]{1,0:T(8,128)(2,1)S(1)}, bf16[64,256]{1,0:T(8,128)(2,1)S(1)}, u32[]{:S(2)}, u32[]{:S(2)}) %collective-permute-start.1) | collective-permute-done | bytes 32800 | tf_op jit(solution)/shard_map/ppermute | solution.py:309
  14.8 2.1 %collective-permute-start.2 = (bf16[64,256]{1,0:T(8,128)(2,1)S(1)}, bf16[64,256]{1,0:T(8,128)(2,1)S(1)}, u32[]{:S(2)}, u32[]{:S(2)}) collective-permute-start(bf16[64,256]{1,0:T(8,128)(2,1)S(1)} %shard_map.90.s_ref), channel_id=1, source_target_pairs={{0,32},{8,40},{16,48},{24,56},{32,0},{40,8},{48,16},{56,24},{64,96... | collective-permute-start | bytes 98312 | tf_op jit(solution)/shard_map/ppermute | solution.py:309
  17.0 3.3 %collective-permute-done.2.r_ref = bf16[64,256]{1,0:T(8,128)(2,1)S(1)} collective-permute-done((bf16[64,256]{1,0:T(8,128)(2,1)S(1)}, bf16[64,256]{1,0:T(8,128)(2,1)S(1)}, u32[]{:S(2)}, u32[]{:S(2)}) %collective-permute-start.2) | collective-permute-done | bytes 32800 | tf_op jit(solution)/shard_map/ppermute | solution.py:309
  20.4 1.3 collective-permute-start.3
  21.9 2.6 %collective-permute-done.3.r_ref = bf16[64,256]{1,0:T(8,128)(2,1)S(1)} collective-permute-done((bf16[64,256]{1,0:T(8,128)(2,1)S(1)}, bf16[64,256]{1,0:T(8,128)(2,1)S(1)}, u32[]{:S(2)}, u32[]{:S(2)}) %collective-permute-start.3) | collective-permute-done | bytes 32800 | tf_op jit(solution)/shard_map/ppermute | solution.py:309
  24.6 2.8 %collective-permute-start.4 = (bf16[64,256]{1,0:T(8,128)(2,1)S(1)}, bf16[64,256]{1,0:T(8,128)(2,1)S(1)}, u32[]{:S(2)}, u32[]{:S(2)}) collective-permute-start(bf16[64,256]{1,0:T(8,128)(2,1)S(1)} %shard_map.94.s_ref), channel_id=1, source_target_pairs={{0,128},{8,136},{16,144},{24,152},{32,160},{40,168},{48,176},{56,1... | collective-permute-start | bytes 98312 | tf_op jit(solution)/shard_map/ppermute | solution.py:309
  27.6 2.5 %collective-permute-done.4.r_ref = bf16[64,256]{1,0:T(8,128)(2,1)S(1)} collective-permute-done((bf16[64,256]{1,0:T(8,128)(2,1)S(1)}, bf16[64,256]{1,0:T(8,128)(2,1)S(1)}, u32[]{:S(2)}, u32[]{:S(2)}) %collective-permute-start.4) | collective-permute-done | bytes 32800 | tf_op jit(solution)/shard_map/ppermute | solution.py:309
  30.3 1.7 %collective-permute-start.5 = (bf16[128,256]{1,0:T(8,128)(2,1)S(1)}, bf16[128,256]{1,0:T(8,128)(2,1)S(1)}, u32[]{:S(2)}, u32[]{:S(2)}) collective-permute-start(bf16[128,256]{1,0:T(8,128)(2,1)S(1)} %shard_map.96.s_ref), channel_id=1, source_target_pairs={{0,1},{1,0},{2,3},{3,2},{4,5},{5,4},{6,7},{7,6},{8,9},{9,8},{10,11... | collective-permute-start | bytes 196616 | tf_op jit(solution)/shard_map/ppermute | solution.py:311
  32.1 2.9 %collective-permute-done.5.r_ref.rc_ref = bf16[128,256]{1,0:T(8,128)(2,1)S(1)} collective-permute-done((bf16[128,256]{1,0:T(8,128)(2,1)S(1)}, bf16[128,256]{1,0:T(8,128)(2,1)S(1)}, u32[]{:S(2)}, u32[]{:S(2)}) %collective-permute-start.5) | collective-permute-done | bytes 65568 | tf_op jit(solution)/shard_map/ppermute | solution.py:311
  35.2 2.7 %collective-permute-start.6 = (bf16[64,256]{1,0:T(8,128)(2,1)S(1)}, bf16[64,256]{1,0:T(8,128)(2,1)S(1)}, u32[]{:S(2)}, u32[]{:S(2)}) collective-permute-start(bf16[64,256]{1,0:T(8,128)(2,1)S(1)} %shard_map.98.s_ref), channel_id=1, source_target_pairs={{0,2},{1,3},{2,0},{3,1},{4,6},{5,7},{6,4},{7,5},{8,10},{9,11},{10,... | collective-permute-start | bytes 98312 | tf_op jit(solution)/shard_map/ppermute | solution.py:311
  37.9 1.9 %collective-permute-start.8 = (bf16[64,256]{1,0:T(8,128)(2,1)S(1)}, bf16[64,256]{1,0:T(8,128)(2,1)S(1)}, u32[]{:S(2)}, u32[]{:S(2)}) collective-permute-start(bf16[64,256]{1,0:T(8,128)(2,1)S(1)} %get-tuple-element.34), channel_id=1, source_target_pairs={{8,16},{24,32},{40,48},{56,64},{72,80},{88,96},{104,112},{120,128}... | collective-permute-start | bytes 98312 | tf_op jit(solution)/shard_map/ppermute | solution.py:315
  40.8 6.7 %collective-permute-start.7 = (bf16[64,256]{1,0:T(8,128)(2,1)S(1)}, bf16[64,256]{1,0:T(8,128)(2,1)S(1)}, u32[]{:S(2)}, u32[]{:S(2)}) collective-permute-start(bf16[64,256]{1,0:T(8,128)(2,1)S(1)} %shard_map.100.s_ref), channel_id=1, source_target_pairs={{0,4},{1,5},{2,6},{3,7},{4,0},{5,1},{6,2},{7,3},{8,12},{9,13},{10,... | collective-permute-start | bytes 98312 | tf_op jit(solution)/shard_map/ppermute | solution.py:311
  50.4 2.4 %shard_map.104 = (f32[1024,128]{1,0:T(8,128)}, bf16[64,2048]{1,0:T(8,128)(2,1)S(1)}, bf16[64,256]{1,0:T(8,128)(2,1)S(1)}, bf16[64,256]{1,0:T(8,128)(2,1)S(1)}) custom-call(f32[64,256]{1,0:T(8,128)S(1)} %shard_map.101.own_ref, bf16[64,256]{1,0:T(8,128)(2,1)S(1)} %collective-permute-done.7.r_ref, bf16[8,2,2,256,256]{4,3,2,1,0:T(8,128)(2,1)S(1)} %bitcast.39, ...), custom_call_target="tpu_custom_call" | custom-call | flops 268435456 | bytes 6914048 | tf_op jit(solution)/shard_map/pallas_call | solution.py:19
  52.8 5.0 %collective-permute-start.10 = (bf16[64,256]{1,0:T(8,128)(2,1)S(1)}, bf16[64,256]{1,0:T(8,128)(2,1)S(1)}, u32[]{:S(2)}, u32[]{:S(2)}) collective-permute-start(bf16[64,256]{1,0:T(8,128)(2,1)S(1)} %get-tuple-element.39), channel_id=1, source_target_pairs={{0,4},{1,5},{2,6},{3,7},{4,0},{5,1},{6,2},{7,3},{8,12},{9,13},{10,... | collective-permute-start | bytes 98312 | tf_op jit(solution)/shard_map/ppermute | solution.py:311
  58.0 2.7 %collective-permute-done.10.r_ref = bf16[64,256]{1,0:T(8,128)(2,1)S(1)} collective-permute-done((bf16[64,256]{1,0:T(8,128)(2,1)S(1)}, bf16[64,256]{1,0:T(8,128)(2,1)S(1)}, u32[]{:S(2)}, u32[]{:S(2)}) %collective-permute-start.10) | collective-permute-done | bytes 32800 | tf_op jit(solution)/shard_map/ppermute | solution.py:311
  60.9 3.5 %collective-permute-start.11 = (bf16[64,256]{1,0:T(8,128)(2,1)S(1)}, bf16[64,256]{1,0:T(8,128)(2,1)S(1)}, u32[]{:S(2)}, u32[]{:S(2)}) collective-permute-start(bf16[64,256]{1,0:T(8,128)(2,1)S(1)} %get-tuple-element.41), channel_id=1, source_target_pairs={{0,2},{1,3},{2,0},{3,1},{4,6},{5,7},{6,4},{7,5},{8,10},{9,11},{10,... | collective-permute-start | bytes 98312 | tf_op jit(solution)/shard_map/ppermute | solution.py:311
  66.5 3.1 %collective-permute-start.12 = (bf16[128,256]{1,0:T(8,128)(2,1)S(1)}, bf16[128,256]{1,0:T(8,128)(2,1)S(1)}, u32[]{:S(2)}, u32[]{:S(2)}) collective-permute-start(bf16[128,256]{1,0:T(8,128)(2,1)S(1)} %get-tuple-element.44), channel_id=1, source_target_pairs={{0,1},{1,0},{2,3},{3,2},{4,5},{5,4},{6,7},{7,6},{8,9},{9,8},{10,11... | collective-permute-start | bytes 196616 | tf_op jit(solution)/shard_map/ppermute | solution.py:311
  69.7 2.0 %collective-permute-done.12.r_ref.rc_ref = bf16[128,256]{1,0:T(8,128)(2,1)S(1)} collective-permute-done((bf16[128,256]{1,0:T(8,128)(2,1)S(1)}, bf16[128,256]{1,0:T(8,128)(2,1)S(1)}, u32[]{:S(2)}, u32[]{:S(2)}) %collective-permute-start.12) | collective-permute-done | bytes 65568 | tf_op jit(solution)/shard_map/ppermute | solution.py:311
  72.0 3.1 %collective-permute-start.13 = (bf16[64,256]{1,0:T(8,128)(2,1)S(1)}, bf16[64,256]{1,0:T(8,128)(2,1)S(1)}, u32[]{:S(2)}, u32[]{:S(2)}) collective-permute-start(bf16[64,256]{1,0:T(8,128)(2,1)S(1)} %get-tuple-element.46), channel_id=1, source_target_pairs={{0,128},{8,136},{16,144},{24,152},{32,160},{40,168},{48,176},{56,1... | collective-permute-start | bytes 98312 | tf_op jit(solution)/shard_map/ppermute | solution.py:309
  75.3 2.2 %collective-permute-done.13.r_ref = bf16[64,256]{1,0:T(8,128)(2,1)S(1)} collective-permute-done((bf16[64,256]{1,0:T(8,128)(2,1)S(1)}, bf16[64,256]{1,0:T(8,128)(2,1)S(1)}, u32[]{:S(2)}, u32[]{:S(2)}) %collective-permute-start.13) | collective-permute-done | bytes 32800 | tf_op jit(solution)/shard_map/ppermute | solution.py:309
  77.7 1.9 %collective-permute-start.14 = (bf16[64,256]{1,0:T(8,128)(2,1)S(1)}, bf16[64,256]{1,0:T(8,128)(2,1)S(1)}, u32[]{:S(2)}, u32[]{:S(2)}) collective-permute-start(bf16[64,256]{1,0:T(8,128)(2,1)S(1)} %get-tuple-element.48), channel_id=1, source_target_pairs={{0,64},{8,72},{16,80},{24,88},{32,96},{40,104},{48,112},{56,120},{... | collective-permute-start | bytes 98312 | tf_op jit(solution)/shard_map/ppermute | solution.py:309
  79.8 1.9 %collective-permute-done.14.r_ref = bf16[64,256]{1,0:T(8,128)(2,1)S(1)} collective-permute-done((bf16[64,256]{1,0:T(8,128)(2,1)S(1)}, bf16[64,256]{1,0:T(8,128)(2,1)S(1)}, u32[]{:S(2)}, u32[]{:S(2)}) %collective-permute-start.14) | collective-permute-done | bytes 32800 | tf_op jit(solution)/shard_map/ppermute | solution.py:309
  81.9 2.7 %collective-permute-start.15 = (bf16[64,256]{1,0:T(8,128)(2,1)S(1)}, bf16[64,256]{1,0:T(8,128)(2,1)S(1)}, u32[]{:S(2)}, u32[]{:S(2)}) collective-permute-start(bf16[64,256]{1,0:T(8,128)(2,1)S(1)} %get-tuple-element.50), channel_id=1, source_target_pairs={{0,32},{8,40},{16,48},{24,56},{32,0},{40,8},{48,16},{56,24},{64,96... | collective-permute-start | bytes 98312 | tf_op jit(solution)/shard_map/ppermute | solution.py:309
  84.8 2.6 %collective-permute-done.15.r_ref = bf16[64,256]{1,0:T(8,128)(2,1)S(1)} collective-permute-done((bf16[64,256]{1,0:T(8,128)(2,1)S(1)}, bf16[64,256]{1,0:T(8,128)(2,1)S(1)}, u32[]{:S(2)}, u32[]{:S(2)}) %collective-permute-start.15) | collective-permute-done | bytes 32800 | tf_op jit(solution)/shard_map/ppermute | solution.py:309
  88.5 3.3 %collective-permute-done.16.r_ref = bf16[64,256]{1,0:T(8,128)(2,1)S(1)} collective-permute-done((bf16[64,256]{1,0:T(8,128)(2,1)S(1)}, bf16[64,256]{1,0:T(8,128)(2,1)S(1)}, u32[]{:S(2)}, u32[]{:S(2)}) %collective-permute-start.16) | collective-permute-done | bytes 32800 | tf_op jit(solution)/shard_map/ppermute | solution.py:309
  92.1 2.4 %collective-permute-start.18 = (bf16[64,256]{1,0:T(8,128)(2,1)S(1)}, bf16[64,256]{1,0:T(8,128)(2,1)S(1)}, u32[]{:S(2)}, u32[]{:S(2)}) collective-permute-start(bf16[64,256]{1,0:T(8,128)(2,1)S(1)} %get-tuple-element.56), channel_id=1, source_target_pairs={{8,16},{24,32},{40,48},{56,64},{72,80},{88,96},{104,112},{120,128}... | collective-permute-start | bytes 98312 | tf_op jit(solution)/shard_map/ppermute | solution.py:315
  96.2 1.1 collective-permute-done.18.rb_ref
  97.6 2.2 %shard_map.122 = (f32[128,2048]{1,0:T(8,128)S(1)}, f32[32,128]{1,0:T(8,128)S(1)}) custom-call(s32[12]{0:T(128)S(1)} %concatenate.3.info, f32[64,2048]{1,0:T(8,128)S(1)} %shard_map.105.near_ref, f32[64,256]{1,0:T(8,128)S(1)} %shard_map.121.own_ref, bf16[128,256]{1,0:T(8,128)(2,1)S(1)} %collective-permute-done.17.ra_ref, ...), custom_call_target="tpu_custom_call" | custom-call | flops 134217728 | bytes 3407920 | tf_op jit(solution)/shard_map/pallas_call | solution.py:19
  99.8 1.3 collective-permute-start.20
  102.4 3.3 %collective-permute-done.21 = f32[32,128]{1,0:T(8,128)S(1)} collective-permute-done((f32[32,128]{1,0:T(8,128)S(1)}, f32[32,128]{1,0:T(8,128)S(1)}, u32[]{:S(2)}, u32[]{:S(2)}) %collective-permute-start.21) | collective-permute-done | bytes 16416 | tf_op jit(solution)/shard_map/ppermute | solution.py:309
  105.7 3.7 %collective-permute-start.22 = (f32[32,128]{1,0:T(8,128)S(1)}, f32[32,128]{1,0:T(8,128)S(1)}, u32[]{:S(2)}, u32[]{:S(2)}) collective-permute-start(f32[32,128]{1,0:T(8,128)S(1)} %add.43), channel_id=1, source_target_pairs={{0,32},{8,40},{16,48},{24,56},{32,0},{40,8},{48,16},{56,24},{64,96... | collective-permute-start | bytes 49160 | tf_op jit(solution)/shard_map/ppermute | solution.py:309
  109.4 1.7 %collective-permute-done.22 = f32[32,128]{1,0:T(8,128)S(1)} collective-permute-done((f32[32,128]{1,0:T(8,128)S(1)}, f32[32,128]{1,0:T(8,128)S(1)}, u32[]{:S(2)}, u32[]{:S(2)}) %collective-permute-start.22) | collective-permute-done | bytes 16416 | tf_op jit(solution)/shard_map/ppermute | solution.py:309
  111.2 1.8 %collective-permute-start.23 = (f32[32,128]{1,0:T(8,128)S(1)}, f32[32,128]{1,0:T(8,128)S(1)}, u32[]{:S(2)}, u32[]{:S(2)}) collective-permute-start(f32[32,128]{1,0:T(8,128)S(1)} %add.44), channel_id=1, source_target_pairs={{0,64},{8,72},{16,80},{24,88},{32,96},{40,104},{48,112},{56,120},{... | collective-permute-start | bytes 49160 | tf_op jit(solution)/shard_map/ppermute | solution.py:309
  112.9 2.0 %collective-permute-done.23 = f32[32,128]{1,0:T(8,128)S(1)} collective-permute-done((f32[32,128]{1,0:T(8,128)S(1)}, f32[32,128]{1,0:T(8,128)S(1)}, u32[]{:S(2)}, u32[]{:S(2)}) %collective-permute-start.23) | collective-permute-done | bytes 16416 | tf_op jit(solution)/shard_map/ppermute | solution.py:309
  114.9 3.0 %collective-permute-start.24 = (f32[32,128]{1,0:T(8,128)S(1)}, f32[32,128]{1,0:T(8,128)S(1)}, u32[]{:S(2)}, u32[]{:S(2)}) collective-permute-start(f32[32,128]{1,0:T(8,128)S(1)} %add.45), channel_id=1, source_target_pairs={{0,128},{8,136},{16,144},{24,152},{32,160},{40,168},{48,176},{56,1... | collective-permute-start | bytes 49160 | tf_op jit(solution)/shard_map/ppermute | solution.py:309
  117.9 2.3 %collective-permute-done.24 = f32[32,128]{1,0:T(8,128)S(1)} collective-permute-done((f32[32,128]{1,0:T(8,128)S(1)}, f32[32,128]{1,0:T(8,128)S(1)}, u32[]{:S(2)}, u32[]{:S(2)}) %collective-permute-start.24) | collective-permute-done | bytes 16416 | tf_op jit(solution)/shard_map/ppermute | solution.py:309
  120.2 4.2 %collective-permute-start.25 = (f32[32,128]{1,0:T(8,128)S(1)}, f32[32,128]{1,0:T(8,128)S(1)}, u32[]{:S(2)}, u32[]{:S(2)}) collective-permute-start(f32[32,128]{1,0:T(8,128)S(1)} %add.46), channel_id=1, source_target_pairs={{0,1},{1,0},{2,3},{3,2},{4,5},{5,4},{6,7},{7,6},{8,9},{9,8},{10,11... | collective-permute-start | bytes 49160 | tf_op jit(solution)/shard_map/ppermute | solution.py:311
  124.4 1.7 %collective-permute-done.25 = f32[32,128]{1,0:T(8,128)S(1)} collective-permute-done((f32[32,128]{1,0:T(8,128)S(1)}, f32[32,128]{1,0:T(8,128)S(1)}, u32[]{:S(2)}, u32[]{:S(2)}) %collective-permute-start.25) | collective-permute-done | bytes 16416 | tf_op jit(solution)/shard_map/ppermute | solution.py:311
  126.1 4.0 %collective-permute-start.26 = (f32[32,128]{1,0:T(8,128)S(1)}, f32[32,128]{1,0:T(8,128)S(1)}, u32[]{:S(2)}, u32[]{:S(2)}) collective-permute-start(f32[32,128]{1,0:T(8,128)S(1)} %add.47), channel_id=1, source_target_pairs={{0,2},{1,3},{2,0},{3,1},{4,6},{5,7},{6,4},{7,5},{8,10},{9,11},{10,... | collective-permute-start | bytes 49160 | tf_op jit(solution)/shard_map/ppermute | solution.py:311
  130.2 1.8 %collective-permute-done.26 = f32[32,128]{1,0:T(8,128)S(1)} collective-permute-done((f32[32,128]{1,0:T(8,128)S(1)}, f32[32,128]{1,0:T(8,128)S(1)}, u32[]{:S(2)}, u32[]{:S(2)}) %collective-permute-start.26) | collective-permute-done | bytes 16416 | tf_op jit(solution)/shard_map/ppermute | solution.py:311
  132.0 4.3 %collective-permute-start.27 = (f32[32,128]{1,0:T(8,128)S(1)}, f32[32,128]{1,0:T(8,128)S(1)}, u32[]{:S(2)}, u32[]{:S(2)}) collective-permute-start(f32[32,128]{1,0:T(8,128)S(1)} %add.48.pa_ref), channel_id=1, source_target_pairs={{0,4},{1,5},{2,6},{3,7},{4,0},{5,1},{6,2},{7,3},{8,12},{9,13},{10,... | collective-permute-start | bytes 49160 | tf_op jit(solution)/shard_map/ppermute | solution.py:311
  136.3 3.3 %collective-permute-done.27.pb_ref = f32[32,128]{1,0:T(8,128)S(1)} collective-permute-done((f32[32,128]{1,0:T(8,128)S(1)}, f32[32,128]{1,0:T(8,128)S(1)}, u32[]{:S(2)}, u32[]{:S(2)}) %collective-permute-start.27) | collective-permute-done | bytes 16416 | tf_op jit(solution)/shard_map/ppermute | solution.py:311
  139.6 7.8 %shard_map.123 = f32[2048,128]{1,0:T(8,128)} custom-call(f32[32,128]{1,0:T(8,128)S(1)} %add.48.pa_ref, f32[32,128]{1,0:T(8,128)S(1)} %collective-permute-done.27.pb_ref, f32[128,2048]{1,0:T(8,128)S(1)} %get-tuple-element.59.x_ref), custom_call_target="tpu_custom_call" | custom-call | flops 67108864 | bytes 1081344 | tf_op jit(solution)/shard_map/pallas_call | solution.py:19
  (76 shorter events, 16.7 us)
Async XLA Ops:
  0.6 0.8 copy-start
  1.8 1.6 %copy-start.3 = (bf16[1,1,2,2048,256]{4,3,2,1,0:T(8,128)(2,1)S(1)}, bf16[1,1,2,2048,256]{4,3,2,1,0:T(8,128)(2,1)}, u32[]{:S(2)}) copy-start(bf16[1,1,2,2048,256]{4,3,2,1,0:T(8,128)(2,1)} %param.11) | copy-start | bytes 6291460
  3.4 1.0 copy-start.8
  5.6 2.5 %collective-permute-start = (bf16[128,256]{1,0:T(8,128)(2,1)S(1)}, bf16[128,256]{1,0:T(8,128)(2,1)S(1)}, u32[]{:S(2)}, u32[]{:S(2)}) collective-permute-start(bf16[128,256]{1,0:T(8,128)(2,1)S(1)} %get-tuple-element.31.s_ref), channel_id=1, source_target_pairs={{0,8},{8,0},{16,24},{24,16},{32,40},{40,32},{48,56},{56,48},{64,72... | collective-permute-start | bytes 196616 | tf_op jit(solution)/shard_map/ppermute | solution.py:309
  5.7 2.2 %copy-start.1 = (bf16[1,1,8,2,2,256,256]{6,5,4,3,2,1,0:T(8,128)(2,1)S(1)}, bf16[1,1,8,2,2,256,256]{6,5,4,3,2,1,0:T(8,128)(2,1)}, u32[]{:S(2)}) copy-start(bf16[1,1,8,2,2,256,256]{6,5,4,3,2,1,0:T(8,128)(2,1)} %param.13) | copy-start | bytes 12582916
  7.9 2.2 %copy-start.2 = (bf16[1,1,8,2,2,256,256]{6,5,4,3,2,1,0:T(8,128)(2,1)S(1)}, bf16[1,1,8,2,2,256,256]{6,5,4,3,2,1,0:T(8,128)(2,1)}, u32[]{:S(2)}) copy-start(bf16[1,1,8,2,2,256,256]{6,5,4,3,2,1,0:T(8,128)(2,1)} %param.13) | copy-start | bytes 12582916
  10.3 4.3 %collective-permute-start.1 = (bf16[64,256]{1,0:T(8,128)(2,1)S(1)}, bf16[64,256]{1,0:T(8,128)(2,1)S(1)}, u32[]{:S(2)}, u32[]{:S(2)}) collective-permute-start(bf16[64,256]{1,0:T(8,128)(2,1)S(1)} %shard_map.88.s_ref), channel_id=1, source_target_pairs={{0,16},{8,24},{16,0},{24,8},{32,48},{40,56},{48,32},{56,40},{64,80... | collective-permute-start | bytes 98312 | tf_op jit(solution)/shard_map/ppermute | solution.py:309
  14.8 5.5 %collective-permute-start.2 = (bf16[64,256]{1,0:T(8,128)(2,1)S(1)}, bf16[64,256]{1,0:T(8,128)(2,1)S(1)}, u32[]{:S(2)}, u32[]{:S(2)}) collective-permute-start(bf16[64,256]{1,0:T(8,128)(2,1)S(1)} %shard_map.90.s_ref), channel_id=1, source_target_pairs={{0,32},{8,40},{16,48},{24,56},{32,0},{40,8},{48,16},{56,24},{64,96... | collective-permute-start | bytes 98312 | tf_op jit(solution)/shard_map/ppermute | solution.py:309
  20.4 4.0 %collective-permute-start.3 = (bf16[64,256]{1,0:T(8,128)(2,1)S(1)}, bf16[64,256]{1,0:T(8,128)(2,1)S(1)}, u32[]{:S(2)}, u32[]{:S(2)}) collective-permute-start(bf16[64,256]{1,0:T(8,128)(2,1)S(1)} %shard_map.92.s_ref), channel_id=1, source_target_pairs={{0,64},{8,72},{16,80},{24,88},{32,96},{40,104},{48,112},{56,120},{... | collective-permute-start | bytes 98312 | tf_op jit(solution)/shard_map/ppermute | solution.py:309
  24.6 5.5 %collective-permute-start.4 = (bf16[64,256]{1,0:T(8,128)(2,1)S(1)}, bf16[64,256]{1,0:T(8,128)(2,1)S(1)}, u32[]{:S(2)}, u32[]{:S(2)}) collective-permute-start(bf16[64,256]{1,0:T(8,128)(2,1)S(1)} %shard_map.94.s_ref), channel_id=1, source_target_pairs={{0,128},{8,136},{16,144},{24,152},{32,160},{40,168},{48,176},{56,1... | collective-permute-start | bytes 98312 | tf_op jit(solution)/shard_map/ppermute | solution.py:309
  30.3 4.7 %collective-permute-start.5 = (bf16[128,256]{1,0:T(8,128)(2,1)S(1)}, bf16[128,256]{1,0:T(8,128)(2,1)S(1)}, u32[]{:S(2)}, u32[]{:S(2)}) collective-permute-start(bf16[128,256]{1,0:T(8,128)(2,1)S(1)} %shard_map.96.s_ref), channel_id=1, source_target_pairs={{0,1},{1,0},{2,3},{3,2},{4,5},{5,4},{6,7},{7,6},{8,9},{9,8},{10,11... | collective-permute-start | bytes 196616 | tf_op jit(solution)/shard_map/ppermute | solution.py:311
  35.2 5.5 %collective-permute-start.6 = (bf16[64,256]{1,0:T(8,128)(2,1)S(1)}, bf16[64,256]{1,0:T(8,128)(2,1)S(1)}, u32[]{:S(2)}, u32[]{:S(2)}) collective-permute-start(bf16[64,256]{1,0:T(8,128)(2,1)S(1)} %shard_map.98.s_ref), channel_id=1, source_target_pairs={{0,2},{1,3},{2,0},{3,1},{4,6},{5,7},{6,4},{7,5},{8,10},{9,11},{10,... | collective-permute-start | bytes 98312 | tf_op jit(solution)/shard_map/ppermute | solution.py:311
  37.9 10.1 %collective-permute-start.8 = (bf16[64,256]{1,0:T(8,128)(2,1)S(1)}, bf16[64,256]{1,0:T(8,128)(2,1)S(1)}, u32[]{:S(2)}, u32[]{:S(2)}) collective-permute-start(bf16[64,256]{1,0:T(8,128)(2,1)S(1)} %get-tuple-element.34), channel_id=1, source_target_pairs={{8,16},{24,32},{40,48},{56,64},{72,80},{88,96},{104,112},{120,128}... | collective-permute-start | bytes 98312 | tf_op jit(solution)/shard_map/ppermute | solution.py:315
  39.8 8.2 %collective-permute-start.9 = (bf16[64,256]{1,0:T(8,128)(2,1)S(1)}, bf16[64,256]{1,0:T(8,128)(2,1)S(1)}, u32[]{:S(2)}, u32[]{:S(2)}) collective-permute-start(bf16[64,256]{1,0:T(8,128)(2,1)S(1)} %get-tuple-element.35), channel_id=1, source_target_pairs={{1,2},{3,4},{5,6},{2,1},{4,3},{6,5},{9,10},{11,12},{13,14},{10,9},... | collective-permute-start | bytes 98312 | tf_op jit(solution)/shard_map/ppermute | solution.py:315
  40.6 6.9 %copy-start.6 = (bf16[1,1,2,16,128,128]{5,4,3,2,1,0:T(8,128)(2,1)S(1)}, bf16[1,1,2,16,128,128]{5,4,3,2,1,0:T(8,128)(2,1)}, u32[]{:S(2)}) copy-start(bf16[1,1,2,16,128,128]{5,4,3,2,1,0:T(8,128)(2,1)} %param.9) | copy-start | bytes 3145732
  40.6 7.3 %copy-start.5 = (bf16[1,1,4,2,256,256]{5,4,3,2,1,0:T(8,128)(2,1)S(1)}, bf16[1,1,4,2,256,256]{5,4,3,2,1,0:T(8,128)(2,1)}, u32[]{:S(2)}) copy-start(bf16[1,1,4,2,256,256]{5,4,3,2,1,0:T(8,128)(2,1)} %param.10) | copy-start | bytes 3145732
  40.8 8.7 %collective-permute-start.7 = (bf16[64,256]{1,0:T(8,128)(2,1)S(1)}, bf16[64,256]{1,0:T(8,128)(2,1)S(1)}, u32[]{:S(2)}, u32[]{:S(2)}) collective-permute-start(bf16[64,256]{1,0:T(8,128)(2,1)S(1)} %shard_map.100.s_ref), channel_id=1, source_target_pairs={{0,4},{1,5},{2,6},{3,7},{4,0},{5,1},{6,2},{7,3},{8,12},{9,13},{10,... | collective-permute-start | bytes 98312 | tf_op jit(solution)/shard_map/ppermute | solution.py:311
  48.8 1.6 %copy-start.7 = (bf16[1,1,2,256,2048]{4,3,2,1,0:T(8,128)(2,1)S(1)}, bf16[1,1,2,256,2048]{4,3,2,1,0:T(8,128)(2,1)}, u32[]{:S(2)}) copy-start(bf16[1,1,2,256,2048]{4,3,2,1,0:T(8,128)(2,1)} %param.12) | copy-start | bytes 6291460
  52.8 7.8 %collective-permute-start.10 = (bf16[64,256]{1,0:T(8,128)(2,1)S(1)}, bf16[64,256]{1,0:T(8,128)(2,1)S(1)}, u32[]{:S(2)}, u32[]{:S(2)}) collective-permute-start(bf16[64,256]{1,0:T(8,128)(2,1)S(1)} %get-tuple-element.39), channel_id=1, source_target_pairs={{0,4},{1,5},{2,6},{3,7},{4,0},{5,1},{6,2},{7,3},{8,12},{9,13},{10,... | collective-permute-start | bytes 98312 | tf_op jit(solution)/shard_map/ppermute | solution.py:311
  60.9 5.4 %collective-permute-start.11 = (bf16[64,256]{1,0:T(8,128)(2,1)S(1)}, bf16[64,256]{1,0:T(8,128)(2,1)S(1)}, u32[]{:S(2)}, u32[]{:S(2)}) collective-permute-start(bf16[64,256]{1,0:T(8,128)(2,1)S(1)} %get-tuple-element.41), channel_id=1, source_target_pairs={{0,2},{1,3},{2,0},{3,1},{4,6},{5,7},{6,4},{7,5},{8,10},{9,11},{10,... | collective-permute-start | bytes 98312 | tf_op jit(solution)/shard_map/ppermute | solution.py:311
  66.5 5.3 %collective-permute-start.12 = (bf16[128,256]{1,0:T(8,128)(2,1)S(1)}, bf16[128,256]{1,0:T(8,128)(2,1)S(1)}, u32[]{:S(2)}, u32[]{:S(2)}) collective-permute-start(bf16[128,256]{1,0:T(8,128)(2,1)S(1)} %get-tuple-element.44), channel_id=1, source_target_pairs={{0,1},{1,0},{2,3},{3,2},{4,5},{5,4},{6,7},{7,6},{8,9},{9,8},{10,11... | collective-permute-start | bytes 196616 | tf_op jit(solution)/shard_map/ppermute | solution.py:311
  72.0 5.5 %collective-permute-start.13 = (bf16[64,256]{1,0:T(8,128)(2,1)S(1)}, bf16[64,256]{1,0:T(8,128)(2,1)S(1)}, u32[]{:S(2)}, u32[]{:S(2)}) collective-permute-start(bf16[64,256]{1,0:T(8,128)(2,1)S(1)} %get-tuple-element.46), channel_id=1, source_target_pairs={{0,128},{8,136},{16,144},{24,152},{32,160},{40,168},{48,176},{56,1... | collective-permute-start | bytes 98312 | tf_op jit(solution)/shard_map/ppermute | solution.py:309
  77.7 4.0 %collective-permute-start.14 = (bf16[64,256]{1,0:T(8,128)(2,1)S(1)}, bf16[64,256]{1,0:T(8,128)(2,1)S(1)}, u32[]{:S(2)}, u32[]{:S(2)}) collective-permute-start(bf16[64,256]{1,0:T(8,128)(2,1)S(1)} %get-tuple-element.48), channel_id=1, source_target_pairs={{0,64},{8,72},{16,80},{24,88},{32,96},{40,104},{48,112},{56,120},{... | collective-permute-start | bytes 98312 | tf_op jit(solution)/shard_map/ppermute | solution.py:309
  81.9 5.5 %collective-permute-start.15 = (bf16[64,256]{1,0:T(8,128)(2,1)S(1)}, bf16[64,256]{1,0:T(8,128)(2,1)S(1)}, u32[]{:S(2)}, u32[]{:S(2)}) collective-permute-start(bf16[64,256]{1,0:T(8,128)(2,1)S(1)} %get-tuple-element.50), channel_id=1, source_target_pairs={{0,32},{8,40},{16,48},{24,56},{32,0},{40,8},{48,16},{56,24},{64,96... | collective-permute-start | bytes 98312 | tf_op jit(solution)/shard_map/ppermute | solution.py:309
  87.6 4.2 %collective-permute-start.16 = (bf16[64,256]{1,0:T(8,128)(2,1)S(1)}, bf16[64,256]{1,0:T(8,128)(2,1)S(1)}, u32[]{:S(2)}, u32[]{:S(2)}) collective-permute-start(bf16[64,256]{1,0:T(8,128)(2,1)S(1)} %get-tuple-element.52), channel_id=1, source_target_pairs={{0,16},{8,24},{16,0},{24,8},{32,48},{40,56},{48,32},{56,40},{64,80... | collective-permute-start | bytes 98312 | tf_op jit(solution)/shard_map/ppermute | solution.py:309
  92.0 5.3 %collective-permute-start.17 = (bf16[128,256]{1,0:T(8,128)(2,1)S(1)}, bf16[128,256]{1,0:T(8,128)(2,1)S(1)}, u32[]{:S(2)}, u32[]{:S(2)}) collective-permute-start(bf16[128,256]{1,0:T(8,128)(2,1)S(1)} %get-tuple-element.55), channel_id=1, source_target_pairs={{0,8},{8,0},{16,24},{24,16},{32,40},{40,32},{48,56},{56,48},{64,72... | collective-permute-start | bytes 196616 | tf_op jit(solution)/shard_map/ppermute | solution.py:309
  92.1 5.2 %collective-permute-start.18 = (bf16[64,256]{1,0:T(8,128)(2,1)S(1)}, bf16[64,256]{1,0:T(8,128)(2,1)S(1)}, u32[]{:S(2)}, u32[]{:S(2)}) collective-permute-start(bf16[64,256]{1,0:T(8,128)(2,1)S(1)} %get-tuple-element.56), channel_id=1, source_target_pairs={{8,16},{24,32},{40,48},{56,64},{72,80},{88,96},{104,112},{120,128}... | collective-permute-start | bytes 98312 | tf_op jit(solution)/shard_map/ppermute | solution.py:315
  94.5 2.8 %collective-permute-start.19 = (bf16[64,256]{1,0:T(8,128)(2,1)S(1)}, bf16[64,256]{1,0:T(8,128)(2,1)S(1)}, u32[]{:S(2)}, u32[]{:S(2)}) collective-permute-start(bf16[64,256]{1,0:T(8,128)(2,1)S(1)} %get-tuple-element.57), channel_id=1, source_target_pairs={{1,2},{3,4},{5,6},{2,1},{4,3},{6,5},{9,10},{11,12},{13,14},{10,9},... | collective-permute-start | bytes 98312 | tf_op jit(solution)/shard_map/ppermute | solution.py:315
  96.0 1.6 %copy-start.4 = (bf16[1,1,2,2048,256]{4,3,2,1,0:T(8,128)(2,1)S(1)}, bf16[1,1,2,2048,256]{4,3,2,1,0:T(8,128)(2,1)}, u32[]{:S(2)}) copy-start(bf16[1,1,2,2048,256]{4,3,2,1,0:T(8,128)(2,1)} %param.11) | copy-start | bytes 6291460
  96.0 1.7 %copy-start.9 = (f32[32,1,1,2,2048]{4,3,2,1,0:T(2,128)S(1)}, f32[32,1,1,2,2048]{4,3,2,1,0:T(2,128)}, u32[]{:S(2)}) copy-start(f32[32,1,1,2,2048]{4,3,2,1,0:T(2,128)} %param.7) | copy-start | bytes 1572868
  99.8 2.1 %collective-permute-start.20 = (f32[32,128]{1,0:T(8,128)S(1)}, f32[32,128]{1,0:T(8,128)S(1)}, u32[]{:S(2)}, u32[]{:S(2)}) collective-permute-start(f32[32,128]{1,0:T(8,128)S(1)} %get-tuple-element.58), channel_id=1, source_target_pairs={{0,8},{8,0},{16,24},{24,16},{32,40},{40,32},{48,56},{56,48},{64,72... | collective-permute-start | bytes 49160 | tf_op jit(solution)/shard_map/ppermute | solution.py:309
  102.0 3.7 %collective-permute-start.21 = (f32[32,128]{1,0:T(8,128)S(1)}, f32[32,128]{1,0:T(8,128)S(1)}, u32[]{:S(2)}, u32[]{:S(2)}) collective-permute-start(f32[32,128]{1,0:T(8,128)S(1)} %add.42), channel_id=1, source_target_pairs={{0,16},{8,24},{16,0},{24,8},{32,48},{40,56},{48,32},{56,40},{64,80... | collective-permute-start | bytes 49160 | tf_op jit(solution)/shard_map/ppermute | solution.py:309
  105.7 5.5 %collective-permute-start.22 = (f32[32,128]{1,0:T(8,128)S(1)}, f32[32,128]{1,0:T(8,128)S(1)}, u32[]{:S(2)}, u32[]{:S(2)}) collective-permute-start(f32[32,128]{1,0:T(8,128)S(1)} %add.43), channel_id=1, source_target_pairs={{0,32},{8,40},{16,48},{24,56},{32,0},{40,8},{48,16},{56,24},{64,96... | collective-permute-start | bytes 49160 | tf_op jit(solution)/shard_map/ppermute | solution.py:309
  111.2 3.7 %collective-permute-start.23 = (f32[32,128]{1,0:T(8,128)S(1)}, f32[32,128]{1,0:T(8,128)S(1)}, u32[]{:S(2)}, u32[]{:S(2)}) collective-permute-start(f32[32,128]{1,0:T(8,128)S(1)} %add.44), channel_id=1, source_target_pairs={{0,64},{8,72},{16,80},{24,88},{32,96},{40,104},{48,112},{56,120},{... | collective-permute-start | bytes 49160 | tf_op jit(solution)/shard_map/ppermute | solution.py:309
  114.9 5.2 %collective-permute-start.24 = (f32[32,128]{1,0:T(8,128)S(1)}, f32[32,128]{1,0:T(8,128)S(1)}, u32[]{:S(2)}, u32[]{:S(2)}) collective-permute-start(f32[32,128]{1,0:T(8,128)S(1)} %add.45), channel_id=1, source_target_pairs={{0,128},{8,136},{16,144},{24,152},{32,160},{40,168},{48,176},{56,1... | collective-permute-start | bytes 49160 | tf_op jit(solution)/shard_map/ppermute | solution.py:309
  120.2 5.9 %collective-permute-start.25 = (f32[32,128]{1,0:T(8,128)S(1)}, f32[32,128]{1,0:T(8,128)S(1)}, u32[]{:S(2)}, u32[]{:S(2)}) collective-permute-start(f32[32,128]{1,0:T(8,128)S(1)} %add.46), channel_id=1, source_target_pairs={{0,1},{1,0},{2,3},{3,2},{4,5},{5,4},{6,7},{7,6},{8,9},{9,8},{10,11... | collective-permute-start | bytes 49160 | tf_op jit(solution)/shard_map/ppermute | solution.py:311
  126.1 5.9 %collective-permute-start.26 = (f32[32,128]{1,0:T(8,128)S(1)}, f32[32,128]{1,0:T(8,128)S(1)}, u32[]{:S(2)}, u32[]{:S(2)}) collective-permute-start(f32[32,128]{1,0:T(8,128)S(1)} %add.47), channel_id=1, source_target_pairs={{0,2},{1,3},{2,0},{3,1},{4,6},{5,7},{6,4},{7,5},{8,10},{9,11},{10,... | collective-permute-start | bytes 49160 | tf_op jit(solution)/shard_map/ppermute | solution.py:311
  132.0 7.6 %collective-permute-start.27 = (f32[32,128]{1,0:T(8,128)S(1)}, f32[32,128]{1,0:T(8,128)S(1)}, u32[]{:S(2)}, u32[]{:S(2)}) collective-permute-start(f32[32,128]{1,0:T(8,128)S(1)} %add.48.pa_ref), channel_id=1, source_target_pairs={{0,4},{1,5},{2,6},{3,7},{4,0},{5,1},{6,2},{7,3},{8,12},{9,13},{10,... | collective-permute-start | bytes 49160 | tf_op jit(solution)/shard_map/ppermute | solution.py:311
where the time goes:
time: 150 us; the launch traced here: 147 us
  starting transfers between devices  68.1 us (45%)
  waiting for transfers between devices  47 us (31%)
  Pallas kernels  22.2 us (15%)
  local copies, waits for them, and re-layouts  9.28 us (6%)
    ppermute x9, starting transfers between devices, partner(): return lax.ppermute(x, 'py', [(i, i ^ 1 << bit) for i in range(col_count)])  35.2 us
    ppermute x15, waiting for transfers between devices, partner(): lax.ppermute(x, 'px', [(i, i ^ 1 << level) for i in range(row_count)])  30.3 us
    ppermute x15, starting transfers between devices, partner(): lax.ppermute(x, 'px', [(i, i ^ 1 << level) for i in range(row_count)])  27.2 us
    pallas_call x38, Pallas kernels, call(): pl.pallas_call(kernel, out_shape=[jax.ShapeDtypeStruct(s, d) for s, d in...  22.2 us
    ppermute x9, waiting for transfers between devices, partner(): return lax.ppermute(x, 'py', [(i, i ^ 1 << bit) for i in range(col_count)])  15.6 us
    unnamed x20, local copies, waits for them, and re-layouts  8.89 us
    ppermute x4, starting transfers between devices, beyond(): return lax.ppermute(x, axis, pairs + [(j, i) for i, j in pairs])  5.65 us
  transfers between devices with their start and end apart: 28, of which 22 were waited for; matrix products, arithmetic and copies ran while one was open for 0% of the time, Pallas kernels for 4%

commit v1 on v0

v1 whole, which is shorter than its diff:
```python
import functools

import jax
import jax.numpy as jnp
from jax import lax
from jax.experimental import pallas as pl
from jax.experimental.pallas import tpu as pltpu
from jax.sharding import PartitionSpec as P

F32 = jnp.float32
BF16 = jnp.bfloat16
NT = (((1,), (1,)), ((), ()))
VM = pl.BlockSpec(memory_space=pltpu.VMEM)
SM = pl.BlockSpec(memory_space=pltpu.SMEM)

HEAD, LOAD = 214, 196


def call(kernel, outs, args, flops, smem=0, limit=24, after=(), out_spec=VM, scratch=()):
    size = sum(a.size * a.dtype.itemsize for a in args)
    args = list(args) + list(after)
    count, extra = len(args), len(after)

    def body(*refs):
        kernel(*refs[: count - extra], *refs[count:])

    return pl.pallas_call(
        body,
        out_shape=[jax.ShapeDtypeStruct(s, d) for s, d in outs],
        in_specs=[SM] * smem + [VM] * (count - smem),
        out_specs=[out_spec] * len(outs),
        scratch_shapes=list(scratch),
        cost_estimate=pl.CostEstimate(flops=flops, bytes_accessed=size, transcendentals=0),
        compiler_params=pltpu.CompilerParams(vmem_limit_bytes=limit * 2**20),
    )(*args)


def mul(x, gr, gi):
    h = x.shape[0] // 2
    re, im = x[:h], x[h:]
    first = jnp.dot(x, gr, preferred_element_type=F32)
    second = jnp.dot(jnp.concatenate([-im, re], 0), gi, preferred_element_type=F32)
    return first + second


def adj(x, gr, gi):
    h = x.shape[0] // 2
    re, im = x[:h], x[h:]
    first = lax.dot_general(x, gr, NT, preferred_element_type=F32)
    second = lax.dot_general(jnp.concatenate([im, -re], 0), gi, NT, preferred_element_type=F32)
    return first + second


def leaf_at(at, leaf):
    return pl.ds(pl.multiple_of(at * leaf, leaf), leaf)


def split(x):
    high = x.astype(BF16)
    return high, (x - high.astype(F32)).astype(BF16)


def piece(ref, info, side, leaf):
    return jnp.concatenate(
        [ref[:, leaf_at(info[2 * side + e], leaf)] for e in range(2)], 1
    )


def head_kernel(leaf, v_in, c_in, vb_ref, m_ref, v_ref, c_ref, v_sems, c_sems):
    cols, lines, _ = v_ref.shape
    count = v_sems.shape[0]
    step = lines // count
    width = step // 2 * leaf
    copies = []
    for at in range(count):
        some = slice(at * step, (at + 1) * step)
        cut = slice(at * width, (at + 1) * width)
        pair = [
            pltpu.make_async_copy(v_in.at[:, some], v_ref.at[:, some], v_sems.at[at]),
            pltpu.make_async_copy(c_in.at[:, cut], c_ref.at[:, cut], c_sems.at[at]),
        ]
        for copy in pair:
            copy.start()
        copies.append(pair)
    total = None
    for at in range(count):
        copies[at][0].wait()
        for row in range(at * step, (at + 1) * step):
            of, part = divmod(row, 2)
            vb_ref[part * cols : (part + 1) * cols, of * leaf : (of + 1) * leaf] = v_ref[
                :, row
            ].astype(BF16)
        copies[at][1].wait()
        cut = slice(at * width, (at + 1) * width)
        product = mul(vb_ref[:, cut], c_ref[0, cut], c_ref[1, cut])
        total = product if total is None else total + product
    m_ref[...] = total.astype(BF16)


def head(leaf, tall, squeeze):
    cols = tall.shape[0]
    unknowns, rank = squeeze.shape[1:]
    count = 4
    return pl.pallas_call(
        functools.partial(head_kernel, leaf),
        in_specs=[pl.BlockSpec(memory_space=pltpu.HBM)] * 2,
        out_specs=[VM] * 2,
        out_shape=[
            jax.ShapeDtypeStruct((2 * cols, unknowns), BF16),
            jax.ShapeDtypeStruct((2 * cols, rank), BF16),
        ],
        scratch_shapes=[
            pltpu.VMEM(tall.shape, F32),
            pltpu.VMEM(squeeze.shape, BF16),
            pltpu.SemaphoreType.DMA((count,)),
            pltpu.SemaphoreType.DMA((count,)),
        ],
        cost_estimate=pl.CostEstimate(
            flops=8 * cols * rank * unknowns,
            bytes_accessed=tall.size * 4 + squeeze.size * 2,
            transcendentals=0,
        ),
        compiler_params=pltpu.CompilerParams(vmem_limit_bytes=HEAD * 2**18),
    )(tall, squeeze)


def load_kernel(f_in, o_ref, sem):
    copy = pltpu.make_async_copy(f_in, o_ref, sem)
    copy.start()
    copy.wait()


def load(sections):
    return pl.pallas_call(
        load_kernel,
        in_specs=[pl.BlockSpec(memory_space=pltpu.HBM)],
        out_specs=VM,
        out_shape=jax.ShapeDtypeStruct(sections.shape, BF16),
        scratch_shapes=[pltpu.SemaphoreType.DMA],
        cost_estimate=pl.CostEstimate(
            flops=0, bytes_accessed=2 * sections.size, transcendentals=0
        ),
        compiler_params=pltpu.CompilerParams(vmem_limit_bytes=LOAD * 2**18),
    )(sections)


def pick_kernel(leaf, info, vb_ref, *outs):
    for at, o_ref in enumerate(outs):
        o_ref[...] = piece(vb_ref, info, info[8 + at], leaf)


def basis_kernel(leaf, v_ref, high_ref, low_ref, p_ref):
    cols = v_ref.shape[0]
    for row in range(v_ref.shape[1]):
        of, part = divmod(row, 2)
        place = (slice(part * cols, (part + 1) * cols), slice(of * leaf, (of + 1) * leaf))
        high, low = split(v_ref[:, row])
        high_ref[place] = high
        low_ref[place] = low
    high = high_ref[...]
    cross = lax.dot_general(high, low_ref[...], NT, preferred_element_type=F32)
    s = lax.dot_general(high, high, NT, preferred_element_type=F32) + cross + cross.T
    p_ref[...] = packed(s, cols)


def packed(s, cols):
    below = lax.broadcasted_iota(jnp.int32, (cols, cols), 0) >= lax.broadcasted_iota(
        jnp.int32, (cols, cols), 1
    )
    re = s[:cols, :cols] + s[cols:, cols:]
    return jnp.where(below, re, s[cols:, :cols] - s[:cols, cols:])


def own_kernel(level, adjoint, s_ref, f_ref, o_ref):
    rows = o_ref.shape[0]
    product = adj if adjoint else mul
    o_ref[...] = product(s_ref[:rows], f_ref[level, 0, 0], f_ref[level, 0, 1])


def up_kernel(level, own_ref, r_ref, f_ref, *rest):
    rows = own_ref.shape[0]
    o_ref = rest[-1]
    state = own_ref[...] + mul(r_ref[:rows], f_ref[level, 1, 0], f_ref[level, 1, 1])
    o_ref[:rows] = state.astype(BF16)
    if len(rest) > 1:
        o_ref[rows:] = rest[0][...]


def leaves_kernel(leaf, adjoint, x_ref, b_ref, o_ref):
    product = adj if adjoint else mul
    for at in range(b_ref.shape[1]):
        cut = slice(at * leaf, (at + 1) * leaf)
        o_ref[:, cut] = product(x_ref[:, cut], b_ref[0, at], b_ref[1, at])


def sides_kernel(leaf, info, near_ref, ra_ref, rb_ref, rc_ref, rd_ref, b_ref, o_ref):
    rows = near_ref.shape[0]
    o_ref[...] = near_ref[...]
    for at, ref in enumerate((ra_ref, rb_ref, rc_ref, rd_ref)):
        side = info[8 + at]
        x = ref[ref.shape[0] - rows :]
        term = mul(x, b_ref[side, 0], b_ref[side, 1])
        for e in range(2):
            o_ref[:, leaf_at(info[2 * side + e], leaf)] += term[:, e * leaf : (e + 1) * leaf]


def field_kernel(level, own_ref, r_ref, f_ref, near_ref, e_ref, y_ref, yb_ref, g_ref, m_ref):
    rows = own_ref.shape[0]
    state = own_ref[...] + mul(r_ref[:rows], f_ref[level, 1, 0], f_ref[level, 1, 1])
    y = near_ref[...] + mul(state.astype(BF16), e_ref[0], e_ref[1])
    y_ref[...] = y
    yb = y.astype(BF16)
    yb_ref[...] = yb
    g = adj(yb, e_ref[0], e_ref[1]).astype(BF16)
    g_ref[...] = g
    m_ref[...] = adj(g, f_ref[level, 1, 0], f_ref[level, 1, 1]).astype(BF16)


def shape_kernel(leaf, y_ref, o_ref):
    cols = o_ref.shape[0]
    for row in range(o_ref.shape[1]):
        of, part = divmod(row, 2)
        o_ref[:, row] = y_ref[part * cols : (part + 1) * cols, of * leaf : (of + 1) * leaf]


def terms_kernel(leaf, info, yb_ref, b_ref, *outs):
    for at, o_ref in enumerate(outs):
        side = info[8 + at]
        x = piece(yb_ref, info, side, leaf)
        o_ref[...] = adj(x, b_ref[side, 0], b_ref[side, 1]).astype(BF16)


def down_kernel(level, own_ref, r_ref, f_ref, *rest):
    rows = own_ref.shape[0]
    g_ref, m_ref = rest[-2:]
    g = (own_ref[...] + r_ref[:rows].astype(F32)).astype(BF16)
    g_ref[...] = g
    m_ref[:rows] = adj(g, f_ref[level, 1, 0], f_ref[level, 1, 1]).astype(BF16)
    if len(rest) > 2:
        m_ref[rows:] = rest[0][...]


def close_kernel(
    leaf, info, near_ref, own_ref, ra_ref, rb_ref, rc_ref, rd_ref, c_ref, vh_ref, vl_ref, vv_ref,
    zh_ref, zl_ref, p_ref, z_ref
):
    rows = own_ref.shape[0]
    cols = rows // 2
    g = (own_ref[...] + ra_ref[:rows].astype(F32)).astype(BF16)
    z_ref[...] = near_ref[...] + adj(g, c_ref[0], c_ref[1])
    for at, ref in enumerate((ra_ref, rb_ref, rc_ref, rd_ref)):
        side = info[8 + at]
        low = ref.shape[0] - rows
        for e in range(2):
            z_ref[:, leaf_at(info[2 * side + e], leaf)] += ref[
                low:, e * leaf : (e + 1) * leaf
            ].astype(F32)
    high, low = split(z_ref[...])
    zh_ref[...] = high
    zl_ref[...] = low
    many = jnp.concatenate([high, low, vh_ref[...], vl_ref[...]], 0)
    s = lax.dot_general(high, many, NT, preferred_element_type=F32)
    cross = s[:, rows : 2 * rows]
    zz = s[:, :rows] + cross + cross.T
    zv = s[:, 2 * rows : 3 * rows] + s[:, 3 * rows :]
    zv += lax.dot_general(low, vh_ref[...], NT, preferred_element_type=F32)
    p_ref[...] = jnp.concatenate(
        [
            packed(zz, cols),
            vv_ref[...],
            zv[:cols, :cols] + zv[cols:, cols:],
            zv[cols:, :cols] - zv[:cols, cols:],
        ],
        1,
    )


def spread_kernel(*refs):
    o_ref = refs[-1]
    total = sum(parts_of(refs[:-1]))
    for at in range(o_ref.shape[0]):
        o_ref[at] = total


def parts_of(refs):
    return [ref[at] for ref in refs for at in range(ref.shape[0])]


def exact_dot(a, b, dims=(((1,), (0,)), ((), ()))):
    return lax.dot_general(a, b, dims, preferred_element_type=F32, precision=lax.Precision.HIGHEST)


def real_form(re, im):
    return jnp.concatenate(
        [jnp.concatenate([re, im], 1), jnp.concatenate([-im, re], 1)], 0
    )


def inverse_factor(gram):
    size, step = gram.shape[0], 8
    eye = (
        lax.broadcasted_iota(jnp.int32, (size, size), 0)
        == lax.broadcasted_iota(jnp.int32, (size, size), 1)
    ).astype(F32)
    wide = jnp.concatenate([gram, eye], 1)
    width = wide.shape[1]
    blocks = [wide[step * j : step * (j + 1)] for j in range(size // step)]
    sub = lax.broadcasted_iota(jnp.int32, (step, width), 0)
    done = []
    for at in range(size // step):
        left = [
            [jnp.broadcast_to(b[:, at * step + p : at * step + p + 1], (step, width)) for b in blocks[at:]]
            for p in range(step)
        ]
        pivot = [
            [jnp.broadcast_to(left[q][0][p : p + 1], (step, width)) for q in range(p + 1)]
            for p in range(step)
        ]
        lines = [jnp.broadcast_to(blocks[at][p : p + 1], (step, width)) for p in range(step)]
        result = jnp.zeros((step, width), F32)
        updates = [None] * len(left[0])
        for p in range(step):
            inverse = 1.0 / pivot[p][p]
            result = jnp.where(sub == p, lines[p] * lax.rsqrt(pivot[p][p]), result)
            scaled = lines[p] * inverse
            for q in range(p + 1, step):
                ratio = pivot[q][p] * inverse
                lines[q] = lines[q] - ratio * lines[p]
                for r in range(p + 1, q + 1):
                    pivot[q][r] = pivot[q][r] - ratio * pivot[r][p]
                for i in range(1, len(left[q])):
                    left[q][i] = left[q][i] - ratio * left[p][i]
            for i in range(1, len(updates)):
                term = left[p][i] * scaled
                updates[i] = term if p == 0 else updates[i] + term
        done.append(result)
        for i in range(1, len(updates)):
            blocks[at + i] = blocks[at + i] - updates[i]
    return jnp.concatenate(done, 0)[:, size:]


def finish_kernel(leaf, total, p_ref, zh_ref, zl_ref, vh_ref, vl_ref, o_ref, buffer, sems):
    p = sum(parts_of([p_ref])) * (1.0 / total)
    cols = p.shape[0]
    lower = lax.broadcasted_iota(jnp.int32, (cols, cols), 0)
    upper = lax.broadcasted_iota(jnp.int32, (cols, cols), 1)
    eye = (lower == upper).astype(F32)

    def turned(a):
        return exact_dot(a, eye, (((0,), (0,)), ((), ())))

    def hermitian(t):
        strict = jnp.where(lower > upper, t, 0.0)
        above = jnp.where(lower < upper, t, 0.0)
        re = jnp.where(lower >= upper, t, 0.0) + turned(strict)
        return real_form(re, above - turned(above))

    zz = hermitian(p[:, :cols])
    vv = hermitian(p[:, cols : 2 * cols])
    h = real_form(p[:, 2 * cols : 3 * cols], p[:, 3 * cols :])
    nt = (((1,), (1,)), ((), ()))
    middle = exact_dot(h, vv) - 2.0 * h
    gram = zz + exact_dot(middle, h, nt)
    inverse = inverse_factor(gram)
    w = exact_dot(inverse, h)
    l1, l2 = inverse[:, :cols], inverse[:, cols:]
    w1, w2 = w[:, :cols], w[:, cols:]
    mix = jnp.concatenate(
        [
            jnp.concatenate([l1, -l2, -w1, w2], 1),
            jnp.concatenate([l2, l1, -w2, -w1], 1),
        ],
        0,
    )
    mix_high, mix_low = split(mix)
    mix = jnp.concatenate([mix_high, mix_high, mix_low], 1)
    rows = 2 * cols
    count, _, lines, _ = buffer.shape
    width = lines // 2 * leaf
    copies = []
    for at in range(count):
        cut = slice(at * width, (at + 1) * width)
        high = [zh_ref[:, cut], vh_ref[:, cut]]
        x = jnp.concatenate(high + [zl_ref[:, cut], vl_ref[:, cut]] + high, 0)
        out = jnp.dot(mix, x, preferred_element_type=F32)
        for line in range(lines):
            of, part = divmod(line, 2)
            buffer[at, :, line] = out[part * rows : (part + 1) * rows, of * leaf : (of + 1) * leaf]
        copy = pltpu.make_async_copy(
            buffer.at[at], o_ref.at[:, at * lines : (at + 1) * lines], sems.at[at]
        )
        copy.start()
        copies.append(copy)
    for copy in copies:
        copy.wait()


def per_device(v_block, edge_leaves, self_blocks, side_blocks, compress, expand, factors):
    cols = v_block.shape[0]
    unknowns = v_block.shape[4]
    leaves = self_blocks.shape[3]
    leaf = self_blocks.shape[4]
    levels = factors.shape[2]
    rank = compress.shape[4]
    rows = 2 * cols
    row_count = lax.axis_size("px")
    col_count = lax.axis_size("py")
    row_bits = row_count.bit_length() - 1
    total = 2 * unknowns * row_count * col_count
    row_at = lax.axis_index("px")
    col_at = lax.axis_index("py")
    selfs = self_blocks.reshape(self_blocks.shape[2:])
    sides = side_blocks.reshape(side_blocks.shape[2:])
    squeeze = compress.reshape(compress.shape[2:])
    spread = expand.reshape(expand.shape[2:])
    sections = factors.reshape(factors.shape[2:])
    own_leaves = lax.dynamic_slice(edge_leaves, (row_at, col_at, 0, 0), (1, 1, 4, 2)).reshape(8)
    odd_row, odd_col = row_at % 2, col_at % 2
    order = jnp.stack([1 - odd_row, odd_row, 3 - odd_col, 2 + odd_col]).astype(jnp.int32)
    info = jnp.concatenate([own_leaves, order])
    tall = v_block.reshape(cols, 2, leaves, leaf).transpose(0, 2, 1, 3).reshape(cols, -1, leaf)

    def partner(x, level):
        if level < row_bits:
            return lax.ppermute(x, "px", [(i, i ^ 1 << level) for i in range(row_count)])
        bit = level - row_bits
        return lax.ppermute(x, "py", [(i, i ^ 1 << bit) for i in range(col_count)])

    def beyond(x, axis, count):
        pairs = [(i, i + 1) for i in range(1, count - 1, 2)]
        return lax.ppermute(x, axis, pairs + [(j, i) for i, j in pairs])

    small = ((rows, rank), BF16)
    double = ((2 * rows, rank), BF16)
    wide = ((rows, rank), F32)
    step_flops = 8 * cols * rank * rank
    patch_flops = 8 * cols * rank * unknowns
    leaf_flops = 8 * cols * leaf * unknowns

    half, sent = head(leaf, tall, squeeze)
    pieces = call(functools.partial(pick_kernel, leaf), [small] * 4, [info, half], 0, smem=1)
    got = {}
    for level in range(levels):
        arrived = partner(sent, level)
        after = []
        if level == 0:
            sections = load(sections)
        if level == 2:
            got["a"] = partner(pieces[0], 0)
            got["b"] = beyond(pieces[1], "px", row_count)
        if level == 3:
            got["d"] = beyond(pieces[3], "py", col_count)
            after = [got["a"], got["b"]]
        if level == 4:
            (near,) = call(
                functools.partial(leaves_kernel, leaf, False),
                [((rows, unknowns), F32)],
                [half, selfs],
                leaf_flops,
            )
            after = [got["d"], near]
        if level == row_bits:
            got["c"] = arrived
        if level == row_bits + 1:
            (near,) = call(
                functools.partial(sides_kernel, leaf),
                [((rows, unknowns), F32)],
                [info, near, got["a"], got["b"], got["c"], got["d"], sides],
                4 * step_flops,
                smem=1,
            )
            after = [near, spread]
        (own,) = call(
            functools.partial(own_kernel, level, False),
            [wide],
            [sent, sections],
            step_flops,
            after=after,
        )
        if level < levels - 1:
            extra = [pieces[2]] if level == row_bits - 1 else []
            (sent,) = call(
                functools.partial(up_kernel, level),
                [double if extra else small],
                [own, arrived, sections] + extra,
                step_flops,
            )
    y, yb, g, message = call(
        functools.partial(field_kernel, levels - 1),
        [((rows, unknowns), F32), ((rows, unknowns), BF16), small, small],
        [own, arrived, sections, near, spread],
        2 * patch_flops,
    )
    terms = call(
        functools.partial(terms_kernel, leaf), [small] * 4, [info, yb, sides], 4 * step_flops, smem=1
    )
    for level in range(levels - 1, -1, -1):
        arrived = partner(message, level)
        after = []
        if level == levels - 1:
            (shaped,) = call(
                functools.partial(shape_kernel, leaf), [((cols, 2 * leaves, leaf), F32)], [y], 0
            )
            after = list(terms)
        if level == levels - 2:
            (z_near,) = call(
                functools.partial(leaves_kernel, leaf, True),
                [((rows, unknowns), F32)],
                [yb, selfs],
                leaf_flops,
            )
            got["b"] = beyond(terms[1], "px", row_count)
            after = [z_near]
        if level == row_bits:
            got["c"] = arrived
            got["d"] = beyond(terms[3], "py", col_count)
            after = [got["b"]]
        if level == row_bits - 1:
            after = [got["d"]]
        if level == 3:
            v_high, v_low, vv = call(
                functools.partial(basis_kernel, leaf),
                [((rows, unknowns), BF16), ((rows, unknowns), BF16), ((cols, cols), F32)],
                [tall],
                leaf_flops,
            )
            after = [v_high, v_low, vv]
        if level == 1:
            after = [squeeze]
        (own,) = call(
            functools.partial(own_kernel, level, True),
            [wide],
            [g, sections],
            step_flops,
            after=after,
        )
        if level > 0:
            extra = [terms[0]] if level == 1 else [terms[2]] if level == row_bits + 1 else []
            g, message = call(
                functools.partial(down_kernel, level - 1),
                [small, double if extra else small],
                [own, arrived, sections] + extra,
                step_flops,
            )
    z_high, z_low, part = call(
        functools.partial(close_kernel, leaf),
        [((rows, unknowns), BF16), ((rows, unknowns), BF16), ((cols, 4 * cols), F32)],
        [info, z_near, own, arrived, got["b"], got["c"], got["d"], squeeze, v_high, v_low, vv],
        patch_flops,
        smem=1,
        scratch=[pltpu.VMEM((rows, unknowns), F32)],
    )
    part = part.reshape(1, cols, 4 * cols)
    chips = row_count // 2
    (part,) = call(
        spread_kernel, [((chips, cols, 4 * cols), F32)], [part, partner(part, 0)], 0
    )
    groups = [[2 * i + core for i in range(chips)] for core in range(2)]
    part = lax.all_to_all(part, "px", 0, 0, axis_index_groups=groups, tiled=True)
    (part,) = call(spread_kernel, [((col_count, cols, 4 * cols), F32)], [part], 0)
    part = lax.all_to_all(part, "py", 0, 0, tiled=True)
    lines = 8
    (basis,) = call(
        functools.partial(finish_kernel, leaf, total),
        [((rows, 2 * leaves, leaf), F32)],
        [part, z_high, z_low, v_high, v_low],
        8 * rows * rows * unknowns,
        out_spec=pl.BlockSpec(memory_space=pl.ANY),
        scratch=[
            pltpu.VMEM((2 * leaves // lines, rows, lines, leaf), F32),
            pltpu.SemaphoreType.DMA((2 * leaves // lines,)),
        ],
    )

    def patch_form(a):
        count = a.shape[0]
        a = a.reshape(count, leaves, 2, leaf).transpose(0, 2, 1, 3)
        return a.reshape(count, 1, 1, 2, unknowns)

    return patch_form(shaped), patch_form(basis)


def solution(mesh):
    in_specs = (
        P(None, "px", "py", None, None),
        P(),
        P("px", "py", None, None, None, None),
        P("px", "py", None, None, None, None),
        P("px", "py", None, None, None),
        P("px", "py", None, None, None),
        P("px", "py", None, None, None, None, None),
    )
    out_specs = (P(None, "px", "py", None, None), P(None, "px", "py", None, None))
    return jax.shard_map(
        per_device, mesh=mesh, in_specs=in_specs, out_specs=out_specs, check_vma=False
    )
```

time: 150 us -> 133 us (0.89); the launches traced: 147 us -> 132 us
  starting transfers between devices: 68.1 us -> 49.1 us
  blocking collectives: 0 us -> 14 us
  waiting for transfers between devices: 47 us -> 39.5 us
  local copies, waits for them, and re-layouts: 9.28 us -> 2.61 us
  Pallas kernels: 22.2 us -> 26.1 us
    all_to_all x0 -> x1, blocking collectives: none -> 14 us  [per_device(): lax.all_to_all(part, 'px', 0, 0, axis_index_groups=groups, tiled=True)]
    ppermute x9 -> x6, starting transfers between devices: 35.2 us -> 21.5 us  [partner(): return lax.ppermute(x, 'py', [(i, i ^ 1 << bit) for i in range(col_count)])]
    ppermute x15 -> x12, waiting for transfers between devices: 30.3 us -> 18.1 us  [partner(): lax.ppermute(x, 'px', [(i, i ^ 1 << level) for i in range(row_count)])]
    ppermute x15 -> x12, starting transfers between devices: 27.2 us -> 16 us  [partner(): lax.ppermute(x, 'px', [(i, i ^ 1 << level) for i in range(row_count)])]
    all_to_all x0 -> x1, waiting for transfers between devices: none -> 7.8 us  [per_device(): part = lax.all_to_all(part, 'py', 0, 0, tiled=True)]
    unnamed x20 -> x18, local copies, waits for them, and re-layouts: 8.89 us -> 2.22 us
    all_to_all x0 -> x1, starting transfers between devices: none -> 4.96 us  [per_device(): part = lax.all_to_all(part, 'py', 0, 0, tiled=True)]
    ppermute x9 -> x6, waiting for transfers between devices: 15.6 us -> 11 us  [partner(): return lax.ppermute(x, 'py', [(i, i ^ 1 << bit) for i in range(col_count)])]
  transfers between devices with their start and end apart: 28 -> 23, of which waited for: 22 -> 16; matrix products, arithmetic and copies ran while one was open for 0% -> 0% of each run, Pallas kernels for 4% -> 9%
where the time goes in v1:
time: 133 us; the launch traced here: 132 us
  starting transfers between devices  49.1 us (37%)
  waiting for transfers between devices  39.5 us (30%)
  Pallas kernels  26.1 us (20%)
  blocking collectives  14 us (11%)
  local copies, waits for them, and re-layouts  2.61 us (2%)
    ppermute x6, starting transfers between devices, partner(): return lax.ppermute(x, 'py', [(i, i ^ 1 << bit) for i in range(col_count)])  21.5 us
    pallas_call x42, Pallas kernels, call(): pl.pallas_call(body, out_shape=[jax.ShapeDtypeStruct(s, d) for s, d in ou...  21.4 us
    ppermute x12, waiting for transfers between devices, partner(): lax.ppermute(x, 'px', [(i, i ^ 1 << level) for i in range(row_count)])  18.1 us
    ppermute x12, starting transfers between devices, partner(): lax.ppermute(x, 'px', [(i, i ^ 1 << level) for i in range(row_count)])  16 us
    all_to_all x1, blocking collectives, per_device(): lax.all_to_all(part, 'px', 0, 0, axis_index_groups=groups, tiled=True)  14 us
    ppermute x6, waiting for transfers between devices, partner(): return lax.ppermute(x, 'py', [(i, i ^ 1 << bit) for i in range(col_count)])  11 us
    all_to_all x1, waiting for transfers between devices, per_device(): part = lax.all_to_all(part, 'py', 0, 0, tiled=True)  7.8 us
    ppermute x4, starting transfers between devices, beyond(): return lax.ppermute(x, axis, pairs + [(j, i) for i, j in pairs])  6.7 us
  transfers between devices with their start and end apart: 23, of which 16 were waited for; matrix products, arithmetic and copies ran while one was open for 0% of the time, Pallas kernels for 9%

profile of v1, /device:TPU:8, one launch (start us, length us, event | category | flops | bytes accessed | tf_op | source)
XLA Modules:
  0.0 132.3 jit_solution(14696092499525662227)
XLA Ops:
  0.6 2.5 %shard_map.86 = (bf16[64,2048]{1,0:T(8,128)(2,1)S(1)}, bf16[64,256]{1,0:T(8,128)(2,1)S(1)}) custom-call(f32[32,32,128]{2,1,0:T(8,128)} %bitcast.34, bf16[2,2048,256]{2,1,0:T(8,128)(2,1)} %bitcast.25), custom_call_target="tpu_custom_call" | custom-call | flops 134217728 | bytes 2621440 | tf_op jit(solution)/shard_map/pallas_call | solution.py:104
  3.2 2.2 %shard_map.87.refs_1_.refs_2_ = bf16[8,2,2,256,256]{4,3,2,1,0:T(8,128)(2,1)S(1)} custom-call(bf16[8,2,2,256,256]{4,3,2,1,0:T(8,128)(2,1)} %bitcast.38), custom_call_target="tpu_custom_call" | custom-call | bytes 4194304 | tf_op jit(solution)/shard_map/pallas_call | solution.py:134
  5.8 2.3 %collective-permute-start.1 = (bf16[64,256]{1,0:T(8,128)(2,1)S(1)}, bf16[64,256]{1,0:T(8,128)(2,1)S(1)}, u32[]{:S(2)}, u32[]{:S(2)}) collective-permute-start(bf16[64,256]{1,0:T(8,128)(2,1)S(1)} %shard_map.89.refs_0_), channel_id=1, source_target_pairs={{0,16},{8,24},{16,0},{24,8},{32,48},{40,56},{48,32},{56,40},{64,80... | collective-permute-start | bytes 98312 | tf_op jit(solution)/shard_map/ppermute | solution.py:425
  8.2 1.9 %collective-permute-done.1.refs_1_ = bf16[64,256]{1,0:T(8,128)(2,1)S(1)} collective-permute-done((bf16[64,256]{1,0:T(8,128)(2,1)S(1)}, bf16[64,256]{1,0:T(8,128)(2,1)S(1)}, u32[]{:S(2)}, u32[]{:S(2)}) %collective-permute-start.1) | collective-permute-done | bytes 32800 | tf_op jit(solution)/shard_map/ppermute | solution.py:425
  10.3 2.1 %collective-permute-start.2 = (bf16[64,256]{1,0:T(8,128)(2,1)S(1)}, bf16[64,256]{1,0:T(8,128)(2,1)S(1)}, u32[]{:S(2)}, u32[]{:S(2)}) collective-permute-start(bf16[64,256]{1,0:T(8,128)(2,1)S(1)} %shard_map.91.refs_0_), channel_id=1, source_target_pairs={{0,32},{8,40},{16,48},{24,56},{32,0},{40,8},{48,16},{56,24},{64,96... | collective-permute-start | bytes 98312 | tf_op jit(solution)/shard_map/ppermute | solution.py:425
  12.8 0.6 shard_map.94
  13.5 3.3 %collective-permute-start.4 = (bf16[64,256]{1,0:T(8,128)(2,1)S(1)}, bf16[64,256]{1,0:T(8,128)(2,1)S(1)}, u32[]{:S(2)}, u32[]{:S(2)}) collective-permute-start(bf16[64,256]{1,0:T(8,128)(2,1)S(1)} %get-tuple-element.39), channel_id=1, source_target_pairs={{8,16},{24,32},{40,48},{56,64},{72,80},{88,96},{104,112},{120,128}... | collective-permute-start | bytes 98312 | tf_op jit(solution)/shard_map/ppermute | solution.py:431
  16.8 2.2 %copy-done.2 = bf16[8,2,2,256,256]{4,3,2,1,0:T(8,128)(2,1)S(1)} copy-done((bf16[8,2,2,256,256]{4,3,2,1,0:T(8,128)(2,1)S(1)}, bf16[8,2,2,256,256]{4,3,2,1,0:T(8,128)(2,1)}, u32[]{:S(2)}) %copy-start.2) | copy-done | bytes 4194328
  19.3 1.6 %collective-permute-start.5 = (bf16[64,256]{1,0:T(8,128)(2,1)S(1)}, bf16[64,256]{1,0:T(8,128)(2,1)S(1)}, u32[]{:S(2)}, u32[]{:S(2)}) collective-permute-start(bf16[64,256]{1,0:T(8,128)(2,1)S(1)} %shard_map.93.refs_0_), channel_id=1, source_target_pairs={{0,64},{8,72},{16,80},{24,88},{32,96},{40,104},{48,112},{56,120},{... | collective-permute-start | bytes 98312 | tf_op jit(solution)/shard_map/ppermute | solution.py:425
  20.9 0.8 collective-permute-start.6
  21.9 1.4 %collective-permute-done.5.refs_1_ = bf16[64,256]{1,0:T(8,128)(2,1)S(1)} collective-permute-done((bf16[64,256]{1,0:T(8,128)(2,1)S(1)}, bf16[64,256]{1,0:T(8,128)(2,1)S(1)}, u32[]{:S(2)}, u32[]{:S(2)}) %collective-permute-start.5) | collective-permute-done | bytes 32800 | tf_op jit(solution)/shard_map/ppermute | solution.py:425
  23.5 3.1 %collective-permute-start.7 = (bf16[64,256]{1,0:T(8,128)(2,1)S(1)}, bf16[64,256]{1,0:T(8,128)(2,1)S(1)}, u32[]{:S(2)}, u32[]{:S(2)}) collective-permute-start(bf16[64,256]{1,0:T(8,128)(2,1)S(1)} %shard_map.96.refs_0_), channel_id=1, source_target_pairs={{0,128},{8,136},{16,144},{24,152},{32,160},{40,168},{48,176},{56,1... | collective-permute-start | bytes 98312 | tf_op jit(solution)/shard_map/ppermute | solution.py:425
  27.2 1.8 %collective-permute-done.7.refs_1_ = bf16[64,256]{1,0:T(8,128)(2,1)S(1)} collective-permute-done((bf16[64,256]{1,0:T(8,128)(2,1)S(1)}, bf16[64,256]{1,0:T(8,128)(2,1)S(1)}, u32[]{:S(2)}, u32[]{:S(2)}) %collective-permute-start.7) | collective-permute-done | bytes 32800 | tf_op jit(solution)/shard_map/ppermute | solution.py:425
  29.2 3.9 %collective-permute-start.8 = (bf16[128,256]{1,0:T(8,128)(2,1)S(1)}, bf16[128,256]{1,0:T(8,128)(2,1)S(1)}, u32[]{:S(2)}, u32[]{:S(2)}) collective-permute-start(bf16[128,256]{1,0:T(8,128)(2,1)S(1)} %shard_map.99.refs_0_), channel_id=1, source_target_pairs={{0,1},{1,0},{2,3},{3,2},{4,5},{5,4},{6,7},{7,6},{8,9},{9,8},{10,11... | collective-permute-start | bytes 196616 | tf_op jit(solution)/shard_map/ppermute | solution.py:427
  33.3 2.1 %collective-permute-done.8.refs_1_.refs_4_ = bf16[128,256]{1,0:T(8,128)(2,1)S(1)} collective-permute-done((bf16[128,256]{1,0:T(8,128)(2,1)S(1)}, bf16[128,256]{1,0:T(8,128)(2,1)S(1)}, u32[]{:S(2)}, u32[]{:S(2)}) %collective-permute-start.8) | collective-permute-done | bytes 65568 | tf_op jit(solution)/shard_map/ppermute | solution.py:427
  35.5 4.9 %collective-permute-start.9 = (bf16[64,256]{1,0:T(8,128)(2,1)S(1)}, bf16[64,256]{1,0:T(8,128)(2,1)S(1)}, u32[]{:S(2)}, u32[]{:S(2)}) collective-permute-start(bf16[64,256]{1,0:T(8,128)(2,1)S(1)} %shard_map.101.refs_0_), channel_id=1, source_target_pairs={{0,2},{1,3},{2,0},{3,1},{4,6},{5,7},{6,4},{7,5},{8,10},{9,11},{10,... | collective-permute-start | bytes 98312 | tf_op jit(solution)/shard_map/ppermute | solution.py:427
  40.4 0.9 shard_map.102.refs_2_.refs_3_
  41.5 0.8 collective-permute-done.9.refs_1_
  42.5 3.7 %collective-permute-start.10 = (bf16[64,256]{1,0:T(8,128)(2,1)S(1)}, bf16[64,256]{1,0:T(8,128)(2,1)S(1)}, u32[]{:S(2)}, u32[]{:S(2)}) collective-permute-start(bf16[64,256]{1,0:T(8,128)(2,1)S(1)} %shard_map.104.refs_0_), channel_id=1, source_target_pairs={{0,4},{1,5},{2,6},{3,7},{4,0},{5,1},{6,2},{7,3},{8,12},{9,13},{10,... | collective-permute-start | bytes 98312 | tf_op jit(solution)/shard_map/ppermute | solution.py:427
  46.3 4.1 %collective-permute-done.10.refs_1_ = bf16[64,256]{1,0:T(8,128)(2,1)S(1)} collective-permute-done((bf16[64,256]{1,0:T(8,128)(2,1)S(1)}, bf16[64,256]{1,0:T(8,128)(2,1)S(1)}, u32[]{:S(2)}, u32[]{:S(2)}) %collective-permute-start.10) | collective-permute-done | bytes 32800 | tf_op jit(solution)/shard_map/ppermute | solution.py:427
  50.4 1.6 %shard_map.106 = (f32[64,2048]{1,0:T(8,128)S(1)}, bf16[64,2048]{1,0:T(8,128)(2,1)S(1)}, bf16[64,256]{1,0:T(8,128)(2,1)S(1)}, bf16[64,256]{1,0:T(8,128)(2,1)S(1)}) custom-call(f32[64,256]{1,0:T(8,128)S(1)} %shard_map.105.refs_0_, bf16[64,256]{1,0:T(8,128)(2,1)S(1)} %collective-permute-done.10.refs_1_, bf16[8,2,2,256,256]{4,3,2,1,0:T(8,128)(2,1)S(1)} %copy-done.3, ...), custom_call_target="tpu_custom_call" | custom-call | flops 268435456 | bytes 6914048 | tf_op jit(solution)/shard_map/pallas_call | solution.py:27
  52.0 3.7 %collective-permute-start.11 = (bf16[64,256]{1,0:T(8,128)(2,1)S(1)}, bf16[64,256]{1,0:T(8,128)(2,1)S(1)}, u32[]{:S(2)}, u32[]{:S(2)}) collective-permute-start(bf16[64,256]{1,0:T(8,128)(2,1)S(1)} %get-tuple-element.49), channel_id=1, source_target_pairs={{0,4},{1,5},{2,6},{3,7},{4,0},{5,1},{6,2},{7,3},{8,12},{9,13},{10,... | collective-permute-start | bytes 98312 | tf_op jit(solution)/shard_map/ppermute | solution.py:427
  55.6 1.0 shard_map.109
  56.8 3.1 %collective-permute-done.11.refs_1_ = bf16[64,256]{1,0:T(8,128)(2,1)S(1)} collective-permute-done((bf16[64,256]{1,0:T(8,128)(2,1)S(1)}, bf16[64,256]{1,0:T(8,128)(2,1)S(1)}, u32[]{:S(2)}, u32[]{:S(2)}) %collective-permute-start.11) | collective-permute-done | bytes 32800 | tf_op jit(solution)/shard_map/ppermute | solution.py:427
  60.1 3.3 %collective-permute-start.12 = (bf16[64,256]{1,0:T(8,128)(2,1)S(1)}, bf16[64,256]{1,0:T(8,128)(2,1)S(1)}, u32[]{:S(2)}, u32[]{:S(2)}) collective-permute-start(bf16[64,256]{1,0:T(8,128)(2,1)S(1)} %get-tuple-element.51), channel_id=1, source_target_pairs={{0,2},{1,3},{2,0},{3,1},{4,6},{5,7},{6,4},{7,5},{8,10},{9,11},{10,... | collective-permute-start | bytes 98312 | tf_op jit(solution)/shard_map/ppermute | solution.py:427
  63.4 0.8 shard_map.108.refs_2_.refs_1_
  64.4 0.9 collective-permute-done.12.refs_1_
  65.5 2.1 %collective-permute-start.14 = (bf16[128,256]{1,0:T(8,128)(2,1)S(1)}, bf16[128,256]{1,0:T(8,128)(2,1)S(1)}, u32[]{:S(2)}, u32[]{:S(2)}) collective-permute-start(bf16[128,256]{1,0:T(8,128)(2,1)S(1)} %get-tuple-element.53), channel_id=1, source_target_pairs={{0,1},{1,0},{2,3},{3,2},{4,5},{5,4},{6,7},{7,6},{8,9},{9,8},{10,11... | collective-permute-start | bytes 196616 | tf_op jit(solution)/shard_map/ppermute | solution.py:427
  67.6 1.9 %collective-permute-start.13 = (bf16[64,256]{1,0:T(8,128)(2,1)S(1)}, bf16[64,256]{1,0:T(8,128)(2,1)S(1)}, u32[]{:S(2)}, u32[]{:S(2)}) collective-permute-start(bf16[64,256]{1,0:T(8,128)(2,1)S(1)} %get-tuple-element.46.refs_3_), channel_id=1, source_target_pairs={{8,16},{24,32},{40,48},{56,64},{72,80},{88,96},{104,112},{120,128}... | collective-permute-start | bytes 98312 | tf_op jit(solution)/shard_map/ppermute | solution.py:431
  69.5 0.7 collective-permute-start.15
  70.2 2.6 %collective-permute-done.13.refs_2_.refs_4_ = bf16[64,256]{1,0:T(8,128)(2,1)S(1)} collective-permute-done((bf16[64,256]{1,0:T(8,128)(2,1)S(1)}, bf16[64,256]{1,0:T(8,128)(2,1)S(1)}, u32[]{:S(2)}, u32[]{:S(2)}) %collective-permute-start.13) | collective-permute-done | bytes 32800 | tf_op jit(solution)/shard_map/ppermute | solution.py:431
  73.2 2.8 %collective-permute-start.16 = (bf16[64,256]{1,0:T(8,128)(2,1)S(1)}, bf16[64,256]{1,0:T(8,128)(2,1)S(1)}, u32[]{:S(2)}, u32[]{:S(2)}) collective-permute-start(bf16[64,256]{1,0:T(8,128)(2,1)S(1)} %get-tuple-element.55), channel_id=1, source_target_pairs={{0,128},{8,136},{16,144},{24,152},{32,160},{40,168},{48,176},{56,1... | collective-permute-start | bytes 98312 | tf_op jit(solution)/shard_map/ppermute | solution.py:425
  76.2 2.5 %collective-permute-done.16.refs_1_ = bf16[64,256]{1,0:T(8,128)(2,1)S(1)} collective-permute-done((bf16[64,256]{1,0:T(8,128)(2,1)S(1)}, bf16[64,256]{1,0:T(8,128)(2,1)S(1)}, u32[]{:S(2)}, u32[]{:S(2)}) %collective-permute-start.16) | collective-permute-done | bytes 32800 | tf_op jit(solution)/shard_map/ppermute | solution.py:425
  78.9 0.7 collective-permute-start.17
  79.6 1.7 %shard_map.118 = (bf16[64,2048]{1,0:T(8,128)(2,1)S(1)}, bf16[64,2048]{1,0:T(8,128)(2,1)S(1)}, f32[32,32]{1,0:T(8,128)S(1)}) custom-call(f32[32,32,128]{2,1,0:T(8,128)S(1)} %bitcast.35), custom_call_target="tpu_custom_call" | custom-call | flops 67108864 | bytes 524288 | tf_op jit(solution)/shard_map/pallas_call | solution.py:27
  81.6 1.5 %collective-permute-done.17.refs_1_ = bf16[64,256]{1,0:T(8,128)(2,1)S(1)} collective-permute-done((bf16[64,256]{1,0:T(8,128)(2,1)S(1)}, bf16[64,256]{1,0:T(8,128)(2,1)S(1)}, u32[]{:S(2)}, u32[]{:S(2)}) %collective-permute-start.17) | collective-permute-done | bytes 32800 | tf_op jit(solution)/shard_map/ppermute | solution.py:425
  83.6 5.2 %collective-permute-done.18.refs_1_ = bf16[64,256]{1,0:T(8,128)(2,1)S(1)} collective-permute-done((bf16[64,256]{1,0:T(8,128)(2,1)S(1)}, bf16[64,256]{1,0:T(8,128)(2,1)S(1)}, u32[]{:S(2)}, u32[]{:S(2)}) %collective-permute-start.18) | collective-permute-done | bytes 32800 | tf_op jit(solution)/shard_map/ppermute | solution.py:425
  89.0 2.8 %collective-permute-start.19 = (bf16[64,256]{1,0:T(8,128)(2,1)S(1)}, bf16[64,256]{1,0:T(8,128)(2,1)S(1)}, u32[]{:S(2)}, u32[]{:S(2)}) collective-permute-start(bf16[64,256]{1,0:T(8,128)(2,1)S(1)} %get-tuple-element.64), channel_id=1, source_target_pairs={{0,16},{8,24},{16,0},{24,8},{32,48},{40,56},{48,32},{56,40},{64,80... | collective-permute-start | bytes 98312 | tf_op jit(solution)/shard_map/ppermute | solution.py:425
  92.0 1.7 %collective-permute-done.19.refs_1_ = bf16[64,256]{1,0:T(8,128)(2,1)S(1)} collective-permute-done((bf16[64,256]{1,0:T(8,128)(2,1)S(1)}, bf16[64,256]{1,0:T(8,128)(2,1)S(1)}, u32[]{:S(2)}, u32[]{:S(2)}) %collective-permute-start.19) | collective-permute-done | bytes 32800 | tf_op jit(solution)/shard_map/ppermute | solution.py:425
  94.2 1.0 collective-permute-done.20.refs_3_
  95.2 2.5 %shard_map.126 = (bf16[64,2048]{1,0:T(8,128)(2,1)S(1)}, bf16[64,2048]{1,0:T(8,128)(2,1)S(1)}, f32[32,128]{1,0:T(8,128)S(1)}) custom-call(s32[12]{0:T(128)S(1)} %concatenate.3.refs_0_, f32[64,2048]{1,0:T(8,128)S(1)} %shard_map.108.refs_2_.refs_1_, f32[64,256]{1,0:T(8,128)S(1)} %shard_map.125.refs_2_, bf16[128,256]{1,0:T(8,128)(2,1)S(1)} %collective-permute-done.20.refs_3_, ...), custom_call_target="tpu_custom_call" | custom-call | flops 134217728 | bytes 3412016 | tf_op jit(solution)/shard_map/pallas_call | solution.py:27
  97.9 1.0 collective-permute-done.21.refs_1_
  99.0 14.0 %all_to_all.10.refs_0_ = f32[16,32,128]{2,1,0:T(8,128)S(1)} all-to-all(f32[16,32,128]{2,1,0:T(8,128)S(1)} %shard_map.127), channel_id=1, replica_groups={{0,16,32,48,64,80,96,112,128,144,160,176,192,208,224,240},{8,24,40,56,7..., dimensions={0} | all-to-all | bytes 524288 | tf_op jit(solution)/shard_map/all_to_all | solution.py:559
  113.0 0.7 shard_map.128
  113.6 5.0 %all-to-all-start.1 = ((f32[8,32,128]{2,1,0:T(8,128)}), f32[8,32,128]{2,1,0:T(8,128)S(1)}, u32[]{:S(2)}, u32[]{:S(2)}) async-start(f32[8,32,128]{2,1,0:T(8,128)} %shard_map.128), calls=%async_computation.1 | async-start | bytes 262144 | tf_op jit(solution)/shard_map/all_to_all | solution.py:561
  118.6 1.3 shard_map.107
  119.9 7.8 %all-to-all-done.1.refs_0_ = f32[8,32,128]{2,1,0:T(8,128)S(1)} async-done(((f32[8,32,128]{2,1,0:T(8,128)}), f32[8,32,128]{2,1,0:T(8,128)S(1)}, u32[]{:S(2)}, u32[]{:S(2)}) %all-to-all-start.1) | async-done | bytes 131104 | tf_op jit(solution)/shard_map/all_to_all | solution.py:561
  127.7 4.5 %shard_map.129 = f32[64,32,128]{2,1,0:T(8,128)} custom-call(f32[8,32,128]{2,1,0:T(8,128)S(1)} %all-to-all-done.1.refs_0_, bf16[64,2048]{1,0:T(8,128)(2,1)S(1)} %get-tuple-element.68.refs_1_, bf16[64,2048]{1,0:T(8,128)(2,1)S(1)} %get-tuple-element.69.refs_2_, bf16[64,2048]{1,0:T(8,128)(2,1)S(1)} %get-tuple-element.57.refs_2_.refs_8_.refs_3_, ...), custom_call_target="tpu_custom_call" | custom-call | flops 67108864 | bytes 1179648 | tf_op jit(solution)/shard_map/pallas_call | solution.py:27
  (64 shorter events, 7.1 us)
Async XLA Ops:
  0.6 11.7 %copy-start = (s32[32,8,4,2]{0,3,2,1:T(2,128)S(1)}, s32[32,8,4,2]{0,3,2,1:T(2,128)}, u32[]{:S(2)}) copy-start(s32[32,8,4,2]{0,3,2,1:T(2,128)} %param.8) | copy-start | bytes 24580
  3.1 2.5 %collective-permute-start = (bf16[64,256]{1,0:T(8,128)(2,1)S(1)}, bf16[64,256]{1,0:T(8,128)(2,1)S(1)}, u32[]{:S(2)}, u32[]{:S(2)}) collective-permute-start(bf16[64,256]{1,0:T(8,128)(2,1)S(1)} %get-tuple-element.36.refs_0_), channel_id=1, source_target_pairs={{0,8},{8,0},{16,24},{24,16},{32,40},{40,32},{48,56},{56,48},{64,72... | collective-permute-start | bytes 98312 | tf_op jit(solution)/shard_map/ppermute | solution.py:425
  5.4 4.7 %copy-start.1 = (bf16[8,2,2,256,256]{4,3,2,1,0:T(8,128)(2,1)}, bf16[8,2,2,256,256]{4,3,2,1,0:T(8,128)(2,1)S(1)}, u32[]{:S(2)}) copy-start(bf16[8,2,2,256,256]{4,3,2,1,0:T(8,128)(2,1)S(1)} %shard_map.87.refs_1_.refs_2_) | copy-start | bytes 12582916
  5.8 4.3 %collective-permute-start.1 = (bf16[64,256]{1,0:T(8,128)(2,1)S(1)}, bf16[64,256]{1,0:T(8,128)(2,1)S(1)}, u32[]{:S(2)}, u32[]{:S(2)}) collective-permute-start(bf16[64,256]{1,0:T(8,128)(2,1)S(1)} %shard_map.89.refs_0_), channel_id=1, source_target_pairs={{0,16},{8,24},{16,0},{24,8},{32,48},{40,56},{48,32},{56,40},{64,80... | collective-permute-start | bytes 98312 | tf_op jit(solution)/shard_map/ppermute | solution.py:425
  10.3 8.9 %collective-permute-start.2 = (bf16[64,256]{1,0:T(8,128)(2,1)S(1)}, bf16[64,256]{1,0:T(8,128)(2,1)S(1)}, u32[]{:S(2)}, u32[]{:S(2)}) collective-permute-start(bf16[64,256]{1,0:T(8,128)(2,1)S(1)} %shard_map.91.refs_0_), channel_id=1, source_target_pairs={{0,32},{8,40},{16,48},{24,56},{32,0},{40,8},{48,16},{56,24},{64,96... | collective-permute-start | bytes 98312 | tf_op jit(solution)/shard_map/ppermute | solution.py:425
  13.4 8.4 %collective-permute-start.3 = (bf16[64,256]{1,0:T(8,128)(2,1)S(1)}, bf16[64,256]{1,0:T(8,128)(2,1)S(1)}, u32[]{:S(2)}, u32[]{:S(2)}) collective-permute-start(bf16[64,256]{1,0:T(8,128)(2,1)S(1)} %get-tuple-element.38), channel_id=1, source_target_pairs={{0,8},{8,0},{16,24},{24,16},{32,40},{40,32},{48,56},{56,48},{64,72... | collective-permute-start | bytes 98312 | tf_op jit(solution)/shard_map/ppermute | solution.py:425
  13.5 8.3 %collective-permute-start.4 = (bf16[64,256]{1,0:T(8,128)(2,1)S(1)}, bf16[64,256]{1,0:T(8,128)(2,1)S(1)}, u32[]{:S(2)}, u32[]{:S(2)}) collective-permute-start(bf16[64,256]{1,0:T(8,128)(2,1)S(1)} %get-tuple-element.39), channel_id=1, source_target_pairs={{8,16},{24,32},{40,48},{56,64},{72,80},{88,96},{104,112},{120,128}... | collective-permute-start | bytes 98312 | tf_op jit(solution)/shard_map/ppermute | solution.py:431
  16.8 2.2 %copy-start.2 = (bf16[8,2,2,256,256]{4,3,2,1,0:T(8,128)(2,1)S(1)}, bf16[8,2,2,256,256]{4,3,2,1,0:T(8,128)(2,1)}, u32[]{:S(2)}) copy-start(bf16[8,2,2,256,256]{4,3,2,1,0:T(8,128)(2,1)} %copy-done.1) | copy-start | bytes 12582916
  19.3 4.0 %collective-permute-start.5 = (bf16[64,256]{1,0:T(8,128)(2,1)S(1)}, bf16[64,256]{1,0:T(8,128)(2,1)S(1)}, u32[]{:S(2)}, u32[]{:S(2)}) collective-permute-start(bf16[64,256]{1,0:T(8,128)(2,1)S(1)} %shard_map.93.refs_0_), channel_id=1, source_target_pairs={{0,64},{8,72},{16,80},{24,88},{32,96},{40,104},{48,112},{56,120},{... | collective-permute-start | bytes 98312 | tf_op jit(solution)/shard_map/ppermute | solution.py:425
  20.9 5.7 %copy-start.7 = (bf16[1,1,2,16,128,128]{5,4,3,2,1,0:T(8,128)(2,1)S(1)}, bf16[1,1,2,16,128,128]{5,4,3,2,1,0:T(8,128)(2,1)}, u32[]{:S(2)}) copy-start(bf16[1,1,2,16,128,128]{5,4,3,2,1,0:T(8,128)(2,1)} %param.9) | copy-start | bytes 3145732
  20.9 6.1 %copy-start.3 = (bf16[8,2,2,256,256]{4,3,2,1,0:T(8,128)(2,1)S(1)}, bf16[8,2,2,256,256]{4,3,2,1,0:T(8,128)(2,1)}, u32[]{:S(2)}) copy-start(bf16[8,2,2,256,256]{4,3,2,1,0:T(8,128)(2,1)} %copy-done.1) | copy-start | bytes 12582916
  20.9 6.1 %collective-permute-start.6 = (bf16[64,256]{1,0:T(8,128)(2,1)S(1)}, bf16[64,256]{1,0:T(8,128)(2,1)S(1)}, u32[]{:S(2)}, u32[]{:S(2)}) collective-permute-start(bf16[64,256]{1,0:T(8,128)(2,1)S(1)} %get-tuple-element.40), channel_id=1, source_target_pairs={{1,2},{3,4},{5,6},{2,1},{4,3},{6,5},{9,10},{11,12},{13,14},{10,9},... | collective-permute-start | bytes 98312 | tf_op jit(solution)/shard_map/ppermute | solution.py:431
  23.5 5.5 %collective-permute-start.7 = (bf16[64,256]{1,0:T(8,128)(2,1)S(1)}, bf16[64,256]{1,0:T(8,128)(2,1)S(1)}, u32[]{:S(2)}, u32[]{:S(2)}) collective-permute-start(bf16[64,256]{1,0:T(8,128)(2,1)S(1)} %shard_map.96.refs_0_), channel_id=1, source_target_pairs={{0,128},{8,136},{16,144},{24,152},{32,160},{40,168},{48,176},{56,1... | collective-permute-start | bytes 98312 | tf_op jit(solution)/shard_map/ppermute | solution.py:425
  29.2 11.2 %copy-start.6 = (bf16[1,1,4,2,256,256]{5,4,3,2,1,0:T(8,128)(2,1)S(1)}, bf16[1,1,4,2,256,256]{5,4,3,2,1,0:T(8,128)(2,1)}, u32[]{:S(2)}) copy-start(bf16[1,1,4,2,256,256]{5,4,3,2,1,0:T(8,128)(2,1)} %param.10) | copy-start | bytes 3145732
  29.2 6.1 %collective-permute-start.8 = (bf16[128,256]{1,0:T(8,128)(2,1)S(1)}, bf16[128,256]{1,0:T(8,128)(2,1)S(1)}, u32[]{:S(2)}, u32[]{:S(2)}) collective-permute-start(bf16[128,256]{1,0:T(8,128)(2,1)S(1)} %shard_map.99.refs_0_), channel_id=1, source_target_pairs={{0,1},{1,0},{2,3},{3,2},{4,5},{5,4},{6,7},{7,6},{8,9},{9,8},{10,11... | collective-permute-start | bytes 196616 | tf_op jit(solution)/shard_map/ppermute | solution.py:427
  33.2 8.0 %copy-start.5 = (bf16[1,1,2,256,2048]{4,3,2,1,0:T(8,128)(2,1)S(1)}, bf16[1,1,2,256,2048]{4,3,2,1,0:T(8,128)(2,1)}, u32[]{:S(2)}) copy-start(bf16[1,1,2,256,2048]{4,3,2,1,0:T(8,128)(2,1)} %param.12) | copy-start | bytes 6291460
  35.5 6.8 %collective-permute-start.9 = (bf16[64,256]{1,0:T(8,128)(2,1)S(1)}, bf16[64,256]{1,0:T(8,128)(2,1)S(1)}, u32[]{:S(2)}, u32[]{:S(2)}) collective-permute-start(bf16[64,256]{1,0:T(8,128)(2,1)S(1)} %shard_map.101.refs_0_), channel_id=1, source_target_pairs={{0,2},{1,3},{2,0},{3,1},{4,6},{5,7},{6,4},{7,5},{8,10},{9,11},{10,... | collective-permute-start | bytes 98312 | tf_op jit(solution)/shard_map/ppermute | solution.py:427
  42.5 7.9 %collective-permute-start.10 = (bf16[64,256]{1,0:T(8,128)(2,1)S(1)}, bf16[64,256]{1,0:T(8,128)(2,1)S(1)}, u32[]{:S(2)}, u32[]{:S(2)}) collective-permute-start(bf16[64,256]{1,0:T(8,128)(2,1)S(1)} %shard_map.104.refs_0_), channel_id=1, source_target_pairs={{0,4},{1,5},{2,6},{3,7},{4,0},{5,1},{6,2},{7,3},{8,12},{9,13},{10,... | collective-permute-start | bytes 98312 | tf_op jit(solution)/shard_map/ppermute | solution.py:427
  52.0 7.9 %collective-permute-start.11 = (bf16[64,256]{1,0:T(8,128)(2,1)S(1)}, bf16[64,256]{1,0:T(8,128)(2,1)S(1)}, u32[]{:S(2)}, u32[]{:S(2)}) collective-permute-start(bf16[64,256]{1,0:T(8,128)(2,1)S(1)} %get-tuple-element.49), channel_id=1, source_target_pairs={{0,4},{1,5},{2,6},{3,7},{4,0},{5,1},{6,2},{7,3},{8,12},{9,13},{10,... | collective-permute-start | bytes 98312 | tf_op jit(solution)/shard_map/ppermute | solution.py:427
  60.1 5.2 %collective-permute-start.12 = (bf16[64,256]{1,0:T(8,128)(2,1)S(1)}, bf16[64,256]{1,0:T(8,128)(2,1)S(1)}, u32[]{:S(2)}, u32[]{:S(2)}) collective-permute-start(bf16[64,256]{1,0:T(8,128)(2,1)S(1)} %get-tuple-element.51), channel_id=1, source_target_pairs={{0,2},{1,3},{2,0},{3,1},{4,6},{5,7},{6,4},{7,5},{8,10},{9,11},{10,... | collective-permute-start | bytes 98312 | tf_op jit(solution)/shard_map/ppermute | solution.py:427
  65.5 7.5 %collective-permute-start.14 = (bf16[128,256]{1,0:T(8,128)(2,1)S(1)}, bf16[128,256]{1,0:T(8,128)(2,1)S(1)}, u32[]{:S(2)}, u32[]{:S(2)}) collective-permute-start(bf16[128,256]{1,0:T(8,128)(2,1)S(1)} %get-tuple-element.53), channel_id=1, source_target_pairs={{0,1},{1,0},{2,3},{3,2},{4,5},{5,4},{6,7},{7,6},{8,9},{9,8},{10,11... | collective-permute-start | bytes 196616 | tf_op jit(solution)/shard_map/ppermute | solution.py:427
  67.6 5.2 %collective-permute-start.13 = (bf16[64,256]{1,0:T(8,128)(2,1)S(1)}, bf16[64,256]{1,0:T(8,128)(2,1)S(1)}, u32[]{:S(2)}, u32[]{:S(2)}) collective-permute-start(bf16[64,256]{1,0:T(8,128)(2,1)S(1)} %get-tuple-element.46.refs_3_), channel_id=1, source_target_pairs={{8,16},{24,32},{40,48},{56,64},{72,80},{88,96},{104,112},{120,128}... | collective-permute-start | bytes 98312 | tf_op jit(solution)/shard_map/ppermute | solution.py:431
  69.5 6.5 %collective-permute-start.15 = (bf16[64,256]{1,0:T(8,128)(2,1)S(1)}, bf16[64,256]{1,0:T(8,128)(2,1)S(1)}, u32[]{:S(2)}, u32[]{:S(2)}) collective-permute-start(bf16[64,256]{1,0:T(8,128)(2,1)S(1)} %get-tuple-element.48.refs_5_), channel_id=1, source_target_pairs={{1,2},{3,4},{5,6},{2,1},{4,3},{6,5},{9,10},{11,12},{13,14},{10,9},... | collective-permute-start | bytes 98312 | tf_op jit(solution)/shard_map/ppermute | solution.py:431
  73.2 5.5 %collective-permute-start.16 = (bf16[64,256]{1,0:T(8,128)(2,1)S(1)}, bf16[64,256]{1,0:T(8,128)(2,1)S(1)}, u32[]{:S(2)}, u32[]{:S(2)}) collective-permute-start(bf16[64,256]{1,0:T(8,128)(2,1)S(1)} %get-tuple-element.55), channel_id=1, source_target_pairs={{0,128},{8,136},{16,144},{24,152},{32,160},{40,168},{48,176},{56,1... | collective-permute-start | bytes 98312 | tf_op jit(solution)/shard_map/ppermute | solution.py:425
  76.0 3.6 %copy-start.8 = (f32[32,1,1,2,2048]{4,3,2,1,0:T(2,128)S(1)}, f32[32,1,1,2,2048]{4,3,2,1,0:T(2,128)}, u32[]{:S(2)}) copy-start(f32[32,1,1,2,2048]{4,3,2,1,0:T(2,128)} %param.7) | copy-start | bytes 1572868
  78.9 4.2 %collective-permute-start.17 = (bf16[64,256]{1,0:T(8,128)(2,1)S(1)}, bf16[64,256]{1,0:T(8,128)(2,1)S(1)}, u32[]{:S(2)}, u32[]{:S(2)}) collective-permute-start(bf16[64,256]{1,0:T(8,128)(2,1)S(1)} %get-tuple-element.60), channel_id=1, source_target_pairs={{0,64},{8,72},{16,80},{24,88},{32,96},{40,104},{48,112},{56,120},{... | collective-permute-start | bytes 98312 | tf_op jit(solution)/shard_map/ppermute | solution.py:425
  83.3 5.5 %collective-permute-start.18 = (bf16[64,256]{1,0:T(8,128)(2,1)S(1)}, bf16[64,256]{1,0:T(8,128)(2,1)S(1)}, u32[]{:S(2)}, u32[]{:S(2)}) collective-permute-start(bf16[64,256]{1,0:T(8,128)(2,1)S(1)} %get-tuple-element.62), channel_id=1, source_target_pairs={{0,32},{8,40},{16,48},{24,56},{32,0},{40,8},{48,16},{56,24},{64,96... | collective-permute-start | bytes 98312 | tf_op jit(solution)/shard_map/ppermute | solution.py:425
  83.4 8.4 %copy-start.4 = (bf16[1,1,2,2048,256]{4,3,2,1,0:T(8,128)(2,1)S(1)}, bf16[1,1,2,2048,256]{4,3,2,1,0:T(8,128)(2,1)}, u32[]{:S(2)}) copy-start(bf16[1,1,2,2048,256]{4,3,2,1,0:T(8,128)(2,1)} %param.11) | copy-start | bytes 6291460
  89.0 4.7 %collective-permute-start.19 = (bf16[64,256]{1,0:T(8,128)(2,1)S(1)}, bf16[64,256]{1,0:T(8,128)(2,1)S(1)}, u32[]{:S(2)}, u32[]{:S(2)}) collective-permute-start(bf16[64,256]{1,0:T(8,128)(2,1)S(1)} %get-tuple-element.64), channel_id=1, source_target_pairs={{0,16},{8,24},{16,0},{24,8},{32,48},{40,56},{48,32},{56,40},{64,80... | collective-permute-start | bytes 98312 | tf_op jit(solution)/shard_map/ppermute | solution.py:425
  93.9 1.3 %collective-permute-start.20 = (bf16[128,256]{1,0:T(8,128)(2,1)S(1)}, bf16[128,256]{1,0:T(8,128)(2,1)S(1)}, u32[]{:S(2)}, u32[]{:S(2)}) collective-permute-start(bf16[128,256]{1,0:T(8,128)(2,1)S(1)} %get-tuple-element.66), channel_id=1, source_target_pairs={{0,8},{8,0},{16,24},{24,16},{32,40},{40,32},{48,56},{56,48},{64,72... | collective-permute-start | bytes 196616 | tf_op jit(solution)/shard_map/ppermute | solution.py:425
  97.7 1.3 collective-permute-start.21
  113.6 14.0 %all-to-all-start.1 = ((f32[8,32,128]{2,1,0:T(8,128)}), f32[8,32,128]{2,1,0:T(8,128)S(1)}, u32[]{:S(2)}, u32[]{:S(2)}) async-start(f32[8,32,128]{2,1,0:T(8,128)} %shard_map.128), calls=%async_computation.1 | async-start | bytes 262144 | tf_op jit(solution)/shard_map/all_to_all | solution.py:561

commit v2 on v1

--- a/solution.py
+++ b/solution.py
@@ -13,7 +13,7 @@
 VM = pl.BlockSpec(memory_space=pltpu.VMEM)
 SM = pl.BlockSpec(memory_space=pltpu.SMEM)
 
-HEAD, LOAD = 214, 196
+HEAD, EARLY, LATE = 214, 203, 200
 
 
 def call(kernel, outs, args, flops, smem=0, limit=24, after=(), out_spec=VM, scratch=()):
@@ -124,23 +124,24 @@
     )(tall, squeeze)
 
 
-def load_kernel(f_in, o_ref, sem):
-    copy = pltpu.make_async_copy(f_in, o_ref, sem)
+def load_kernel(begin, f_in, o_ref, sem):
+    copy = pltpu.make_async_copy(f_in.at[begin : begin + o_ref.shape[0]], o_ref, sem)
     copy.start()
     copy.wait()
 
 
-def load(sections):
+def load(sections, begin, end, limit):
+    shape = (end - begin,) + sections.shape[1:]
     return pl.pallas_call(
-        load_kernel,
+        functools.partial(load_kernel, begin),
         in_specs=[pl.BlockSpec(memory_space=pltpu.HBM)],
         out_specs=VM,
-        out_shape=jax.ShapeDtypeStruct(sections.shape, BF16),
+        out_shape=jax.ShapeDtypeStruct(shape, BF16),
         scratch_shapes=[pltpu.SemaphoreType.DMA],
         cost_estimate=pl.CostEstimate(
             flops=0, bytes_accessed=2 * sections.size, transcendentals=0
         ),
-        compiler_params=pltpu.CompilerParams(vmem_limit_bytes=LOAD * 2**18),
+        compiler_params=pltpu.CompilerParams(vmem_limit_bytes=limit * 2**18),
     )(sections)
 
 
@@ -240,22 +241,23 @@
         m_ref[rows:] = rest[0][...]
 
 
-def close_kernel(
-    leaf, info, near_ref, own_ref, ra_ref, rb_ref, rc_ref, rd_ref, c_ref, vh_ref, vl_ref, vv_ref,
-    zh_ref, zl_ref, p_ref, z_ref
-):
-    rows = own_ref.shape[0]
-    cols = rows // 2
-    g = (own_ref[...] + ra_ref[:rows].astype(F32)).astype(BF16)
-    z_ref[...] = near_ref[...] + adj(g, c_ref[0], c_ref[1])
+def gather_kernel(leaf, info, near_ref, ra_ref, rb_ref, rc_ref, rd_ref, o_ref):
+    rows = near_ref.shape[0]
+    o_ref[...] = near_ref[...]
     for at, ref in enumerate((ra_ref, rb_ref, rc_ref, rd_ref)):
         side = info[8 + at]
         low = ref.shape[0] - rows
         for e in range(2):
-            z_ref[:, leaf_at(info[2 * side + e], leaf)] += ref[
+            o_ref[:, leaf_at(info[2 * side + e], leaf)] += ref[
                 low:, e * leaf : (e + 1) * leaf
             ].astype(F32)
-    high, low = split(z_ref[...])
+
+
+def close_kernel(near_ref, own_ref, r_ref, c_ref, vh_ref, vl_ref, vv_ref, zh_ref, zl_ref, p_ref):
+    rows = own_ref.shape[0]
+    cols = rows // 2
+    g = (own_ref[...] + r_ref[...].astype(F32)).astype(BF16)
+    high, low = split(near_ref[...] + adj(g, c_ref[0], c_ref[1]))
     zh_ref[...] = high
     zl_ref[...] = low
     many = jnp.concatenate([high, low, vh_ref[...], vl_ref[...]], 0)
@@ -344,16 +346,12 @@
     cols = p.shape[0]
     lower = lax.broadcasted_iota(jnp.int32, (cols, cols), 0)
     upper = lax.broadcasted_iota(jnp.int32, (cols, cols), 1)
-    eye = (lower == upper).astype(F32)
-
-    def turned(a):
-        return exact_dot(a, eye, (((0,), (0,)), ((), ())))
 
     def hermitian(t):
-        strict = jnp.where(lower > upper, t, 0.0)
-        above = jnp.where(lower < upper, t, 0.0)
-        re = jnp.where(lower >= upper, t, 0.0) + turned(strict)
-        return real_form(re, above - turned(above))
+        turned = t.T
+        re = jnp.where(lower >= upper, t, turned)
+        im = jnp.where(lower < upper, t, jnp.where(lower > upper, -turned, 0.0))
+        return real_form(re, im)
 
     zz = hermitian(p[:, :cols])
     vv = hermitian(p[:, cols : 2 * cols])
@@ -438,69 +436,80 @@
     leaf_flops = 8 * cols * leaf * unknowns
 
     half, sent = head(leaf, tall, squeeze)
-    pieces = call(functools.partial(pick_kernel, leaf), [small] * 4, [info, half], 0, smem=1)
+    early = 3
+    first = load(sections, 0, early, EARLY)
+    rest = load(sections, early, levels, LATE)
+
+    def weights(level):
+        return (first, level) if level < early else (rest, level - early)
+
     got = {}
     for level in range(levels):
         arrived = partner(sent, level)
         after = []
-        if level == 0:
-            sections = load(sections)
+        if level == 1:
+            pieces = call(
+                functools.partial(pick_kernel, leaf), [small] * 4, [info, half], 0, smem=1, after=[sent]
+            )
+            after = list(pieces) + [rest]
         if level == 2:
-            got["a"] = partner(pieces[0], 0)
-            got["b"] = beyond(pieces[1], "px", row_count)
-        if level == 3:
-            got["d"] = beyond(pieces[3], "py", col_count)
-            after = [got["a"], got["b"]]
-        if level == 4:
             (near,) = call(
                 functools.partial(leaves_kernel, leaf, False),
                 [((rows, unknowns), F32)],
                 [half, selfs],
                 leaf_flops,
-            )
-            after = [got["d"], near]
+                after=[sent],
+            )
+            after = [near]
+            got["a"] = partner(pieces[0], 0)
+        if level == 3:
+            after = [got["a"]]
         if level == row_bits:
             got["c"] = arrived
-        if level == row_bits + 1:
+            got["b"] = beyond(pieces[1], "px", row_count)
+            got["d"] = beyond(pieces[3], "py", col_count)
+        if level == levels - 1:
             (near,) = call(
                 functools.partial(sides_kernel, leaf),
                 [((rows, unknowns), F32)],
                 [info, near, got["a"], got["b"], got["c"], got["d"], sides],
                 4 * step_flops,
                 smem=1,
+                after=[sent],
             )
             after = [near, spread]
+        f, at = weights(level)
         (own,) = call(
-            functools.partial(own_kernel, level, False),
+            functools.partial(own_kernel, at, False),
             [wide],
-            [sent, sections],
+            [sent, f],
             step_flops,
             after=after,
         )
         if level < levels - 1:
             extra = [pieces[2]] if level == row_bits - 1 else []
             (sent,) = call(
-                functools.partial(up_kernel, level),
+                functools.partial(up_kernel, at),
                 [double if extra else small],
-                [own, arrived, sections] + extra,
+                [own, arrived, f] + extra,
                 step_flops,
             )
     y, yb, g, message = call(
-        functools.partial(field_kernel, levels - 1),
+        functools.partial(field_kernel, at),
         [((rows, unknowns), F32), ((rows, unknowns), BF16), small, small],
-        [own, arrived, sections, near, spread],
+        [own, arrived, f, near, spread],
         2 * patch_flops,
     )
     terms = call(
         functools.partial(terms_kernel, leaf), [small] * 4, [info, yb, sides], 4 * step_flops, smem=1
+    )
+    (shaped,) = call(
+        functools.partial(shape_kernel, leaf), [((cols, 2 * leaves, leaf), F32)], [y], 0
     )
     for level in range(levels - 1, -1, -1):
         arrived = partner(message, level)
         after = []
         if level == levels - 1:
-            (shaped,) = call(
-                functools.partial(shape_kernel, leaf), [((cols, 2 * leaves, leaf), F32)], [y], 0
-            )
             after = list(terms)
         if level == levels - 2:
             (z_near,) = call(
@@ -508,47 +517,59 @@
                 [((rows, unknowns), F32)],
                 [yb, selfs],
                 leaf_flops,
-            )
-            got["b"] = beyond(terms[1], "px", row_count)
+                after=[message],
+            )
             after = [z_near]
         if level == row_bits:
             got["c"] = arrived
-            got["d"] = beyond(terms[3], "py", col_count)
-            after = [got["b"]]
-        if level == row_bits - 1:
-            after = [got["d"]]
-        if level == 3:
+        if level == 4:
             v_high, v_low, vv = call(
                 functools.partial(basis_kernel, leaf),
                 [((rows, unknowns), BF16), ((rows, unknowns), BF16), ((cols, cols), F32)],
                 [tall],
                 leaf_flops,
+                after=[message],
             )
             after = [v_high, v_low, vv]
+        if level == 3:
+            got["d"] = beyond(terms[3], "py", col_count)
+        if level == 2:
+            after = [got["d"]]
+            got["a"] = partner(terms[0], 0)
         if level == 1:
-            after = [squeeze]
+            after = [got["a"], squeeze]
+            got["b"] = beyond(terms[1], "px", row_count)
+        if level == 0:
+            (z_near,) = call(
+                functools.partial(gather_kernel, leaf),
+                [((rows, unknowns), F32)],
+                [info, z_near, got["a"], got["b"], got["c"], got["d"]],
+                0,
+                smem=1,
+            )
+            after = [z_near]
+        f, at = weights(level)
         (own,) = call(
-            functools.partial(own_kernel, level, True),
+            functools.partial(own_kernel, at, True),
             [wide],
-            [g, sections],
+            [g, f],
             step_flops,
             after=after,
         )
         if level > 0:
-            extra = [terms[0]] if level == 1 else [terms[2]] if level == row_bits + 1 else []
+            extra = [terms[2]] if level == row_bits + 1 else []
+            f, at = weights(level - 1)
             g, message = call(
-                functools.partial(down_kernel, level - 1),
+                functools.partial(down_kernel, at),
                 [small, double if extra else small],
-                [own, arrived, sections] + extra,
+                [own, arrived, f] + extra,
                 step_flops,
             )
     z_high, z_low, part = call(
-        functools.partial(close_kernel, leaf),
+        close_kernel,
         [((rows, unknowns), BF16), ((rows, unknowns), BF16), ((cols, 4 * cols), F32)],
-        [info, z_near, own, arrived, got["b"], got["c"], got["d"], squeeze, v_high, v_low, vv],
+        [z_near, own, arrived, squeeze, v_high, v_low, vv],
         patch_flops,
-        smem=1,
-        scratch=[pltpu.VMEM((rows, unknowns), F32)],
     )
     part = part.reshape(1, cols, 4 * cols)
     chips = row_count // 2

time: 133 us -> 131 us (0.985)
  waiting for transfers between devices: 39.5 us -> 37.1 us
  starting transfers between devices: 49.1 us -> 47.7 us
    all_to_all x1, starting transfers between devices: 4.96 us -> 7.65 us  [per_device(): part = lax.all_to_all(part, 'py', 0, 0, tiled=True)]
    ppermute x6, starting transfers between devices: 21.5 us -> 19.3 us  [partner(): return lax.ppermute(x, 'py', [(i, i ^ 1 << bit) for i in range(col_count)])]
    ppermute x4, waiting for transfers between devices: 2.64 us -> 0.64 us  [beyond(): return lax.ppermute(x, axis, pairs + [(j, i) for i, j in pairs])]
    ppermute x4, starting transfers between devices: 6.7 us -> 5.13 us  [beyond(): return lax.ppermute(x, axis, pairs + [(j, i) for i, j in pairs])]
    pallas_call x1 -> x2, Pallas kernels: 2.2 us -> 3.17 us  [load(): pl.pallas_call(functools.partial(load_kernel, begin), in_specs=[pl.BlockS...]
    ppermute x12 -> x13, waiting for transfers between devices: 18.1 us -> 17.7 us  [partner(): lax.ppermute(x, 'px', [(i, i ^ 1 << level) for i in range(row_count)])]
    pallas_call x42 -> x43, Pallas kernels: 21.4 us -> 21.1 us  [call(): pl.pallas_call(body, out_shape=[jax.ShapeDtypeStruct(s, d) for s, d in ou...]
    ppermute x12 -> x13, starting transfers between devices: 16 us -> 15.7 us  [partner(): lax.ppermute(x, 'px', [(i, i ^ 1 << level) for i in range(row_count)])]
  transfers between devices with their start and end apart: 23 -> 24, of which waited for: 16 -> 16; matrix products, arithmetic and copies ran while one was open for 0% -> 0% of each run, Pallas kernels for 9% -> 11%
where the time goes in v2:
time: 131 us
  starting transfers between devices  47.7 us (36%)
  waiting for transfers between devices  37.1 us (28%)
  Pallas kernels  26.7 us (20%)
  blocking collectives  15.1 us (12%)
  local copies, waits for them, and re-layouts  2.9 us (2%)
    pallas_call x43, Pallas kernels, call(): pl.pallas_call(body, out_shape=[jax.ShapeDtypeStruct(s, d) for s, d in ou...  21.1 us
    ppermute x6, starting transfers between devices, partner(): return lax.ppermute(x, 'py', [(i, i ^ 1 << bit) for i in range(col_count)])  19.3 us
    ppermute x13, waiting for transfers between devices, partner(): lax.ppermute(x, 'px', [(i, i ^ 1 << level) for i in range(row_count)])  17.7 us
    ppermute x13, starting transfers between devices, partner(): lax.ppermute(x, 'px', [(i, i ^ 1 << level) for i in range(row_count)])  15.7 us
    all_to_all x1, blocking collectives, per_device(): lax.all_to_all(part, 'px', 0, 0, axis_index_groups=groups, tiled=True)  15.1 us
    ppermute x6, waiting for transfers between devices, partner(): return lax.ppermute(x, 'py', [(i, i ^ 1 << bit) for i in range(col_count)])  11 us
    all_to_all x1, waiting for transfers between devices, per_device(): part = lax.all_to_all(part, 'py', 0, 0, tiled=True)  7.79 us
    all_to_all x1, starting transfers between devices, per_device(): part = lax.all_to_all(part, 'py', 0, 0, tiled=True)  7.65 us
  transfers between devices with their start and end apart: 24, of which 16 were waited for; matrix products, arithmetic and copies ran while one was open for 0% of the time, Pallas kernels for 11%

profile of v2, /device:TPU:8, one launch (start us, length us, event | category | flops | bytes accessed | tf_op | source)
XLA Modules:
  0.0 130.7 jit_solution(8244003938808135985)
XLA Ops:
  0.6 2.5 %shard_map.86 = (bf16[64,2048]{1,0:T(8,128)(2,1)S(1)}, bf16[64,256]{1,0:T(8,128)(2,1)S(1)}) custom-call(f32[32,32,128]{2,1,0:T(8,128)} %bitcast.34, bf16[2,2048,256]{2,1,0:T(8,128)(2,1)} %bitcast.25), custom_call_target="tpu_custom_call" | custom-call | flops 134217728 | bytes 2621440 | tf_op jit(solution)/shard_map/pallas_call | solution.py:104
  3.2 1.4 %shard_map.87.refs_1_.refs_2_ = bf16[3,2,2,256,256]{4,3,2,1,0:T(8,128)(2,1)S(1)} custom-call(bf16[8,2,2,256,256]{4,3,2,1,0:T(8,128)(2,1)} %bitcast.38), custom_call_target="tpu_custom_call" | custom-call | bytes 4194304 | tf_op jit(solution)/shard_map/pallas_call | solution.py:135
  4.9 1.0 copy-done.1
  6.0 2.3 %collective-permute-start.1 = (bf16[64,256]{1,0:T(8,128)(2,1)S(1)}, bf16[64,256]{1,0:T(8,128)(2,1)S(1)}, u32[]{:S(2)}, u32[]{:S(2)}) collective-permute-start(bf16[64,256]{1,0:T(8,128)(2,1)S(1)} %shard_map.89.refs_2_.refs_0_), channel_id=1, source_target_pairs={{0,16},{8,24},{16,0},{24,8},{32,48},{40,56},{48,32},{56,40},{64,80... | collective-permute-start | bytes 98312 | tf_op jit(solution)/shard_map/ppermute | solution.py:423
  8.3 1.7 %shard_map.91.refs_6_.refs_1_.refs_2_ = bf16[5,2,2,256,256]{4,3,2,1,0:T(8,128)(2,1)S(1)} custom-call(bf16[8,2,2,256,256]{4,3,2,1,0:T(8,128)(2,1)} %bitcast.39), custom_call_target="tpu_custom_call" | custom-call | bytes 4194304 | tf_op jit(solution)/shard_map/pallas_call | solution.py:135
  11.1 1.4 %copy-done.2 = bf16[3,2,2,256,256]{4,3,2,1,0:T(8,128)(2,1)S(1)} copy-done((bf16[3,2,2,256,256]{4,3,2,1,0:T(8,128)(2,1)S(1)}, bf16[3,2,2,256,256]{4,3,2,1,0:T(8,128)(2,1)}, u32[]{:S(2)}) %copy-start.2) | copy-done | bytes 1572888
  12.8 0.9 collective-permute-start.2
  14.4 3.9 %collective-permute-done.2.refs_1_ = bf16[64,256]{1,0:T(8,128)(2,1)S(1)} collective-permute-done((bf16[64,256]{1,0:T(8,128)(2,1)S(1)}, bf16[64,256]{1,0:T(8,128)(2,1)S(1)}, u32[]{:S(2)}, u32[]{:S(2)}) %collective-permute-start.2) | collective-permute-done | bytes 32800 | tf_op jit(solution)/shard_map/ppermute | solution.py:423
  18.8 3.7 %collective-permute-done.4.refs_1_ = bf16[64,256]{1,0:T(8,128)(2,1)S(1)} collective-permute-done((bf16[64,256]{1,0:T(8,128)(2,1)S(1)}, bf16[64,256]{1,0:T(8,128)(2,1)S(1)}, u32[]{:S(2)}, u32[]{:S(2)}) %collective-permute-start.4) | collective-permute-done | bytes 32800 | tf_op jit(solution)/shard_map/ppermute | solution.py:423
  22.7 1.4 %collective-permute-start.5 = (bf16[64,256]{1,0:T(8,128)(2,1)S(1)}, bf16[64,256]{1,0:T(8,128)(2,1)S(1)}, u32[]{:S(2)}, u32[]{:S(2)}) collective-permute-start(bf16[64,256]{1,0:T(8,128)(2,1)S(1)} %shard_map.98.refs_0_), channel_id=1, source_target_pairs={{0,128},{8,136},{16,144},{24,152},{32,160},{40,168},{48,176},{56,1... | collective-permute-start | bytes 98312 | tf_op jit(solution)/shard_map/ppermute | solution.py:423
  24.2 4.0 %collective-permute-done.5.refs_1_ = bf16[64,256]{1,0:T(8,128)(2,1)S(1)} collective-permute-done((bf16[64,256]{1,0:T(8,128)(2,1)S(1)}, bf16[64,256]{1,0:T(8,128)(2,1)S(1)}, u32[]{:S(2)}, u32[]{:S(2)}) %collective-permute-start.5) | collective-permute-done | bytes 32800 | tf_op jit(solution)/shard_map/ppermute | solution.py:423
  28.8 4.3 %collective-permute-done.6.refs_1_.refs_4_ = bf16[128,256]{1,0:T(8,128)(2,1)S(1)} collective-permute-done((bf16[128,256]{1,0:T(8,128)(2,1)S(1)}, bf16[128,256]{1,0:T(8,128)(2,1)S(1)}, u32[]{:S(2)}, u32[]{:S(2)}) %collective-permute-start.6) | collective-permute-done | bytes 65568 | tf_op jit(solution)/shard_map/ppermute | solution.py:425
  33.2 1.3 collective-permute-start.7
  34.5 1.9 %collective-permute-start.8 = (bf16[64,256]{1,0:T(8,128)(2,1)S(1)}, bf16[64,256]{1,0:T(8,128)(2,1)S(1)}, u32[]{:S(2)}, u32[]{:S(2)}) collective-permute-start(bf16[64,256]{1,0:T(8,128)(2,1)S(1)} %get-tuple-element.39.refs_3_), channel_id=1, source_target_pairs={{8,16},{24,32},{40,48},{56,64},{72,80},{88,96},{104,112},{120,128}... | collective-permute-start | bytes 98312 | tf_op jit(solution)/shard_map/ppermute | solution.py:429
  36.4 0.7 collective-permute-start.9
  37.3 1.2 collective-permute-done.7.refs_1_
  38.6 5.6 %collective-permute-start.10 = (bf16[64,256]{1,0:T(8,128)(2,1)S(1)}, bf16[64,256]{1,0:T(8,128)(2,1)S(1)}, u32[]{:S(2)}, u32[]{:S(2)}) collective-permute-start(bf16[64,256]{1,0:T(8,128)(2,1)S(1)} %shard_map.104.refs_7_.refs_0_), channel_id=1, source_target_pairs={{0,4},{1,5},{2,6},{3,7},{4,0},{5,1},{6,2},{7,3},{8,12},{9,13},{10,... | collective-permute-start | bytes 98312 | tf_op jit(solution)/shard_map/ppermute | solution.py:425
  44.2 0.9 shard_map.105.refs_2_.refs_3_
  45.3 1.4 %collective-permute-done.10.refs_1_ = bf16[64,256]{1,0:T(8,128)(2,1)S(1)} collective-permute-done((bf16[64,256]{1,0:T(8,128)(2,1)S(1)}, bf16[64,256]{1,0:T(8,128)(2,1)S(1)}, u32[]{:S(2)}, u32[]{:S(2)}) %collective-permute-start.10) | collective-permute-done | bytes 32800 | tf_op jit(solution)/shard_map/ppermute | solution.py:425
  46.6 1.6 %shard_map.107 = (f32[64,2048]{1,0:T(8,128)S(1)}, bf16[64,2048]{1,0:T(8,128)(2,1)S(1)}, bf16[64,256]{1,0:T(8,128)(2,1)S(1)}, bf16[64,256]{1,0:T(8,128)(2,1)S(1)}) custom-call(f32[64,256]{1,0:T(8,128)S(1)} %shard_map.106.refs_0_, bf16[64,256]{1,0:T(8,128)(2,1)S(1)} %collective-permute-done.10.refs_1_, ...), custom_call_target="tpu_custom_call" | custom-call | flops 268435456 | bytes 5341184 | tf_op jit(solution)/shard_map/pallas_call | solution.py:27
  48.2 5.5 %collective-permute-start.11 = (bf16[64,256]{1,0:T(8,128)(2,1)S(1)}, bf16[64,256]{1,0:T(8,128)(2,1)S(1)}, u32[]{:S(2)}, u32[]{:S(2)}) collective-permute-start(bf16[64,256]{1,0:T(8,128)(2,1)S(1)} %get-tuple-element.49), channel_id=1, source_target_pairs={{0,4},{1,5},{2,6},{3,7},{4,0},{5,1},{6,2},{7,3},{8,12},{9,13},{10,... | collective-permute-start | bytes 98312 | tf_op jit(solution)/shard_map/ppermute | solution.py:425
  53.7 1.0 shard_map.109
  54.9 1.2 collective-permute-done.11.refs_1_
  56.4 4.3 %collective-permute-start.14 = (bf16[64,256]{1,0:T(8,128)(2,1)S(1)}, bf16[64,256]{1,0:T(8,128)(2,1)S(1)}, u32[]{:S(2)}, u32[]{:S(2)}) collective-permute-start(bf16[64,256]{1,0:T(8,128)(2,1)S(1)} %get-tuple-element.50.refs_2_), channel_id=1, source_target_pairs={{0,2},{1,3},{2,0},{3,1},{4,6},{5,7},{6,4},{7,5},{8,10},{9,11},{10,... | collective-permute-start | bytes 98312 | tf_op jit(solution)/shard_map/ppermute | solution.py:425
  60.6 0.8 shard_map.112.refs_2_.refs_1_
  61.6 0.9 collective-permute-done.14.refs_1_
  62.7 2.4 %collective-permute-start.15 = (bf16[128,256]{1,0:T(8,128)(2,1)S(1)}, bf16[128,256]{1,0:T(8,128)(2,1)S(1)}, u32[]{:S(2)}, u32[]{:S(2)}) collective-permute-start(bf16[128,256]{1,0:T(8,128)(2,1)S(1)} %get-tuple-element.52), channel_id=1, source_target_pairs={{0,1},{1,0},{2,3},{3,2},{4,5},{5,4},{6,7},{7,6},{8,9},{9,8},{10,11... | collective-permute-start | bytes 196616 | tf_op jit(solution)/shard_map/ppermute | solution.py:425
  65.3 2.0 %collective-permute-done.15.refs_4_.refs_1_ = bf16[128,256]{1,0:T(8,128)(2,1)S(1)} collective-permute-done((bf16[128,256]{1,0:T(8,128)(2,1)S(1)}, bf16[128,256]{1,0:T(8,128)(2,1)S(1)}, u32[]{:S(2)}, u32[]{:S(2)}) %collective-permute-start.15) | collective-permute-done | bytes 65568 | tf_op jit(solution)/shard_map/ppermute | solution.py:425
  67.6 3.3 %collective-permute-start.17 = (bf16[64,256]{1,0:T(8,128)(2,1)S(1)}, bf16[64,256]{1,0:T(8,128)(2,1)S(1)}, u32[]{:S(2)}, u32[]{:S(2)}) collective-permute-start(bf16[64,256]{1,0:T(8,128)(2,1)S(1)} %get-tuple-element.55.refs_1_), channel_id=1, source_target_pairs={{0,128},{8,136},{16,144},{24,152},{32,160},{40,168},{48,176},{56,1... | collective-permute-start | bytes 98312 | tf_op jit(solution)/shard_map/ppermute | solution.py:423
  70.9 1.7 %shard_map.118 = (bf16[64,2048]{1,0:T(8,128)(2,1)S(1)}, bf16[64,2048]{1,0:T(8,128)(2,1)S(1)}, f32[32,32]{1,0:T(8,128)S(1)}) custom-call(f32[32,32,128]{2,1,0:T(8,128)S(1)} %bitcast.35, bf16[64,256]{1,0:T(8,128)(2,1)S(1)} %get-tuple-element.55.refs_1_), custom_call_target="tpu_custom_call" | custom-call | flops 67108864 | bytes 524288 | tf_op jit(solution)/shard_map/pallas_call | solution.py:27
  73.5 1.6 %collective-permute-start.18 = (bf16[64,256]{1,0:T(8,128)(2,1)S(1)}, bf16[64,256]{1,0:T(8,128)(2,1)S(1)}, u32[]{:S(2)}, u32[]{:S(2)}) collective-permute-start(bf16[64,256]{1,0:T(8,128)(2,1)S(1)} %get-tuple-element.60), channel_id=1, source_target_pairs={{0,64},{8,72},{16,80},{24,88},{32,96},{40,104},{48,112},{56,120},{... | collective-permute-start | bytes 98312 | tf_op jit(solution)/shard_map/ppermute | solution.py:423
  75.0 0.7 collective-permute-start.16
  75.9 1.6 %collective-permute-done.18.refs_1_ = bf16[64,256]{1,0:T(8,128)(2,1)S(1)} collective-permute-done((bf16[64,256]{1,0:T(8,128)(2,1)S(1)}, bf16[64,256]{1,0:T(8,128)(2,1)S(1)}, u32[]{:S(2)}, u32[]{:S(2)}) %collective-permute-start.18) | collective-permute-done | bytes 32800 | tf_op jit(solution)/shard_map/ppermute | solution.py:423
  77.7 2.7 %collective-permute-start.19 = (bf16[64,256]{1,0:T(8,128)(2,1)S(1)}, bf16[64,256]{1,0:T(8,128)(2,1)S(1)}, u32[]{:S(2)}, u32[]{:S(2)}) collective-permute-start(bf16[64,256]{1,0:T(8,128)(2,1)S(1)} %get-tuple-element.62), channel_id=1, source_target_pairs={{0,32},{8,40},{16,48},{24,56},{32,0},{40,8},{48,16},{56,24},{64,96... | collective-permute-start | bytes 98312 | tf_op jit(solution)/shard_map/ppermute | solution.py:423
  80.6 2.6 %collective-permute-done.19.refs_1_ = bf16[64,256]{1,0:T(8,128)(2,1)S(1)} collective-permute-done((bf16[64,256]{1,0:T(8,128)(2,1)S(1)}, bf16[64,256]{1,0:T(8,128)(2,1)S(1)}, u32[]{:S(2)}, u32[]{:S(2)}) %collective-permute-start.19) | collective-permute-done | bytes 32800 | tf_op jit(solution)/shard_map/ppermute | solution.py:423
  83.4 1.2 collective-permute-start.20
  84.6 1.9 %collective-permute-start.13 = (bf16[64,256]{1,0:T(8,128)(2,1)S(1)}, bf16[64,256]{1,0:T(8,128)(2,1)S(1)}, u32[]{:S(2)}, u32[]{:S(2)}) collective-permute-start(bf16[64,256]{1,0:T(8,128)(2,1)S(1)} %get-tuple-element.46.refs_3_), channel_id=1, source_target_pairs={{8,16},{24,32},{40,48},{56,64},{72,80},{88,96},{104,112},{120,128}... | collective-permute-start | bytes 98312 | tf_op jit(solution)/shard_map/ppermute | solution.py:429
  86.8 0.6 collective-permute-done.20.refs_1_
  87.6 1.6 %collective-permute-start.21 = (bf16[64,256]{1,0:T(8,128)(2,1)S(1)}, bf16[64,256]{1,0:T(8,128)(2,1)S(1)}, u32[]{:S(2)}, u32[]{:S(2)}) collective-permute-start(bf16[64,256]{1,0:T(8,128)(2,1)S(1)} %get-tuple-element.66), channel_id=1, source_target_pairs={{0,8},{8,0},{16,24},{24,16},{32,40},{40,32},{48,56},{56,48},{64,72... | collective-permute-start | bytes 98312 | tf_op jit(solution)/shard_map/ppermute | solution.py:423
  89.2 0.6 collective-permute-done.13.refs_3_
  90.7 1.6 %shard_map.128 = (bf16[64,2048]{1,0:T(8,128)(2,1)S(1)}, bf16[64,2048]{1,0:T(8,128)(2,1)S(1)}, f32[32,128]{1,0:T(8,128)S(1)}) custom-call(f32[64,2048]{1,0:T(8,128)S(1)} %shard_map.115.refs_2_.refs_0_, f32[64,256]{1,0:T(8,128)S(1)} %shard_map.127.refs_1_, bf16[64,256]{1,0:T(8,128)(2,1)S(1)} %collective-permute-done.21.refs_2_, ...), custom_call_target="tpu_custom_call" | custom-call | flops 134217728 | bytes 3248128 | tf_op jit(solution)/shard_map/pallas_call | solution.py:27
  92.8 0.8 collective-permute-done.22.refs_1_
  93.7 15.1 %all_to_all.10.refs_0_ = f32[16,32,128]{2,1,0:T(8,128)S(1)} all-to-all(f32[16,32,128]{2,1,0:T(8,128)S(1)} %shard_map.129), channel_id=1, replica_groups={{0,16,32,48,64,80,96,112,128,144,160,176,192,208,224,240},{8,24,40,56,7..., dimensions={0} | all-to-all | bytes 524288 | tf_op jit(solution)/shard_map/all_to_all | solution.py:580
  108.8 0.7 shard_map.130
  109.5 7.6 %all-to-all-start.1 = ((f32[8,32,128]{2,1,0:T(8,128)}), f32[8,32,128]{2,1,0:T(8,128)S(1)}, u32[]{:S(2)}, u32[]{:S(2)}) async-start(f32[8,32,128]{2,1,0:T(8,128)} %shard_map.130), calls=%async_computation.1 | async-start | bytes 262144 | tf_op jit(solution)/shard_map/all_to_all | solution.py:582
  117.1 1.3 shard_map.108
  118.4 7.8 %all-to-all-done.1.refs_0_ = f32[8,32,128]{2,1,0:T(8,128)S(1)} async-done(((f32[8,32,128]{2,1,0:T(8,128)}), f32[8,32,128]{2,1,0:T(8,128)S(1)}, u32[]{:S(2)}, u32[]{:S(2)}) %all-to-all-start.1) | async-done | bytes 131104 | tf_op jit(solution)/shard_map/all_to_all | solution.py:582
  126.2 4.3 %shard_map.131 = f32[64,32,128]{2,1,0:T(8,128)} custom-call(f32[8,32,128]{2,1,0:T(8,128)S(1)} %all-to-all-done.1.refs_0_, bf16[64,2048]{1,0:T(8,128)(2,1)S(1)} %get-tuple-element.68.refs_1_, bf16[64,2048]{1,0:T(8,128)(2,1)S(1)} %get-tuple-element.69.refs_2_, bf16[64,2048]{1,0:T(8,128)(2,1)S(1)} %get-tuple-element.56.refs_2_.refs_4_.refs_3_, ...), custom_call_target="tpu_custom_call" | custom-call | flops 67108864 | bytes 1179648 | tf_op jit(solution)/shard_map/pallas_call | solution.py:27
  (72 shorter events, 9.2 us)
Async XLA Ops:
  0.6 9.4 %copy-start = (s32[32,8,4,2]{0,3,2,1:T(2,128)S(1)}, s32[32,8,4,2]{0,3,2,1:T(2,128)}, u32[]{:S(2)}) copy-start(s32[32,8,4,2]{0,3,2,1:T(2,128)} %param.8) | copy-start | bytes 24580
  3.1 1.7 %collective-permute-start = (bf16[64,256]{1,0:T(8,128)(2,1)S(1)}, bf16[64,256]{1,0:T(8,128)(2,1)S(1)}, u32[]{:S(2)}, u32[]{:S(2)}) collective-permute-start(bf16[64,256]{1,0:T(8,128)(2,1)S(1)} %get-tuple-element.36.refs_0_), channel_id=1, source_target_pairs={{0,8},{8,0},{16,24},{24,16},{32,40},{40,32},{48,56},{56,48},{64,72... | collective-permute-start | bytes 98312 | tf_op jit(solution)/shard_map/ppermute | solution.py:423
  4.7 1.2 copy-start.1
  6.0 6.6 %collective-permute-start.1 = (bf16[64,256]{1,0:T(8,128)(2,1)S(1)}, bf16[64,256]{1,0:T(8,128)(2,1)S(1)}, u32[]{:S(2)}, u32[]{:S(2)}) collective-permute-start(bf16[64,256]{1,0:T(8,128)(2,1)S(1)} %shard_map.89.refs_2_.refs_0_), channel_id=1, source_target_pairs={{0,16},{8,24},{16,0},{24,8},{32,48},{40,56},{48,32},{56,40},{64,80... | collective-permute-start | bytes 98312 | tf_op jit(solution)/shard_map/ppermute | solution.py:423
  11.1 1.4 %copy-start.2 = (bf16[3,2,2,256,256]{4,3,2,1,0:T(8,128)(2,1)S(1)}, bf16[3,2,2,256,256]{4,3,2,1,0:T(8,128)(2,1)}, u32[]{:S(2)}) copy-start(bf16[3,2,2,256,256]{4,3,2,1,0:T(8,128)(2,1)} %copy-done.1) | copy-start | bytes 4718596
  12.5 1.3 %copy-start.7 = (bf16[1,1,2,16,128,128]{5,4,3,2,1,0:T(8,128)(2,1)S(1)}, bf16[1,1,2,16,128,128]{5,4,3,2,1,0:T(8,128)(2,1)}, u32[]{:S(2)}) copy-start(bf16[1,1,2,16,128,128]{5,4,3,2,1,0:T(8,128)(2,1)} %param.9) | copy-start | bytes 3145732
  12.6 1.6 %copy-start.3 = (bf16[3,2,2,256,256]{4,3,2,1,0:T(8,128)(2,1)S(1)}, bf16[3,2,2,256,256]{4,3,2,1,0:T(8,128)(2,1)}, u32[]{:S(2)}) copy-start(bf16[3,2,2,256,256]{4,3,2,1,0:T(8,128)(2,1)} %copy-done.1) | copy-start | bytes 4718596
  12.8 5.5 %collective-permute-start.2 = (bf16[64,256]{1,0:T(8,128)(2,1)S(1)}, bf16[64,256]{1,0:T(8,128)(2,1)S(1)}, u32[]{:S(2)}, u32[]{:S(2)}) collective-permute-start(bf16[64,256]{1,0:T(8,128)(2,1)S(1)} %shard_map.93.refs_2_.refs_0_), channel_id=1, source_target_pairs={{0,32},{8,40},{16,48},{24,56},{32,0},{40,8},{48,16},{56,24},{64,96... | collective-permute-start | bytes 98312 | tf_op jit(solution)/shard_map/ppermute | solution.py:423
  13.8 4.8 %collective-permute-start.3 = (bf16[64,256]{1,0:T(8,128)(2,1)S(1)}, bf16[64,256]{1,0:T(8,128)(2,1)S(1)}, u32[]{:S(2)}, u32[]{:S(2)}) collective-permute-start(bf16[64,256]{1,0:T(8,128)(2,1)S(1)} %get-tuple-element.38.refs_2_), channel_id=1, source_target_pairs={{0,8},{8,0},{16,24},{24,16},{32,40},{40,32},{48,56},{56,48},{64,72... | collective-permute-start | bytes 98312 | tf_op jit(solution)/shard_map/ppermute | solution.py:423
  18.5 4.0 %collective-permute-start.4 = (bf16[64,256]{1,0:T(8,128)(2,1)S(1)}, bf16[64,256]{1,0:T(8,128)(2,1)S(1)}, u32[]{:S(2)}, u32[]{:S(2)}) collective-permute-start(bf16[64,256]{1,0:T(8,128)(2,1)S(1)} %shard_map.96.refs_0_), channel_id=1, source_target_pairs={{0,64},{8,72},{16,80},{24,88},{32,96},{40,104},{48,112},{56,120},{... | collective-permute-start | bytes 98312 | tf_op jit(solution)/shard_map/ppermute | solution.py:423
  22.7 5.5 %collective-permute-start.5 = (bf16[64,256]{1,0:T(8,128)(2,1)S(1)}, bf16[64,256]{1,0:T(8,128)(2,1)S(1)}, u32[]{:S(2)}, u32[]{:S(2)}) collective-permute-start(bf16[64,256]{1,0:T(8,128)(2,1)S(1)} %shard_map.98.refs_0_), channel_id=1, source_target_pairs={{0,128},{8,136},{16,144},{24,152},{32,160},{40,168},{48,176},{56,1... | collective-permute-start | bytes 98312 | tf_op jit(solution)/shard_map/ppermute | solution.py:423
  28.4 4.7 %collective-permute-start.6 = (bf16[128,256]{1,0:T(8,128)(2,1)S(1)}, bf16[128,256]{1,0:T(8,128)(2,1)S(1)}, u32[]{:S(2)}, u32[]{:S(2)}) collective-permute-start(bf16[128,256]{1,0:T(8,128)(2,1)S(1)} %shard_map.100.refs_0_), channel_id=1, source_target_pairs={{0,1},{1,0},{2,3},{3,2},{4,5},{5,4},{6,7},{7,6},{8,9},{9,8},{10,11... | collective-permute-start | bytes 196616 | tf_op jit(solution)/shard_map/ppermute | solution.py:425
  33.2 11.0 %copy-start.6 = (bf16[1,1,4,2,256,256]{5,4,3,2,1,0:T(8,128)(2,1)S(1)}, bf16[1,1,4,2,256,256]{5,4,3,2,1,0:T(8,128)(2,1)}, u32[]{:S(2)}) copy-start(bf16[1,1,4,2,256,256]{5,4,3,2,1,0:T(8,128)(2,1)} %param.10) | copy-start | bytes 3145732
  33.2 5.2 %collective-permute-start.7 = (bf16[64,256]{1,0:T(8,128)(2,1)S(1)}, bf16[64,256]{1,0:T(8,128)(2,1)S(1)}, u32[]{:S(2)}, u32[]{:S(2)}) collective-permute-start(bf16[64,256]{1,0:T(8,128)(2,1)S(1)} %shard_map.102.refs_0_), channel_id=1, source_target_pairs={{0,2},{1,3},{2,0},{3,1},{4,6},{5,7},{6,4},{7,5},{8,10},{9,11},{10,... | collective-permute-start | bytes 98312 | tf_op jit(solution)/shard_map/ppermute | solution.py:425
  34.5 9.7 %collective-permute-start.8 = (bf16[64,256]{1,0:T(8,128)(2,1)S(1)}, bf16[64,256]{1,0:T(8,128)(2,1)S(1)}, u32[]{:S(2)}, u32[]{:S(2)}) collective-permute-start(bf16[64,256]{1,0:T(8,128)(2,1)S(1)} %get-tuple-element.39.refs_3_), channel_id=1, source_target_pairs={{8,16},{24,32},{40,48},{56,64},{72,80},{88,96},{104,112},{120,128}... | collective-permute-start | bytes 98312 | tf_op jit(solution)/shard_map/ppermute | solution.py:429
  36.4 7.8 %collective-permute-start.9 = (bf16[64,256]{1,0:T(8,128)(2,1)S(1)}, bf16[64,256]{1,0:T(8,128)(2,1)S(1)}, u32[]{:S(2)}, u32[]{:S(2)}) collective-permute-start(bf16[64,256]{1,0:T(8,128)(2,1)S(1)} %get-tuple-element.41.refs_5_), channel_id=1, source_target_pairs={{1,2},{3,4},{5,6},{2,1},{4,3},{6,5},{9,10},{11,12},{13,14},{10,9},... | collective-permute-start | bytes 98312 | tf_op jit(solution)/shard_map/ppermute | solution.py:429
  37.3 7.8 %copy-start.5 = (bf16[1,1,2,256,2048]{4,3,2,1,0:T(8,128)(2,1)S(1)}, bf16[1,1,2,256,2048]{4,3,2,1,0:T(8,128)(2,1)}, u32[]{:S(2)}) copy-start(bf16[1,1,2,256,2048]{4,3,2,1,0:T(8,128)(2,1)} %param.12) | copy-start | bytes 6291460
  38.6 8.0 %collective-permute-start.10 = (bf16[64,256]{1,0:T(8,128)(2,1)S(1)}, bf16[64,256]{1,0:T(8,128)(2,1)S(1)}, u32[]{:S(2)}, u32[]{:S(2)}) collective-permute-start(bf16[64,256]{1,0:T(8,128)(2,1)S(1)} %shard_map.104.refs_7_.refs_0_), channel_id=1, source_target_pairs={{0,4},{1,5},{2,6},{3,7},{4,0},{5,1},{6,2},{7,3},{8,12},{9,13},{10,... | collective-permute-start | bytes 98312 | tf_op jit(solution)/shard_map/ppermute | solution.py:425
  48.2 8.1 %copy-start.9 = (f32[64,2048]{1,0:T(8,128)}, f32[64,2048]{1,0:T(8,128)S(1)}, u32[]{:S(2)}) copy-start(f32[64,2048]{1,0:T(8,128)S(1)} %get-tuple-element.42.refs_0_) | copy-start | bytes 1572868
  48.2 7.9 %collective-permute-start.11 = (bf16[64,256]{1,0:T(8,128)(2,1)S(1)}, bf16[64,256]{1,0:T(8,128)(2,1)S(1)}, u32[]{:S(2)}, u32[]{:S(2)}) collective-permute-start(bf16[64,256]{1,0:T(8,128)(2,1)S(1)} %get-tuple-element.49), channel_id=1, source_target_pairs={{0,4},{1,5},{2,6},{3,7},{4,0},{5,1},{6,2},{7,3},{8,12},{9,13},{10,... | collective-permute-start | bytes 98312 | tf_op jit(solution)/shard_map/ppermute | solution.py:425
  56.4 6.1 %collective-permute-start.14 = (bf16[64,256]{1,0:T(8,128)(2,1)S(1)}, bf16[64,256]{1,0:T(8,128)(2,1)S(1)}, u32[]{:S(2)}, u32[]{:S(2)}) collective-permute-start(bf16[64,256]{1,0:T(8,128)(2,1)S(1)} %get-tuple-element.50.refs_2_), channel_id=1, source_target_pairs={{0,2},{1,3},{2,0},{3,1},{4,6},{5,7},{6,4},{7,5},{8,10},{9,11},{10,... | collective-permute-start | bytes 98312 | tf_op jit(solution)/shard_map/ppermute | solution.py:425
  62.7 4.7 %collective-permute-start.15 = (bf16[128,256]{1,0:T(8,128)(2,1)S(1)}, bf16[128,256]{1,0:T(8,128)(2,1)S(1)}, u32[]{:S(2)}, u32[]{:S(2)}) collective-permute-start(bf16[128,256]{1,0:T(8,128)(2,1)S(1)} %get-tuple-element.52), channel_id=1, source_target_pairs={{0,1},{1,0},{2,3},{3,2},{4,5},{5,4},{6,7},{7,6},{8,9},{9,8},{10,11... | collective-permute-start | bytes 196616 | tf_op jit(solution)/shard_map/ppermute | solution.py:425
  65.1 5.7 %copy-start.8 = (f32[32,1,1,2,2048]{4,3,2,1,0:T(2,128)S(1)}, f32[32,1,1,2,2048]{4,3,2,1,0:T(2,128)}, u32[]{:S(2)}) copy-start(f32[32,1,1,2,2048]{4,3,2,1,0:T(2,128)} %param.7) | copy-start | bytes 1572868
  67.6 5.7 %collective-permute-start.17 = (bf16[64,256]{1,0:T(8,128)(2,1)S(1)}, bf16[64,256]{1,0:T(8,128)(2,1)S(1)}, u32[]{:S(2)}, u32[]{:S(2)}) collective-permute-start(bf16[64,256]{1,0:T(8,128)(2,1)S(1)} %get-tuple-element.55.refs_1_), channel_id=1, source_target_pairs={{0,128},{8,136},{16,144},{24,152},{32,160},{40,168},{48,176},{56,1... | collective-permute-start | bytes 98312 | tf_op jit(solution)/shard_map/ppermute | solution.py:423
  73.5 4.0 %collective-permute-start.18 = (bf16[64,256]{1,0:T(8,128)(2,1)S(1)}, bf16[64,256]{1,0:T(8,128)(2,1)S(1)}, u32[]{:S(2)}, u32[]{:S(2)}) collective-permute-start(bf16[64,256]{1,0:T(8,128)(2,1)S(1)} %get-tuple-element.60), channel_id=1, source_target_pairs={{0,64},{8,72},{16,80},{24,88},{32,96},{40,104},{48,112},{56,120},{... | collective-permute-start | bytes 98312 | tf_op jit(solution)/shard_map/ppermute | solution.py:423
  75.0 5.4 %collective-permute-start.16 = (bf16[64,256]{1,0:T(8,128)(2,1)S(1)}, bf16[64,256]{1,0:T(8,128)(2,1)S(1)}, u32[]{:S(2)}, u32[]{:S(2)}) collective-permute-start(bf16[64,256]{1,0:T(8,128)(2,1)S(1)} %get-tuple-element.48.refs_5_), channel_id=1, source_target_pairs={{1,2},{3,4},{5,6},{2,1},{4,3},{6,5},{9,10},{11,12},{13,14},{10,9},... | collective-permute-start | bytes 98312 | tf_op jit(solution)/shard_map/ppermute | solution.py:429
  77.7 8.9 %copy-start.4 = (bf16[1,1,2,2048,256]{4,3,2,1,0:T(8,128)(2,1)S(1)}, bf16[1,1,2,2048,256]{4,3,2,1,0:T(8,128)(2,1)}, u32[]{:S(2)}) copy-start(bf16[1,1,2,2048,256]{4,3,2,1,0:T(8,128)(2,1)} %param.11) | copy-start | bytes 6291460
  77.7 5.5 %collective-permute-start.19 = (bf16[64,256]{1,0:T(8,128)(2,1)S(1)}, bf16[64,256]{1,0:T(8,128)(2,1)S(1)}, u32[]{:S(2)}, u32[]{:S(2)}) collective-permute-start(bf16[64,256]{1,0:T(8,128)(2,1)S(1)} %get-tuple-element.62), channel_id=1, source_target_pairs={{0,32},{8,40},{16,48},{24,56},{32,0},{40,8},{48,16},{56,24},{64,96... | collective-permute-start | bytes 98312 | tf_op jit(solution)/shard_map/ppermute | solution.py:423
  80.4 6.1 %collective-permute-start.12 = (bf16[64,256]{1,0:T(8,128)(2,1)S(1)}, bf16[64,256]{1,0:T(8,128)(2,1)S(1)}, u32[]{:S(2)}, u32[]{:S(2)}) collective-permute-start(bf16[64,256]{1,0:T(8,128)(2,1)S(1)} %get-tuple-element.45.refs_2_), channel_id=1, source_target_pairs={{0,8},{8,0},{16,24},{24,16},{32,40},{40,32},{48,56},{56,48},{64,72... | collective-permute-start | bytes 98312 | tf_op jit(solution)/shard_map/ppermute | solution.py:423
  83.4 4.0 %collective-permute-start.20 = (bf16[64,256]{1,0:T(8,128)(2,1)S(1)}, bf16[64,256]{1,0:T(8,128)(2,1)S(1)}, u32[]{:S(2)}, u32[]{:S(2)}) collective-permute-start(bf16[64,256]{1,0:T(8,128)(2,1)S(1)} %get-tuple-element.64), channel_id=1, source_target_pairs={{0,16},{8,24},{16,0},{24,8},{32,48},{40,56},{48,32},{56,40},{64,80... | collective-permute-start | bytes 98312 | tf_op jit(solution)/shard_map/ppermute | solution.py:423
  84.6 5.2 %collective-permute-start.13 = (bf16[64,256]{1,0:T(8,128)(2,1)S(1)}, bf16[64,256]{1,0:T(8,128)(2,1)S(1)}, u32[]{:S(2)}, u32[]{:S(2)}) collective-permute-start(bf16[64,256]{1,0:T(8,128)(2,1)S(1)} %get-tuple-element.46.refs_3_), channel_id=1, source_target_pairs={{8,16},{24,32},{40,48},{56,64},{72,80},{88,96},{104,112},{120,128}... | collective-permute-start | bytes 98312 | tf_op jit(solution)/shard_map/ppermute | solution.py:429
  87.6 3.1 %collective-permute-start.21 = (bf16[64,256]{1,0:T(8,128)(2,1)S(1)}, bf16[64,256]{1,0:T(8,128)(2,1)S(1)}, u32[]{:S(2)}, u32[]{:S(2)}) collective-permute-start(bf16[64,256]{1,0:T(8,128)(2,1)S(1)} %get-tuple-element.66), channel_id=1, source_target_pairs={{0,8},{8,0},{16,24},{24,16},{32,40},{40,32},{48,56},{56,48},{64,72... | collective-permute-start | bytes 98312 | tf_op jit(solution)/shard_map/ppermute | solution.py:423
  90.7 26.4 %copy-start.10 = (f32[64,2048]{1,0:T(8,128)S(1)}, f32[64,2048]{1,0:T(8,128)}, u32[]{:S(2)}) copy-start(f32[64,2048]{1,0:T(8,128)} %copy-done.9) | copy-start | bytes 1572868
  92.3 1.4 %collective-permute-start.22 = (f32[1,32,128]{2,1,0:T(8,128)S(1)}, f32[1,32,128]{2,1,0:T(8,128)S(1)}, u32[]{:S(2)}, u32[]{:S(2)}) collective-permute-start(f32[1,32,128]{2,1,0:T(8,128)S(1)} %bitcast.36), channel_id=1, source_target_pairs={{0,8},{8,0},{16,24},{24,16},{32,40},{40,32},{48,56},{56,48},{64,72... | collective-permute-start | bytes 49160 | tf_op jit(solution)/shard_map/ppermute | solution.py:423
  109.5 16.7 %all-to-all-start.1 = ((f32[8,32,128]{2,1,0:T(8,128)}), f32[8,32,128]{2,1,0:T(8,128)S(1)}, u32[]{:S(2)}, u32[]{:S(2)}) async-start(f32[8,32,128]{2,1,0:T(8,128)} %shard_map.130), calls=%async_computation.1 | async-start | bytes 262144 | tf_op jit(solution)/shard_map/all_to_all | solution.py:582

commit v3 on v2

--- a/solution.py
+++ b/solution.py
@@ -1,4 +1,5 @@
 import functools
+import math
 
 import jax
 import jax.numpy as jnp
@@ -13,7 +14,7 @@
 VM = pl.BlockSpec(memory_space=pltpu.VMEM)
 SM = pl.BlockSpec(memory_space=pltpu.SMEM)
 
-HEAD, EARLY, LATE = 214, 203, 200
+HEAD, EARLY, LATE, OTHER = 214, 200, 188, 180
 
 
 def call(kernel, outs, args, flops, smem=0, limit=24, after=(), out_spec=VM, scratch=()):
@@ -124,25 +125,26 @@
     )(tall, squeeze)
 
 
-def load_kernel(begin, f_in, o_ref, sem):
+def load_kernel(begin, f_in, *rest):
+    o_ref, sem = rest[-2:]
     copy = pltpu.make_async_copy(f_in.at[begin : begin + o_ref.shape[0]], o_ref, sem)
     copy.start()
     copy.wait()
 
 
-def load(sections, begin, end, limit):
+def load(sections, begin, end, limit, after=()):
     shape = (end - begin,) + sections.shape[1:]
     return pl.pallas_call(
         functools.partial(load_kernel, begin),
-        in_specs=[pl.BlockSpec(memory_space=pltpu.HBM)],
+        in_specs=[pl.BlockSpec(memory_space=pltpu.HBM)] + [VM] * len(after),
         out_specs=VM,
         out_shape=jax.ShapeDtypeStruct(shape, BF16),
         scratch_shapes=[pltpu.SemaphoreType.DMA],
         cost_estimate=pl.CostEstimate(
-            flops=0, bytes_accessed=2 * sections.size, transcendentals=0
+            flops=0, bytes_accessed=2 * math.prod(shape), transcendentals=0
         ),
         compiler_params=pltpu.CompilerParams(vmem_limit_bytes=limit * 2**18),
-    )(sections)
+    )(sections, *after)
 
 
 def pick_kernel(leaf, info, vb_ref, *outs):
@@ -172,19 +174,31 @@
     return jnp.where(below, re, s[cols:, :cols] - s[:cols, cols:])
 
 
-def own_kernel(level, adjoint, s_ref, f_ref, o_ref):
-    rows = o_ref.shape[0]
+def own_kernel(at, adjoint, s_ref, f_ref, *rest):
+    o_ref = rest[-1]
+    rows = o_ref.shape[0] // len(rest)
     product = adj if adjoint else mul
-    o_ref[...] = product(s_ref[:rows], f_ref[level, 0, 0], f_ref[level, 0, 1])
-
-
-def up_kernel(level, own_ref, r_ref, f_ref, *rest):
-    rows = own_ref.shape[0]
-    o_ref = rest[-1]
-    state = own_ref[...] + mul(r_ref[:rows], f_ref[level, 1, 0], f_ref[level, 1, 1])
-    o_ref[:rows] = state.astype(BF16)
-    if len(rest) > 1:
-        o_ref[rows:] = rest[0][...]
+    for part, f in enumerate((f_ref,) + rest[:-1]):
+        cut = slice(part * rows, (part + 1) * rows)
+        o_ref[cut] = product(s_ref[cut], f[at, 0, 0], f[at, 0, 1])
+
+
+def up_kernel(at, count, own_ref, r_ref, *rest):
+    rows = own_ref.shape[0] // count
+    outs = rest[count:]
+    for part, f in enumerate(rest[:count]):
+        cut = slice(part * rows, (part + 1) * rows)
+        state = own_ref[cut] + mul(r_ref[cut], f[at, 1, 0], f[at, 1, 1])
+        if len(outs) == count:
+            outs[part][...] = state.astype(BF16)
+        else:
+            outs[0][cut] = state.astype(BF16)
+
+
+def join_kernel(a_ref, b_ref, o_ref):
+    rows = a_ref.shape[0]
+    o_ref[:rows] = a_ref[...]
+    o_ref[rows:] = b_ref[...]
 
 
 def leaves_kernel(leaf, adjoint, x_ref, b_ref, o_ref):
@@ -195,26 +209,31 @@
 
 
 def sides_kernel(leaf, info, near_ref, ra_ref, rb_ref, rc_ref, rd_ref, b_ref, o_ref):
-    rows = near_ref.shape[0]
     o_ref[...] = near_ref[...]
     for at, ref in enumerate((ra_ref, rb_ref, rc_ref, rd_ref)):
         side = info[8 + at]
-        x = ref[ref.shape[0] - rows :]
-        term = mul(x, b_ref[side, 0], b_ref[side, 1])
+        term = mul(ref[...], b_ref[side, 0], b_ref[side, 1])
         for e in range(2):
             o_ref[:, leaf_at(info[2 * side + e], leaf)] += term[:, e * leaf : (e + 1) * leaf]
 
 
-def field_kernel(level, own_ref, r_ref, f_ref, near_ref, e_ref, y_ref, yb_ref, g_ref, m_ref):
-    rows = own_ref.shape[0]
-    state = own_ref[...] + mul(r_ref[:rows], f_ref[level, 1, 0], f_ref[level, 1, 1])
-    y = near_ref[...] + mul(state.astype(BF16), e_ref[0], e_ref[1])
+def field_kernel(info, mine_ref, sent_ref, near_ref, e_ref, y_ref, yb_ref, g_ref, state_ref):
+    chosen(info, mine_ref, sent_ref, state_ref)
+    y = near_ref[...] + mul(state_ref[...], e_ref[0], e_ref[1])
     y_ref[...] = y
     yb = y.astype(BF16)
     yb_ref[...] = yb
-    g = adj(yb, e_ref[0], e_ref[1]).astype(BF16)
-    g_ref[...] = g
-    m_ref[...] = adj(g, f_ref[level, 1, 0], f_ref[level, 1, 1]).astype(BF16)
+    g_ref[...] = adj(yb, e_ref[0], e_ref[1]).astype(BF16)
+
+
+def chosen(info, mine_ref, sent_ref, o_ref):
+    @pl.when(info[12] == 1)
+    def _():
+        o_ref[...] = mine_ref[...]
+
+    @pl.when(info[12] == 0)
+    def _():
+        o_ref[...] = sent_ref[...]
 
 
 def shape_kernel(leaf, y_ref, o_ref):
@@ -231,33 +250,49 @@
         o_ref[...] = adj(x, b_ref[side, 0], b_ref[side, 1]).astype(BF16)
 
 
-def down_kernel(level, own_ref, r_ref, f_ref, *rest):
-    rows = own_ref.shape[0]
-    g_ref, m_ref = rest[-2:]
-    g = (own_ref[...] + r_ref[:rows].astype(F32)).astype(BF16)
-    g_ref[...] = g
-    m_ref[:rows] = adj(g, f_ref[level, 1, 0], f_ref[level, 1, 1]).astype(BF16)
-    if len(rest) > 2:
-        m_ref[rows:] = rest[0][...]
+def turn_kernel(at, a_ref, b_ref, f_ref, fo_ref, g_ref, m_ref):
+    rows = a_ref.shape[0]
+    for part, (x, f) in enumerate(((a_ref, f_ref), (b_ref, fo_ref))):
+        cut = slice(part * rows, (part + 1) * rows)
+        g_ref[cut] = x[...]
+        m_ref[cut] = adj(x[...], f[at, 1, 0], f[at, 1, 1]).astype(BF16)
+
+
+def down_kernel(at, own_ref, r_ref, f_ref, fo_ref, g_ref, m_ref):
+    rows = own_ref.shape[0] // 2
+    for part, f in enumerate((f_ref, fo_ref)):
+        cut = slice(part * rows, (part + 1) * rows)
+        g = (own_ref[cut] + r_ref[cut].astype(F32)).astype(BF16)
+        g_ref[cut] = g
+        m_ref[cut] = adj(g, f[at, 1, 0], f[at, 1, 1]).astype(BF16)
+
+
+def last_kernel(own_ref, r_ref, f_ref, fo_ref, mine_ref, other_ref):
+    rows = mine_ref.shape[0]
+    a, b = [
+        (own_ref[cut] + r_ref[cut].astype(F32)).astype(BF16)
+        for cut in (slice(0, rows), slice(rows, 2 * rows))
+    ]
+    for x, f, y, h, o_ref in ((a, f_ref, b, fo_ref, mine_ref), (b, fo_ref, a, f_ref, other_ref)):
+        message = adj(y, h[0, 1, 0], h[0, 1, 1]).astype(BF16).astype(F32)
+        o_ref[...] = (adj(x, f[0, 0, 0], f[0, 0, 1]) + message).astype(BF16)
 
 
 def gather_kernel(leaf, info, near_ref, ra_ref, rb_ref, rc_ref, rd_ref, o_ref):
-    rows = near_ref.shape[0]
     o_ref[...] = near_ref[...]
     for at, ref in enumerate((ra_ref, rb_ref, rc_ref, rd_ref)):
         side = info[8 + at]
-        low = ref.shape[0] - rows
         for e in range(2):
-            o_ref[:, leaf_at(info[2 * side + e], leaf)] += ref[
-                low:, e * leaf : (e + 1) * leaf
-            ].astype(F32)
-
-
-def close_kernel(near_ref, own_ref, r_ref, c_ref, vh_ref, vl_ref, vv_ref, zh_ref, zl_ref, p_ref):
-    rows = own_ref.shape[0]
+            o_ref[:, leaf_at(info[2 * side + e], leaf)] += ref[:, e * leaf : (e + 1) * leaf].astype(F32)
+
+
+def close_kernel(
+    info, near_ref, mine_ref, sent_ref, c_ref, vh_ref, vl_ref, vv_ref, zh_ref, zl_ref, p_ref, g_ref
+):
+    rows = mine_ref.shape[0]
     cols = rows // 2
-    g = (own_ref[...] + r_ref[...].astype(F32)).astype(BF16)
-    high, low = split(near_ref[...] + adj(g, c_ref[0], c_ref[1]))
+    chosen(info, mine_ref, sent_ref, g_ref)
+    high, low = split(near_ref[...] + adj(g_ref[...], c_ref[0], c_ref[1]))
     zh_ref[...] = high
     zl_ref[...] = low
     many = jnp.concatenate([high, low, vh_ref[...], vl_ref[...]], 0)
@@ -415,14 +450,26 @@
     own_leaves = lax.dynamic_slice(edge_leaves, (row_at, col_at, 0, 0), (1, 1, 4, 2)).reshape(8)
     odd_row, odd_col = row_at % 2, col_at % 2
     order = jnp.stack([1 - odd_row, odd_row, 3 - odd_col, 2 + odd_col]).astype(jnp.int32)
-    info = jnp.concatenate([own_leaves, order])
+    info = jnp.concatenate([own_leaves, order, odd_row[None].astype(jnp.int32)])
     tall = v_block.reshape(cols, 2, leaves, leaf).transpose(0, 2, 1, 3).reshape(cols, -1, leaf)
 
     def partner(x, level):
-        if level < row_bits:
-            return lax.ppermute(x, "px", [(i, i ^ 1 << level) for i in range(row_count)])
-        bit = level - row_bits
-        return lax.ppermute(x, "py", [(i, i ^ 1 << bit) for i in range(col_count)])
+        near_bit, far_bit = (1 << level, 0) if level < row_bits else (0, 1 << level - row_bits)
+        pairs = [
+            (i * col_count + j, (i ^ near_bit) * col_count + (j ^ far_bit))
+            for i in range(1, row_count, 2)
+            for j in range(col_count)
+        ]
+        return lax.ppermute(x, ("px", "py"), pairs)
+
+    def swapped(x, axis, count):
+        return lax.ppermute(x, axis, [(i, i ^ 1) for i in range(count)])
+
+    def over(x):
+        return lax.ppermute(x, "px", [(i, i + 1) for i in range(0, row_count, 2)])
+
+    def back(x):
+        return lax.ppermute(x, "px", [(i + 1, i) for i in range(0, row_count, 2)])
 
     def beyond(x, axis, count):
         pairs = [(i, i + 1) for i in range(1, count - 1, 2)]
@@ -431,28 +478,43 @@
     small = ((rows, rank), BF16)
     double = ((2 * rows, rank), BF16)
     wide = ((rows, rank), F32)
+    wide_double = ((2 * rows, rank), F32)
     step_flops = 8 * cols * rank * rank
     patch_flops = 8 * cols * rank * unknowns
     leaf_flops = 8 * cols * leaf * unknowns
 
     half, sent = head(leaf, tall, squeeze)
-    early = 3
-    first = load(sections, 0, early, EARLY)
-    rest = load(sections, early, levels, LATE)
+    bounds = [0, 1, 3, levels]
+    sections_sent = over(sections)
+    zero = load(sections, 0, 1, EARLY, [sent])
+    arrived = swapped(sent, "px", row_count)
+    (own,) = call(functools.partial(own_kernel, 0, False), [wide], [sent, zero], step_flops)
+    (sent,) = call(functools.partial(up_kernel, 0, 1), [small], [own, arrived, zero], step_flops)
+    first = load(sections, 1, 3, EARLY, [sent])
+    other = over(sent)
+    (sent,) = call(join_kernel, [double], [sent, other], 0, after=[first])
+    held = {0: zero, 1: first}
+    held_other = {}
 
     def weights(level):
-        return (first, level) if level < early else (rest, level - early)
+        at = sum(level >= low for low in bounds[1:-1])
+        for now, array, limit in ((held, sections, LATE), (held_other, sections_sent, OTHER)):
+            if at not in now:
+                now[at] = load(array, bounds[at], bounds[at + 1], limit, [sent])
+        return [held[at], held_other[at]], level - bounds[at]
 
     got = {}
-    for level in range(levels):
+    for level in range(1, levels):
         arrived = partner(sent, level)
-        after = []
+        after, ended = [], []
         if level == 1:
             pieces = call(
                 functools.partial(pick_kernel, leaf), [small] * 4, [info, half], 0, smem=1, after=[sent]
             )
-            after = list(pieces) + [rest]
+            after = list(pieces)
         if level == 2:
+            f, _ = weights(level + 1)
+            ended = f
             (near,) = call(
                 functools.partial(leaves_kernel, leaf, False),
                 [((rows, unknowns), F32)],
@@ -461,54 +523,63 @@
                 after=[sent],
             )
             after = [near]
-            got["a"] = partner(pieces[0], 0)
         if level == 3:
-            after = [got["a"]]
-        if level == row_bits:
-            got["c"] = arrived
+            got["a"] = swapped(pieces[0], "px", row_count)
+            ended = [got["a"]]
+        if level == row_bits + 1:
             got["b"] = beyond(pieces[1], "px", row_count)
+            ended = [got["b"]]
+            got["c"] = swapped(pieces[2], "py", col_count)
             got["d"] = beyond(pieces[3], "py", col_count)
-        if level == levels - 1:
-            (near,) = call(
-                functools.partial(sides_kernel, leaf),
-                [((rows, unknowns), F32)],
-                [info, near, got["a"], got["b"], got["c"], got["d"], sides],
-                4 * step_flops,
-                smem=1,
-                after=[sent],
-            )
-            after = [near, spread]
         f, at = weights(level)
         (own,) = call(
             functools.partial(own_kernel, at, False),
-            [wide],
-            [sent, f],
-            step_flops,
+            [wide_double],
+            [sent] + f,
+            2 * step_flops,
             after=after,
         )
-        if level < levels - 1:
-            extra = [pieces[2]] if level == row_bits - 1 else []
-            (sent,) = call(
-                functools.partial(up_kernel, at),
-                [double if extra else small],
-                [own, arrived, f] + extra,
-                step_flops,
-            )
-    y, yb, g, message = call(
-        functools.partial(field_kernel, at),
-        [((rows, unknowns), F32), ((rows, unknowns), BF16), small, small],
-        [own, arrived, f, near, spread],
+        last = level == levels - 1
+        outs = call(
+            functools.partial(up_kernel, at, 2),
+            [small, small] if last else [double],
+            [own, arrived] + f,
+            2 * step_flops,
+            after=ended,
+        )
+        sent = outs[0]
+    mine, other = outs
+    other = back(other)
+    (near,) = call(
+        functools.partial(sides_kernel, leaf),
+        [((rows, unknowns), F32)],
+        [info, near, got["a"], got["b"], got["c"], got["d"], sides],
+        4 * step_flops,
+        smem=1,
+        after=[mine],
+    )
+    y, yb, g = call(
+        field_kernel,
+        [((rows, unknowns), F32), ((rows, unknowns), BF16), small],
+        [info, mine, other, near, spread],
         2 * patch_flops,
-    )
+        smem=1,
+        scratch=[pltpu.VMEM((rows, rank), BF16)],
+    )
+    other = over(g)
     terms = call(
         functools.partial(terms_kernel, leaf), [small] * 4, [info, yb, sides], 4 * step_flops, smem=1
     )
     (shaped,) = call(
         functools.partial(shape_kernel, leaf), [((cols, 2 * leaves, leaf), F32)], [y], 0
     )
-    for level in range(levels - 1, -1, -1):
+    f, at = weights(levels - 1)
+    g, message = call(
+        functools.partial(turn_kernel, at), [double, double], [g, other] + f, 2 * step_flops
+    )
+    for level in range(levels - 1, 0, -1):
         arrived = partner(message, level)
-        after = []
+        after, ended = [], []
         if level == levels - 1:
             after = list(terms)
         if level == levels - 2:
@@ -520,8 +591,6 @@
                 after=[message],
             )
             after = [z_near]
-        if level == row_bits:
-            got["c"] = arrived
         if level == 4:
             v_high, v_low, vv = call(
                 functools.partial(basis_kernel, leaf),
@@ -531,50 +600,58 @@
                 after=[message],
             )
             after = [v_high, v_low, vv]
+            got["c"] = swapped(terms[2], "py", col_count)
+            ended = [got["c"]]
         if level == 3:
             got["d"] = beyond(terms[3], "py", col_count)
+            ended = [got["d"]]
         if level == 2:
-            after = [got["d"]]
-            got["a"] = partner(terms[0], 0)
+            got["a"] = swapped(terms[0], "px", row_count)
+            ended = [got["a"]]
         if level == 1:
-            after = [got["a"], squeeze]
+            after = [squeeze]
             got["b"] = beyond(terms[1], "px", row_count)
-        if level == 0:
-            (z_near,) = call(
-                functools.partial(gather_kernel, leaf),
-                [((rows, unknowns), F32)],
-                [info, z_near, got["a"], got["b"], got["c"], got["d"]],
-                0,
-                smem=1,
-            )
-            after = [z_near]
         f, at = weights(level)
         (own,) = call(
             functools.partial(own_kernel, at, True),
-            [wide],
-            [g, f],
-            step_flops,
+            [wide_double],
+            [g] + f,
+            2 * step_flops,
             after=after,
         )
-        if level > 0:
-            extra = [terms[2]] if level == row_bits + 1 else []
+        if level > 1:
             f, at = weights(level - 1)
             g, message = call(
                 functools.partial(down_kernel, at),
-                [small, double if extra else small],
-                [own, arrived, f] + extra,
-                step_flops,
+                [double, double],
+                [own, arrived] + f,
+                2 * step_flops,
+                after=ended,
             )
+    f, at = weights(0)
+    mine, other = call(
+        last_kernel, [small, small], [own, arrived] + f, 4 * step_flops
+    )
+    other = back(other)
+    (z_near,) = call(
+        functools.partial(gather_kernel, leaf),
+        [((rows, unknowns), F32)],
+        [info, z_near, got["a"], got["b"], got["c"], got["d"]],
+        0,
+        smem=1,
+    )
     z_high, z_low, part = call(
         close_kernel,
         [((rows, unknowns), BF16), ((rows, unknowns), BF16), ((cols, 4 * cols), F32)],
-        [z_near, own, arrived, squeeze, v_high, v_low, vv],
+        [info, z_near, mine, other, squeeze, v_high, v_low, vv],
         patch_flops,
+        smem=1,
+        scratch=[pltpu.VMEM((rows, rank), BF16)],
     )
     part = part.reshape(1, cols, 4 * cols)
     chips = row_count // 2
     (part,) = call(
-        spread_kernel, [((chips, cols, 4 * cols), F32)], [part, partner(part, 0)], 0
+        spread_kernel, [((chips, cols, 4 * cols), F32)], [part, swapped(part, "px", row_count)], 0
     )
     groups = [[2 * i + core for i in range(chips)] for core in range(2)]
     part = lax.all_to_all(part, "px", 0, 0, axis_index_groups=groups, tiled=True)

time: 131 us -> 165 us (1.26)
  starting transfers between devices: 47.7 us -> 93.8 us
  waiting for transfers between devices: 37.1 us -> 20.4 us
  Pallas kernels: 26.7 us -> 33 us
    ppermute x19 -> x25, starting transfers between devices: 35 us -> 59.5 us  [the longest x6 39.1 us: swapped(): return lax.ppermute(x, axis, [(i, i ^ 1) for i in range(count)])]
    ppermute x4, starting transfers between devices: 5.13 us -> 25 us  [beyond(): return lax.ppermute(x, axis, pairs + [(j, i) for i, j in pairs])]
    ppermute x19 -> x25, waiting for transfers between devices: 28.7 us -> 11.3 us  [the longest x2 6.77 us: back(): return lax.ppermute(x, 'px', [(i + 1, i) for i in range(0, row_count, 2)])]
    pallas_call x2 -> x6, Pallas kernels: 3.17 us -> 6.6 us  [load(): pl.pallas_call(functools.partial(load_kernel, begin), in_specs=[pl.BlockS...]
    pallas_call x43 -> x45, Pallas kernels: 21.1 us -> 23.9 us  [call(): pl.pallas_call(body, out_shape=[jax.ShapeDtypeStruct(s, d) for s, d in ou...]
  transfers between devices with their start and end apart: 24 -> 30, of which waited for: 16 -> 10; matrix products, arithmetic and copies ran while one was open for 0% -> 0% of each run, Pallas kernels for 11% -> 13%
where the time goes in v3:
time: 165 us; the launch traced here: 164 us
  starting transfers between devices  93.8 us (57%)
  Pallas kernels  33 us (20%)
  waiting for transfers between devices  20.4 us (12%)
  blocking collectives  14.2 us (9%)
    ppermute x6, starting transfers between devices, swapped(): return lax.ppermute(x, axis, [(i, i ^ 1) for i in range(count)])  39.1 us
    ppermute x4, starting transfers between devices, beyond(): return lax.ppermute(x, axis, pairs + [(j, i) for i, j in pairs])  25 us
    pallas_call x45, Pallas kernels, call(): pl.pallas_call(body, out_shape=[jax.ShapeDtypeStruct(s, d) for s, d in ou...  23.9 us
    all_to_all x1, blocking collectives, per_device(): lax.all_to_all(part, 'px', 0, 0, axis_index_groups=groups, tiled=True)  14.2 us
    ppermute x14, starting transfers between devices, partner(): return lax.ppermute(x, ('px', 'py'), pairs)  9.57 us
    all_to_all x1, starting transfers between devices, per_device(): part = lax.all_to_all(part, 'py', 0, 0, tiled=True)  9.28 us
    ppermute x3, starting transfers between devices, over(): return lax.ppermute(x, 'px', [(i, i + 1) for i in range(0, row_count, 2)])  8.14 us
    all_to_all x1, waiting for transfers between devices, per_device(): part = lax.all_to_all(part, 'py', 0, 0, tiled=True)  7.8 us
  transfers between devices with their start and end apart: 30, of which 10 were waited for; matrix products, arithmetic and copies ran while one was open for 0% of the time, Pallas kernels for 13%

profile of v3, /device:TPU:8, one launch (start us, length us, event | category | flops | bytes accessed | tf_op | source)
XLA Modules:
  0.0 164.4 jit_solution(14692531827951086839)
XLA Ops:
  0.6 3.7 %collective-permute-start.2 = (bf16[8,2,2,256,256]{4,3,2,1,0:T(8,128)(2,1)}, bf16[8,2,2,256,256]{4,3,2,1,0:T(8,128)(2,1)}, u32[]{:S(2)}, u32[]{:S(2)}) collective-permute-start(bf16[8,2,2,256,256]{4,3,2,1,0:T(8,128)(2,1)} %bitcast.25), channel_id=1, source_target_pairs={{0,8},{16,24},{32,40},{48,56},{64,72},{80,88},{96,104},{112,120},{... | collective-permute-start | bytes 12582920 | tf_op jit(solution)/shard_map/ppermute | solution.py:469
  4.3 2.5 %shard_map.86 = (bf16[64,2048]{1,0:T(8,128)(2,1)S(1)}, bf16[64,256]{1,0:T(8,128)(2,1)S(1)}) custom-call(f32[32,32,128]{2,1,0:T(8,128)} %bitcast.36, bf16[2,2048,256]{2,1,0:T(8,128)(2,1)} %bitcast.29), custom_call_target="tpu_custom_call" | custom-call | flops 134217728 | bytes 2621440 | tf_op jit(solution)/shard_map/pallas_call | solution.py:105
  6.9 1.1 shard_map.87.refs_1_.refs_2_
  8.2 1.0 collective-permute-done.refs_1_
  9.4 2.3 %collective-permute-start.1 = (bf16[64,256]{1,0:T(8,128)(2,1)S(1)}, bf16[64,256]{1,0:T(8,128)(2,1)S(1)}, u32[]{:S(2)}, u32[]{:S(2)}) collective-permute-start(bf16[64,256]{1,0:T(8,128)(2,1)S(1)} %shard_map.89.rest_0_.refs_0_), channel_id=1, source_target_pairs={{0,8},{16,24},{32,40},{48,56},{64,72},{80,88},{96,104},{112,120},{... | collective-permute-start | bytes 98312 | tf_op jit(solution)/shard_map/ppermute | solution.py:469
  11.7 1.2 shard_map.90.refs_2_.refs_1_
  12.9 0.7 collective-permute-start.3
  14.6 1.2 shard_map.92.refs_2_.refs_3_
  16.3 0.8 collective-permute-start.4
  17.1 0.9 copy-done.1
  18.3 1.8 %shard_map.99.refs_5_.refs_2_.refs_3_ = bf16[5,2,2,256,256]{4,3,2,1,0:T(8,128)(2,1)S(1)} custom-call(bf16[8,2,2,256,256]{4,3,2,1,0:T(8,128)(2,1)} %collective-permute-done.2.f_in, bf16[128,256]{1,0:T(8,128)(2,1)S(1)} %shard_map.95.refs_2_.refs_0_.rest_0_), custom_call_target="tpu_custom_call" | custom-call | bytes 2621440 | tf_op jit(solution)/shard_map/pallas_call | solution.py:137
  21.1 0.7 collective-permute-start.5
  21.8 6.6 %collective-permute-start.6 = (bf16[64,256]{1,0:T(8,128)(2,1)S(1)}, bf16[64,256]{1,0:T(8,128)(2,1)S(1)}, u32[]{:S(2)}, u32[]{:S(2)}) collective-permute-start(bf16[64,256]{1,0:T(8,128)(2,1)S(1)} %get-tuple-element.41.refs_3_), channel_id=1, source_target_pairs={{0,8},{8,0},{16,24},{24,16},{32,40},{40,32},{48,56},{56,48},{64,72... | collective-permute-start | bytes 98312 | tf_op jit(solution)/shard_map/ppermute | solution.py:466
  29.5 0.7 collective-permute-start.7
  30.6 0.7 collective-permute-start.8
  31.7 0.7 collective-permute-start.9
  32.4 18.5 %collective-permute-start.10 = (bf16[64,256]{1,0:T(8,128)(2,1)S(1)}, bf16[64,256]{1,0:T(8,128)(2,1)S(1)}, u32[]{:S(2)}, u32[]{:S(2)}) collective-permute-start(bf16[64,256]{1,0:T(8,128)(2,1)S(1)} %get-tuple-element.42.refs_4_), channel_id=1, source_target_pairs={{8,16},{24,32},{40,48},{56,64},{72,80},{88,96},{104,112},{120,128}... | collective-permute-start | bytes 98312 | tf_op jit(solution)/shard_map/ppermute | solution.py:476
  51.1 1.4 collective-permute-done.10.refs_4_.refs_3_
  52.7 0.7 collective-permute-start.11
  53.4 2.0 %collective-permute-start.13 = (bf16[64,256]{1,0:T(8,128)(2,1)S(1)}, bf16[64,256]{1,0:T(8,128)(2,1)S(1)}, u32[]{:S(2)}, u32[]{:S(2)}) collective-permute-start(bf16[64,256]{1,0:T(8,128)(2,1)S(1)} %get-tuple-element.43.refs_5_), channel_id=1, source_target_pairs={{0,1},{1,0},{2,3},{3,2},{4,5},{5,4},{6,7},{7,6},{8,9},{9,8},{10,11... | collective-permute-start | bytes 98312 | tf_op jit(solution)/shard_map/ppermute | solution.py:466
  56.5 1.4 collective-permute-start.12
  57.9 0.9 shard_map.111.refs_3_
  58.8 5.6 %collective-permute-done.12.refs_2_ = bf16[64,256]{1,0:T(8,128)(2,1)S(1)} collective-permute-done((bf16[64,256]{1,0:T(8,128)(2,1)S(1)}, bf16[64,256]{1,0:T(8,128)(2,1)S(1)}, u32[]{:S(2)}, u32[]{:S(2)}) %collective-permute-start.12) | collective-permute-done | bytes 32800 | tf_op jit(solution)/shard_map/ppermute | solution.py:472
  64.4 1.7 %shard_map.112 = (f32[64,2048]{1,0:T(8,128)S(1)}, bf16[64,2048]{1,0:T(8,128)(2,1)S(1)}, bf16[64,256]{1,0:T(8,128)(2,1)S(1)}) custom-call(s32[13]{0:T(128)S(1)} %concatenate.3.refs_0_, bf16[64,256]{1,0:T(8,128)(2,1)S(1)} %get-tuple-element.45.refs_7_.refs_1_.rest_0_, bf16[64,256]{1,0:T(8,128)(2,1)S(1)} %collective-permute-done.12.refs_2_, ...), custom_call_target="tpu_custom_call" | custom-call | flops 268435456 | bytes 2687028 | tf_op jit(solution)/shard_map/pallas_call | solution.py:28
  66.1 2.2 %collective-permute-start.15 = (bf16[64,256]{1,0:T(8,128)(2,1)S(1)}, bf16[64,256]{1,0:T(8,128)(2,1)S(1)}, u32[]{:S(2)}, u32[]{:S(2)}) collective-permute-start(bf16[64,256]{1,0:T(8,128)(2,1)S(1)} %get-tuple-element.49.refs_0_), channel_id=1, source_target_pairs={{0,8},{16,24},{32,40},{48,56},{64,72},{80,88},{96,104},{112,120},{... | collective-permute-start | bytes 98312 | tf_op jit(solution)/shard_map/ppermute | solution.py:469
  68.3 0.8 collective-permute-done.15.refs_1_
  69.4 0.7 collective-permute-start.16
  70.1 1.0 shard_map.115
  71.6 0.7 collective-permute-start.21
  72.3 0.8 shard_map.118.refs_1_.refs_3_
  74.9 0.7 collective-permute-start.23
  75.6 2.6 %collective-permute-start.19 = (bf16[64,256]{1,0:T(8,128)(2,1)S(1)}, bf16[64,256]{1,0:T(8,128)(2,1)S(1)}, u32[]{:S(2)}, u32[]{:S(2)}) collective-permute-start(bf16[64,256]{1,0:T(8,128)(2,1)S(1)} %get-tuple-element.53.refs_5_), channel_id=1, source_target_pairs={{0,1},{1,0},{2,3},{3,2},{4,5},{5,4},{6,7},{7,6},{8,9},{9,8},{10,11... | collective-permute-start | bytes 98312 | tf_op jit(solution)/shard_map/ppermute | solution.py:466
  78.2 1.7 %shard_map.124 = (bf16[64,2048]{1,0:T(8,128)(2,1)S(1)}, bf16[64,2048]{1,0:T(8,128)(2,1)S(1)}, f32[32,32]{1,0:T(8,128)S(1)}) custom-call(f32[32,32,128]{2,1,0:T(8,128)S(1)} %bitcast.37, bf16[128,256]{1,0:T(8,128)(2,1)S(1)} %get-tuple-element.61.refs_1_), custom_call_target="tpu_custom_call" | custom-call | flops 67108864 | bytes 524288 | tf_op jit(solution)/shard_map/pallas_call | solution.py:28
  80.8 0.7 collective-permute-start.24
  83.4 27.6 %collective-permute-start.17 = (bf16[64,256]{1,0:T(8,128)(2,1)S(1)}, bf16[64,256]{1,0:T(8,128)(2,1)S(1)}, u32[]{:S(2)}, u32[]{:S(2)}) collective-permute-start(bf16[64,256]{1,0:T(8,128)(2,1)S(1)} %get-tuple-element.51.refs_3_), channel_id=1, source_target_pairs={{0,8},{8,0},{16,24},{24,16},{32,40},{40,32},{48,56},{56,48},{64,72... | collective-permute-start | bytes 98312 | tf_op jit(solution)/shard_map/ppermute | solution.py:466
  112.1 0.8 collective-permute-start.26
  112.9 1.1 shard_map.132.refs_3_
  114.0 5.2 %collective-permute-start.18 = (bf16[64,256]{1,0:T(8,128)(2,1)S(1)}, bf16[64,256]{1,0:T(8,128)(2,1)S(1)}, u32[]{:S(2)}, u32[]{:S(2)}) collective-permute-start(bf16[64,256]{1,0:T(8,128)(2,1)S(1)} %get-tuple-element.52.refs_4_), channel_id=1, source_target_pairs={{8,16},{24,32},{40,48},{56,64},{72,80},{88,96},{104,112},{120,128}... | collective-permute-start | bytes 98312 | tf_op jit(solution)/shard_map/ppermute | solution.py:476
  119.9 1.3 collective-permute-start.27
  121.8 1.2 collective-permute-done.27.refs_3_
  123.0 2.3 %shard_map.134 = (bf16[64,2048]{1,0:T(8,128)(2,1)S(1)}, bf16[64,2048]{1,0:T(8,128)(2,1)S(1)}, f32[32,128]{1,0:T(8,128)S(1)}) custom-call(s32[13]{0:T(128)S(1)} %concatenate.3.refs_0_, f32[64,2048]{1,0:T(8,128)S(1)} %shard_map.119.refs_1_, bf16[64,256]{1,0:T(8,128)(2,1)S(1)} %get-tuple-element.71.refs_2_, ...), custom_call_target="tpu_custom_call" | custom-call | flops 134217728 | bytes 3215412 | tf_op jit(solution)/shard_map/pallas_call | solution.py:28
  125.6 1.0 collective-permute-done.28.refs_1_
  126.6 14.2 %all_to_all.10.refs_0_ = f32[16,32,128]{2,1,0:T(8,128)S(1)} all-to-all(f32[16,32,128]{2,1,0:T(8,128)S(1)} %shard_map.135), channel_id=1, replica_groups={{0,16,32,48,64,80,96,112,128,144,160,176,192,208,224,240},{8,24,40,56,7..., dimensions={0} | all-to-all | bytes 524288 | tf_op jit(solution)/shard_map/all_to_all | solution.py:657
  140.9 0.7 shard_map.136
  141.6 9.3 %all-to-all-start.1 = ((f32[8,32,128]{2,1,0:T(8,128)}), f32[8,32,128]{2,1,0:T(8,128)S(1)}, u32[]{:S(2)}, u32[]{:S(2)}) async-start(f32[8,32,128]{2,1,0:T(8,128)} %shard_map.136), calls=%async_computation.1 | async-start | bytes 262144 | tf_op jit(solution)/shard_map/all_to_all | solution.py:659
  150.8 1.3 shard_map.113
  152.1 7.8 %all-to-all-done.1.refs_0_ = f32[8,32,128]{2,1,0:T(8,128)S(1)} async-done(((f32[8,32,128]{2,1,0:T(8,128)}), f32[8,32,128]{2,1,0:T(8,128)S(1)}, u32[]{:S(2)}, u32[]{:S(2)}) %all-to-all-start.1) | async-done | bytes 131104 | tf_op jit(solution)/shard_map/all_to_all | solution.py:659
  159.9 4.3 %shard_map.137 = f32[64,32,128]{2,1,0:T(8,128)} custom-call(f32[8,32,128]{2,1,0:T(8,128)S(1)} %all-to-all-done.1.refs_0_, bf16[64,2048]{1,0:T(8,128)(2,1)S(1)} %get-tuple-element.74.refs_1_, bf16[64,2048]{1,0:T(8,128)(2,1)S(1)} %get-tuple-element.75.refs_2_, bf16[64,2048]{1,0:T(8,128)(2,1)S(1)} %get-tuple-element.62.refs_3_.refs_5_, ...), custom_call_target="tpu_custom_call" | custom-call | flops 67108864 | bytes 1179648 | tf_op jit(solution)/shard_map/pallas_call | solution.py:28
  (82 shorter events, 14.6 us)
Async XLA Ops:
  0.6 13.0 %copy-start = (s32[32,8,4,2]{0,3,2,1:T(2,128)S(1)}, s32[32,8,4,2]{0,3,2,1:T(2,128)}, u32[]{:S(2)}) copy-start(s32[32,8,4,2]{0,3,2,1:T(2,128)} %param.8) | copy-start | bytes 24580
  0.6 14.0 %collective-permute-start.2 = (bf16[8,2,2,256,256]{4,3,2,1,0:T(8,128)(2,1)}, bf16[8,2,2,256,256]{4,3,2,1,0:T(8,128)(2,1)}, u32[]{:S(2)}, u32[]{:S(2)}) collective-permute-start(bf16[8,2,2,256,256]{4,3,2,1,0:T(8,128)(2,1)} %bitcast.25), channel_id=1, source_target_pairs={{0,8},{16,24},{32,40},{48,56},{64,72},{80,88},{96,104},{112,120},{... | collective-permute-start | bytes 12582920 | tf_op jit(solution)/shard_map/ppermute | solution.py:469
  6.8 2.4 %collective-permute-start = (bf16[64,256]{1,0:T(8,128)(2,1)S(1)}, bf16[64,256]{1,0:T(8,128)(2,1)S(1)}, u32[]{:S(2)}, u32[]{:S(2)}) collective-permute-start(bf16[64,256]{1,0:T(8,128)(2,1)S(1)} %get-tuple-element.39.rest_0_.refs_0_), channel_id=1, source_target_pairs={{0,8},{8,0},{16,24},{24,16},{32,40},{40,32},{48,56},{56,48},{64,72... | collective-permute-start | bytes 98312 | tf_op jit(solution)/shard_map/ppermute | solution.py:466
  9.4 3.5 %collective-permute-start.1 = (bf16[64,256]{1,0:T(8,128)(2,1)S(1)}, bf16[64,256]{1,0:T(8,128)(2,1)S(1)}, u32[]{:S(2)}, u32[]{:S(2)}) collective-permute-start(bf16[64,256]{1,0:T(8,128)(2,1)S(1)} %shard_map.89.rest_0_.refs_0_), channel_id=1, source_target_pairs={{0,8},{16,24},{32,40},{48,56},{64,72},{80,88},{96,104},{112,120},{... | collective-permute-start | bytes 98312 | tf_op jit(solution)/shard_map/ppermute | solution.py:469
  12.9 3.2 %collective-permute-start.3 = (bf16[128,256]{1,0:T(8,128)(2,1)S(1)}, bf16[128,256]{1,0:T(8,128)(2,1)S(1)}, u32[]{:S(2)}, u32[]{:S(2)}) collective-permute-start(bf16[128,256]{1,0:T(8,128)(2,1)S(1)} %shard_map.91.rest_0_.refs_2_.refs_0_), channel_id=1, source_target_pairs={{8,24},{9,25},{10,26},{11,27},{12,28},{13,29},{14,30},{15,31},{24,... | collective-permute-start | bytes 196616 | tf_op jit(solution)/shard_map/ppermute | solution.py:463
  15.9 2.2 %copy-start.1 = (bf16[1,1,8,2,2,256,256]{6,5,4,3,2,1,0:T(8,128)(2,1)S(1)}, bf16[1,1,8,2,2,256,256]{6,5,4,3,2,1,0:T(8,128)(2,1)}, u32[]{:S(2)}) copy-start(bf16[1,1,8,2,2,256,256]{6,5,4,3,2,1,0:T(8,128)(2,1)} %param.13) | copy-start | bytes 12582916
  16.3 4.6 %collective-permute-start.4 = (bf16[128,256]{1,0:T(8,128)(2,1)S(1)}, bf16[128,256]{1,0:T(8,128)(2,1)S(1)}, u32[]{:S(2)}, u32[]{:S(2)}) collective-permute-start(bf16[128,256]{1,0:T(8,128)(2,1)S(1)} %shard_map.95.refs_2_.refs_0_.rest_0_), channel_id=1, source_target_pairs={{8,40},{9,41},{10,42},{11,43},{12,44},{13,45},{14,46},{15,47},{24,... | collective-permute-start | bytes 196616 | tf_op jit(solution)/shard_map/ppermute | solution.py:463
  18.3 2.0 %copy-start.4 = (bf16[1,1,2,16,128,128]{5,4,3,2,1,0:T(8,128)(2,1)S(1)}, bf16[1,1,2,16,128,128]{5,4,3,2,1,0:T(8,128)(2,1)}, u32[]{:S(2)}) copy-start(bf16[1,1,2,16,128,128]{5,4,3,2,1,0:T(8,128)(2,1)} %param.9) | copy-start | bytes 3145732
  21.1 8.2 %collective-permute-start.5 = (bf16[128,256]{1,0:T(8,128)(2,1)S(1)}, bf16[128,256]{1,0:T(8,128)(2,1)S(1)}, u32[]{:S(2)}, u32[]{:S(2)}) collective-permute-start(bf16[128,256]{1,0:T(8,128)(2,1)S(1)} %shard_map.100.refs_0_), channel_id=1, source_target_pairs={{8,72},{9,73},{10,74},{11,75},{12,76},{13,77},{14,78},{15,79},{24,... | collective-permute-start | bytes 196616 | tf_op jit(solution)/shard_map/ppermute | solution.py:463
  21.8 7.5 %collective-permute-start.6 = (bf16[64,256]{1,0:T(8,128)(2,1)S(1)}, bf16[64,256]{1,0:T(8,128)(2,1)S(1)}, u32[]{:S(2)}, u32[]{:S(2)}) collective-permute-start(bf16[64,256]{1,0:T(8,128)(2,1)S(1)} %get-tuple-element.41.refs_3_), channel_id=1, source_target_pairs={{0,8},{8,0},{16,24},{24,16},{32,40},{40,32},{48,56},{56,48},{64,72... | collective-permute-start | bytes 98312 | tf_op jit(solution)/shard_map/ppermute | solution.py:466
  29.5 0.9 collective-permute-start.7
  30.6 0.9 collective-permute-start.8
  31.7 20.8 %collective-permute-start.9 = (bf16[128,256]{1,0:T(8,128)(2,1)S(1)}, bf16[128,256]{1,0:T(8,128)(2,1)S(1)}, u32[]{:S(2)}, u32[]{:S(2)}) collective-permute-start(bf16[128,256]{1,0:T(8,128)(2,1)S(1)} %shard_map.106.refs_0_), channel_id=1, source_target_pairs={{8,10},{9,11},{10,8},{11,9},{12,14},{13,15},{14,12},{15,13},{24,26... | collective-permute-start | bytes 196616 | tf_op jit(solution)/shard_map/ppermute | solution.py:463
  32.4 20.1 %collective-permute-start.10 = (bf16[64,256]{1,0:T(8,128)(2,1)S(1)}, bf16[64,256]{1,0:T(8,128)(2,1)S(1)}, u32[]{:S(2)}, u32[]{:S(2)}) collective-permute-start(bf16[64,256]{1,0:T(8,128)(2,1)S(1)} %get-tuple-element.42.refs_4_), channel_id=1, source_target_pairs={{8,16},{24,32},{40,48},{56,64},{72,80},{88,96},{104,112},{120,128}... | collective-permute-start | bytes 98312 | tf_op jit(solution)/shard_map/ppermute | solution.py:476
  52.7 3.5 %collective-permute-start.11 = (bf16[128,256]{1,0:T(8,128)(2,1)S(1)}, bf16[128,256]{1,0:T(8,128)(2,1)S(1)}, u32[]{:S(2)}, u32[]{:S(2)}) collective-permute-start(bf16[128,256]{1,0:T(8,128)(2,1)S(1)} %shard_map.108.refs_0_), channel_id=1, source_target_pairs={{8,12},{9,13},{10,14},{11,15},{12,8},{13,9},{14,10},{15,11},{24,28... | collective-permute-start | bytes 196616 | tf_op jit(solution)/shard_map/ppermute | solution.py:463
  53.4 4.5 %collective-permute-start.13 = (bf16[64,256]{1,0:T(8,128)(2,1)S(1)}, bf16[64,256]{1,0:T(8,128)(2,1)S(1)}, u32[]{:S(2)}, u32[]{:S(2)}) collective-permute-start(bf16[64,256]{1,0:T(8,128)(2,1)S(1)} %get-tuple-element.43.refs_5_), channel_id=1, source_target_pairs={{0,1},{1,0},{2,3},{3,2},{4,5},{5,4},{6,7},{7,6},{8,9},{9,8},{10,11... | collective-permute-start | bytes 98312 | tf_op jit(solution)/shard_map/ppermute | solution.py:466
  55.3 2.6 %collective-permute-start.14 = (bf16[64,256]{1,0:T(8,128)(2,1)S(1)}, bf16[64,256]{1,0:T(8,128)(2,1)S(1)}, u32[]{:S(2)}, u32[]{:S(2)}) collective-permute-start(bf16[64,256]{1,0:T(8,128)(2,1)S(1)} %get-tuple-element.44.refs_6_), channel_id=1, source_target_pairs={{1,2},{3,4},{5,6},{2,1},{4,3},{6,5},{9,10},{11,12},{13,14},{10,9},... | collective-permute-start | bytes 98312 | tf_op jit(solution)/shard_map/ppermute | solution.py:476
  56.2 1.7 %copy-start.3 = (bf16[1,1,4,2,256,256]{5,4,3,2,1,0:T(8,128)(2,1)S(1)}, bf16[1,1,4,2,256,256]{5,4,3,2,1,0:T(8,128)(2,1)}, u32[]{:S(2)}) copy-start(bf16[1,1,4,2,256,256]{5,4,3,2,1,0:T(8,128)(2,1)} %param.10) | copy-start | bytes 3145732
  56.2 8.2 %copy-start.6 = (bf16[1,1,2,256,2048]{4,3,2,1,0:T(8,128)(2,1)S(1)}, bf16[1,1,2,256,2048]{4,3,2,1,0:T(8,128)(2,1)}, u32[]{:S(2)}) copy-start(bf16[1,1,2,256,2048]{4,3,2,1,0:T(8,128)(2,1)} %param.12) | copy-start | bytes 6291460
  56.5 8.0 %collective-permute-start.12 = (bf16[64,256]{1,0:T(8,128)(2,1)S(1)}, bf16[64,256]{1,0:T(8,128)(2,1)S(1)}, u32[]{:S(2)}, u32[]{:S(2)}) collective-permute-start(bf16[64,256]{1,0:T(8,128)(2,1)S(1)} %get-tuple-element.46), channel_id=1, source_target_pairs={{8,0},{24,16},{40,32},{56,48},{72,64},{88,80},{104,96},{120,112},{... | collective-permute-start | bytes 98312 | tf_op jit(solution)/shard_map/ppermute | solution.py:472
  66.1 3.0 %collective-permute-start.15 = (bf16[64,256]{1,0:T(8,128)(2,1)S(1)}, bf16[64,256]{1,0:T(8,128)(2,1)S(1)}, u32[]{:S(2)}, u32[]{:S(2)}) collective-permute-start(bf16[64,256]{1,0:T(8,128)(2,1)S(1)} %get-tuple-element.49.refs_0_), channel_id=1, source_target_pairs={{0,8},{16,24},{32,40},{48,56},{64,72},{80,88},{96,104},{112,120},{... | collective-permute-start | bytes 98312 | tf_op jit(solution)/shard_map/ppermute | solution.py:469
  69.4 1.9 %collective-permute-start.16 = (bf16[128,256]{1,0:T(8,128)(2,1)S(1)}, bf16[128,256]{1,0:T(8,128)(2,1)S(1)}, u32[]{:S(2)}, u32[]{:S(2)}) collective-permute-start(bf16[128,256]{1,0:T(8,128)(2,1)S(1)} %get-tuple-element.55), channel_id=1, source_target_pairs={{8,12},{9,13},{10,14},{11,15},{12,8},{13,9},{14,10},{15,11},{24,28... | collective-permute-start | bytes 196616 | tf_op jit(solution)/shard_map/ppermute | solution.py:463
  71.6 1.8 %collective-permute-start.21 = (bf16[128,256]{1,0:T(8,128)(2,1)S(1)}, bf16[128,256]{1,0:T(8,128)(2,1)S(1)}, u32[]{:S(2)}, u32[]{:S(2)}) collective-permute-start(bf16[128,256]{1,0:T(8,128)(2,1)S(1)} %get-tuple-element.56.refs_2_), channel_id=1, source_target_pairs={{8,10},{9,11},{10,8},{11,9},{12,14},{13,15},{14,12},{15,13},{24,26... | collective-permute-start | bytes 196616 | tf_op jit(solution)/shard_map/ppermute | solution.py:463
  73.7 1.0 collective-permute-start.22
  74.6 3.5 %copy-start.5 = (f32[32,1,1,2,2048]{4,3,2,1,0:T(2,128)S(1)}, f32[32,1,1,2,2048]{4,3,2,1,0:T(2,128)}, u32[]{:S(2)}) copy-start(f32[32,1,1,2,2048]{4,3,2,1,0:T(2,128)} %param.7) | copy-start | bytes 1572868
  74.9 5.6 %collective-permute-start.23 = (bf16[128,256]{1,0:T(8,128)(2,1)S(1)}, bf16[128,256]{1,0:T(8,128)(2,1)S(1)}, u32[]{:S(2)}, u32[]{:S(2)}) collective-permute-start(bf16[128,256]{1,0:T(8,128)(2,1)S(1)} %get-tuple-element.61.refs_1_), channel_id=1, source_target_pairs={{8,136},{9,137},{10,138},{11,139},{12,140},{13,141},{14,142},{15,1... | collective-permute-start | bytes 196616 | tf_op jit(solution)/shard_map/ppermute | solution.py:463
  75.6 4.9 %collective-permute-start.19 = (bf16[64,256]{1,0:T(8,128)(2,1)S(1)}, bf16[64,256]{1,0:T(8,128)(2,1)S(1)}, u32[]{:S(2)}, u32[]{:S(2)}) collective-permute-start(bf16[64,256]{1,0:T(8,128)(2,1)S(1)} %get-tuple-element.53.refs_5_), channel_id=1, source_target_pairs={{0,1},{1,0},{2,3},{3,2},{4,5},{5,4},{6,7},{7,6},{8,9},{9,8},{10,11... | collective-permute-start | bytes 98312 | tf_op jit(solution)/shard_map/ppermute | solution.py:466
  80.8 1.6 collective-permute-start.24
  81.5 1.0 collective-permute-start.20
  82.7 29.1 %collective-permute-start.25 = (bf16[128,256]{1,0:T(8,128)(2,1)S(1)}, bf16[128,256]{1,0:T(8,128)(2,1)S(1)}, u32[]{:S(2)}, u32[]{:S(2)}) collective-permute-start(bf16[128,256]{1,0:T(8,128)(2,1)S(1)} %get-tuple-element.68), channel_id=1, source_target_pairs={{8,40},{9,41},{10,42},{11,43},{12,44},{13,45},{14,46},{15,47},{24,... | collective-permute-start | bytes 196616 | tf_op jit(solution)/shard_map/ppermute | solution.py:463
  83.4 28.4 %collective-permute-start.17 = (bf16[64,256]{1,0:T(8,128)(2,1)S(1)}, bf16[64,256]{1,0:T(8,128)(2,1)S(1)}, u32[]{:S(2)}, u32[]{:S(2)}) collective-permute-start(bf16[64,256]{1,0:T(8,128)(2,1)S(1)} %get-tuple-element.51.refs_3_), channel_id=1, source_target_pairs={{0,8},{8,0},{16,24},{24,16},{32,40},{40,32},{48,56},{56,48},{64,72... | collective-permute-start | bytes 98312 | tf_op jit(solution)/shard_map/ppermute | solution.py:466
  112.1 7.1 %copy-start.2 = (bf16[1,1,2,2048,256]{4,3,2,1,0:T(8,128)(2,1)S(1)}, bf16[1,1,2,2048,256]{4,3,2,1,0:T(8,128)(2,1)}, u32[]{:S(2)}) copy-start(bf16[1,1,2,2048,256]{4,3,2,1,0:T(8,128)(2,1)} %param.11) | copy-start | bytes 6291460
  112.1 7.4 %collective-permute-start.26 = (bf16[128,256]{1,0:T(8,128)(2,1)S(1)}, bf16[128,256]{1,0:T(8,128)(2,1)S(1)}, u32[]{:S(2)}, u32[]{:S(2)}) collective-permute-start(bf16[128,256]{1,0:T(8,128)(2,1)S(1)} %get-tuple-element.70), channel_id=1, source_target_pairs={{8,24},{9,25},{10,26},{11,27},{12,28},{13,29},{14,30},{15,31},{24,... | collective-permute-start | bytes 196616 | tf_op jit(solution)/shard_map/ppermute | solution.py:463
  114.0 7.2 %collective-permute-start.18 = (bf16[64,256]{1,0:T(8,128)(2,1)S(1)}, bf16[64,256]{1,0:T(8,128)(2,1)S(1)}, u32[]{:S(2)}, u32[]{:S(2)}) collective-permute-start(bf16[64,256]{1,0:T(8,128)(2,1)S(1)} %get-tuple-element.52.refs_4_), channel_id=1, source_target_pairs={{8,16},{24,32},{40,48},{56,64},{72,80},{88,96},{104,112},{120,128}... | collective-permute-start | bytes 98312 | tf_op jit(solution)/shard_map/ppermute | solution.py:476
  119.9 3.1 %collective-permute-start.27 = (bf16[64,256]{1,0:T(8,128)(2,1)S(1)}, bf16[64,256]{1,0:T(8,128)(2,1)S(1)}, u32[]{:S(2)}, u32[]{:S(2)}) collective-permute-start(bf16[64,256]{1,0:T(8,128)(2,1)S(1)} %get-tuple-element.72), channel_id=1, source_target_pairs={{8,0},{24,16},{40,32},{56,48},{72,64},{88,80},{104,96},{120,112},{... | collective-permute-start | bytes 98312 | tf_op jit(solution)/shard_map/ppermute | solution.py:472
  125.3 1.3 collective-permute-start.28
  141.6 18.4 %all-to-all-start.1 = ((f32[8,32,128]{2,1,0:T(8,128)}), f32[8,32,128]{2,1,0:T(8,128)S(1)}, u32[]{:S(2)}, u32[]{:S(2)}) async-start(f32[8,32,128]{2,1,0:T(8,128)} %shard_map.136), calls=%async_computation.1 | async-start | bytes 262144 | tf_op jit(solution)/shard_map/all_to_all | solution.py:659

commit v4 on v2

--- a/solution.py
+++ b/solution.py
@@ -201,8 +201,11 @@
         side = info[8 + at]
         x = ref[ref.shape[0] - rows :]
         term = mul(x, b_ref[side, 0], b_ref[side, 1])
-        for e in range(2):
-            o_ref[:, leaf_at(info[2 * side + e], leaf)] += term[:, e * leaf : (e + 1) * leaf]
+
+        @pl.when(info[12 + at] == 1)
+        def _():
+            for e in range(2):
+                o_ref[:, leaf_at(info[2 * side + e], leaf)] += term[:, e * leaf : (e + 1) * leaf]
 
 
 def field_kernel(level, own_ref, r_ref, f_ref, near_ref, e_ref, y_ref, yb_ref, g_ref, m_ref):
@@ -247,10 +250,13 @@
     for at, ref in enumerate((ra_ref, rb_ref, rc_ref, rd_ref)):
         side = info[8 + at]
         low = ref.shape[0] - rows
-        for e in range(2):
-            o_ref[:, leaf_at(info[2 * side + e], leaf)] += ref[
-                low:, e * leaf : (e + 1) * leaf
-            ].astype(F32)
+
+        @pl.when(info[12 + at] == 1)
+        def _():
+            for e in range(2):
+                o_ref[:, leaf_at(info[2 * side + e], leaf)] += ref[
+                    low:, e * leaf : (e + 1) * leaf
+                ].astype(F32)
 
 
 def close_kernel(near_ref, own_ref, r_ref, c_ref, vh_ref, vl_ref, vv_ref, zh_ref, zl_ref, p_ref):
@@ -415,7 +421,11 @@
     own_leaves = lax.dynamic_slice(edge_leaves, (row_at, col_at, 0, 0), (1, 1, 4, 2)).reshape(8)
     odd_row, odd_col = row_at % 2, col_at % 2
     order = jnp.stack([1 - odd_row, odd_row, 3 - odd_col, 2 + odd_col]).astype(jnp.int32)
-    info = jnp.concatenate([own_leaves, order])
+    inner_row = (row_at > 0) & (row_at < row_count - 1)
+    inner_col = (col_at > 0) & (col_at < col_count - 1)
+    inner = jnp.stack([inner_row, inner_row, inner_col, inner_col]).astype(jnp.int32)
+    ones = jnp.array([1, 0, 1, 0], jnp.int32)
+    info = jnp.concatenate([own_leaves, order, jnp.maximum(inner, ones)])
     tall = v_block.reshape(cols, 2, leaves, leaf).transpose(0, 2, 1, 3).reshape(cols, -1, leaf)
 
     def partner(x, level):
@@ -425,7 +435,7 @@
         return lax.ppermute(x, "py", [(i, i ^ 1 << bit) for i in range(col_count)])
 
     def beyond(x, axis, count):
-        pairs = [(i, i + 1) for i in range(1, count - 1, 2)]
+        pairs = [(i, (i + 1) % count) for i in range(1, count, 2)]
         return lax.ppermute(x, axis, pairs + [(j, i) for i, j in pairs])
 
     small = ((rows, rank), BF16)

time: 131 us -> 126 us (0.962)
  starting transfers between devices: 47.7 us -> 39.8 us
  waiting for transfers between devices: 37.1 us -> 40.9 us
    ppermute x6, starting transfers between devices: 19.3 us -> 12.1 us  [partner(): return lax.ppermute(x, 'py', [(i, i ^ 1 << bit) for i in range(col_count)])]
    ppermute x6, waiting for transfers between devices: 11 us -> 15.2 us  [partner(): return lax.ppermute(x, 'py', [(i, i ^ 1 << bit) for i in range(col_count)])]
    all_to_all x1, starting transfers between devices: 7.65 us -> 5.07 us  [per_device(): part = lax.all_to_all(part, 'py', 0, 0, tiled=True)]
    ppermute x4, starting transfers between devices: 5.13 us -> 7.56 us  [beyond(): return lax.ppermute(x, axis, pairs + [(j, i) for i, j in pairs])]
  transfers between devices with their start and end apart: 24 -> 24, of which waited for: 16 -> 14; matrix products, arithmetic and copies ran while one was open for 0% -> 0% of each run, Pallas kernels for 11% -> 12%
where the time goes in v4:
time: 126 us
  waiting for transfers between devices  40.9 us (32%)
  starting transfers between devices  39.8 us (32%)
  Pallas kernels  27.2 us (22%)
  blocking collectives  14.8 us (12%)
  local copies, waits for them, and re-layouts  1.95 us (2%)
    pallas_call x43, Pallas kernels, call(): pl.pallas_call(body, out_shape=[jax.ShapeDtypeStruct(s, d) for s, d in ou...  21.5 us
    ppermute x13, waiting for transfers between devices, partner(): lax.ppermute(x, 'px', [(i, i ^ 1 << level) for i in range(row_count)])  16.9 us
    ppermute x6, waiting for transfers between devices, partner(): return lax.ppermute(x, 'py', [(i, i ^ 1 << bit) for i in range(col_count)])  15.2 us
    ppermute x13, starting transfers between devices, partner(): lax.ppermute(x, 'px', [(i, i ^ 1 << level) for i in range(row_count)])  15.1 us
    all_to_all x1, blocking collectives, per_device(): lax.all_to_all(part, 'px', 0, 0, axis_index_groups=groups, tiled=True)  14.8 us
    ppermute x6, starting transfers between devices, partner(): return lax.ppermute(x, 'py', [(i, i ^ 1 << bit) for i in range(col_count)])  12.1 us
    all_to_all x1, waiting for transfers between devices, per_device(): part = lax.all_to_all(part, 'py', 0, 0, tiled=True)  7.79 us
    ppermute x4, starting transfers between devices, beyond(): return lax.ppermute(x, axis, pairs + [(j, i) for i, j in pairs])  7.56 us
  transfers between devices with their start and end apart: 24, of which 14 were waited for; matrix products, arithmetic and copies ran while one was open for 0% of the time, Pallas kernels for 12%

profile of v4, /device:TPU:8, one launch (start us, length us, event | category | flops | bytes accessed | tf_op | source)
XLA Modules:
  0.0 125.9 jit_solution(6879018354298444469)
XLA Ops:
  0.6 2.5 %shard_map.95 = (bf16[64,2048]{1,0:T(8,128)(2,1)S(1)}, bf16[64,256]{1,0:T(8,128)(2,1)S(1)}) custom-call(f32[32,32,128]{2,1,0:T(8,128)} %bitcast.36, bf16[2,2048,256]{2,1,0:T(8,128)(2,1)} %bitcast.27), custom_call_target="tpu_custom_call" | custom-call | flops 134217728 | bytes 2621440 | tf_op jit(solution)/shard_map/pallas_call | solution.py:104
  3.2 1.4 %shard_map.96.refs_1_.refs_2_ = bf16[3,2,2,256,256]{4,3,2,1,0:T(8,128)(2,1)S(1)} custom-call(bf16[8,2,2,256,256]{4,3,2,1,0:T(8,128)(2,1)} %bitcast.40), custom_call_target="tpu_custom_call" | custom-call | bytes 4194304 | tf_op jit(solution)/shard_map/pallas_call | solution.py:135
  5.1 2.3 %collective-permute-start.1 = (bf16[64,256]{1,0:T(8,128)(2,1)S(1)}, bf16[64,256]{1,0:T(8,128)(2,1)S(1)}, u32[]{:S(2)}, u32[]{:S(2)}) collective-permute-start(bf16[64,256]{1,0:T(8,128)(2,1)S(1)} %shard_map.98.refs_2_.refs_0_), channel_id=1, source_target_pairs={{0,16},{8,24},{16,0},{24,8},{32,48},{40,56},{48,32},{56,40},{64,80... | collective-permute-start | bytes 98312 | tf_op jit(solution)/shard_map/ppermute | solution.py:433
  7.4 1.8 %shard_map.100.refs_6_.refs_1_.refs_2_ = bf16[5,2,2,256,256]{4,3,2,1,0:T(8,128)(2,1)S(1)} custom-call(bf16[8,2,2,256,256]{4,3,2,1,0:T(8,128)(2,1)} %bitcast.41), custom_call_target="tpu_custom_call" | custom-call | bytes 4194304 | tf_op jit(solution)/shard_map/pallas_call | solution.py:135
  9.2 0.2 dynamic-slice_reduce_fusion
  9.6 0.6 shard_map.99
  10.2 1.4 %copy-done.2 = bf16[3,2,2,256,256]{4,3,2,1,0:T(8,128)(2,1)S(1)} copy-done((bf16[3,2,2,256,256]{4,3,2,1,0:T(8,128)(2,1)S(1)}, bf16[3,2,2,256,256]{4,3,2,1,0:T(8,128)(2,1)}, u32[]{:S(2)}) %copy-start.2) | copy-done | bytes 1572888
  12.0 1.0 collective-permute-start.2
  13.0 0.4 shard_map.103.refs_2_.refs_1_
  13.6 3.9 %collective-permute-done.2.refs_1_ = bf16[64,256]{1,0:T(8,128)(2,1)S(1)} collective-permute-done((bf16[64,256]{1,0:T(8,128)(2,1)S(1)}, bf16[64,256]{1,0:T(8,128)(2,1)S(1)}, u32[]{:S(2)}, u32[]{:S(2)}) %collective-permute-start.2) | collective-permute-done | bytes 32800 | tf_op jit(solution)/shard_map/ppermute | solution.py:433
  17.9 3.7 %collective-permute-done.4.refs_1_ = bf16[64,256]{1,0:T(8,128)(2,1)S(1)} collective-permute-done((bf16[64,256]{1,0:T(8,128)(2,1)S(1)}, bf16[64,256]{1,0:T(8,128)(2,1)S(1)}, u32[]{:S(2)}, u32[]{:S(2)}) %collective-permute-start.4) | collective-permute-done | bytes 32800 | tf_op jit(solution)/shard_map/ppermute | solution.py:433
  21.8 1.5 %collective-permute-start.5 = (bf16[64,256]{1,0:T(8,128)(2,1)S(1)}, bf16[64,256]{1,0:T(8,128)(2,1)S(1)}, u32[]{:S(2)}, u32[]{:S(2)}) collective-permute-start(bf16[64,256]{1,0:T(8,128)(2,1)S(1)} %shard_map.107.refs_0_), channel_id=1, source_target_pairs={{0,128},{8,136},{16,144},{24,152},{32,160},{40,168},{48,176},{56,1... | collective-permute-start | bytes 98312 | tf_op jit(solution)/shard_map/ppermute | solution.py:433
  23.5 3.8 %collective-permute-done.5.refs_1_ = bf16[64,256]{1,0:T(8,128)(2,1)S(1)} collective-permute-done((bf16[64,256]{1,0:T(8,128)(2,1)S(1)}, bf16[64,256]{1,0:T(8,128)(2,1)S(1)}, u32[]{:S(2)}, u32[]{:S(2)}) %collective-permute-start.5) | collective-permute-done | bytes 32800 | tf_op jit(solution)/shard_map/ppermute | solution.py:433
  27.5 0.4 collective-permute-start.6
  28.1 4.1 %collective-permute-done.6.refs_1_.refs_4_ = bf16[128,256]{1,0:T(8,128)(2,1)S(1)} collective-permute-done((bf16[128,256]{1,0:T(8,128)(2,1)S(1)}, bf16[128,256]{1,0:T(8,128)(2,1)S(1)}, u32[]{:S(2)}, u32[]{:S(2)}) %collective-permute-start.6) | collective-permute-done | bytes 65568 | tf_op jit(solution)/shard_map/ppermute | solution.py:435
  32.4 1.4 %collective-permute-start.7 = (bf16[64,256]{1,0:T(8,128)(2,1)S(1)}, bf16[64,256]{1,0:T(8,128)(2,1)S(1)}, u32[]{:S(2)}, u32[]{:S(2)}) collective-permute-start(bf16[64,256]{1,0:T(8,128)(2,1)S(1)} %shard_map.111.refs_0_), channel_id=1, source_target_pairs={{0,2},{1,3},{2,0},{3,1},{4,6},{5,7},{6,4},{7,5},{8,10},{9,11},{10,... | collective-permute-start | bytes 98312 | tf_op jit(solution)/shard_map/ppermute | solution.py:435
  33.8 4.3 %collective-permute-start.9 = (bf16[64,256]{1,0:T(8,128)(2,1)S(1)}, bf16[64,256]{1,0:T(8,128)(2,1)S(1)}, u32[]{:S(2)}, u32[]{:S(2)}) collective-permute-start(bf16[64,256]{1,0:T(8,128)(2,1)S(1)} %get-tuple-element.41.refs_5_), channel_id=1, source_target_pairs={{1,2},{3,4},{5,6},{7,0},{2,1},{4,3},{6,5},{0,7},{9,10},{11,12},{13... | collective-permute-start | bytes 98312 | tf_op jit(solution)/shard_map/ppermute | solution.py:439
  38.5 4.7 %collective-permute-start.10 = (bf16[64,256]{1,0:T(8,128)(2,1)S(1)}, bf16[64,256]{1,0:T(8,128)(2,1)S(1)}, u32[]{:S(2)}, u32[]{:S(2)}) collective-permute-start(bf16[64,256]{1,0:T(8,128)(2,1)S(1)} %shard_map.113.refs_7_.refs_0_), channel_id=1, source_target_pairs={{0,4},{1,5},{2,6},{3,7},{4,0},{5,1},{6,2},{7,3},{8,12},{9,13},{10,... | collective-permute-start | bytes 98312 | tf_op jit(solution)/shard_map/ppermute | solution.py:435
  43.2 1.3 %shard_map.114.refs_2_.refs_3_ = f32[64,2048]{1,0:T(8,128)S(1)} custom-call(s32[16]{0:T(128)S(1)} %concatenate.3.refs_0_, f32[64,2048]{1,0:T(8,128)S(1)} %shard_map.103.refs_2_.refs_1_, bf16[64,256]{1,0:T(8,128)(2,1)S(1)} %collective-permute-done.3.refs_2_, bf16[64,256]{1,0:T(8,128)(2,1)S(1)} %collective-permute-done.8.refs_3_, ...), custom_call_target="tpu_custom_call" | custom-call | flops 67108864 | bytes 1736768 | tf_op jit(solution)/shard_map/pallas_call | solution.py:27
  44.8 1.6 %collective-permute-done.10.refs_1_ = bf16[64,256]{1,0:T(8,128)(2,1)S(1)} collective-permute-done((bf16[64,256]{1,0:T(8,128)(2,1)S(1)}, bf16[64,256]{1,0:T(8,128)(2,1)S(1)}, u32[]{:S(2)}, u32[]{:S(2)}) %collective-permute-start.10) | collective-permute-done | bytes 32800 | tf_op jit(solution)/shard_map/ppermute | solution.py:435
  46.4 1.6 %shard_map.116 = (f32[64,2048]{1,0:T(8,128)S(1)}, bf16[64,2048]{1,0:T(8,128)(2,1)S(1)}, bf16[64,256]{1,0:T(8,128)(2,1)S(1)}, bf16[64,256]{1,0:T(8,128)(2,1)S(1)}) custom-call(f32[64,256]{1,0:T(8,128)S(1)} %shard_map.115.refs_0_, bf16[64,256]{1,0:T(8,128)(2,1)S(1)} %collective-permute-done.10.refs_1_, ...), custom_call_target="tpu_custom_call" | custom-call | flops 268435456 | bytes 5341184 | tf_op jit(solution)/shard_map/pallas_call | solution.py:27
  48.0 4.7 %collective-permute-start.11 = (bf16[64,256]{1,0:T(8,128)(2,1)S(1)}, bf16[64,256]{1,0:T(8,128)(2,1)S(1)}, u32[]{:S(2)}, u32[]{:S(2)}) collective-permute-start(bf16[64,256]{1,0:T(8,128)(2,1)S(1)} %get-tuple-element.49), channel_id=1, source_target_pairs={{0,4},{1,5},{2,6},{3,7},{4,0},{5,1},{6,2},{7,3},{8,12},{9,13},{10,... | collective-permute-start | bytes 98312 | tf_op jit(solution)/shard_map/ppermute | solution.py:435
  52.7 1.0 shard_map.118
  53.9 2.1 %collective-permute-done.11.refs_1_ = bf16[64,256]{1,0:T(8,128)(2,1)S(1)} collective-permute-done((bf16[64,256]{1,0:T(8,128)(2,1)S(1)}, bf16[64,256]{1,0:T(8,128)(2,1)S(1)}, u32[]{:S(2)}, u32[]{:S(2)}) %collective-permute-start.11) | collective-permute-done | bytes 32800 | tf_op jit(solution)/shard_map/ppermute | solution.py:435
  56.1 0.5 collective-permute-start.14
  56.7 0.8 shard_map.121.refs_2_.refs_1_
  57.7 3.4 %collective-permute-done.14.refs_1_ = bf16[64,256]{1,0:T(8,128)(2,1)S(1)} collective-permute-done((bf16[64,256]{1,0:T(8,128)(2,1)S(1)}, bf16[64,256]{1,0:T(8,128)(2,1)S(1)}, u32[]{:S(2)}, u32[]{:S(2)}) %collective-permute-start.14) | collective-permute-done | bytes 32800 | tf_op jit(solution)/shard_map/ppermute | solution.py:435
  61.3 0.3 collective-permute-start.15
  61.7 4.0 %collective-permute-done.15.refs_4_.refs_1_ = bf16[128,256]{1,0:T(8,128)(2,1)S(1)} collective-permute-done((bf16[128,256]{1,0:T(8,128)(2,1)S(1)}, bf16[128,256]{1,0:T(8,128)(2,1)S(1)}, u32[]{:S(2)}, u32[]{:S(2)}) %collective-permute-start.15) | collective-permute-done | bytes 65568 | tf_op jit(solution)/shard_map/ppermute | solution.py:435
  66.0 3.1 %collective-permute-start.17 = (bf16[64,256]{1,0:T(8,128)(2,1)S(1)}, bf16[64,256]{1,0:T(8,128)(2,1)S(1)}, u32[]{:S(2)}, u32[]{:S(2)}) collective-permute-start(bf16[64,256]{1,0:T(8,128)(2,1)S(1)} %get-tuple-element.55.refs_1_), channel_id=1, source_target_pairs={{0,128},{8,136},{16,144},{24,152},{32,160},{40,168},{48,176},{56,1... | collective-permute-start | bytes 98312 | tf_op jit(solution)/shard_map/ppermute | solution.py:433
  69.1 1.7 %shard_map.127 = (bf16[64,2048]{1,0:T(8,128)(2,1)S(1)}, bf16[64,2048]{1,0:T(8,128)(2,1)S(1)}, f32[32,32]{1,0:T(8,128)S(1)}) custom-call(f32[32,32,128]{2,1,0:T(8,128)S(1)} %bitcast.37, bf16[64,256]{1,0:T(8,128)(2,1)S(1)} %get-tuple-element.55.refs_1_), custom_call_target="tpu_custom_call" | custom-call | flops 67108864 | bytes 524288 | tf_op jit(solution)/shard_map/pallas_call | solution.py:27
  71.1 0.4 collective-permute-done.17.refs_1_
  71.7 1.6 %collective-permute-start.18 = (bf16[64,256]{1,0:T(8,128)(2,1)S(1)}, bf16[64,256]{1,0:T(8,128)(2,1)S(1)}, u32[]{:S(2)}, u32[]{:S(2)}) collective-permute-start(bf16[64,256]{1,0:T(8,128)(2,1)S(1)} %get-tuple-element.60), channel_id=1, source_target_pairs={{0,64},{8,72},{16,80},{24,88},{32,96},{40,104},{48,112},{56,120},{... | collective-permute-start | bytes 98312 | tf_op jit(solution)/shard_map/ppermute | solution.py:433
  73.3 3.3 %collective-permute-start.16 = (bf16[64,256]{1,0:T(8,128)(2,1)S(1)}, bf16[64,256]{1,0:T(8,128)(2,1)S(1)}, u32[]{:S(2)}, u32[]{:S(2)}) collective-permute-start(bf16[64,256]{1,0:T(8,128)(2,1)S(1)} %get-tuple-element.48.refs_5_), channel_id=1, source_target_pairs={{1,2},{3,4},{5,6},{7,0},{2,1},{4,3},{6,5},{0,7},{9,10},{11,12},{13... | collective-permute-start | bytes 98312 | tf_op jit(solution)/shard_map/ppermute | solution.py:439
  77.0 3.1 %collective-permute-start.19 = (bf16[64,256]{1,0:T(8,128)(2,1)S(1)}, bf16[64,256]{1,0:T(8,128)(2,1)S(1)}, u32[]{:S(2)}, u32[]{:S(2)}) collective-permute-start(bf16[64,256]{1,0:T(8,128)(2,1)S(1)} %get-tuple-element.62), channel_id=1, source_target_pairs={{0,32},{8,40},{16,48},{24,56},{32,0},{40,8},{48,16},{56,24},{64,96... | collective-permute-start | bytes 98312 | tf_op jit(solution)/shard_map/ppermute | solution.py:433
  80.3 2.2 %collective-permute-done.19.refs_1_ = bf16[64,256]{1,0:T(8,128)(2,1)S(1)} collective-permute-done((bf16[64,256]{1,0:T(8,128)(2,1)S(1)}, bf16[64,256]{1,0:T(8,128)(2,1)S(1)}, u32[]{:S(2)}, u32[]{:S(2)}) %collective-permute-start.19) | collective-permute-done | bytes 32800 | tf_op jit(solution)/shard_map/ppermute | solution.py:433
  82.7 2.0 %collective-permute-start.20 = (bf16[64,256]{1,0:T(8,128)(2,1)S(1)}, bf16[64,256]{1,0:T(8,128)(2,1)S(1)}, u32[]{:S(2)}, u32[]{:S(2)}) collective-permute-start(bf16[64,256]{1,0:T(8,128)(2,1)S(1)} %get-tuple-element.64), channel_id=1, source_target_pairs={{0,16},{8,24},{16,0},{24,8},{32,48},{40,56},{48,32},{56,40},{64,80... | collective-permute-start | bytes 98312 | tf_op jit(solution)/shard_map/ppermute | solution.py:433
  84.9 1.8 %collective-permute-done.20.refs_1_ = bf16[64,256]{1,0:T(8,128)(2,1)S(1)} collective-permute-done((bf16[64,256]{1,0:T(8,128)(2,1)S(1)}, bf16[64,256]{1,0:T(8,128)(2,1)S(1)}, u32[]{:S(2)}, u32[]{:S(2)}) %collective-permute-start.20) | collective-permute-done | bytes 32800 | tf_op jit(solution)/shard_map/ppermute | solution.py:433
  87.0 1.0 collective-permute-done.13.refs_3_
  88.0 0.6 shard_map.124.refs_2_.refs_0_
  88.9 1.6 %shard_map.137 = (bf16[64,2048]{1,0:T(8,128)(2,1)S(1)}, bf16[64,2048]{1,0:T(8,128)(2,1)S(1)}, f32[32,128]{1,0:T(8,128)S(1)}) custom-call(f32[64,2048]{1,0:T(8,128)S(1)} %shard_map.124.refs_2_.refs_0_, f32[64,256]{1,0:T(8,128)S(1)} %shard_map.136.refs_1_, bf16[64,256]{1,0:T(8,128)(2,1)S(1)} %collective-permute-done.21.refs_2_, ...), custom_call_target="tpu_custom_call" | custom-call | flops 134217728 | bytes 3248128 | tf_op jit(solution)/shard_map/pallas_call | solution.py:27
  90.7 1.1 collective-permute-done.22.refs_1_
  91.8 14.8 %all_to_all.10.refs_0_ = f32[16,32,128]{2,1,0:T(8,128)S(1)} all-to-all(f32[16,32,128]{2,1,0:T(8,128)S(1)} %shard_map.138), channel_id=1, replica_groups={{0,16,32,48,64,80,96,112,128,144,160,176,192,208,224,240},{8,24,40,56,7..., dimensions={0} | all-to-all | bytes 524288 | tf_op jit(solution)/shard_map/all_to_all | solution.py:590
  106.6 0.7 shard_map.139
  107.2 5.1 %all-to-all-start.1 = ((f32[8,32,128]{2,1,0:T(8,128)}), f32[8,32,128]{2,1,0:T(8,128)S(1)}, u32[]{:S(2)}, u32[]{:S(2)}) async-start(f32[8,32,128]{2,1,0:T(8,128)} %shard_map.139), calls=%async_computation.1 | async-start | bytes 262144 | tf_op jit(solution)/shard_map/all_to_all | solution.py:592
  112.3 1.3 %shard_map.117 = f32[32,32,128]{2,1,0:T(8,128)} custom-call(f32[64,2048]{1,0:T(8,128)S(1)} %copy-done.10), custom_call_target="tpu_custom_call" | custom-call | bytes 524288 | tf_op jit(solution)/shard_map/pallas_call | solution.py:27
  113.6 7.8 %all-to-all-done.1.refs_0_ = f32[8,32,128]{2,1,0:T(8,128)S(1)} async-done(((f32[8,32,128]{2,1,0:T(8,128)}), f32[8,32,128]{2,1,0:T(8,128)S(1)}, u32[]{:S(2)}, u32[]{:S(2)}) %all-to-all-start.1) | async-done | bytes 131104 | tf_op jit(solution)/shard_map/all_to_all | solution.py:592
  121.4 4.3 %shard_map.140 = f32[64,32,128]{2,1,0:T(8,128)} custom-call(f32[8,32,128]{2,1,0:T(8,128)S(1)} %all-to-all-done.1.refs_0_, bf16[64,2048]{1,0:T(8,128)(2,1)S(1)} %get-tuple-element.68.refs_1_, bf16[64,2048]{1,0:T(8,128)(2,1)S(1)} %get-tuple-element.69.refs_2_, bf16[64,2048]{1,0:T(8,128)(2,1)S(1)} %get-tuple-element.56.refs_2_.refs_4_.refs_3_, ...), custom_call_target="tpu_custom_call" | custom-call | flops 67108864 | bytes 1179648 | tf_op jit(solution)/shard_map/pallas_call | solution.py:27
  (75 shorter events, 6.6 us)
Async XLA Ops:
  0.6 8.6 %copy-start = (s32[32,8,4,2]{0,3,2,1:T(2,128)S(1)}, s32[32,8,4,2]{0,3,2,1:T(2,128)}, u32[]{:S(2)}) copy-start(s32[32,8,4,2]{0,3,2,1:T(2,128)} %param.9) | copy-start | bytes 24580
  3.1 1.7 %collective-permute-start = (bf16[64,256]{1,0:T(8,128)(2,1)S(1)}, bf16[64,256]{1,0:T(8,128)(2,1)S(1)}, u32[]{:S(2)}, u32[]{:S(2)}) collective-permute-start(bf16[64,256]{1,0:T(8,128)(2,1)S(1)} %get-tuple-element.36.refs_0_), channel_id=1, source_target_pairs={{0,8},{8,0},{16,24},{24,16},{32,40},{40,32},{48,56},{56,48},{64,72... | collective-permute-start | bytes 98312 | tf_op jit(solution)/shard_map/ppermute | solution.py:433
  4.7 2.7 %copy-start.1 = (bf16[3,2,2,256,256]{4,3,2,1,0:T(8,128)(2,1)}, bf16[3,2,2,256,256]{4,3,2,1,0:T(8,128)(2,1)S(1)}, u32[]{:S(2)}) copy-start(bf16[3,2,2,256,256]{4,3,2,1,0:T(8,128)(2,1)S(1)} %shard_map.96.refs_1_.refs_2_) | copy-start | bytes 4718596
  4.7 2.6 %copy-start.11 = (s32[4]{0:T(128)S(1)}, s32[4]{0:T(128)}, u32[]{:S(2)}) copy-start(s32[4]{0:T(128)} %constant.40.clone) | copy-start | bytes 52
  5.1 6.7 %collective-permute-start.1 = (bf16[64,256]{1,0:T(8,128)(2,1)S(1)}, bf16[64,256]{1,0:T(8,128)(2,1)S(1)}, u32[]{:S(2)}, u32[]{:S(2)}) collective-permute-start(bf16[64,256]{1,0:T(8,128)(2,1)S(1)} %shard_map.98.refs_2_.refs_0_), channel_id=1, source_target_pairs={{0,16},{8,24},{16,0},{24,8},{32,48},{40,56},{48,32},{56,40},{64,80... | collective-permute-start | bytes 98312 | tf_op jit(solution)/shard_map/ppermute | solution.py:433
  10.2 1.4 %copy-start.2 = (bf16[3,2,2,256,256]{4,3,2,1,0:T(8,128)(2,1)S(1)}, bf16[3,2,2,256,256]{4,3,2,1,0:T(8,128)(2,1)}, u32[]{:S(2)}) copy-start(bf16[3,2,2,256,256]{4,3,2,1,0:T(8,128)(2,1)} %copy-done.1) | copy-start | bytes 4718596
  11.6 1.4 %copy-start.7 = (bf16[1,1,2,16,128,128]{5,4,3,2,1,0:T(8,128)(2,1)S(1)}, bf16[1,1,2,16,128,128]{5,4,3,2,1,0:T(8,128)(2,1)}, u32[]{:S(2)}) copy-start(bf16[1,1,2,16,128,128]{5,4,3,2,1,0:T(8,128)(2,1)} %param.10) | copy-start | bytes 3145732
  11.8 1.6 %copy-start.3 = (bf16[3,2,2,256,256]{4,3,2,1,0:T(8,128)(2,1)S(1)}, bf16[3,2,2,256,256]{4,3,2,1,0:T(8,128)(2,1)}, u32[]{:S(2)}) copy-start(bf16[3,2,2,256,256]{4,3,2,1,0:T(8,128)(2,1)} %copy-done.1) | copy-start | bytes 4718596
  12.0 5.5 %collective-permute-start.2 = (bf16[64,256]{1,0:T(8,128)(2,1)S(1)}, bf16[64,256]{1,0:T(8,128)(2,1)S(1)}, u32[]{:S(2)}, u32[]{:S(2)}) collective-permute-start(bf16[64,256]{1,0:T(8,128)(2,1)S(1)} %shard_map.102.refs_2_.refs_0_), channel_id=1, source_target_pairs={{0,32},{8,40},{16,48},{24,56},{32,0},{40,8},{48,16},{56,24},{64,96... | collective-permute-start | bytes 98312 | tf_op jit(solution)/shard_map/ppermute | solution.py:433
  12.9 4.8 %collective-permute-start.3 = (bf16[64,256]{1,0:T(8,128)(2,1)S(1)}, bf16[64,256]{1,0:T(8,128)(2,1)S(1)}, u32[]{:S(2)}, u32[]{:S(2)}) collective-permute-start(bf16[64,256]{1,0:T(8,128)(2,1)S(1)} %get-tuple-element.38.refs_2_), channel_id=1, source_target_pairs={{0,8},{8,0},{16,24},{24,16},{32,40},{40,32},{48,56},{56,48},{64,72... | collective-permute-start | bytes 98312 | tf_op jit(solution)/shard_map/ppermute | solution.py:433
  17.6 4.0 %collective-permute-start.4 = (bf16[64,256]{1,0:T(8,128)(2,1)S(1)}, bf16[64,256]{1,0:T(8,128)(2,1)S(1)}, u32[]{:S(2)}, u32[]{:S(2)}) collective-permute-start(bf16[64,256]{1,0:T(8,128)(2,1)S(1)} %shard_map.105.refs_0_), channel_id=1, source_target_pairs={{0,64},{8,72},{16,80},{24,88},{32,96},{40,104},{48,112},{56,120},{... | collective-permute-start | bytes 98312 | tf_op jit(solution)/shard_map/ppermute | solution.py:433
  21.8 5.5 %collective-permute-start.5 = (bf16[64,256]{1,0:T(8,128)(2,1)S(1)}, bf16[64,256]{1,0:T(8,128)(2,1)S(1)}, u32[]{:S(2)}, u32[]{:S(2)}) collective-permute-start(bf16[64,256]{1,0:T(8,128)(2,1)S(1)} %shard_map.107.refs_0_), channel_id=1, source_target_pairs={{0,128},{8,136},{16,144},{24,152},{32,160},{40,168},{48,176},{56,1... | collective-permute-start | bytes 98312 | tf_op jit(solution)/shard_map/ppermute | solution.py:433
  27.5 4.7 %collective-permute-start.6 = (bf16[128,256]{1,0:T(8,128)(2,1)S(1)}, bf16[128,256]{1,0:T(8,128)(2,1)S(1)}, u32[]{:S(2)}, u32[]{:S(2)}) collective-permute-start(bf16[128,256]{1,0:T(8,128)(2,1)S(1)} %shard_map.109.refs_0_), channel_id=1, source_target_pairs={{0,1},{1,0},{2,3},{3,2},{4,5},{5,4},{6,7},{7,6},{8,9},{9,8},{10,11... | collective-permute-start | bytes 196616 | tf_op jit(solution)/shard_map/ppermute | solution.py:435
  32.4 10.8 %copy-start.6 = (bf16[1,1,4,2,256,256]{5,4,3,2,1,0:T(8,128)(2,1)S(1)}, bf16[1,1,4,2,256,256]{5,4,3,2,1,0:T(8,128)(2,1)}, u32[]{:S(2)}) copy-start(bf16[1,1,4,2,256,256]{5,4,3,2,1,0:T(8,128)(2,1)} %param.11) | copy-start | bytes 3145732
  32.4 5.9 %collective-permute-start.7 = (bf16[64,256]{1,0:T(8,128)(2,1)S(1)}, bf16[64,256]{1,0:T(8,128)(2,1)S(1)}, u32[]{:S(2)}, u32[]{:S(2)}) collective-permute-start(bf16[64,256]{1,0:T(8,128)(2,1)S(1)} %shard_map.111.refs_0_), channel_id=1, source_target_pairs={{0,2},{1,3},{2,0},{3,1},{4,6},{5,7},{6,4},{7,5},{8,10},{9,11},{10,... | collective-permute-start | bytes 98312 | tf_op jit(solution)/shard_map/ppermute | solution.py:435
  33.8 9.3 %collective-permute-start.8 = (bf16[64,256]{1,0:T(8,128)(2,1)S(1)}, bf16[64,256]{1,0:T(8,128)(2,1)S(1)}, u32[]{:S(2)}, u32[]{:S(2)}) collective-permute-start(bf16[64,256]{1,0:T(8,128)(2,1)S(1)} %get-tuple-element.39.refs_3_), channel_id=1, source_target_pairs={{8,16},{24,32},{40,48},{56,64},{72,80},{88,96},{104,112},{120,128}... | collective-permute-start | bytes 98312 | tf_op jit(solution)/shard_map/ppermute | solution.py:439
  33.8 9.3 %collective-permute-start.9 = (bf16[64,256]{1,0:T(8,128)(2,1)S(1)}, bf16[64,256]{1,0:T(8,128)(2,1)S(1)}, u32[]{:S(2)}, u32[]{:S(2)}) collective-permute-start(bf16[64,256]{1,0:T(8,128)(2,1)S(1)} %get-tuple-element.41.refs_5_), channel_id=1, source_target_pairs={{1,2},{3,4},{5,6},{7,0},{2,1},{4,3},{6,5},{0,7},{9,10},{11,12},{13... | collective-permute-start | bytes 98312 | tf_op jit(solution)/shard_map/ppermute | solution.py:439
  38.3 6.3 %copy-start.5 = (bf16[1,1,2,256,2048]{4,3,2,1,0:T(8,128)(2,1)S(1)}, bf16[1,1,2,256,2048]{4,3,2,1,0:T(8,128)(2,1)}, u32[]{:S(2)}) copy-start(bf16[1,1,2,256,2048]{4,3,2,1,0:T(8,128)(2,1)} %param.13) | copy-start | bytes 6291460
  38.5 7.9 %collective-permute-start.10 = (bf16[64,256]{1,0:T(8,128)(2,1)S(1)}, bf16[64,256]{1,0:T(8,128)(2,1)S(1)}, u32[]{:S(2)}, u32[]{:S(2)}) collective-permute-start(bf16[64,256]{1,0:T(8,128)(2,1)S(1)} %shard_map.113.refs_7_.refs_0_), channel_id=1, source_target_pairs={{0,4},{1,5},{2,6},{3,7},{4,0},{5,1},{6,2},{7,3},{8,12},{9,13},{10,... | collective-permute-start | bytes 98312 | tf_op jit(solution)/shard_map/ppermute | solution.py:435
  48.0 8.2 %copy-start.9 = (f32[64,2048]{1,0:T(8,128)}, f32[64,2048]{1,0:T(8,128)S(1)}, u32[]{:S(2)}) copy-start(f32[64,2048]{1,0:T(8,128)S(1)} %get-tuple-element.42.refs_0_) | copy-start | bytes 1572868
  48.0 8.0 %collective-permute-start.11 = (bf16[64,256]{1,0:T(8,128)(2,1)S(1)}, bf16[64,256]{1,0:T(8,128)(2,1)S(1)}, u32[]{:S(2)}, u32[]{:S(2)}) collective-permute-start(bf16[64,256]{1,0:T(8,128)(2,1)S(1)} %get-tuple-element.49), channel_id=1, source_target_pairs={{0,4},{1,5},{2,6},{3,7},{4,0},{5,1},{6,2},{7,3},{8,12},{9,13},{10,... | collective-permute-start | bytes 98312 | tf_op jit(solution)/shard_map/ppermute | solution.py:435
  56.1 4.9 %collective-permute-start.14 = (bf16[64,256]{1,0:T(8,128)(2,1)S(1)}, bf16[64,256]{1,0:T(8,128)(2,1)S(1)}, u32[]{:S(2)}, u32[]{:S(2)}) collective-permute-start(bf16[64,256]{1,0:T(8,128)(2,1)S(1)} %get-tuple-element.50.refs_2_), channel_id=1, source_target_pairs={{0,2},{1,3},{2,0},{3,1},{4,6},{5,7},{6,4},{7,5},{8,10},{9,11},{10,... | collective-permute-start | bytes 98312 | tf_op jit(solution)/shard_map/ppermute | solution.py:435
  61.3 4.5 %collective-permute-start.15 = (bf16[128,256]{1,0:T(8,128)(2,1)S(1)}, bf16[128,256]{1,0:T(8,128)(2,1)S(1)}, u32[]{:S(2)}, u32[]{:S(2)}) collective-permute-start(bf16[128,256]{1,0:T(8,128)(2,1)S(1)} %get-tuple-element.52), channel_id=1, source_target_pairs={{0,1},{1,0},{2,3},{3,2},{4,5},{5,4},{6,7},{7,6},{8,9},{9,8},{10,11... | collective-permute-start | bytes 196616 | tf_op jit(solution)/shard_map/ppermute | solution.py:435
  61.5 7.6 %copy-start.8 = (f32[32,1,1,2,2048]{4,3,2,1,0:T(2,128)S(1)}, f32[32,1,1,2,2048]{4,3,2,1,0:T(2,128)}, u32[]{:S(2)}) copy-start(f32[32,1,1,2,2048]{4,3,2,1,0:T(2,128)} %param.8) | copy-start | bytes 1572868
  66.0 5.5 %collective-permute-start.17 = (bf16[64,256]{1,0:T(8,128)(2,1)S(1)}, bf16[64,256]{1,0:T(8,128)(2,1)S(1)}, u32[]{:S(2)}, u32[]{:S(2)}) collective-permute-start(bf16[64,256]{1,0:T(8,128)(2,1)S(1)} %get-tuple-element.55.refs_1_), channel_id=1, source_target_pairs={{0,128},{8,136},{16,144},{24,152},{32,160},{40,168},{48,176},{56,1... | collective-permute-start | bytes 98312 | tf_op jit(solution)/shard_map/ppermute | solution.py:433
  71.7 5.0 %collective-permute-start.18 = (bf16[64,256]{1,0:T(8,128)(2,1)S(1)}, bf16[64,256]{1,0:T(8,128)(2,1)S(1)}, u32[]{:S(2)}, u32[]{:S(2)}) collective-permute-start(bf16[64,256]{1,0:T(8,128)(2,1)S(1)} %get-tuple-element.60), channel_id=1, source_target_pairs={{0,64},{8,72},{16,80},{24,88},{32,96},{40,104},{48,112},{56,120},{... | collective-permute-start | bytes 98312 | tf_op jit(solution)/shard_map/ppermute | solution.py:433
  73.3 6.8 %collective-permute-start.16 = (bf16[64,256]{1,0:T(8,128)(2,1)S(1)}, bf16[64,256]{1,0:T(8,128)(2,1)S(1)}, u32[]{:S(2)}, u32[]{:S(2)}) collective-permute-start(bf16[64,256]{1,0:T(8,128)(2,1)S(1)} %get-tuple-element.48.refs_5_), channel_id=1, source_target_pairs={{1,2},{3,4},{5,6},{7,0},{2,1},{4,3},{6,5},{0,7},{9,10},{11,12},{13... | collective-permute-start | bytes 98312 | tf_op jit(solution)/shard_map/ppermute | solution.py:439
  77.0 7.7 %copy-start.4 = (bf16[1,1,2,2048,256]{4,3,2,1,0:T(8,128)(2,1)S(1)}, bf16[1,1,2,2048,256]{4,3,2,1,0:T(8,128)(2,1)}, u32[]{:S(2)}) copy-start(bf16[1,1,2,2048,256]{4,3,2,1,0:T(8,128)(2,1)} %param.12) | copy-start | bytes 6291460
  77.0 5.5 %collective-permute-start.19 = (bf16[64,256]{1,0:T(8,128)(2,1)S(1)}, bf16[64,256]{1,0:T(8,128)(2,1)S(1)}, u32[]{:S(2)}, u32[]{:S(2)}) collective-permute-start(bf16[64,256]{1,0:T(8,128)(2,1)S(1)} %get-tuple-element.62), channel_id=1, source_target_pairs={{0,32},{8,40},{16,48},{24,56},{32,0},{40,8},{48,16},{56,24},{64,96... | collective-permute-start | bytes 98312 | tf_op jit(solution)/shard_map/ppermute | solution.py:433
  80.1 4.6 %collective-permute-start.12 = (bf16[64,256]{1,0:T(8,128)(2,1)S(1)}, bf16[64,256]{1,0:T(8,128)(2,1)S(1)}, u32[]{:S(2)}, u32[]{:S(2)}) collective-permute-start(bf16[64,256]{1,0:T(8,128)(2,1)S(1)} %get-tuple-element.45.refs_2_), channel_id=1, source_target_pairs={{0,8},{8,0},{16,24},{24,16},{32,40},{40,32},{48,56},{56,48},{64,72... | collective-permute-start | bytes 98312 | tf_op jit(solution)/shard_map/ppermute | solution.py:433
  82.7 4.0 %collective-permute-start.20 = (bf16[64,256]{1,0:T(8,128)(2,1)S(1)}, bf16[64,256]{1,0:T(8,128)(2,1)S(1)}, u32[]{:S(2)}, u32[]{:S(2)}) collective-permute-start(bf16[64,256]{1,0:T(8,128)(2,1)S(1)} %get-tuple-element.64), channel_id=1, source_target_pairs={{0,16},{8,24},{16,0},{24,8},{32,48},{40,56},{48,32},{56,40},{64,80... | collective-permute-start | bytes 98312 | tf_op jit(solution)/shard_map/ppermute | solution.py:433
  84.7 3.3 %collective-permute-start.13 = (bf16[64,256]{1,0:T(8,128)(2,1)S(1)}, bf16[64,256]{1,0:T(8,128)(2,1)S(1)}, u32[]{:S(2)}, u32[]{:S(2)}) collective-permute-start(bf16[64,256]{1,0:T(8,128)(2,1)S(1)} %get-tuple-element.46.refs_3_), channel_id=1, source_target_pairs={{8,16},{24,32},{40,48},{56,64},{72,80},{88,96},{104,112},{120,128}... | collective-permute-start | bytes 98312 | tf_op jit(solution)/shard_map/ppermute | solution.py:439
  86.9 2.0 %collective-permute-start.21 = (bf16[64,256]{1,0:T(8,128)(2,1)S(1)}, bf16[64,256]{1,0:T(8,128)(2,1)S(1)}, u32[]{:S(2)}, u32[]{:S(2)}) collective-permute-start(bf16[64,256]{1,0:T(8,128)(2,1)S(1)} %get-tuple-element.66), channel_id=1, source_target_pairs={{0,8},{8,0},{16,24},{24,16},{32,40},{40,32},{48,56},{56,48},{64,72... | collective-permute-start | bytes 98312 | tf_op jit(solution)/shard_map/ppermute | solution.py:433
  88.9 23.5 %copy-start.10 = (f32[64,2048]{1,0:T(8,128)S(1)}, f32[64,2048]{1,0:T(8,128)}, u32[]{:S(2)}) copy-start(f32[64,2048]{1,0:T(8,128)} %copy-done.9) | copy-start | bytes 1572868
  90.5 1.3 %collective-permute-start.22 = (f32[1,32,128]{2,1,0:T(8,128)S(1)}, f32[1,32,128]{2,1,0:T(8,128)S(1)}, u32[]{:S(2)}, u32[]{:S(2)}) collective-permute-start(f32[1,32,128]{2,1,0:T(8,128)S(1)} %bitcast.38), channel_id=1, source_target_pairs={{0,8},{8,0},{16,24},{24,16},{32,40},{40,32},{48,56},{56,48},{64,72... | collective-permute-start | bytes 49160 | tf_op jit(solution)/shard_map/ppermute | solution.py:433
  107.2 14.1 %all-to-all-start.1 = ((f32[8,32,128]{2,1,0:T(8,128)}), f32[8,32,128]{2,1,0:T(8,128)S(1)}, u32[]{:S(2)}, u32[]{:S(2)}) async-start(f32[8,32,128]{2,1,0:T(8,128)} %shard_map.139), calls=%async_computation.1 | async-start | bytes 262144 | tf_op jit(solution)/shard_map/all_to_all | solution.py:592

commit v5 on v3

--- a/solution.py
+++ b/solution.py
@@ -183,13 +183,15 @@
         o_ref[cut] = product(s_ref[cut], f[at, 0, 0], f[at, 0, 1])
 
 
-def up_kernel(at, count, own_ref, r_ref, *rest):
+def up_kernel(at, count, extra, own_ref, r_ref, *rest):
     rows = own_ref.shape[0] // count
-    outs = rest[count:]
+    outs = rest[count + extra :]
+    for piece_ref in rest[count : count + extra]:
+        outs[0][count * rows :] = piece_ref[...]
     for part, f in enumerate(rest[:count]):
         cut = slice(part * rows, (part + 1) * rows)
         state = own_ref[cut] + mul(r_ref[cut], f[at, 1, 0], f[at, 1, 1])
-        if len(outs) == count:
+        if len(outs) > 1:
             outs[part][...] = state.astype(BF16)
         else:
             outs[0][cut] = state.astype(BF16)
@@ -209,12 +211,16 @@
 
 
 def sides_kernel(leaf, info, near_ref, ra_ref, rb_ref, rc_ref, rd_ref, b_ref, o_ref):
+    rows = near_ref.shape[0]
     o_ref[...] = near_ref[...]
     for at, ref in enumerate((ra_ref, rb_ref, rc_ref, rd_ref)):
         side = info[8 + at]
-        term = mul(ref[...], b_ref[side, 0], b_ref[side, 1])
-        for e in range(2):
-            o_ref[:, leaf_at(info[2 * side + e], leaf)] += term[:, e * leaf : (e + 1) * leaf]
+        term = mul(ref[ref.shape[0] - rows :], b_ref[side, 0], b_ref[side, 1])
+
+        @pl.when(info[13 + at] == 1)
+        def _():
+            for e in range(2):
+                o_ref[:, leaf_at(info[2 * side + e], leaf)] += term[:, e * leaf : (e + 1) * leaf]
 
 
 def field_kernel(info, mine_ref, sent_ref, near_ref, e_ref, y_ref, yb_ref, g_ref, state_ref):
@@ -258,8 +264,11 @@
         m_ref[cut] = adj(x[...], f[at, 1, 0], f[at, 1, 1]).astype(BF16)
 
 
-def down_kernel(at, own_ref, r_ref, f_ref, fo_ref, g_ref, m_ref):
+def down_kernel(at, own_ref, r_ref, f_ref, fo_ref, *rest):
     rows = own_ref.shape[0] // 2
+    g_ref, m_ref = rest[-2:]
+    if len(rest) > 2:
+        m_ref[2 * rows :] = rest[0][...]
     for part, f in enumerate((f_ref, fo_ref)):
         cut = slice(part * rows, (part + 1) * rows)
         g = (own_ref[cut] + r_ref[cut].astype(F32)).astype(BF16)
@@ -279,11 +288,18 @@
 
 
 def gather_kernel(leaf, info, near_ref, ra_ref, rb_ref, rc_ref, rd_ref, o_ref):
+    rows = near_ref.shape[0]
     o_ref[...] = near_ref[...]
     for at, ref in enumerate((ra_ref, rb_ref, rc_ref, rd_ref)):
         side = info[8 + at]
-        for e in range(2):
-            o_ref[:, leaf_at(info[2 * side + e], leaf)] += ref[:, e * leaf : (e + 1) * leaf].astype(F32)
+        low = ref.shape[0] - rows
+
+        @pl.when(info[13 + at] == 1)
+        def _():
+            for e in range(2):
+                o_ref[:, leaf_at(info[2 * side + e], leaf)] += ref[
+                    low:, e * leaf : (e + 1) * leaf
+                ].astype(F32)
 
 
 def close_kernel(
@@ -450,14 +466,20 @@
     own_leaves = lax.dynamic_slice(edge_leaves, (row_at, col_at, 0, 0), (1, 1, 4, 2)).reshape(8)
     odd_row, odd_col = row_at % 2, col_at % 2
     order = jnp.stack([1 - odd_row, odd_row, 3 - odd_col, 2 + odd_col]).astype(jnp.int32)
-    info = jnp.concatenate([own_leaves, order, odd_row[None].astype(jnp.int32)])
+    inner_row = (row_at > 0) & (row_at < row_count - 1)
+    inner_col = (col_at > 0) & (col_at < col_count - 1)
+    flags = jnp.stack([odd_row == 1, row_at >= 0, inner_row, row_at >= 0, inner_col])
+    info = jnp.concatenate([own_leaves, order, flags.astype(jnp.int32)])
     tall = v_block.reshape(cols, 2, leaves, leaf).transpose(0, 2, 1, 3).reshape(cols, -1, leaf)
 
     def partner(x, level):
         near_bit, far_bit = (1 << level, 0) if level < row_bits else (0, 1 << level - row_bits)
+        flips = [(2, 0), (near_bit, far_bit)]
+        if level == row_bits:
+            flips[0] = flips[1]
         pairs = [
-            (i * col_count + j, (i ^ near_bit) * col_count + (j ^ far_bit))
-            for i in range(1, row_count, 2)
+            (i * col_count + j, (i ^ flips[i % 2][0]) * col_count + (j ^ flips[i % 2][1]))
+            for i in range(row_count)
             for j in range(col_count)
         ]
         return lax.ppermute(x, ("px", "py"), pairs)
@@ -466,17 +488,15 @@
         return lax.ppermute(x, axis, [(i, i ^ 1) for i in range(count)])
 
     def over(x):
-        return lax.ppermute(x, "px", [(i, i + 1) for i in range(0, row_count, 2)])
-
-    def back(x):
-        return lax.ppermute(x, "px", [(i + 1, i) for i in range(0, row_count, 2)])
+        return swapped(x, "px", row_count)
 
     def beyond(x, axis, count):
-        pairs = [(i, i + 1) for i in range(1, count - 1, 2)]
+        pairs = [(i, (i + 1) % count) for i in range(1, count, 2)]
         return lax.ppermute(x, axis, pairs + [(j, i) for i, j in pairs])
 
     small = ((rows, rank), BF16)
     double = ((2 * rows, rank), BF16)
+    triple = ((3 * rows, rank), BF16)
     wide = ((rows, rank), F32)
     wide_double = ((2 * rows, rank), F32)
     step_flops = 8 * cols * rank * rank
@@ -489,7 +509,7 @@
     zero = load(sections, 0, 1, EARLY, [sent])
     arrived = swapped(sent, "px", row_count)
     (own,) = call(functools.partial(own_kernel, 0, False), [wide], [sent, zero], step_flops)
-    (sent,) = call(functools.partial(up_kernel, 0, 1), [small], [own, arrived, zero], step_flops)
+    (sent,) = call(functools.partial(up_kernel, 0, 1, 0), [small], [own, arrived, zero], step_flops)
     first = load(sections, 1, 3, EARLY, [sent])
     other = over(sent)
     (sent,) = call(join_kernel, [double], [sent, other], 0, after=[first])
@@ -515,6 +535,7 @@
         if level == 2:
             f, _ = weights(level + 1)
             ended = f
+        if level == 3:
             (near,) = call(
                 functools.partial(leaves_kernel, leaf, False),
                 [((rows, unknowns), F32)],
@@ -528,9 +549,9 @@
             ended = [got["a"]]
         if level == row_bits + 1:
             got["b"] = beyond(pieces[1], "px", row_count)
-            ended = [got["b"]]
-            got["c"] = swapped(pieces[2], "py", col_count)
             got["d"] = beyond(pieces[3], "py", col_count)
+        if level == row_bits:
+            got["c"] = arrived
         f, at = weights(level)
         (own,) = call(
             functools.partial(own_kernel, at, False),
@@ -540,16 +561,17 @@
             after=after,
         )
         last = level == levels - 1
+        extra = [pieces[2]] if level == row_bits - 1 else []
         outs = call(
-            functools.partial(up_kernel, at, 2),
-            [small, small] if last else [double],
-            [own, arrived] + f,
+            functools.partial(up_kernel, at, 2, len(extra)),
+            [small, small] if last else [triple if extra else double],
+            [own, arrived] + f + extra,
             2 * step_flops,
             after=ended,
         )
         sent = outs[0]
     mine, other = outs
-    other = back(other)
+    other = over(other)
     (near,) = call(
         functools.partial(sides_kernel, leaf),
         [((rows, unknowns), F32)],
@@ -600,8 +622,6 @@
                 after=[message],
             )
             after = [v_high, v_low, vv]
-            got["c"] = swapped(terms[2], "py", col_count)
-            ended = [got["c"]]
         if level == 3:
             got["d"] = beyond(terms[3], "py", col_count)
             ended = [got["d"]]
@@ -611,6 +631,8 @@
         if level == 1:
             after = [squeeze]
             got["b"] = beyond(terms[1], "px", row_count)
+        if level == row_bits:
+            got["c"] = arrived
         f, at = weights(level)
         (own,) = call(
             functools.partial(own_kernel, at, True),
@@ -621,10 +643,11 @@
         )
         if level > 1:
             f, at = weights(level - 1)
+            extra = [terms[2]] if level == row_bits + 1 else []
             g, message = call(
                 functools.partial(down_kernel, at),
-                [double, double],
-                [own, arrived] + f,
+                [double, triple if extra else double],
+                [own, arrived] + f + extra,
                 2 * step_flops,
                 after=ended,
             )
@@ -632,7 +655,7 @@
     mine, other = call(
         last_kernel, [small, small], [own, arrived] + f, 4 * step_flops
     )
-    other = back(other)
+    other = over(other)
     (z_near,) = call(
         functools.partial(gather_kernel, leaf),
         [((rows, unknowns), F32)],

time: 165 us -> 130 us (0.79)
  starting transfers between devices: 93.8 us -> 34.6 us
  waiting for transfers between devices: 20.4 us -> 45.7 us
    ppermute x6 -> x9, starting transfers between devices: 39.1 us -> 3.49 us  [swapped(): return lax.ppermute(x, axis, [(i, i ^ 1) for i in range(count)])]
    ppermute x14, waiting for transfers between devices: 0.04 us -> 23.9 us  [partner(): return lax.ppermute(x, ('px', 'py'), pairs)]
    ppermute x4, starting transfers between devices: 25 us -> 4.92 us  [beyond(): return lax.ppermute(x, axis, pairs + [(j, i) for i, j in pairs])]
    ppermute x14, starting transfers between devices: 9.57 us -> 22.2 us  [partner(): return lax.ppermute(x, ('px', 'py'), pairs)]
    ppermute x5 -> x0, starting transfers between devices: 10.9 us -> none  [the longest x3 8.14 us: over(): return lax.ppermute(x, 'px', [(i, i + 1) for i in range(0, row_count, 2)])]
    ppermute x5 -> x0, waiting for transfers between devices: 7.62 us -> none  [the longest x2 6.77 us: back(): return lax.ppermute(x, 'px', [(i + 1, i) for i in range(0, row_count, 2)])]
    ppermute x4, waiting for transfers between devices: 1.38 us -> 7.04 us  [beyond(): return lax.ppermute(x, axis, pairs + [(j, i) for i, j in pairs])]
    all_to_all x1, starting transfers between devices: 9.28 us -> 4.03 us  [per_device(): part = lax.all_to_all(part, 'py', 0, 0, tiled=True)]
  transfers between devices with their start and end apart: 30 -> 28, of which waited for: 10 -> 22; matrix products, arithmetic and copies ran while one was open for 0% -> 0% of each run, Pallas kernels for 13% -> 16%
where the time goes in v5:
time: 130 us
  waiting for transfers between devices  45.7 us (35%)
  starting transfers between devices  34.6 us (27%)
  Pallas kernels  33.1 us (25%)
  blocking collectives  14.6 us (11%)
    pallas_call x45, Pallas kernels, call(): pl.pallas_call(body, out_shape=[jax.ShapeDtypeStruct(s, d) for s, d in ou...  24.1 us
    ppermute x14, waiting for transfers between devices, partner(): return lax.ppermute(x, ('px', 'py'), pairs)  23.9 us
    ppermute x14, starting transfers between devices, partner(): return lax.ppermute(x, ('px', 'py'), pairs)  22.2 us
    all_to_all x1, blocking collectives, per_device(): lax.all_to_all(part, 'px', 0, 0, axis_index_groups=groups, tiled=True)  14.6 us
    all_to_all x1, waiting for transfers between devices, per_device(): part = lax.all_to_all(part, 'py', 0, 0, tiled=True)  7.8 us
    ppermute x4, waiting for transfers between devices, beyond(): return lax.ppermute(x, axis, pairs + [(j, i) for i, j in pairs])  7.04 us
    ppermute x9, waiting for transfers between devices, swapped(): return lax.ppermute(x, axis, [(i, i ^ 1) for i in range(count)])  7.03 us
    pallas_call x6, Pallas kernels, load(): pl.pallas_call(functools.partial(load_kernel, begin), in_specs=[pl.BlockS...  6.53 us
  transfers between devices with their start and end apart: 28, of which 22 were waited for; matrix products, arithmetic and copies ran while one was open for 0% of the time, Pallas kernels for 16%

profile of v5, /device:TPU:8, one launch (start us, length us, event | category | flops | bytes accessed | tf_op | source)
XLA Modules:
  0.0 129.8 jit_solution(5877990538325593232)
XLA Ops:
  0.7 2.5 %shard_map.86 = (bf16[64,2048]{1,0:T(8,128)(2,1)S(1)}, bf16[64,256]{1,0:T(8,128)(2,1)S(1)}) custom-call(f32[32,32,128]{2,1,0:T(8,128)} %bitcast.40, bf16[2,2048,256]{2,1,0:T(8,128)(2,1)} %bitcast.33), custom_call_target="tpu_custom_call" | custom-call | flops 134217728 | bytes 2621440 | tf_op jit(solution)/shard_map/pallas_call | solution.py:105
  3.8 1.0 shard_map.87.refs_1_.refs_2_
  5.0 2.9 %collective-permute-done.refs_1_ = bf16[64,256]{1,0:T(8,128)(2,1)S(1)} collective-permute-done((bf16[64,256]{1,0:T(8,128)(2,1)S(1)}, bf16[64,256]{1,0:T(8,128)(2,1)S(1)}, u32[]{:S(2)}, u32[]{:S(2)}) %collective-permute-start) | collective-permute-done | bytes 32800 | tf_op jit(solution)/shard_map/ppermute | solution.py:488
  8.3 1.2 shard_map.90.refs_2_.refs_1_
  9.6 2.3 %collective-permute-start.3 = (bf16[128,256]{1,0:T(8,128)(2,1)S(1)}, bf16[128,256]{1,0:T(8,128)(2,1)S(1)}, u32[]{:S(2)}, u32[]{:S(2)}) collective-permute-start(bf16[128,256]{1,0:T(8,128)(2,1)S(1)} %shard_map.91.rest_0_.refs_2_.refs_0_), channel_id=1, source_target_pairs={{0,16},{1,17},{2,18},{3,19},{4,20},{5,21},{6,22},{7,23},{8,24},{9,... | collective-permute-start | bytes 196616 | tf_op jit(solution)/shard_map/ppermute | solution.py:485
  13.0 1.2 shard_map.92.refs_2_.refs_3_
  14.7 1.8 %collective-permute-start.4 = (bf16[128,256]{1,0:T(8,128)(2,1)S(1)}, bf16[128,256]{1,0:T(8,128)(2,1)S(1)}, u32[]{:S(2)}, u32[]{:S(2)}) collective-permute-start(bf16[128,256]{1,0:T(8,128)(2,1)S(1)} %shard_map.95.refs_0_.rest_0_), channel_id=1, source_target_pairs={{0,16},{1,17},{2,18},{3,19},{4,20},{5,21},{6,22},{7,23},{8,40},{9,... | collective-permute-start | bytes 196616 | tf_op jit(solution)/shard_map/ppermute | solution.py:485
  16.7 1.8 %shard_map.98.refs_5_.refs_2_.refs_3_ = bf16[5,2,2,256,256]{4,3,2,1,0:T(8,128)(2,1)S(1)} custom-call(bf16[8,2,2,256,256]{4,3,2,1,0:T(8,128)(2,1)} %collective-permute-done.2.f_in, bf16[128,256]{1,0:T(8,128)(2,1)S(1)} %shard_map.95.refs_0_.rest_0_), custom_call_target="tpu_custom_call" | custom-call | bytes 2621440 | tf_op jit(solution)/shard_map/pallas_call | solution.py:137
  18.7 0.9 collective-permute-done.4.refs_1_
  19.8 1.3 %collective-permute-start.5 = (bf16[128,256]{1,0:T(8,128)(2,1)S(1)}, bf16[128,256]{1,0:T(8,128)(2,1)S(1)}, u32[]{:S(2)}, u32[]{:S(2)}) collective-permute-start(bf16[128,256]{1,0:T(8,128)(2,1)S(1)} %shard_map.99.refs_2_.refs_0_), channel_id=1, source_target_pairs={{0,16},{1,17},{2,18},{3,19},{4,20},{5,21},{6,22},{7,23},{8,72},{9,... | collective-permute-start | bytes 196616 | tf_op jit(solution)/shard_map/ppermute | solution.py:485
  22.3 1.8 %collective-permute-done.5.refs_1_ = bf16[128,256]{1,0:T(8,128)(2,1)S(1)} collective-permute-done((bf16[128,256]{1,0:T(8,128)(2,1)S(1)}, bf16[128,256]{1,0:T(8,128)(2,1)S(1)}, u32[]{:S(2)}, u32[]{:S(2)}) %collective-permute-start.5) | collective-permute-done | bytes 65568 | tf_op jit(solution)/shard_map/ppermute | solution.py:485
  24.4 1.3 %collective-permute-start.7 = (bf16[128,256]{1,0:T(8,128)(2,1)S(1)}, bf16[128,256]{1,0:T(8,128)(2,1)S(1)}, u32[]{:S(2)}, u32[]{:S(2)}) collective-permute-start(bf16[128,256]{1,0:T(8,128)(2,1)S(1)} %shard_map.102.refs_0_), channel_id=1, source_target_pairs={{0,16},{1,17},{2,18},{3,19},{4,20},{5,21},{6,22},{7,23},{8,136},{9... | collective-permute-start | bytes 196616 | tf_op jit(solution)/shard_map/ppermute | solution.py:485
  25.9 2.8 %collective-permute-done.7.refs_1_ = bf16[128,256]{1,0:T(8,128)(2,1)S(1)} collective-permute-done((bf16[128,256]{1,0:T(8,128)(2,1)S(1)}, bf16[128,256]{1,0:T(8,128)(2,1)S(1)}, u32[]{:S(2)}, u32[]{:S(2)}) %collective-permute-start.7) | collective-permute-done | bytes 65568 | tf_op jit(solution)/shard_map/ppermute | solution.py:485
  28.9 1.5 %collective-permute-start.8 = (bf16[192,256]{1,0:T(8,128)(2,1)S(1)}, bf16[192,256]{1,0:T(8,128)(2,1)S(1)}, u32[]{:S(2)}, u32[]{:S(2)}) collective-permute-start(bf16[192,256]{1,0:T(8,128)(2,1)S(1)} %shard_map.104.refs_0_), channel_id=1, source_target_pairs={{0,1},{1,0},{2,3},{3,2},{4,5},{5,4},{6,7},{7,6},{8,9},{9,8},{10,11... | collective-permute-start | bytes 294920 | tf_op jit(solution)/shard_map/ppermute | solution.py:485
  30.6 3.2 %collective-permute-done.8.refs_1_.refs_4_ = bf16[192,256]{1,0:T(8,128)(2,1)S(1)} collective-permute-done((bf16[192,256]{1,0:T(8,128)(2,1)S(1)}, bf16[192,256]{1,0:T(8,128)(2,1)S(1)}, u32[]{:S(2)}, u32[]{:S(2)}) %collective-permute-start.8) | collective-permute-done | bytes 98336 | tf_op jit(solution)/shard_map/ppermute | solution.py:485
  34.0 1.2 collective-permute-start.9
  35.4 3.0 %collective-permute-done.9.refs_1_ = bf16[128,256]{1,0:T(8,128)(2,1)S(1)} collective-permute-done((bf16[128,256]{1,0:T(8,128)(2,1)S(1)}, bf16[128,256]{1,0:T(8,128)(2,1)S(1)}, u32[]{:S(2)}, u32[]{:S(2)}) %collective-permute-start.9) | collective-permute-done | bytes 65568 | tf_op jit(solution)/shard_map/ppermute | solution.py:485
  38.6 1.2 collective-permute-start.10
  39.7 3.7 %collective-permute-start.12 = (bf16[64,256]{1,0:T(8,128)(2,1)S(1)}, bf16[64,256]{1,0:T(8,128)(2,1)S(1)}, u32[]{:S(2)}, u32[]{:S(2)}) collective-permute-start(bf16[64,256]{1,0:T(8,128)(2,1)S(1)} %get-tuple-element.42.refs_4_), channel_id=1, source_target_pairs={{8,16},{24,32},{40,48},{56,64},{72,80},{88,96},{104,112},{120,128}... | collective-permute-start | bytes 98312 | tf_op jit(solution)/shard_map/ppermute | solution.py:495
  43.5 0.7 collective-permute-start.13
  44.7 2.0 %collective-permute-start.11 = (bf16[64,256]{1,0:T(8,128)(2,1)S(1)}, bf16[64,256]{1,0:T(8,128)(2,1)S(1)}, u32[]{:S(2)}, u32[]{:S(2)}) collective-permute-start(bf16[64,256]{1,0:T(8,128)(2,1)S(1)} %get-tuple-element.46), channel_id=1, source_target_pairs={{0,8},{8,0},{16,24},{24,16},{32,40},{40,32},{48,56},{56,48},{64,72... | collective-permute-start | bytes 98312 | tf_op jit(solution)/shard_map/ppermute | solution.py:488
  46.6 1.9 %collective-permute-done.13.refs_5_ = bf16[64,256]{1,0:T(8,128)(2,1)S(1)} collective-permute-done((bf16[64,256]{1,0:T(8,128)(2,1)S(1)}, bf16[64,256]{1,0:T(8,128)(2,1)S(1)}, u32[]{:S(2)}, u32[]{:S(2)}) %collective-permute-start.13) | collective-permute-done | bytes 32800 | tf_op jit(solution)/shard_map/ppermute | solution.py:495
  48.6 1.3 shard_map.111.refs_3_
  50.0 1.7 %shard_map.112 = (f32[64,2048]{1,0:T(8,128)S(1)}, bf16[64,2048]{1,0:T(8,128)(2,1)S(1)}, bf16[64,256]{1,0:T(8,128)(2,1)S(1)}) custom-call(s32[17]{0:T(128)S(1)} %concatenate.3.refs_0_, bf16[64,256]{1,0:T(8,128)(2,1)S(1)} %get-tuple-element.45.refs_7_.refs_1_.rest_0_, bf16[64,256]{1,0:T(8,128)(2,1)S(1)} %collective-permute-done.11.refs_2_, ...), custom_call_target="tpu_custom_call" | custom-call | flops 268435456 | bytes 2687044 | tf_op jit(solution)/shard_map/pallas_call | solution.py:28
  52.0 1.2 collective-permute-done.14.refs_1_
  53.5 5.0 %collective-permute-start.15 = (bf16[128,256]{1,0:T(8,128)(2,1)S(1)}, bf16[128,256]{1,0:T(8,128)(2,1)S(1)}, u32[]{:S(2)}, u32[]{:S(2)}) collective-permute-start(bf16[128,256]{1,0:T(8,128)(2,1)S(1)} %get-tuple-element.55), channel_id=1, source_target_pairs={{0,16},{1,17},{2,18},{3,19},{4,20},{5,21},{6,22},{7,23},{8,12},{9,... | collective-permute-start | bytes 196616 | tf_op jit(solution)/shard_map/ppermute | solution.py:485
  58.5 1.0 shard_map.115
  59.7 1.0 collective-permute-done.15.refs_1_
  61.0 2.1 %collective-permute-start.18 = (bf16[128,256]{1,0:T(8,128)(2,1)S(1)}, bf16[128,256]{1,0:T(8,128)(2,1)S(1)}, u32[]{:S(2)}, u32[]{:S(2)}) collective-permute-start(bf16[128,256]{1,0:T(8,128)(2,1)S(1)} %get-tuple-element.56.refs_2_), channel_id=1, source_target_pairs={{0,16},{1,17},{2,18},{3,19},{4,20},{5,21},{6,22},{7,23},{8,10},{9,... | collective-permute-start | bytes 196616 | tf_op jit(solution)/shard_map/ppermute | solution.py:485
  63.1 0.8 shard_map.118.refs_3_.refs_1_
  64.2 1.2 collective-permute-done.18.refs_1_
  66.0 4.8 %collective-permute-done.19.refs_4_.refs_1_ = bf16[192,256]{1,0:T(8,128)(2,1)S(1)} collective-permute-done((bf16[192,256]{1,0:T(8,128)(2,1)S(1)}, bf16[192,256]{1,0:T(8,128)(2,1)S(1)}, u32[]{:S(2)}, u32[]{:S(2)}) %collective-permute-start.19) | collective-permute-done | bytes 98336 | tf_op jit(solution)/shard_map/ppermute | solution.py:485
  71.2 1.6 %collective-permute-start.21 = (bf16[128,256]{1,0:T(8,128)(2,1)S(1)}, bf16[128,256]{1,0:T(8,128)(2,1)S(1)}, u32[]{:S(2)}, u32[]{:S(2)}) collective-permute-start(bf16[128,256]{1,0:T(8,128)(2,1)S(1)} %get-tuple-element.61.refs_1_), channel_id=1, source_target_pairs={{0,16},{1,17},{2,18},{3,19},{4,20},{5,21},{6,22},{7,23},{8,136},{9... | collective-permute-start | bytes 196616 | tf_op jit(solution)/shard_map/ppermute | solution.py:485
  72.7 1.7 %shard_map.124 = (bf16[64,2048]{1,0:T(8,128)(2,1)S(1)}, bf16[64,2048]{1,0:T(8,128)(2,1)S(1)}, f32[32,32]{1,0:T(8,128)S(1)}) custom-call(f32[32,32,128]{2,1,0:T(8,128)S(1)} %bitcast.41, bf16[128,256]{1,0:T(8,128)(2,1)S(1)} %get-tuple-element.61.refs_1_), custom_call_target="tpu_custom_call" | custom-call | flops 67108864 | bytes 524288 | tf_op jit(solution)/shard_map/pallas_call | solution.py:28
  74.8 0.7 collective-permute-done.21.refs_1_
  75.8 1.6 %collective-permute-start.22 = (bf16[128,256]{1,0:T(8,128)(2,1)S(1)}, bf16[128,256]{1,0:T(8,128)(2,1)S(1)}, u32[]{:S(2)}, u32[]{:S(2)}) collective-permute-start(bf16[128,256]{1,0:T(8,128)(2,1)S(1)} %get-tuple-element.66), channel_id=1, source_target_pairs={{0,16},{1,17},{2,18},{3,19},{4,20},{5,21},{6,22},{7,23},{8,72},{9,... | collective-permute-start | bytes 196616 | tf_op jit(solution)/shard_map/ppermute | solution.py:485
  77.6 4.8 %collective-permute-done.20.refs_5_.refs_4_ = bf16[64,256]{1,0:T(8,128)(2,1)S(1)} collective-permute-done((bf16[64,256]{1,0:T(8,128)(2,1)S(1)}, bf16[64,256]{1,0:T(8,128)(2,1)S(1)}, u32[]{:S(2)}, u32[]{:S(2)}) %collective-permute-start.20) | collective-permute-done | bytes 32800 | tf_op jit(solution)/shard_map/ppermute | solution.py:495
  83.7 0.9 collective-permute-done.16.refs_2_.refs_4_
  84.6 2.5 %collective-permute-done.23.refs_1_ = bf16[128,256]{1,0:T(8,128)(2,1)S(1)} collective-permute-done((bf16[128,256]{1,0:T(8,128)(2,1)S(1)}, bf16[128,256]{1,0:T(8,128)(2,1)S(1)}, u32[]{:S(2)}, u32[]{:S(2)}) %collective-permute-start.23) | collective-permute-done | bytes 65568 | tf_op jit(solution)/shard_map/ppermute | solution.py:485
  88.0 1.1 shard_map.132.refs_3_
  89.9 1.9 %collective-permute-done.24.refs_1_ = bf16[128,256]{1,0:T(8,128)(2,1)S(1)} collective-permute-done((bf16[128,256]{1,0:T(8,128)(2,1)S(1)}, bf16[128,256]{1,0:T(8,128)(2,1)S(1)}, u32[]{:S(2)}, u32[]{:S(2)}) %collective-permute-start.24) | collective-permute-done | bytes 65568 | tf_op jit(solution)/shard_map/ppermute | solution.py:485
  93.5 2.1 %shard_map.134 = (bf16[64,2048]{1,0:T(8,128)(2,1)S(1)}, bf16[64,2048]{1,0:T(8,128)(2,1)S(1)}, f32[32,128]{1,0:T(8,128)S(1)}) custom-call(s32[17]{0:T(128)S(1)} %concatenate.3.refs_0_, f32[64,2048]{1,0:T(8,128)S(1)} %shard_map.121.refs_1_, bf16[64,256]{1,0:T(8,128)(2,1)S(1)} %get-tuple-element.71.refs_2_, ...), custom_call_target="tpu_custom_call" | custom-call | flops 134217728 | bytes 3215428 | tf_op jit(solution)/shard_map/pallas_call | solution.py:28
  95.9 1.0 collective-permute-done.26.refs_1_
  97.0 14.6 %all_to_all.10.refs_0_ = f32[16,32,128]{2,1,0:T(8,128)S(1)} all-to-all(f32[16,32,128]{2,1,0:T(8,128)S(1)} %shard_map.135), channel_id=1, replica_groups={{0,16,32,48,64,80,96,112,128,144,160,176,192,208,224,240},{8,24,40,56,7..., dimensions={0} | all-to-all | bytes 524288 | tf_op jit(solution)/shard_map/all_to_all | solution.py:680
  112.2 4.0 %all-to-all-start.1 = ((f32[8,32,128]{2,1,0:T(8,128)}), f32[8,32,128]{2,1,0:T(8,128)S(1)}, u32[]{:S(2)}, u32[]{:S(2)}) async-start(f32[8,32,128]{2,1,0:T(8,128)} %shard_map.136), calls=%async_computation.1 | async-start | bytes 262144 | tf_op jit(solution)/shard_map/all_to_all | solution.py:682
  116.2 1.3 shard_map.113
  117.5 7.8 %all-to-all-done.1.refs_0_ = f32[8,32,128]{2,1,0:T(8,128)S(1)} async-done(((f32[8,32,128]{2,1,0:T(8,128)}), f32[8,32,128]{2,1,0:T(8,128)S(1)}, u32[]{:S(2)}, u32[]{:S(2)}) %all-to-all-start.1) | async-done | bytes 131104 | tf_op jit(solution)/shard_map/all_to_all | solution.py:682
  125.3 4.3 %shard_map.137 = f32[64,32,128]{2,1,0:T(8,128)} custom-call(f32[8,32,128]{2,1,0:T(8,128)S(1)} %all-to-all-done.1.refs_0_, bf16[64,2048]{1,0:T(8,128)(2,1)S(1)} %get-tuple-element.74.refs_1_, bf16[64,2048]{1,0:T(8,128)(2,1)S(1)} %get-tuple-element.75.refs_2_, bf16[64,2048]{1,0:T(8,128)(2,1)S(1)} %get-tuple-element.62.refs_3_.refs_5_, ...), custom_call_target="tpu_custom_call" | custom-call | flops 67108864 | bytes 1179648 | tf_op jit(solution)/shard_map/pallas_call | solution.py:28
  (80 shorter events, 15.2 us)
Async XLA Ops:
  0.6 11.4 %copy-start = (s32[32,8,4,2]{0,3,2,1:T(2,128)S(1)}, s32[32,8,4,2]{0,3,2,1:T(2,128)}, u32[]{:S(2)}) copy-start(s32[32,8,4,2]{0,3,2,1:T(2,128)} %param.8) | copy-start | bytes 24580
  0.6 12.3 %collective-permute-start.2 = (bf16[8,2,2,256,256]{4,3,2,1,0:T(8,128)(2,1)}, bf16[8,2,2,256,256]{4,3,2,1,0:T(8,128)(2,1)}, u32[]{:S(2)}, u32[]{:S(2)}) collective-permute-start(bf16[8,2,2,256,256]{4,3,2,1,0:T(8,128)(2,1)} %bitcast.29), channel_id=1, source_target_pairs={{0,8},{8,0},{16,24},{24,16},{32,40},{40,32},{48,56},{56,48},{64,72... | collective-permute-start | bytes 12582920 | tf_op jit(solution)/shard_map/ppermute | solution.py:488
  3.2 4.7 %collective-permute-start = (bf16[64,256]{1,0:T(8,128)(2,1)S(1)}, bf16[64,256]{1,0:T(8,128)(2,1)S(1)}, u32[]{:S(2)}, u32[]{:S(2)}) collective-permute-start(bf16[64,256]{1,0:T(8,128)(2,1)S(1)} %get-tuple-element.39.rest_0_.refs_0_), channel_id=1, source_target_pairs={{0,8},{8,0},{16,24},{24,16},{32,40},{40,32},{48,56},{56,48},{64,72... | collective-permute-start | bytes 98312 | tf_op jit(solution)/shard_map/ppermute | solution.py:488
  8.1 1.5 %collective-permute-start.1 = (bf16[64,256]{1,0:T(8,128)(2,1)S(1)}, bf16[64,256]{1,0:T(8,128)(2,1)S(1)}, u32[]{:S(2)}, u32[]{:S(2)}) collective-permute-start(bf16[64,256]{1,0:T(8,128)(2,1)S(1)} %shard_map.89.rest_0_.refs_0_), channel_id=1, source_target_pairs={{0,8},{8,0},{16,24},{24,16},{32,40},{40,32},{48,56},{56,48},{64,72... | collective-permute-start | bytes 98312 | tf_op jit(solution)/shard_map/ppermute | solution.py:488
  9.6 4.9 %collective-permute-start.3 = (bf16[128,256]{1,0:T(8,128)(2,1)S(1)}, bf16[128,256]{1,0:T(8,128)(2,1)S(1)}, u32[]{:S(2)}, u32[]{:S(2)}) collective-permute-start(bf16[128,256]{1,0:T(8,128)(2,1)S(1)} %shard_map.91.rest_0_.refs_2_.refs_0_), channel_id=1, source_target_pairs={{0,16},{1,17},{2,18},{3,19},{4,20},{5,21},{6,22},{7,23},{8,24},{9,... | collective-permute-start | bytes 196616 | tf_op jit(solution)/shard_map/ppermute | solution.py:485
  14.2 2.3 %copy-start.1 = (bf16[1,1,8,2,2,256,256]{6,5,4,3,2,1,0:T(8,128)(2,1)S(1)}, bf16[1,1,8,2,2,256,256]{6,5,4,3,2,1,0:T(8,128)(2,1)}, u32[]{:S(2)}) copy-start(bf16[1,1,8,2,2,256,256]{6,5,4,3,2,1,0:T(8,128)(2,1)} %param.13) | copy-start | bytes 12582916
  14.7 4.9 %collective-permute-start.4 = (bf16[128,256]{1,0:T(8,128)(2,1)S(1)}, bf16[128,256]{1,0:T(8,128)(2,1)S(1)}, u32[]{:S(2)}, u32[]{:S(2)}) collective-permute-start(bf16[128,256]{1,0:T(8,128)(2,1)S(1)} %shard_map.95.refs_0_.rest_0_), channel_id=1, source_target_pairs={{0,16},{1,17},{2,18},{3,19},{4,20},{5,21},{6,22},{7,23},{8,40},{9,... | collective-permute-start | bytes 196616 | tf_op jit(solution)/shard_map/ppermute | solution.py:485
  18.7 2.4 %copy-start.4 = (bf16[1,1,2,16,128,128]{5,4,3,2,1,0:T(8,128)(2,1)S(1)}, bf16[1,1,2,16,128,128]{5,4,3,2,1,0:T(8,128)(2,1)}, u32[]{:S(2)}) copy-start(bf16[1,1,2,16,128,128]{5,4,3,2,1,0:T(8,128)(2,1)} %param.9) | copy-start | bytes 3145732
  19.8 4.4 %collective-permute-start.5 = (bf16[128,256]{1,0:T(8,128)(2,1)S(1)}, bf16[128,256]{1,0:T(8,128)(2,1)S(1)}, u32[]{:S(2)}, u32[]{:S(2)}) collective-permute-start(bf16[128,256]{1,0:T(8,128)(2,1)S(1)} %shard_map.99.refs_2_.refs_0_), channel_id=1, source_target_pairs={{0,16},{1,17},{2,18},{3,19},{4,20},{5,21},{6,22},{7,23},{8,72},{9,... | collective-permute-start | bytes 196616 | tf_op jit(solution)/shard_map/ppermute | solution.py:485
  21.1 1.2 collective-permute-start.6
  24.4 4.4 %collective-permute-start.7 = (bf16[128,256]{1,0:T(8,128)(2,1)S(1)}, bf16[128,256]{1,0:T(8,128)(2,1)S(1)}, u32[]{:S(2)}, u32[]{:S(2)}) collective-permute-start(bf16[128,256]{1,0:T(8,128)(2,1)S(1)} %shard_map.102.refs_0_), channel_id=1, source_target_pairs={{0,16},{1,17},{2,18},{3,19},{4,20},{5,21},{6,22},{7,23},{8,136},{9... | collective-permute-start | bytes 196616 | tf_op jit(solution)/shard_map/ppermute | solution.py:485
  28.9 4.9 %collective-permute-start.8 = (bf16[192,256]{1,0:T(8,128)(2,1)S(1)}, bf16[192,256]{1,0:T(8,128)(2,1)S(1)}, u32[]{:S(2)}, u32[]{:S(2)}) collective-permute-start(bf16[192,256]{1,0:T(8,128)(2,1)S(1)} %shard_map.104.refs_0_), channel_id=1, source_target_pairs={{0,1},{1,0},{2,3},{3,2},{4,5},{5,4},{6,7},{7,6},{8,9},{9,8},{10,11... | collective-permute-start | bytes 294920 | tf_op jit(solution)/shard_map/ppermute | solution.py:485
  34.0 4.4 %collective-permute-start.9 = (bf16[128,256]{1,0:T(8,128)(2,1)S(1)}, bf16[128,256]{1,0:T(8,128)(2,1)S(1)}, u32[]{:S(2)}, u32[]{:S(2)}) collective-permute-start(bf16[128,256]{1,0:T(8,128)(2,1)S(1)} %shard_map.106.refs_0_), channel_id=1, source_target_pairs={{0,16},{1,17},{2,18},{3,19},{4,20},{5,21},{6,22},{7,23},{8,10},{9,... | collective-permute-start | bytes 196616 | tf_op jit(solution)/shard_map/ppermute | solution.py:485
  38.6 5.9 %collective-permute-start.10 = (bf16[128,256]{1,0:T(8,128)(2,1)S(1)}, bf16[128,256]{1,0:T(8,128)(2,1)S(1)}, u32[]{:S(2)}, u32[]{:S(2)}) collective-permute-start(bf16[128,256]{1,0:T(8,128)(2,1)S(1)} %shard_map.108.refs_0_), channel_id=1, source_target_pairs={{0,16},{1,17},{2,18},{3,19},{4,20},{5,21},{6,22},{7,23},{8,12},{9,... | collective-permute-start | bytes 196616 | tf_op jit(solution)/shard_map/ppermute | solution.py:485
  39.7 6.9 %collective-permute-start.12 = (bf16[64,256]{1,0:T(8,128)(2,1)S(1)}, bf16[64,256]{1,0:T(8,128)(2,1)S(1)}, u32[]{:S(2)}, u32[]{:S(2)}) collective-permute-start(bf16[64,256]{1,0:T(8,128)(2,1)S(1)} %get-tuple-element.42.refs_4_), channel_id=1, source_target_pairs={{8,16},{24,32},{40,48},{56,64},{72,80},{88,96},{104,112},{120,128}... | collective-permute-start | bytes 98312 | tf_op jit(solution)/shard_map/ppermute | solution.py:495
  43.5 5.1 %collective-permute-start.13 = (bf16[64,256]{1,0:T(8,128)(2,1)S(1)}, bf16[64,256]{1,0:T(8,128)(2,1)S(1)}, u32[]{:S(2)}, u32[]{:S(2)}) collective-permute-start(bf16[64,256]{1,0:T(8,128)(2,1)S(1)} %get-tuple-element.44.refs_6_), channel_id=1, source_target_pairs={{1,2},{3,4},{5,6},{7,0},{2,1},{4,3},{6,5},{0,7},{9,10},{11,12},{13... | collective-permute-start | bytes 98312 | tf_op jit(solution)/shard_map/ppermute | solution.py:495
  44.4 4.2 %copy-start.3 = (bf16[1,1,4,2,256,256]{5,4,3,2,1,0:T(8,128)(2,1)S(1)}, bf16[1,1,4,2,256,256]{5,4,3,2,1,0:T(8,128)(2,1)}, u32[]{:S(2)}) copy-start(bf16[1,1,4,2,256,256]{5,4,3,2,1,0:T(8,128)(2,1)} %param.10) | copy-start | bytes 3145732
  44.4 5.6 %copy-start.6 = (bf16[1,1,2,256,2048]{4,3,2,1,0:T(8,128)(2,1)S(1)}, bf16[1,1,2,256,2048]{4,3,2,1,0:T(8,128)(2,1)}, u32[]{:S(2)}) copy-start(bf16[1,1,2,256,2048]{4,3,2,1,0:T(8,128)(2,1)} %param.12) | copy-start | bytes 6291460
  44.7 5.3 %collective-permute-start.11 = (bf16[64,256]{1,0:T(8,128)(2,1)S(1)}, bf16[64,256]{1,0:T(8,128)(2,1)S(1)}, u32[]{:S(2)}, u32[]{:S(2)}) collective-permute-start(bf16[64,256]{1,0:T(8,128)(2,1)S(1)} %get-tuple-element.46), channel_id=1, source_target_pairs={{0,8},{8,0},{16,24},{24,16},{32,40},{40,32},{48,56},{56,48},{64,72... | collective-permute-start | bytes 98312 | tf_op jit(solution)/shard_map/ppermute | solution.py:488
  51.7 1.5 %collective-permute-start.14 = (bf16[64,256]{1,0:T(8,128)(2,1)S(1)}, bf16[64,256]{1,0:T(8,128)(2,1)S(1)}, u32[]{:S(2)}, u32[]{:S(2)}) collective-permute-start(bf16[64,256]{1,0:T(8,128)(2,1)S(1)} %get-tuple-element.49.refs_0_), channel_id=1, source_target_pairs={{0,8},{8,0},{16,24},{24,16},{32,40},{40,32},{48,56},{56,48},{64,72... | collective-permute-start | bytes 98312 | tf_op jit(solution)/shard_map/ppermute | solution.py:488
  53.5 7.3 %collective-permute-start.15 = (bf16[128,256]{1,0:T(8,128)(2,1)S(1)}, bf16[128,256]{1,0:T(8,128)(2,1)S(1)}, u32[]{:S(2)}, u32[]{:S(2)}) collective-permute-start(bf16[128,256]{1,0:T(8,128)(2,1)S(1)} %get-tuple-element.55), channel_id=1, source_target_pairs={{0,16},{1,17},{2,18},{3,19},{4,20},{5,21},{6,22},{7,23},{8,12},{9,... | collective-permute-start | bytes 196616 | tf_op jit(solution)/shard_map/ppermute | solution.py:485
  61.0 4.4 %collective-permute-start.18 = (bf16[128,256]{1,0:T(8,128)(2,1)S(1)}, bf16[128,256]{1,0:T(8,128)(2,1)S(1)}, u32[]{:S(2)}, u32[]{:S(2)}) collective-permute-start(bf16[128,256]{1,0:T(8,128)(2,1)S(1)} %get-tuple-element.56.refs_2_), channel_id=1, source_target_pairs={{0,16},{1,17},{2,18},{3,19},{4,20},{5,21},{6,22},{7,23},{8,10},{9,... | collective-permute-start | bytes 196616 | tf_op jit(solution)/shard_map/ppermute | solution.py:485
  65.6 5.2 %collective-permute-start.19 = (bf16[192,256]{1,0:T(8,128)(2,1)S(1)}, bf16[192,256]{1,0:T(8,128)(2,1)S(1)}, u32[]{:S(2)}, u32[]{:S(2)}) collective-permute-start(bf16[192,256]{1,0:T(8,128)(2,1)S(1)} %get-tuple-element.58), channel_id=1, source_target_pairs={{0,1},{1,0},{2,3},{3,2},{4,5},{5,4},{6,7},{7,6},{8,9},{9,8},{10,11... | collective-permute-start | bytes 294920 | tf_op jit(solution)/shard_map/ppermute | solution.py:485
  66.0 6.7 %copy-start.5 = (f32[32,1,1,2,2048]{4,3,2,1,0:T(2,128)S(1)}, f32[32,1,1,2,2048]{4,3,2,1,0:T(2,128)}, u32[]{:S(2)}) copy-start(f32[32,1,1,2,2048]{4,3,2,1,0:T(2,128)} %param.7) | copy-start | bytes 1572868
  71.2 4.4 %collective-permute-start.21 = (bf16[128,256]{1,0:T(8,128)(2,1)S(1)}, bf16[128,256]{1,0:T(8,128)(2,1)S(1)}, u32[]{:S(2)}, u32[]{:S(2)}) collective-permute-start(bf16[128,256]{1,0:T(8,128)(2,1)S(1)} %get-tuple-element.61.refs_1_), channel_id=1, source_target_pairs={{0,16},{1,17},{2,18},{3,19},{4,20},{5,21},{6,22},{7,23},{8,136},{9... | collective-permute-start | bytes 196616 | tf_op jit(solution)/shard_map/ppermute | solution.py:485
  75.8 6.7 %collective-permute-start.22 = (bf16[128,256]{1,0:T(8,128)(2,1)S(1)}, bf16[128,256]{1,0:T(8,128)(2,1)S(1)}, u32[]{:S(2)}, u32[]{:S(2)}) collective-permute-start(bf16[128,256]{1,0:T(8,128)(2,1)S(1)} %get-tuple-element.66), channel_id=1, source_target_pairs={{0,16},{1,17},{2,18},{3,19},{4,20},{5,21},{6,22},{7,23},{8,72},{9,... | collective-permute-start | bytes 196616 | tf_op jit(solution)/shard_map/ppermute | solution.py:485
  77.4 5.1 %collective-permute-start.20 = (bf16[64,256]{1,0:T(8,128)(2,1)S(1)}, bf16[64,256]{1,0:T(8,128)(2,1)S(1)}, u32[]{:S(2)}, u32[]{:S(2)}) collective-permute-start(bf16[64,256]{1,0:T(8,128)(2,1)S(1)} %get-tuple-element.54.refs_6_), channel_id=1, source_target_pairs={{1,2},{3,4},{5,6},{7,0},{2,1},{4,3},{6,5},{0,7},{9,10},{11,12},{13... | collective-permute-start | bytes 98312 | tf_op jit(solution)/shard_map/ppermute | solution.py:495
  82.8 4.4 %collective-permute-start.23 = (bf16[128,256]{1,0:T(8,128)(2,1)S(1)}, bf16[128,256]{1,0:T(8,128)(2,1)S(1)}, u32[]{:S(2)}, u32[]{:S(2)}) collective-permute-start(bf16[128,256]{1,0:T(8,128)(2,1)S(1)} %get-tuple-element.68), channel_id=1, source_target_pairs={{0,16},{1,17},{2,18},{3,19},{4,20},{5,21},{6,22},{7,23},{8,40},{9,... | collective-permute-start | bytes 196616 | tf_op jit(solution)/shard_map/ppermute | solution.py:485
  83.4 1.2 collective-permute-start.16
  87.4 2.2 %copy-start.2 = (bf16[1,1,2,2048,256]{4,3,2,1,0:T(8,128)(2,1)S(1)}, bf16[1,1,2,2048,256]{4,3,2,1,0:T(8,128)(2,1)}, u32[]{:S(2)}) copy-start(bf16[1,1,2,2048,256]{4,3,2,1,0:T(8,128)(2,1)} %param.11) | copy-start | bytes 6291460
  87.4 4.4 %collective-permute-start.24 = (bf16[128,256]{1,0:T(8,128)(2,1)S(1)}, bf16[128,256]{1,0:T(8,128)(2,1)S(1)}, u32[]{:S(2)}, u32[]{:S(2)}) collective-permute-start(bf16[128,256]{1,0:T(8,128)(2,1)S(1)} %get-tuple-element.70), channel_id=1, source_target_pairs={{0,16},{1,17},{2,18},{3,19},{4,20},{5,21},{6,22},{7,23},{8,24},{9,... | collective-permute-start | bytes 196616 | tf_op jit(solution)/shard_map/ppermute | solution.py:485
  89.1 3.4 %collective-permute-start.17 = (bf16[64,256]{1,0:T(8,128)(2,1)S(1)}, bf16[64,256]{1,0:T(8,128)(2,1)S(1)}, u32[]{:S(2)}, u32[]{:S(2)}) collective-permute-start(bf16[64,256]{1,0:T(8,128)(2,1)S(1)} %get-tuple-element.52.refs_4_), channel_id=1, source_target_pairs={{8,16},{24,32},{40,48},{56,64},{72,80},{88,96},{104,112},{120,128}... | collective-permute-start | bytes 98312 | tf_op jit(solution)/shard_map/ppermute | solution.py:495
  92.2 1.3 collective-permute-start.25
  95.7 1.3 collective-permute-start.26
  112.2 13.1 %all-to-all-start.1 = ((f32[8,32,128]{2,1,0:T(8,128)}), f32[8,32,128]{2,1,0:T(8,128)S(1)}, u32[]{:S(2)}, u32[]{:S(2)}) async-start(f32[8,32,128]{2,1,0:T(8,128)} %shard_map.136), calls=%async_computation.1 | async-start | bytes 262144 | tf_op jit(solution)/shard_map/all_to_all | solution.py:682

commit v6 on v4

--- a/solution.py
+++ b/solution.py
@@ -1,4 +1,5 @@
 import functools
+import math
 
 import jax
 import jax.numpy as jnp
@@ -13,7 +14,7 @@
 VM = pl.BlockSpec(memory_space=pltpu.VMEM)
 SM = pl.BlockSpec(memory_space=pltpu.SMEM)
 
-HEAD, EARLY, LATE = 214, 203, 200
+HEAD, EARLY, LATE = 214, 200, 196
 
 
 def call(kernel, outs, args, flops, smem=0, limit=24, after=(), out_spec=VM, scratch=()):
@@ -124,25 +125,26 @@
     )(tall, squeeze)
 
 
-def load_kernel(begin, f_in, o_ref, sem):
+def load_kernel(begin, f_in, *rest):
+    o_ref, sem = rest[-2:]
     copy = pltpu.make_async_copy(f_in.at[begin : begin + o_ref.shape[0]], o_ref, sem)
     copy.start()
     copy.wait()
 
 
-def load(sections, begin, end, limit):
+def load(sections, begin, end, limit, after=()):
     shape = (end - begin,) + sections.shape[1:]
     return pl.pallas_call(
         functools.partial(load_kernel, begin),
-        in_specs=[pl.BlockSpec(memory_space=pltpu.HBM)],
+        in_specs=[pl.BlockSpec(memory_space=pltpu.HBM)] + [VM] * len(after),
         out_specs=VM,
         out_shape=jax.ShapeDtypeStruct(shape, BF16),
         scratch_shapes=[pltpu.SemaphoreType.DMA],
         cost_estimate=pl.CostEstimate(
-            flops=0, bytes_accessed=2 * sections.size, transcendentals=0
+            flops=0, bytes_accessed=2 * math.prod(shape), transcendentals=0
         ),
         compiler_params=pltpu.CompilerParams(vmem_limit_bytes=limit * 2**18),
-    )(sections)
+    )(sections, *after)
 
 
 def pick_kernel(leaf, info, vb_ref, *outs):
@@ -446,23 +448,26 @@
     leaf_flops = 8 * cols * leaf * unknowns
 
     half, sent = head(leaf, tall, squeeze)
-    early = 3
-    first = load(sections, 0, early, EARLY)
-    rest = load(sections, early, levels, LATE)
+    bounds = [0, 1, 3, levels]
+    held = {}
 
     def weights(level):
-        return (first, level) if level < early else (rest, level - early)
+        at = sum(level >= low for low in bounds[1:-1])
+        if at not in held:
+            limit = LATE if at == 2 else EARLY
+            held[at] = load(sections, bounds[at], bounds[at + 1], limit, [sent])
+        return held[at], level - bounds[at]
 
     got = {}
     for level in range(levels):
         arrived = partner(sent, level)
         after = []
-        if level == 1:
+        if level == 2:
+            after = [weights(3)[0]]
+        if level == 3:
             pieces = call(
                 functools.partial(pick_kernel, leaf), [small] * 4, [info, half], 0, smem=1, after=[sent]
             )
-            after = list(pieces) + [rest]
-        if level == 2:
             (near,) = call(
                 functools.partial(leaves_kernel, leaf, False),
                 [((rows, unknowns), F32)],
@@ -470,9 +475,10 @@
                 leaf_flops,
                 after=[sent],
             )
-            after = [near]
+            after = list(pieces) + [near]
+        if level == 4:
             got["a"] = partner(pieces[0], 0)
-        if level == 3:
+        if level == row_bits:
             after = [got["a"]]
         if level == row_bits:
             got["c"] = arrived

time: 126 us -> 123 us (0.976)
  waiting for transfers between devices: 40.9 us -> 33.3 us
  starting transfers between devices: 39.8 us -> 44.7 us
  blocking collectives: 14.8 us -> 13.5 us
    ppermute x13, waiting for transfers between devices: 16.9 us -> 12.3 us  [partner(): lax.ppermute(x, 'px', [(i, i ^ 1 << level) for i in range(row_count)])]
    ppermute x6, starting transfers between devices: 12.1 us -> 15.5 us  [partner(): return lax.ppermute(x, 'py', [(i, i ^ 1 << bit) for i in range(col_count)])]
    ppermute x6, waiting for transfers between devices: 15.2 us -> 12.1 us  [partner(): return lax.ppermute(x, 'py', [(i, i ^ 1 << bit) for i in range(col_count)])]
    ppermute x13, starting transfers between devices: 15.1 us -> 17.4 us  [partner(): lax.ppermute(x, 'px', [(i, i ^ 1 << level) for i in range(row_count)])]
    all_to_all x1, blocking collectives: 14.8 us -> 13.5 us  [per_device(): lax.all_to_all(part, 'px', 0, 0, axis_index_groups=groups, tiled=True)]
    pallas_call x2 -> x3, Pallas kernels: 3.17 us -> 4.12 us  [load(): pl.pallas_call(functools.partial(load_kernel, begin), in_specs=[pl.BlockS...]
  transfers between devices with their start and end apart: 24 -> 24, of which waited for: 14 -> 15; matrix products, arithmetic and copies ran while one was open for 0% -> 0% of each run, Pallas kernels for 12% -> 13%
where the time goes in v6:
time: 123 us
  starting transfers between devices  44.7 us (36%)
  waiting for transfers between devices  33.3 us (27%)
  Pallas kernels  28.1 us (23%)
  blocking collectives  13.5 us (11%)
  local copies, waits for them, and re-layouts  2.11 us (2%)
    pallas_call x43, Pallas kernels, call(): pl.pallas_call(body, out_shape=[jax.ShapeDtypeStruct(s, d) for s, d in ou...  21.5 us
    ppermute x13, starting transfers between devices, partner(): lax.ppermute(x, 'px', [(i, i ^ 1 << level) for i in range(row_count)])  17.4 us
    ppermute x6, starting transfers between devices, partner(): return lax.ppermute(x, 'py', [(i, i ^ 1 << bit) for i in range(col_count)])  15.5 us
    all_to_all x1, blocking collectives, per_device(): lax.all_to_all(part, 'px', 0, 0, axis_index_groups=groups, tiled=True)  13.5 us
    ppermute x13, waiting for transfers between devices, partner(): lax.ppermute(x, 'px', [(i, i ^ 1 << level) for i in range(row_count)])  12.3 us
    ppermute x6, waiting for transfers between devices, partner(): return lax.ppermute(x, 'py', [(i, i ^ 1 << bit) for i in range(col_count)])  12.1 us
    all_to_all x1, waiting for transfers between devices, per_device(): part = lax.all_to_all(part, 'py', 0, 0, tiled=True)  7.79 us
    ppermute x4, starting transfers between devices, beyond(): return lax.ppermute(x, axis, pairs + [(j, i) for i, j in pairs])  6.85 us
  transfers between devices with their start and end apart: 24, of which 15 were waited for; matrix products, arithmetic and copies ran while one was open for 0% of the time, Pallas kernels for 13%

profile of v6, /device:TPU:8, one launch (start us, length us, event | category | flops | bytes accessed | tf_op | source)
XLA Modules:
  0.0 123.0 jit_solution(6799993306532355320)
XLA Ops:
  0.6 2.5 %shard_map.95 = (bf16[64,2048]{1,0:T(8,128)(2,1)S(1)}, bf16[64,256]{1,0:T(8,128)(2,1)S(1)}) custom-call(f32[32,32,128]{2,1,0:T(8,128)} %bitcast.36, bf16[2,2048,256]{2,1,0:T(8,128)(2,1)} %bitcast.27), custom_call_target="tpu_custom_call" | custom-call | flops 134217728 | bytes 2621440 | tf_op jit(solution)/shard_map/pallas_call | solution.py:105
  3.2 1.1 shard_map.96.refs_1_.refs_2_
  4.6 2.3 %collective-permute-start.1 = (bf16[64,256]{1,0:T(8,128)(2,1)S(1)}, bf16[64,256]{1,0:T(8,128)(2,1)S(1)}, u32[]{:S(2)}, u32[]{:S(2)}) collective-permute-start(bf16[64,256]{1,0:T(8,128)(2,1)S(1)} %shard_map.98.rest_0_.refs_0_), channel_id=1, source_target_pairs={{0,16},{8,24},{16,0},{24,8},{32,48},{40,56},{48,32},{56,40},{64,80... | collective-permute-start | bytes 98312 | tf_op jit(solution)/shard_map/ppermute | solution.py:435
  6.9 1.2 %shard_map.99.refs_1_.refs_2_ = bf16[2,2,2,256,256]{4,3,2,1,0:T(8,128)(2,1)S(1)} custom-call(bf16[8,2,2,256,256]{4,3,2,1,0:T(8,128)(2,1)} %bitcast.41, bf16[64,256]{1,0:T(8,128)(2,1)S(1)} %shard_map.98.rest_0_.refs_0_), custom_call_target="tpu_custom_call" | custom-call | bytes 1048576 | tf_op jit(solution)/shard_map/pallas_call | solution.py:137
  8.3 0.6 collective-permute-done.1.refs_1_
  9.3 1.9 %collective-permute-start.2 = (bf16[64,256]{1,0:T(8,128)(2,1)S(1)}, bf16[64,256]{1,0:T(8,128)(2,1)S(1)}, u32[]{:S(2)}, u32[]{:S(2)}) collective-permute-start(bf16[64,256]{1,0:T(8,128)(2,1)S(1)} %shard_map.101.rest_0_.refs_0_), channel_id=1, source_target_pairs={{0,32},{8,40},{16,48},{24,56},{32,0},{40,8},{48,16},{56,24},{64,96... | collective-permute-start | bytes 98312 | tf_op jit(solution)/shard_map/ppermute | solution.py:435
  11.2 1.8 %shard_map.102.refs_2_.refs_1_ = bf16[5,2,2,256,256]{4,3,2,1,0:T(8,128)(2,1)S(1)} custom-call(bf16[8,2,2,256,256]{4,3,2,1,0:T(8,128)(2,1)} %bitcast.42, bf16[64,256]{1,0:T(8,128)(2,1)S(1)} %shard_map.101.rest_0_.refs_0_), custom_call_target="tpu_custom_call" | custom-call | bytes 2621440 | tf_op jit(solution)/shard_map/pallas_call | solution.py:137
  13.4 1.4 %collective-permute-done.2.refs_1_ = bf16[64,256]{1,0:T(8,128)(2,1)S(1)} collective-permute-done((bf16[64,256]{1,0:T(8,128)(2,1)S(1)}, bf16[64,256]{1,0:T(8,128)(2,1)S(1)}, u32[]{:S(2)}, u32[]{:S(2)}) %collective-permute-start.2) | collective-permute-done | bytes 32800 | tf_op jit(solution)/shard_map/ppermute | solution.py:435
  15.0 1.1 collective-permute-start.3
  16.5 0.6 shard_map.105
  17.2 1.2 copy-done.7
  19.1 2.8 %collective-permute-start.4 = (bf16[64,256]{1,0:T(8,128)(2,1)S(1)}, bf16[64,256]{1,0:T(8,128)(2,1)S(1)}, u32[]{:S(2)}, u32[]{:S(2)}) collective-permute-start(bf16[64,256]{1,0:T(8,128)(2,1)S(1)} %shard_map.108.refs_0_), channel_id=1, source_target_pairs={{0,128},{8,136},{16,144},{24,152},{32,160},{40,168},{48,176},{56,1... | collective-permute-start | bytes 98312 | tf_op jit(solution)/shard_map/ppermute | solution.py:435
  22.1 2.5 %collective-permute-done.4.refs_1_ = bf16[64,256]{1,0:T(8,128)(2,1)S(1)} collective-permute-done((bf16[64,256]{1,0:T(8,128)(2,1)S(1)}, bf16[64,256]{1,0:T(8,128)(2,1)S(1)}, u32[]{:S(2)}, u32[]{:S(2)}) %collective-permute-start.4) | collective-permute-done | bytes 32800 | tf_op jit(solution)/shard_map/ppermute | solution.py:435
  24.8 2.0 %collective-permute-start.6 = (bf16[128,256]{1,0:T(8,128)(2,1)S(1)}, bf16[128,256]{1,0:T(8,128)(2,1)S(1)}, u32[]{:S(2)}, u32[]{:S(2)}) collective-permute-start(bf16[128,256]{1,0:T(8,128)(2,1)S(1)} %shard_map.110.refs_0_), channel_id=1, source_target_pairs={{0,1},{1,0},{2,3},{3,2},{4,5},{5,4},{6,7},{7,6},{8,9},{9,8},{10,11... | collective-permute-start | bytes 196616 | tf_op jit(solution)/shard_map/ppermute | solution.py:437
  26.8 1.2 collective-permute-done.5.refs_2_
  28.2 1.0 collective-permute-done.6.refs_1_.refs_4_
  29.4 3.3 %collective-permute-start.7 = (bf16[64,256]{1,0:T(8,128)(2,1)S(1)}, bf16[64,256]{1,0:T(8,128)(2,1)S(1)}, u32[]{:S(2)}, u32[]{:S(2)}) collective-permute-start(bf16[64,256]{1,0:T(8,128)(2,1)S(1)} %shard_map.112.refs_0_), channel_id=1, source_target_pairs={{0,2},{1,3},{2,0},{3,1},{4,6},{5,7},{6,4},{7,5},{8,10},{9,11},{10,... | collective-permute-start | bytes 98312 | tf_op jit(solution)/shard_map/ppermute | solution.py:437
  32.7 4.0 %collective-permute-start.9 = (bf16[64,256]{1,0:T(8,128)(2,1)S(1)}, bf16[64,256]{1,0:T(8,128)(2,1)S(1)}, u32[]{:S(2)}, u32[]{:S(2)}) collective-permute-start(bf16[64,256]{1,0:T(8,128)(2,1)S(1)} %get-tuple-element.41.refs_5_), channel_id=1, source_target_pairs={{1,2},{3,4},{5,6},{7,0},{2,1},{4,3},{6,5},{0,7},{9,10},{11,12},{13... | collective-permute-start | bytes 98312 | tf_op jit(solution)/shard_map/ppermute | solution.py:441
  37.1 4.6 %collective-permute-start.10 = (bf16[64,256]{1,0:T(8,128)(2,1)S(1)}, bf16[64,256]{1,0:T(8,128)(2,1)S(1)}, u32[]{:S(2)}, u32[]{:S(2)}) collective-permute-start(bf16[64,256]{1,0:T(8,128)(2,1)S(1)} %shard_map.114.refs_7_.refs_0_), channel_id=1, source_target_pairs={{0,4},{1,5},{2,6},{3,7},{4,0},{5,1},{6,2},{7,3},{8,12},{9,13},{10,... | collective-permute-start | bytes 98312 | tf_op jit(solution)/shard_map/ppermute | solution.py:437
  41.7 1.3 %shard_map.115.refs_2_.refs_3_ = f32[64,2048]{1,0:T(8,128)S(1)} custom-call(s32[16]{0:T(128)S(1)} %concatenate.3.refs_0_, f32[64,2048]{1,0:T(8,128)S(1)} %shard_map.106.refs_6_.refs_1_, bf16[64,256]{1,0:T(8,128)(2,1)S(1)} %collective-permute-done.5.refs_2_, bf16[64,256]{1,0:T(8,128)(2,1)S(1)} %collective-permute-done.8.refs_3_, ...), custom_call_target="tpu_custom_call" | custom-call | flops 67108864 | bytes 1736768 | tf_op jit(solution)/shard_map/pallas_call | solution.py:28
  43.3 1.7 %collective-permute-done.10.refs_1_ = bf16[64,256]{1,0:T(8,128)(2,1)S(1)} collective-permute-done((bf16[64,256]{1,0:T(8,128)(2,1)S(1)}, bf16[64,256]{1,0:T(8,128)(2,1)S(1)}, u32[]{:S(2)}, u32[]{:S(2)}) %collective-permute-start.10) | collective-permute-done | bytes 32800 | tf_op jit(solution)/shard_map/ppermute | solution.py:437
  45.0 1.6 %shard_map.117 = (f32[64,2048]{1,0:T(8,128)S(1)}, bf16[64,2048]{1,0:T(8,128)(2,1)S(1)}, bf16[64,256]{1,0:T(8,128)(2,1)S(1)}, bf16[64,256]{1,0:T(8,128)(2,1)S(1)}) custom-call(f32[64,256]{1,0:T(8,128)S(1)} %shard_map.116.refs_0_, bf16[64,256]{1,0:T(8,128)(2,1)S(1)} %collective-permute-done.10.refs_1_, ...), custom_call_target="tpu_custom_call" | custom-call | flops 268435456 | bytes 5341184 | tf_op jit(solution)/shard_map/pallas_call | solution.py:28
  46.6 4.6 %collective-permute-start.11 = (bf16[64,256]{1,0:T(8,128)(2,1)S(1)}, bf16[64,256]{1,0:T(8,128)(2,1)S(1)}, u32[]{:S(2)}, u32[]{:S(2)}) collective-permute-start(bf16[64,256]{1,0:T(8,128)(2,1)S(1)} %get-tuple-element.49), channel_id=1, source_target_pairs={{0,4},{1,5},{2,6},{3,7},{4,0},{5,1},{6,2},{7,3},{8,12},{9,13},{10,... | collective-permute-start | bytes 98312 | tf_op jit(solution)/shard_map/ppermute | solution.py:437
  51.2 1.0 shard_map.119
  52.4 2.1 %collective-permute-done.11.refs_1_ = bf16[64,256]{1,0:T(8,128)(2,1)S(1)} collective-permute-done((bf16[64,256]{1,0:T(8,128)(2,1)S(1)}, bf16[64,256]{1,0:T(8,128)(2,1)S(1)}, u32[]{:S(2)}, u32[]{:S(2)}) %collective-permute-start.11) | collective-permute-done | bytes 32800 | tf_op jit(solution)/shard_map/ppermute | solution.py:437
  54.7 0.7 collective-permute-start.14
  55.4 0.8 shard_map.122.refs_2_.refs_1_
  56.4 3.2 %collective-permute-done.14.refs_1_ = bf16[64,256]{1,0:T(8,128)(2,1)S(1)} collective-permute-done((bf16[64,256]{1,0:T(8,128)(2,1)S(1)}, bf16[64,256]{1,0:T(8,128)(2,1)S(1)}, u32[]{:S(2)}, u32[]{:S(2)}) %collective-permute-start.14) | collective-permute-done | bytes 32800 | tf_op jit(solution)/shard_map/ppermute | solution.py:437
  60.3 4.0 %collective-permute-done.15.refs_4_.refs_1_ = bf16[128,256]{1,0:T(8,128)(2,1)S(1)} collective-permute-done((bf16[128,256]{1,0:T(8,128)(2,1)S(1)}, bf16[128,256]{1,0:T(8,128)(2,1)S(1)}, u32[]{:S(2)}, u32[]{:S(2)}) %collective-permute-start.15) | collective-permute-done | bytes 65568 | tf_op jit(solution)/shard_map/ppermute | solution.py:437
  64.6 2.8 %collective-permute-start.17 = (bf16[64,256]{1,0:T(8,128)(2,1)S(1)}, bf16[64,256]{1,0:T(8,128)(2,1)S(1)}, u32[]{:S(2)}, u32[]{:S(2)}) collective-permute-start(bf16[64,256]{1,0:T(8,128)(2,1)S(1)} %get-tuple-element.55.refs_1_), channel_id=1, source_target_pairs={{0,128},{8,136},{16,144},{24,152},{32,160},{40,168},{48,176},{56,1... | collective-permute-start | bytes 98312 | tf_op jit(solution)/shard_map/ppermute | solution.py:435
  67.4 1.7 %shard_map.128 = (bf16[64,2048]{1,0:T(8,128)(2,1)S(1)}, bf16[64,2048]{1,0:T(8,128)(2,1)S(1)}, f32[32,32]{1,0:T(8,128)S(1)}) custom-call(f32[32,32,128]{2,1,0:T(8,128)S(1)} %bitcast.37, bf16[64,256]{1,0:T(8,128)(2,1)S(1)} %get-tuple-element.55.refs_1_), custom_call_target="tpu_custom_call" | custom-call | flops 67108864 | bytes 524288 | tf_op jit(solution)/shard_map/pallas_call | solution.py:28
  69.4 0.7 collective-permute-done.17.refs_1_
  70.3 1.5 %collective-permute-start.18 = (bf16[64,256]{1,0:T(8,128)(2,1)S(1)}, bf16[64,256]{1,0:T(8,128)(2,1)S(1)}, u32[]{:S(2)}, u32[]{:S(2)}) collective-permute-start(bf16[64,256]{1,0:T(8,128)(2,1)S(1)} %get-tuple-element.60), channel_id=1, source_target_pairs={{0,64},{8,72},{16,80},{24,88},{32,96},{40,104},{48,112},{56,120},{... | collective-permute-start | bytes 98312 | tf_op jit(solution)/shard_map/ppermute | solution.py:435
  71.7 2.8 %collective-permute-start.16 = (bf16[64,256]{1,0:T(8,128)(2,1)S(1)}, bf16[64,256]{1,0:T(8,128)(2,1)S(1)}, u32[]{:S(2)}, u32[]{:S(2)}) collective-permute-start(bf16[64,256]{1,0:T(8,128)(2,1)S(1)} %get-tuple-element.48.refs_5_), channel_id=1, source_target_pairs={{1,2},{3,4},{5,6},{7,0},{2,1},{4,3},{6,5},{0,7},{9,10},{11,12},{13... | collective-permute-start | bytes 98312 | tf_op jit(solution)/shard_map/ppermute | solution.py:441
  75.0 2.4 %collective-permute-start.19 = (bf16[64,256]{1,0:T(8,128)(2,1)S(1)}, bf16[64,256]{1,0:T(8,128)(2,1)S(1)}, u32[]{:S(2)}, u32[]{:S(2)}) collective-permute-start(bf16[64,256]{1,0:T(8,128)(2,1)S(1)} %get-tuple-element.62), channel_id=1, source_target_pairs={{0,32},{8,40},{16,48},{24,56},{32,0},{40,8},{48,16},{56,24},{64,96... | collective-permute-start | bytes 98312 | tf_op jit(solution)/shard_map/ppermute | solution.py:435
  77.6 2.9 %collective-permute-done.19.refs_1_ = bf16[64,256]{1,0:T(8,128)(2,1)S(1)} collective-permute-done((bf16[64,256]{1,0:T(8,128)(2,1)S(1)}, bf16[64,256]{1,0:T(8,128)(2,1)S(1)}, u32[]{:S(2)}, u32[]{:S(2)}) %collective-permute-start.19) | collective-permute-done | bytes 32800 | tf_op jit(solution)/shard_map/ppermute | solution.py:435
  80.7 2.4 %collective-permute-start.20 = (bf16[64,256]{1,0:T(8,128)(2,1)S(1)}, bf16[64,256]{1,0:T(8,128)(2,1)S(1)}, u32[]{:S(2)}, u32[]{:S(2)}) collective-permute-start(bf16[64,256]{1,0:T(8,128)(2,1)S(1)} %get-tuple-element.64), channel_id=1, source_target_pairs={{0,16},{8,24},{16,0},{24,8},{32,48},{40,56},{48,32},{56,40},{64,80... | collective-permute-start | bytes 98312 | tf_op jit(solution)/shard_map/ppermute | solution.py:435
  83.3 1.7 %collective-permute-done.20.refs_1_ = bf16[64,256]{1,0:T(8,128)(2,1)S(1)} collective-permute-done((bf16[64,256]{1,0:T(8,128)(2,1)S(1)}, bf16[64,256]{1,0:T(8,128)(2,1)S(1)}, u32[]{:S(2)}, u32[]{:S(2)}) %collective-permute-start.20) | collective-permute-done | bytes 32800 | tf_op jit(solution)/shard_map/ppermute | solution.py:435
  85.3 1.1 collective-permute-done.13.refs_3_
  86.4 0.6 shard_map.125.refs_2_.refs_0_
  87.3 1.6 %shard_map.138 = (bf16[64,2048]{1,0:T(8,128)(2,1)S(1)}, bf16[64,2048]{1,0:T(8,128)(2,1)S(1)}, f32[32,128]{1,0:T(8,128)S(1)}) custom-call(f32[64,2048]{1,0:T(8,128)S(1)} %shard_map.125.refs_2_.refs_0_, f32[64,256]{1,0:T(8,128)S(1)} %shard_map.137.refs_1_, bf16[64,256]{1,0:T(8,128)(2,1)S(1)} %collective-permute-done.21.refs_2_, ...), custom_call_target="tpu_custom_call" | custom-call | flops 134217728 | bytes 3248128 | tf_op jit(solution)/shard_map/pallas_call | solution.py:28
  89.0 1.2 collective-permute-done.22.refs_1_
  90.2 13.5 %all_to_all.10.refs_0_ = f32[16,32,128]{2,1,0:T(8,128)S(1)} all-to-all(f32[16,32,128]{2,1,0:T(8,128)S(1)} %shard_map.139), channel_id=1, replica_groups={{0,16,32,48,64,80,96,112,128,144,160,176,192,208,224,240},{8,24,40,56,7..., dimensions={0} | all-to-all | bytes 524288 | tf_op jit(solution)/shard_map/all_to_all | solution.py:596
  103.7 0.7 shard_map.140
  104.4 5.0 %all-to-all-start.1 = ((f32[8,32,128]{2,1,0:T(8,128)}), f32[8,32,128]{2,1,0:T(8,128)S(1)}, u32[]{:S(2)}, u32[]{:S(2)}) async-start(f32[8,32,128]{2,1,0:T(8,128)} %shard_map.140), calls=%async_computation.1 | async-start | bytes 262144 | tf_op jit(solution)/shard_map/all_to_all | solution.py:598
  109.4 1.3 %shard_map.118 = f32[32,32,128]{2,1,0:T(8,128)} custom-call(f32[64,2048]{1,0:T(8,128)S(1)} %copy-done.13), custom_call_target="tpu_custom_call" | custom-call | bytes 524288 | tf_op jit(solution)/shard_map/pallas_call | solution.py:28
  110.7 7.8 %all-to-all-done.1.refs_0_ = f32[8,32,128]{2,1,0:T(8,128)S(1)} async-done(((f32[8,32,128]{2,1,0:T(8,128)}), f32[8,32,128]{2,1,0:T(8,128)S(1)}, u32[]{:S(2)}, u32[]{:S(2)}) %all-to-all-start.1) | async-done | bytes 131104 | tf_op jit(solution)/shard_map/all_to_all | solution.py:598
  118.5 4.3 %shard_map.141 = f32[64,32,128]{2,1,0:T(8,128)} custom-call(f32[8,32,128]{2,1,0:T(8,128)S(1)} %all-to-all-done.1.refs_0_, bf16[64,2048]{1,0:T(8,128)(2,1)S(1)} %get-tuple-element.68.refs_1_, bf16[64,2048]{1,0:T(8,128)(2,1)S(1)} %get-tuple-element.69.refs_2_, bf16[64,2048]{1,0:T(8,128)(2,1)S(1)} %get-tuple-element.56.refs_2_.refs_4_.refs_3_, ...), custom_call_target="tpu_custom_call" | custom-call | flops 67108864 | bytes 1179648 | tf_op jit(solution)/shard_map/pallas_call | solution.py:28
  (82 shorter events, 7.6 us)
Async XLA Ops:
  0.6 15.5 %copy-start = (s32[32,8,4,2]{0,3,2,1:T(2,128)S(1)}, s32[32,8,4,2]{0,3,2,1:T(2,128)}, u32[]{:S(2)}) copy-start(s32[32,8,4,2]{0,3,2,1:T(2,128)} %param.9) | copy-start | bytes 24580
  3.1 1.3 %collective-permute-start = (bf16[64,256]{1,0:T(8,128)(2,1)S(1)}, bf16[64,256]{1,0:T(8,128)(2,1)S(1)}, u32[]{:S(2)}, u32[]{:S(2)}) collective-permute-start(bf16[64,256]{1,0:T(8,128)(2,1)S(1)} %get-tuple-element.36.rest_0_.refs_0_), channel_id=1, source_target_pairs={{0,8},{8,0},{16,24},{24,16},{32,40},{40,32},{48,56},{56,48},{64,72... | collective-permute-start | bytes 98312 | tf_op jit(solution)/shard_map/ppermute | solution.py:435
  4.6 4.3 %collective-permute-start.1 = (bf16[64,256]{1,0:T(8,128)(2,1)S(1)}, bf16[64,256]{1,0:T(8,128)(2,1)S(1)}, u32[]{:S(2)}, u32[]{:S(2)}) collective-permute-start(bf16[64,256]{1,0:T(8,128)(2,1)S(1)} %shard_map.98.rest_0_.refs_0_), channel_id=1, source_target_pairs={{0,16},{8,24},{16,0},{24,8},{32,48},{40,56},{48,32},{56,40},{64,80... | collective-permute-start | bytes 98312 | tf_op jit(solution)/shard_map/ppermute | solution.py:435
  8.2 1.0 copy-start.1
  9.3 5.5 %collective-permute-start.2 = (bf16[64,256]{1,0:T(8,128)(2,1)S(1)}, bf16[64,256]{1,0:T(8,128)(2,1)S(1)}, u32[]{:S(2)}, u32[]{:S(2)}) collective-permute-start(bf16[64,256]{1,0:T(8,128)(2,1)S(1)} %shard_map.101.rest_0_.refs_0_), channel_id=1, source_target_pairs={{0,32},{8,40},{16,48},{24,56},{32,0},{40,8},{48,16},{56,24},{64,96... | collective-permute-start | bytes 98312 | tf_op jit(solution)/shard_map/ppermute | solution.py:435
  11.2 2.0 %copy-start.2 = (bf16[2,2,2,256,256]{4,3,2,1,0:T(8,128)(2,1)S(1)}, bf16[2,2,2,256,256]{4,3,2,1,0:T(8,128)(2,1)}, u32[]{:S(2)}) copy-start(bf16[2,2,2,256,256]{4,3,2,1,0:T(8,128)(2,1)} %copy-done.1) | copy-start | bytes 3145732
  13.2 2.9 %copy-start.14 = (s32[4]{0:T(128)S(1)}, s32[4]{0:T(128)}, u32[]{:S(2)}) copy-start(s32[4]{0:T(128)} %constant.40.clone) | copy-start | bytes 52
  15.0 4.0 %collective-permute-start.3 = (bf16[64,256]{1,0:T(8,128)(2,1)S(1)}, bf16[64,256]{1,0:T(8,128)(2,1)S(1)}, u32[]{:S(2)}, u32[]{:S(2)}) collective-permute-start(bf16[64,256]{1,0:T(8,128)(2,1)S(1)} %shard_map.104.refs_2_.refs_0_), channel_id=1, source_target_pairs={{0,64},{8,72},{16,80},{24,88},{32,96},{40,104},{48,112},{56,120},{... | collective-permute-start | bytes 98312 | tf_op jit(solution)/shard_map/ppermute | solution.py:435
  17.2 1.2 copy-start.7
  19.1 5.5 %collective-permute-start.4 = (bf16[64,256]{1,0:T(8,128)(2,1)S(1)}, bf16[64,256]{1,0:T(8,128)(2,1)S(1)}, u32[]{:S(2)}, u32[]{:S(2)}) collective-permute-start(bf16[64,256]{1,0:T(8,128)(2,1)S(1)} %shard_map.108.refs_0_), channel_id=1, source_target_pairs={{0,128},{8,136},{16,144},{24,152},{32,160},{40,168},{48,176},{56,1... | collective-permute-start | bytes 98312 | tf_op jit(solution)/shard_map/ppermute | solution.py:435
  24.8 4.4 %collective-permute-start.6 = (bf16[128,256]{1,0:T(8,128)(2,1)S(1)}, bf16[128,256]{1,0:T(8,128)(2,1)S(1)}, u32[]{:S(2)}, u32[]{:S(2)}) collective-permute-start(bf16[128,256]{1,0:T(8,128)(2,1)S(1)} %shard_map.110.refs_0_), channel_id=1, source_target_pairs={{0,1},{1,0},{2,3},{3,2},{4,5},{5,4},{6,7},{7,6},{8,9},{9,8},{10,11... | collective-permute-start | bytes 196616 | tf_op jit(solution)/shard_map/ppermute | solution.py:437
  26.8 1.2 collective-permute-start.5
  29.3 12.4 %copy-start.6 = (bf16[1,1,4,2,256,256]{5,4,3,2,1,0:T(8,128)(2,1)S(1)}, bf16[1,1,4,2,256,256]{5,4,3,2,1,0:T(8,128)(2,1)}, u32[]{:S(2)}) copy-start(bf16[1,1,4,2,256,256]{5,4,3,2,1,0:T(8,128)(2,1)} %param.11) | copy-start | bytes 3145732
  29.4 7.6 %collective-permute-start.7 = (bf16[64,256]{1,0:T(8,128)(2,1)S(1)}, bf16[64,256]{1,0:T(8,128)(2,1)S(1)}, u32[]{:S(2)}, u32[]{:S(2)}) collective-permute-start(bf16[64,256]{1,0:T(8,128)(2,1)S(1)} %shard_map.112.refs_0_), channel_id=1, source_target_pairs={{0,2},{1,3},{2,0},{3,1},{4,6},{5,7},{6,4},{7,5},{8,10},{9,11},{10,... | collective-permute-start | bytes 98312 | tf_op jit(solution)/shard_map/ppermute | solution.py:437
  32.7 9.0 %collective-permute-start.8 = (bf16[64,256]{1,0:T(8,128)(2,1)S(1)}, bf16[64,256]{1,0:T(8,128)(2,1)S(1)}, u32[]{:S(2)}, u32[]{:S(2)}) collective-permute-start(bf16[64,256]{1,0:T(8,128)(2,1)S(1)} %get-tuple-element.39.refs_3_), channel_id=1, source_target_pairs={{8,16},{24,32},{40,48},{56,64},{72,80},{88,96},{104,112},{120,128}... | collective-permute-start | bytes 98312 | tf_op jit(solution)/shard_map/ppermute | solution.py:441
  32.7 9.0 %collective-permute-start.9 = (bf16[64,256]{1,0:T(8,128)(2,1)S(1)}, bf16[64,256]{1,0:T(8,128)(2,1)S(1)}, u32[]{:S(2)}, u32[]{:S(2)}) collective-permute-start(bf16[64,256]{1,0:T(8,128)(2,1)S(1)} %get-tuple-element.41.refs_5_), channel_id=1, source_target_pairs={{1,2},{3,4},{5,6},{7,0},{2,1},{4,3},{6,5},{0,7},{9,10},{11,12},{13... | collective-permute-start | bytes 98312 | tf_op jit(solution)/shard_map/ppermute | solution.py:441
  36.9 6.2 %copy-start.5 = (bf16[1,1,2,256,2048]{4,3,2,1,0:T(8,128)(2,1)S(1)}, bf16[1,1,2,256,2048]{4,3,2,1,0:T(8,128)(2,1)}, u32[]{:S(2)}) copy-start(bf16[1,1,2,256,2048]{4,3,2,1,0:T(8,128)(2,1)} %param.13) | copy-start | bytes 6291460
  37.1 7.9 %collective-permute-start.10 = (bf16[64,256]{1,0:T(8,128)(2,1)S(1)}, bf16[64,256]{1,0:T(8,128)(2,1)S(1)}, u32[]{:S(2)}, u32[]{:S(2)}) collective-permute-start(bf16[64,256]{1,0:T(8,128)(2,1)S(1)} %shard_map.114.refs_7_.refs_0_), channel_id=1, source_target_pairs={{0,4},{1,5},{2,6},{3,7},{4,0},{5,1},{6,2},{7,3},{8,12},{9,13},{10,... | collective-permute-start | bytes 98312 | tf_op jit(solution)/shard_map/ppermute | solution.py:437
  46.6 8.1 %copy-start.12 = (f32[64,2048]{1,0:T(8,128)}, f32[64,2048]{1,0:T(8,128)S(1)}, u32[]{:S(2)}) copy-start(f32[64,2048]{1,0:T(8,128)S(1)} %get-tuple-element.42.refs_0_) | copy-start | bytes 1572868
  46.6 7.9 %collective-permute-start.11 = (bf16[64,256]{1,0:T(8,128)(2,1)S(1)}, bf16[64,256]{1,0:T(8,128)(2,1)S(1)}, u32[]{:S(2)}, u32[]{:S(2)}) collective-permute-start(bf16[64,256]{1,0:T(8,128)(2,1)S(1)} %get-tuple-element.49), channel_id=1, source_target_pairs={{0,4},{1,5},{2,6},{3,7},{4,0},{5,1},{6,2},{7,3},{8,12},{9,13},{10,... | collective-permute-start | bytes 98312 | tf_op jit(solution)/shard_map/ppermute | solution.py:437
  52.2 3.2 %copy-start.8 = (bf16[1,1,2,16,128,128]{5,4,3,2,1,0:T(8,128)(2,1)S(1)}, bf16[1,1,2,16,128,128]{5,4,3,2,1,0:T(8,128)(2,1)}, u32[]{:S(2)}) copy-start(bf16[1,1,2,16,128,128]{5,4,3,2,1,0:T(8,128)(2,1)} %param.10) | copy-start | bytes 3145732
  54.7 4.9 %collective-permute-start.14 = (bf16[64,256]{1,0:T(8,128)(2,1)S(1)}, bf16[64,256]{1,0:T(8,128)(2,1)S(1)}, u32[]{:S(2)}, u32[]{:S(2)}) collective-permute-start(bf16[64,256]{1,0:T(8,128)(2,1)S(1)} %get-tuple-element.50.refs_2_), channel_id=1, source_target_pairs={{0,2},{1,3},{2,0},{3,1},{4,6},{5,7},{6,4},{7,5},{8,10},{9,11},{10,... | collective-permute-start | bytes 98312 | tf_op jit(solution)/shard_map/ppermute | solution.py:437
  59.8 4.5 %collective-permute-start.15 = (bf16[128,256]{1,0:T(8,128)(2,1)S(1)}, bf16[128,256]{1,0:T(8,128)(2,1)S(1)}, u32[]{:S(2)}, u32[]{:S(2)}) collective-permute-start(bf16[128,256]{1,0:T(8,128)(2,1)S(1)} %get-tuple-element.52), channel_id=1, source_target_pairs={{0,1},{1,0},{2,3},{3,2},{4,5},{5,4},{6,7},{7,6},{8,9},{9,8},{10,11... | collective-permute-start | bytes 196616 | tf_op jit(solution)/shard_map/ppermute | solution.py:437
  60.1 7.3 %copy-start.11 = (f32[32,1,1,2,2048]{4,3,2,1,0:T(2,128)S(1)}, f32[32,1,1,2,2048]{4,3,2,1,0:T(2,128)}, u32[]{:S(2)}) copy-start(f32[32,1,1,2,2048]{4,3,2,1,0:T(2,128)} %param.8) | copy-start | bytes 1572868
  64.6 5.5 %collective-permute-start.17 = (bf16[64,256]{1,0:T(8,128)(2,1)S(1)}, bf16[64,256]{1,0:T(8,128)(2,1)S(1)}, u32[]{:S(2)}, u32[]{:S(2)}) collective-permute-start(bf16[64,256]{1,0:T(8,128)(2,1)S(1)} %get-tuple-element.55.refs_1_), channel_id=1, source_target_pairs={{0,128},{8,136},{16,144},{24,152},{32,160},{40,168},{48,176},{56,1... | collective-permute-start | bytes 98312 | tf_op jit(solution)/shard_map/ppermute | solution.py:435
  69.2 18.2 %copy-start.9 = (bf16[64,2048]{1,0:T(8,128)(2,1)}, bf16[64,2048]{1,0:T(8,128)(2,1)S(1)}, u32[]{:S(2)}) copy-start(bf16[64,2048]{1,0:T(8,128)(2,1)S(1)} %get-tuple-element.57.refs_3_.refs_5_.refs_4_) | copy-start | bytes 786436
  69.4 5.4 %copy-start.3 = (bf16[2,2,2,256,256]{4,3,2,1,0:T(8,128)(2,1)S(1)}, bf16[2,2,2,256,256]{4,3,2,1,0:T(8,128)(2,1)}, u32[]{:S(2)}) copy-start(bf16[2,2,2,256,256]{4,3,2,1,0:T(8,128)(2,1)} %copy-done.1) | copy-start | bytes 3145732
  70.3 4.5 %collective-permute-start.18 = (bf16[64,256]{1,0:T(8,128)(2,1)S(1)}, bf16[64,256]{1,0:T(8,128)(2,1)S(1)}, u32[]{:S(2)}, u32[]{:S(2)}) collective-permute-start(bf16[64,256]{1,0:T(8,128)(2,1)S(1)} %get-tuple-element.60), channel_id=1, source_target_pairs={{0,64},{8,72},{16,80},{24,88},{32,96},{40,104},{48,112},{56,120},{... | collective-permute-start | bytes 98312 | tf_op jit(solution)/shard_map/ppermute | solution.py:435
  71.7 5.6 %collective-permute-start.16 = (bf16[64,256]{1,0:T(8,128)(2,1)S(1)}, bf16[64,256]{1,0:T(8,128)(2,1)S(1)}, u32[]{:S(2)}, u32[]{:S(2)}) collective-permute-start(bf16[64,256]{1,0:T(8,128)(2,1)S(1)} %get-tuple-element.48.refs_5_), channel_id=1, source_target_pairs={{1,2},{3,4},{5,6},{7,0},{2,1},{4,3},{6,5},{0,7},{9,10},{11,12},{13... | collective-permute-start | bytes 98312 | tf_op jit(solution)/shard_map/ppermute | solution.py:441
  74.6 8.5 %copy-start.4 = (bf16[1,1,2,2048,256]{4,3,2,1,0:T(8,128)(2,1)S(1)}, bf16[1,1,2,2048,256]{4,3,2,1,0:T(8,128)(2,1)}, u32[]{:S(2)}) copy-start(bf16[1,1,2,2048,256]{4,3,2,1,0:T(8,128)(2,1)} %param.12) | copy-start | bytes 6291460
  75.0 5.5 %collective-permute-start.19 = (bf16[64,256]{1,0:T(8,128)(2,1)S(1)}, bf16[64,256]{1,0:T(8,128)(2,1)S(1)}, u32[]{:S(2)}, u32[]{:S(2)}) collective-permute-start(bf16[64,256]{1,0:T(8,128)(2,1)S(1)} %get-tuple-element.62), channel_id=1, source_target_pairs={{0,32},{8,40},{16,48},{24,56},{32,0},{40,8},{48,16},{56,24},{64,96... | collective-permute-start | bytes 98312 | tf_op jit(solution)/shard_map/ppermute | solution.py:435
  77.4 5.7 %collective-permute-start.12 = (bf16[64,256]{1,0:T(8,128)(2,1)S(1)}, bf16[64,256]{1,0:T(8,128)(2,1)S(1)}, u32[]{:S(2)}, u32[]{:S(2)}) collective-permute-start(bf16[64,256]{1,0:T(8,128)(2,1)S(1)} %get-tuple-element.45.refs_2_), channel_id=1, source_target_pairs={{0,8},{8,0},{16,24},{24,16},{32,40},{40,32},{48,56},{56,48},{64,72... | collective-permute-start | bytes 98312 | tf_op jit(solution)/shard_map/ppermute | solution.py:435
  80.7 4.3 %collective-permute-start.20 = (bf16[64,256]{1,0:T(8,128)(2,1)S(1)}, bf16[64,256]{1,0:T(8,128)(2,1)S(1)}, u32[]{:S(2)}, u32[]{:S(2)}) collective-permute-start(bf16[64,256]{1,0:T(8,128)(2,1)S(1)} %get-tuple-element.64), channel_id=1, source_target_pairs={{0,16},{8,24},{16,0},{24,8},{32,48},{40,56},{48,32},{56,40},{64,80... | collective-permute-start | bytes 98312 | tf_op jit(solution)/shard_map/ppermute | solution.py:435
  83.1 3.3 %collective-permute-start.13 = (bf16[64,256]{1,0:T(8,128)(2,1)S(1)}, bf16[64,256]{1,0:T(8,128)(2,1)S(1)}, u32[]{:S(2)}, u32[]{:S(2)}) collective-permute-start(bf16[64,256]{1,0:T(8,128)(2,1)S(1)} %get-tuple-element.46.refs_3_), channel_id=1, source_target_pairs={{8,16},{24,32},{40,48},{56,64},{72,80},{88,96},{104,112},{120,128}... | collective-permute-start | bytes 98312 | tf_op jit(solution)/shard_map/ppermute | solution.py:441
  85.2 2.1 %collective-permute-start.21 = (bf16[64,256]{1,0:T(8,128)(2,1)S(1)}, bf16[64,256]{1,0:T(8,128)(2,1)S(1)}, u32[]{:S(2)}, u32[]{:S(2)}) collective-permute-start(bf16[64,256]{1,0:T(8,128)(2,1)S(1)} %get-tuple-element.66), channel_id=1, source_target_pairs={{0,8},{8,0},{16,24},{24,16},{32,40},{40,32},{48,56},{56,48},{64,72... | collective-permute-start | bytes 98312 | tf_op jit(solution)/shard_map/ppermute | solution.py:435
  87.3 22.1 %copy-start.13 = (f32[64,2048]{1,0:T(8,128)S(1)}, f32[64,2048]{1,0:T(8,128)}, u32[]{:S(2)}) copy-start(f32[64,2048]{1,0:T(8,128)} %copy-done.12) | copy-start | bytes 1572868
  88.9 29.6 %copy-start.10 = (bf16[64,2048]{1,0:T(8,128)(2,1)S(1)}, bf16[64,2048]{1,0:T(8,128)(2,1)}, u32[]{:S(2)}) copy-start(bf16[64,2048]{1,0:T(8,128)(2,1)} %copy-done.9) | copy-start | bytes 786436
  88.9 1.3 %collective-permute-start.22 = (f32[1,32,128]{2,1,0:T(8,128)S(1)}, f32[1,32,128]{2,1,0:T(8,128)S(1)}, u32[]{:S(2)}, u32[]{:S(2)}) collective-permute-start(f32[1,32,128]{2,1,0:T(8,128)S(1)} %bitcast.38), channel_id=1, source_target_pairs={{0,8},{8,0},{16,24},{24,16},{32,40},{40,32},{48,56},{56,48},{64,72... | collective-permute-start | bytes 49160 | tf_op jit(solution)/shard_map/ppermute | solution.py:435
  104.4 14.1 %all-to-all-start.1 = ((f32[8,32,128]{2,1,0:T(8,128)}), f32[8,32,128]{2,1,0:T(8,128)S(1)}, u32[]{:S(2)}, u32[]{:S(2)}) async-start(f32[8,32,128]{2,1,0:T(8,128)} %shard_map.140), calls=%async_computation.1 | async-start | bytes 262144 | tf_op jit(solution)/shard_map/all_to_all | solution.py:598

commit v7 on v6

--- a/solution.py
+++ b/solution.py
@@ -210,7 +210,9 @@
                 o_ref[:, leaf_at(info[2 * side + e], leaf)] += term[:, e * leaf : (e + 1) * leaf]
 
 
-def field_kernel(level, own_ref, r_ref, f_ref, near_ref, e_ref, y_ref, yb_ref, g_ref, m_ref):
+def field_kernel(
+    level, own_ref, r_ref, f_ref, near_ref, e_ref, vv_ref, y_ref, yb_ref, g_ref, m_ref, sum_ref
+):
     rows = own_ref.shape[0]
     state = own_ref[...] + mul(r_ref[:rows], f_ref[level, 1, 0], f_ref[level, 1, 1])
     y = near_ref[...] + mul(state.astype(BF16), e_ref[0], e_ref[1])
@@ -219,7 +221,25 @@
     yb_ref[...] = yb
     g = adj(yb, e_ref[0], e_ref[1]).astype(BF16)
     g_ref[...] = g
-    m_ref[...] = adj(g, f_ref[level, 1, 0], f_ref[level, 1, 1]).astype(BF16)
+    m_ref[:rows] = adj(g, f_ref[level, 1, 0], f_ref[level, 1, 1]).astype(BF16)
+    yy = packed(lax.dot_general(yb, yb, NT, preferred_element_type=F32), rows // 2)
+    total = jnp.concatenate([yy, vv_ref[...]], 1)
+    sum_ref[...] = total
+    share(total, m_ref, rows)
+
+
+def share(total, m_ref, low):
+    high = total.astype(BF16)
+    middle, least = split(total - high.astype(F32))
+    parts = [high, middle, least, jnp.zeros_like(high)]
+    m_ref[low : low + total.shape[0]] = jnp.concatenate([p.astype(F32) for p in parts], 1).astype(BF16)
+
+
+def shared(r_ref, low, total):
+    width = total.shape[1]
+    rows = r_ref[low : low + total.shape[0]].astype(F32)
+    other = rows[:, :width] + rows[:, width : 2 * width] + rows[:, 2 * width : 3 * width]
+    return total + other
 
 
 def shape_kernel(leaf, y_ref, o_ref):
@@ -233,17 +253,23 @@
     for at, o_ref in enumerate(outs):
         side = info[8 + at]
         x = piece(yb_ref, info, side, leaf)
-        o_ref[...] = adj(x, b_ref[side, 0], b_ref[side, 1]).astype(BF16)
-
-
-def down_kernel(level, own_ref, r_ref, f_ref, *rest):
+        low = o_ref.shape[0] - x.shape[0]
+        if low:
+            o_ref[:low] = jnp.zeros((low, o_ref.shape[1]), BF16)
+        o_ref[low:] = adj(x, b_ref[side, 0], b_ref[side, 1]).astype(BF16)
+
+
+def down_kernel(level, own_ref, r_ref, sum_ref, f_ref, *rest):
     rows = own_ref.shape[0]
-    g_ref, m_ref = rest[-2:]
+    g_ref, m_ref, total_ref = rest[-3:]
     g = (own_ref[...] + r_ref[:rows].astype(F32)).astype(BF16)
     g_ref[...] = g
     m_ref[:rows] = adj(g, f_ref[level, 1, 0], f_ref[level, 1, 1]).astype(BF16)
-    if len(rest) > 2:
-        m_ref[rows:] = rest[0][...]
+    total = shared(r_ref, rows, sum_ref[...])
+    total_ref[...] = total
+    share(total, m_ref, rows)
+    if len(rest) > 3:
+        m_ref[rows + rows // 2 :] = rest[0][...]
 
 
 def gather_kernel(leaf, info, near_ref, ra_ref, rb_ref, rc_ref, rd_ref, o_ref):
@@ -261,28 +287,21 @@
                 ].astype(F32)
 
 
-def close_kernel(near_ref, own_ref, r_ref, c_ref, vh_ref, vl_ref, vv_ref, zh_ref, zl_ref, p_ref):
+def close_kernel(near_ref, own_ref, r_ref, sum_ref, c_ref, zh_ref, zl_ref, p_ref, total_ref):
     rows = own_ref.shape[0]
     cols = rows // 2
-    g = (own_ref[...] + r_ref[...].astype(F32)).astype(BF16)
+    g = (own_ref[...] + r_ref[:rows].astype(F32)).astype(BF16)
     high, low = split(near_ref[...] + adj(g, c_ref[0], c_ref[1]))
     zh_ref[...] = high
     zl_ref[...] = low
-    many = jnp.concatenate([high, low, vh_ref[...], vl_ref[...]], 0)
-    s = lax.dot_general(high, many, NT, preferred_element_type=F32)
-    cross = s[:, rows : 2 * rows]
-    zz = s[:, :rows] + cross + cross.T
-    zv = s[:, 2 * rows : 3 * rows] + s[:, 3 * rows :]
-    zv += lax.dot_general(low, vh_ref[...], NT, preferred_element_type=F32)
-    p_ref[...] = jnp.concatenate(
-        [
-            packed(zz, cols),
-            vv_ref[...],
-            zv[:cols, :cols] + zv[cols:, cols:],
-            zv[cols:, :cols] - zv[:cols, cols:],
-        ],
-        1,
-    )
+    s = lax.dot_general(high, jnp.concatenate([high, low], 0), NT, preferred_element_type=F32)
+    cross = s[:, rows:]
+    zz = packed(s[:, :rows] + cross + cross.T, cols)
+    lines = p_ref.shape[1]
+    part = jnp.concatenate([zz[at : at + lines] for at in range(0, cols, lines)], 1)
+    for at in range(p_ref.shape[0]):
+        p_ref[at] = part
+    total_ref[...] = shared(r_ref, rows, sum_ref[...])
 
 
 def spread_kernel(*refs):
@@ -349,9 +368,10 @@
     return jnp.concatenate(done, 0)[:, size:]
 
 
-def finish_kernel(leaf, total, p_ref, zh_ref, zl_ref, vh_ref, vl_ref, o_ref, buffer, sems):
+def finish_kernel(leaf, total, p_ref, sum_ref, zh_ref, zl_ref, vh_ref, vl_ref, o_ref, buffer, sems):
     p = sum(parts_of([p_ref])) * (1.0 / total)
-    cols = p.shape[0]
+    known = sum_ref[...] * (1.0 / total)
+    cols = known.shape[0]
     lower = lax.broadcasted_iota(jnp.int32, (cols, cols), 0)
     upper = lax.broadcasted_iota(jnp.int32, (cols, cols), 1)
 
@@ -361,9 +381,9 @@
         im = jnp.where(lower < upper, t, jnp.where(lower > upper, -turned, 0.0))
         return real_form(re, im)
 
-    zz = hermitian(p[:, :cols])
-    vv = hermitian(p[:, cols : 2 * cols])
-    h = real_form(p[:, 2 * cols : 3 * cols], p[:, 3 * cols :])
+    zz = hermitian(jnp.concatenate([p[:, at : at + cols] for at in range(0, p.shape[1], cols)], 0))
+    h = hermitian(known[:, :cols])
+    vv = hermitian(known[:, cols:])
     nt = (((1,), (1,)), ((), ()))
     middle = exact_dot(h, vv) - 2.0 * h
     gram = zz + exact_dot(middle, h, nt)
@@ -477,6 +497,14 @@
             )
             after = list(pieces) + [near]
         if level == 4:
+            v_high, v_low, vv = call(
+                functools.partial(basis_kernel, leaf),
+                [((rows, unknowns), BF16), ((rows, unknowns), BF16), ((cols, cols), F32)],
+                [tall],
+                leaf_flops,
+                after=[sent],
+            )
+            after = [v_high, v_low, vv]
             got["a"] = partner(pieces[0], 0)
         if level == row_bits:
             after = [got["a"]]
@@ -510,14 +538,21 @@
                 [own, arrived, f] + extra,
                 step_flops,
             )
-    y, yb, g, message = call(
+    longer = ((rows + cols, rank), BF16)
+    longest = ((2 * rows + cols, rank), BF16)
+    sums = ((cols, 2 * cols), F32)
+    y, yb, g, message, running = call(
         functools.partial(field_kernel, at),
-        [((rows, unknowns), F32), ((rows, unknowns), BF16), small, small],
-        [own, arrived, f, near, spread],
+        [((rows, unknowns), F32), ((rows, unknowns), BF16), small, longer, sums],
+        [own, arrived, f, near, spread, vv],
         2 * patch_flops,
     )
     terms = call(
-        functools.partial(terms_kernel, leaf), [small] * 4, [info, yb, sides], 4 * step_flops, smem=1
+        functools.partial(terms_kernel, leaf),
+        [longer, longer, small, longer],
+        [info, yb, sides],
+        4 * step_flops,
+        smem=1,
     )
     (shaped,) = call(
         functools.partial(shape_kernel, leaf), [((cols, 2 * leaves, leaf), F32)], [y], 0
@@ -538,15 +573,6 @@
             after = [z_near]
         if level == row_bits:
             got["c"] = arrived
-        if level == 4:
-            v_high, v_low, vv = call(
-                functools.partial(basis_kernel, leaf),
-                [((rows, unknowns), BF16), ((rows, unknowns), BF16), ((cols, cols), F32)],
-                [tall],
-                leaf_flops,
-                after=[message],
-            )
-            after = [v_high, v_low, vv]
         if level == 3:
             got["d"] = beyond(terms[3], "py", col_count)
         if level == 2:
@@ -575,32 +601,32 @@
         if level > 0:
             extra = [terms[2]] if level == row_bits + 1 else []
             f, at = weights(level - 1)
-            g, message = call(
+            g, message, running = call(
                 functools.partial(down_kernel, at),
-                [small, double if extra else small],
-                [own, arrived, f] + extra,
+                [small, longest if extra else longer, sums],
+                [own, arrived, running, f] + extra,
                 step_flops,
             )
-    z_high, z_low, part = call(
+    payload = (8, cols * cols // 8)
+    z_high, z_low, part, running = call(
         close_kernel,
-        [((rows, unknowns), BF16), ((rows, unknowns), BF16), ((cols, 4 * cols), F32)],
-        [z_near, own, arrived, squeeze, v_high, v_low, vv],
+        [
+            ((rows, unknowns), BF16),
+            ((rows, unknowns), BF16),
+            ((row_count,) + payload, F32),
+            sums,
+        ],
+        [z_near, own, arrived, running, squeeze],
         patch_flops,
     )
-    part = part.reshape(1, cols, 4 * cols)
-    chips = row_count // 2
-    (part,) = call(
-        spread_kernel, [((chips, cols, 4 * cols), F32)], [part, partner(part, 0)], 0
-    )
-    groups = [[2 * i + core for i in range(chips)] for core in range(2)]
-    part = lax.all_to_all(part, "px", 0, 0, axis_index_groups=groups, tiled=True)
-    (part,) = call(spread_kernel, [((col_count, cols, 4 * cols), F32)], [part], 0)
+    part = lax.all_to_all(part, "px", 0, 0, tiled=True)
+    (part,) = call(spread_kernel, [((col_count,) + payload, F32)], [part], 0)
     part = lax.all_to_all(part, "py", 0, 0, tiled=True)
     lines = 8
     (basis,) = call(
         functools.partial(finish_kernel, leaf, total),
         [((rows, 2 * leaves, leaf), F32)],
-        [part, z_high, z_low, v_high, v_low],
+        [part, running, z_high, z_low, v_high, v_low],
         8 * rows * rows * unknowns,
         out_spec=pl.BlockSpec(memory_space=pl.ANY),
         scratch=[

time: 123 us -> 123 us (level)
  waiting for transfers between devices: 33.3 us -> 31.6 us
    ppermute x13 -> x12, waiting for transfers between devices: 12.3 us -> 11.1 us  [partner(): lax.ppermute(x, 'px', [(i, i ^ 1 << level) for i in range(row_count)])]
    ppermute x13 -> x12, starting transfers between devices: 17.4 us -> 18.2 us  [partner(): lax.ppermute(x, 'px', [(i, i ^ 1 << level) for i in range(row_count)])]
    pallas_call x43 -> x42, Pallas kernels: 21.5 us -> 21.6 us  [call(): pl.pallas_call(body, out_shape=[jax.ShapeDtypeStruct(s, d) for s, d in ou...]
  transfers between devices with their start and end apart: 24 -> 23, of which waited for: 15 -> 14; matrix products, arithmetic and copies ran while one was open for 0% -> 0% of each run, Pallas kernels for 13% -> 13%
where the time goes in v7:
time: 123 us; the launch traced here: 122 us
  starting transfers between devices  45.9 us (37%)
  waiting for transfers between devices  31.6 us (26%)
  Pallas kernels  28.2 us (23%)
  blocking collectives  12.8 us (10%)
  local copies, waits for them, and re-layouts  2.1 us (2%)
    pallas_call x42, Pallas kernels, call(): pl.pallas_call(body, out_shape=[jax.ShapeDtypeStruct(s, d) for s, d in ou...  21.6 us
    ppermute x12, starting transfers between devices, partner(): lax.ppermute(x, 'px', [(i, i ^ 1 << level) for i in range(row_count)])  18.2 us
    ppermute x6, starting transfers between devices, partner(): return lax.ppermute(x, 'py', [(i, i ^ 1 << bit) for i in range(col_count)])  15.5 us
    all_to_all x1, blocking collectives, per_device(): part = lax.all_to_all(part, 'px', 0, 0, tiled=True)  12.8 us
    ppermute x6, waiting for transfers between devices, partner(): return lax.ppermute(x, 'py', [(i, i ^ 1 << bit) for i in range(col_count)])  12.7 us
    ppermute x12, waiting for transfers between devices, partner(): lax.ppermute(x, 'px', [(i, i ^ 1 << level) for i in range(row_count)])  11.1 us
    ppermute x4, starting transfers between devices, beyond(): return lax.ppermute(x, axis, pairs + [(j, i) for i, j in pairs])  6.83 us
    all_to_all x1, waiting for transfers between devices, per_device(): part = lax.all_to_all(part, 'py', 0, 0, tiled=True)  6.74 us
  transfers between devices with their start and end apart: 23, of which 14 were waited for; matrix products, arithmetic and copies ran while one was open for 0% of the time, Pallas kernels for 13%

profile of v7, /device:TPU:8, one launch (start us, length us, event | category | flops | bytes accessed | tf_op | source)
XLA Modules:
  0.0 121.7 jit_solution(16835143388518314664)
XLA Ops:
  0.6 2.5 %shard_map.95 = (bf16[64,2048]{1,0:T(8,128)(2,1)S(1)}, bf16[64,256]{1,0:T(8,128)(2,1)S(1)}) custom-call(f32[32,32,128]{2,1,0:T(8,128)} %bitcast.35, bf16[2,2048,256]{2,1,0:T(8,128)(2,1)} %bitcast.26), custom_call_target="tpu_custom_call" | custom-call | flops 134217728 | bytes 2621440 | tf_op jit(solution)/shard_map/pallas_call | solution.py:105
  3.2 1.1 shard_map.96.refs_1_.refs_2_.refs_3_
  4.6 2.3 %collective-permute-start.1 = (bf16[64,256]{1,0:T(8,128)(2,1)S(1)}, bf16[64,256]{1,0:T(8,128)(2,1)S(1)}, u32[]{:S(2)}, u32[]{:S(2)}) collective-permute-start(bf16[64,256]{1,0:T(8,128)(2,1)S(1)} %shard_map.98.rest_0_.refs_0_), channel_id=1, source_target_pairs={{0,16},{8,24},{16,0},{24,8},{32,48},{40,56},{48,32},{56,40},{64,80... | collective-permute-start | bytes 98312 | tf_op jit(solution)/shard_map/ppermute | solution.py:455
  6.9 1.2 %shard_map.99.refs_1_.refs_2_.refs_3_ = bf16[2,2,2,256,256]{4,3,2,1,0:T(8,128)(2,1)S(1)} custom-call(bf16[8,2,2,256,256]{4,3,2,1,0:T(8,128)(2,1)} %bitcast.38, bf16[64,256]{1,0:T(8,128)(2,1)S(1)} %shard_map.98.rest_0_.refs_0_), custom_call_target="tpu_custom_call" | custom-call | bytes 1048576 | tf_op jit(solution)/shard_map/pallas_call | solution.py:137
  8.3 0.6 collective-permute-done.1.refs_1_
  9.3 1.9 %collective-permute-start.2 = (bf16[64,256]{1,0:T(8,128)(2,1)S(1)}, bf16[64,256]{1,0:T(8,128)(2,1)S(1)}, u32[]{:S(2)}, u32[]{:S(2)}) collective-permute-start(bf16[64,256]{1,0:T(8,128)(2,1)S(1)} %shard_map.101.rest_0_.refs_0_), channel_id=1, source_target_pairs={{0,32},{8,40},{16,48},{24,56},{32,0},{40,8},{48,16},{56,24},{64,96... | collective-permute-start | bytes 98312 | tf_op jit(solution)/shard_map/ppermute | solution.py:455
  11.2 1.8 %shard_map.102.refs_2_.refs_1_.refs_3_ = bf16[5,2,2,256,256]{4,3,2,1,0:T(8,128)(2,1)S(1)} custom-call(bf16[8,2,2,256,256]{4,3,2,1,0:T(8,128)(2,1)} %bitcast.39, bf16[64,256]{1,0:T(8,128)(2,1)S(1)} %shard_map.101.rest_0_.refs_0_), custom_call_target="tpu_custom_call" | custom-call | bytes 2621440 | tf_op jit(solution)/shard_map/pallas_call | solution.py:137
  13.4 1.4 %collective-permute-done.2.refs_1_ = bf16[64,256]{1,0:T(8,128)(2,1)S(1)} collective-permute-done((bf16[64,256]{1,0:T(8,128)(2,1)S(1)}, bf16[64,256]{1,0:T(8,128)(2,1)S(1)}, u32[]{:S(2)}, u32[]{:S(2)}) %collective-permute-start.2) | collective-permute-done | bytes 32800 | tf_op jit(solution)/shard_map/ppermute | solution.py:455
  15.0 1.1 collective-permute-start.3
  16.5 0.6 shard_map.105
  17.2 1.2 copy-done.7
  18.4 0.4 shard_map.106.refs_6_.refs_1_
  19.1 2.8 %collective-permute-start.4 = (bf16[64,256]{1,0:T(8,128)(2,1)S(1)}, bf16[64,256]{1,0:T(8,128)(2,1)S(1)}, u32[]{:S(2)}, u32[]{:S(2)}) collective-permute-start(bf16[64,256]{1,0:T(8,128)(2,1)S(1)} %shard_map.108.refs_1_.refs_0_), channel_id=1, source_target_pairs={{0,128},{8,136},{16,144},{24,152},{32,160},{40,168},{48,176},{56,1... | collective-permute-start | bytes 98312 | tf_op jit(solution)/shard_map/ppermute | solution.py:455
  22.0 1.7 %shard_map.109 = (bf16[64,2048]{1,0:T(8,128)(2,1)S(1)}, bf16[64,2048]{1,0:T(8,128)(2,1)S(1)}, f32[32,32]{1,0:T(8,128)S(1)}) custom-call(f32[32,32,128]{2,1,0:T(8,128)S(1)} %bitcast.36, bf16[64,256]{1,0:T(8,128)(2,1)S(1)} %shard_map.108.refs_1_.refs_0_), custom_call_target="tpu_custom_call" | custom-call | flops 67108864 | bytes 524288 | tf_op jit(solution)/shard_map/pallas_call | solution.py:28
  23.9 0.8 collective-permute-done.4.refs_1_
  24.8 2.0 %collective-permute-start.6 = (bf16[128,256]{1,0:T(8,128)(2,1)S(1)}, bf16[128,256]{1,0:T(8,128)(2,1)S(1)}, u32[]{:S(2)}, u32[]{:S(2)}) collective-permute-start(bf16[128,256]{1,0:T(8,128)(2,1)S(1)} %shard_map.111.refs_0_), channel_id=1, source_target_pairs={{0,1},{1,0},{2,3},{3,2},{4,5},{5,4},{6,7},{7,6},{8,9},{9,8},{10,11... | collective-permute-start | bytes 196616 | tf_op jit(solution)/shard_map/ppermute | solution.py:457
  26.8 1.2 collective-permute-done.5.refs_2_
  28.2 1.0 collective-permute-done.6.refs_1_.refs_4_
  29.4 3.3 %collective-permute-start.7 = (bf16[64,256]{1,0:T(8,128)(2,1)S(1)}, bf16[64,256]{1,0:T(8,128)(2,1)S(1)}, u32[]{:S(2)}, u32[]{:S(2)}) collective-permute-start(bf16[64,256]{1,0:T(8,128)(2,1)S(1)} %shard_map.113.refs_0_), channel_id=1, source_target_pairs={{0,2},{1,3},{2,0},{3,1},{4,6},{5,7},{6,4},{7,5},{8,10},{9,11},{10,... | collective-permute-start | bytes 98312 | tf_op jit(solution)/shard_map/ppermute | solution.py:457
  32.7 4.0 %collective-permute-start.9 = (bf16[64,256]{1,0:T(8,128)(2,1)S(1)}, bf16[64,256]{1,0:T(8,128)(2,1)S(1)}, u32[]{:S(2)}, u32[]{:S(2)}) collective-permute-start(bf16[64,256]{1,0:T(8,128)(2,1)S(1)} %get-tuple-element.50.refs_5_), channel_id=1, source_target_pairs={{1,2},{3,4},{5,6},{7,0},{2,1},{4,3},{6,5},{0,7},{9,10},{11,12},{13... | collective-permute-start | bytes 98312 | tf_op jit(solution)/shard_map/ppermute | solution.py:461
  37.1 4.6 %collective-permute-start.10 = (bf16[64,256]{1,0:T(8,128)(2,1)S(1)}, bf16[64,256]{1,0:T(8,128)(2,1)S(1)}, u32[]{:S(2)}, u32[]{:S(2)}) collective-permute-start(bf16[64,256]{1,0:T(8,128)(2,1)S(1)} %shard_map.115.refs_7_.refs_0_), channel_id=1, source_target_pairs={{0,4},{1,5},{2,6},{3,7},{4,0},{5,1},{6,2},{7,3},{8,12},{9,13},{10,... | collective-permute-start | bytes 98312 | tf_op jit(solution)/shard_map/ppermute | solution.py:457
  41.7 1.3 %shard_map.116.refs_2_.refs_3_ = f32[64,2048]{1,0:T(8,128)S(1)} custom-call(s32[16]{0:T(128)S(1)} %concatenate.3.refs_0_, f32[64,2048]{1,0:T(8,128)S(1)} %shard_map.106.refs_6_.refs_1_, bf16[64,256]{1,0:T(8,128)(2,1)S(1)} %collective-permute-done.5.refs_2_, bf16[64,256]{1,0:T(8,128)(2,1)S(1)} %collective-permute-done.8.refs_3_, ...), custom_call_target="tpu_custom_call" | custom-call | flops 67108864 | bytes 1736768 | tf_op jit(solution)/shard_map/pallas_call | solution.py:28
  43.3 1.7 %collective-permute-done.10.refs_1_ = bf16[64,256]{1,0:T(8,128)(2,1)S(1)} collective-permute-done((bf16[64,256]{1,0:T(8,128)(2,1)S(1)}, bf16[64,256]{1,0:T(8,128)(2,1)S(1)}, u32[]{:S(2)}, u32[]{:S(2)}) %collective-permute-start.10) | collective-permute-done | bytes 32800 | tf_op jit(solution)/shard_map/ppermute | solution.py:457
  45.0 2.0 %shard_map.118 = (f32[64,2048]{1,0:T(8,128)S(1)}, bf16[64,2048]{1,0:T(8,128)(2,1)S(1)}, bf16[64,256]{1,0:T(8,128)(2,1)S(1)}, bf16[96,256]{1,0:T(8,128)(2,1)S(1)}, f32[32,64]{1,0:T(8,128)S(1)}) custom-call(f32[64,256]{1,0:T(8,128)S(1)} %shard_map.117.refs_0_, bf16[64,256]{1,0:T(8,128)(2,1)S(1)} %collective-permute-done.10.refs_1_, ...), custom_call_target="tpu_custom_call" | custom-call | flops 268435456 | bytes 5345280 | tf_op jit(solution)/shard_map/pallas_call | solution.py:28
  47.0 4.7 %collective-permute-start.11 = (bf16[96,256]{1,0:T(8,128)(2,1)S(1)}, bf16[96,256]{1,0:T(8,128)(2,1)S(1)}, u32[]{:S(2)}, u32[]{:S(2)}) collective-permute-start(bf16[96,256]{1,0:T(8,128)(2,1)S(1)} %get-tuple-element.61), channel_id=1, source_target_pairs={{0,4},{1,5},{2,6},{3,7},{4,0},{5,1},{6,2},{7,3},{8,12},{9,13},{10,... | collective-permute-start | bytes 147464 | tf_op jit(solution)/shard_map/ppermute | solution.py:457
  51.7 1.0 shard_map.120
  52.9 2.3 %collective-permute-done.11.refs_1_ = bf16[96,256]{1,0:T(8,128)(2,1)S(1)} collective-permute-done((bf16[96,256]{1,0:T(8,128)(2,1)S(1)}, bf16[96,256]{1,0:T(8,128)(2,1)S(1)}, u32[]{:S(2)}, u32[]{:S(2)}) %collective-permute-start.11) | collective-permute-done | bytes 49184 | tf_op jit(solution)/shard_map/ppermute | solution.py:457
  55.4 0.7 collective-permute-start.14
  56.1 0.8 shard_map.123.refs_2_.refs_1_
  57.1 3.5 %collective-permute-done.14.refs_1_ = bf16[96,256]{1,0:T(8,128)(2,1)S(1)} collective-permute-done((bf16[96,256]{1,0:T(8,128)(2,1)S(1)}, bf16[96,256]{1,0:T(8,128)(2,1)S(1)}, u32[]{:S(2)}, u32[]{:S(2)}) %collective-permute-start.14) | collective-permute-done | bytes 49184 | tf_op jit(solution)/shard_map/ppermute | solution.py:457
  61.1 4.2 %collective-permute-done.15.refs_4_.refs_1_ = bf16[160,256]{1,0:T(8,128)(2,1)S(1)} collective-permute-done((bf16[160,256]{1,0:T(8,128)(2,1)S(1)}, bf16[160,256]{1,0:T(8,128)(2,1)S(1)}, u32[]{:S(2)}, u32[]{:S(2)}) %collective-permute-start.15) | collective-permute-done | bytes 81952 | tf_op jit(solution)/shard_map/ppermute | solution.py:457
  65.5 2.8 %collective-permute-start.17 = (bf16[96,256]{1,0:T(8,128)(2,1)S(1)}, bf16[96,256]{1,0:T(8,128)(2,1)S(1)}, u32[]{:S(2)}, u32[]{:S(2)}) collective-permute-start(bf16[96,256]{1,0:T(8,128)(2,1)S(1)} %get-tuple-element.70), channel_id=1, source_target_pairs={{0,128},{8,136},{16,144},{24,152},{32,160},{40,168},{48,176},{56,1... | collective-permute-start | bytes 147464 | tf_op jit(solution)/shard_map/ppermute | solution.py:455
  68.5 2.7 %collective-permute-done.17.refs_1_ = bf16[96,256]{1,0:T(8,128)(2,1)S(1)} collective-permute-done((bf16[96,256]{1,0:T(8,128)(2,1)S(1)}, bf16[96,256]{1,0:T(8,128)(2,1)S(1)}, u32[]{:S(2)}, u32[]{:S(2)}) %collective-permute-start.17) | collective-permute-done | bytes 49184 | tf_op jit(solution)/shard_map/ppermute | solution.py:455
  71.4 1.5 %collective-permute-start.18 = (bf16[96,256]{1,0:T(8,128)(2,1)S(1)}, bf16[96,256]{1,0:T(8,128)(2,1)S(1)}, u32[]{:S(2)}, u32[]{:S(2)}) collective-permute-start(bf16[96,256]{1,0:T(8,128)(2,1)S(1)} %get-tuple-element.73), channel_id=1, source_target_pairs={{0,64},{8,72},{16,80},{24,88},{32,96},{40,104},{48,112},{56,120},{... | collective-permute-start | bytes 147464 | tf_op jit(solution)/shard_map/ppermute | solution.py:455
  72.9 2.8 %collective-permute-start.16 = (bf16[96,256]{1,0:T(8,128)(2,1)S(1)}, bf16[96,256]{1,0:T(8,128)(2,1)S(1)}, u32[]{:S(2)}, u32[]{:S(2)}) collective-permute-start(bf16[96,256]{1,0:T(8,128)(2,1)S(1)} %get-tuple-element.60.refs_5_), channel_id=1, source_target_pairs={{1,2},{3,4},{5,6},{7,0},{2,1},{4,3},{6,5},{0,7},{9,10},{11,12},{13... | collective-permute-start | bytes 147464 | tf_op jit(solution)/shard_map/ppermute | solution.py:461
  76.1 2.9 %collective-permute-start.19 = (bf16[96,256]{1,0:T(8,128)(2,1)S(1)}, bf16[96,256]{1,0:T(8,128)(2,1)S(1)}, u32[]{:S(2)}, u32[]{:S(2)}) collective-permute-start(bf16[96,256]{1,0:T(8,128)(2,1)S(1)} %get-tuple-element.76), channel_id=1, source_target_pairs={{0,32},{8,40},{16,48},{24,56},{32,0},{40,8},{48,16},{56,24},{64,96... | collective-permute-start | bytes 147464 | tf_op jit(solution)/shard_map/ppermute | solution.py:455
  79.3 2.5 %collective-permute-done.19.refs_1_ = bf16[96,256]{1,0:T(8,128)(2,1)S(1)} collective-permute-done((bf16[96,256]{1,0:T(8,128)(2,1)S(1)}, bf16[96,256]{1,0:T(8,128)(2,1)S(1)}, u32[]{:S(2)}, u32[]{:S(2)}) %collective-permute-start.19) | collective-permute-done | bytes 49184 | tf_op jit(solution)/shard_map/ppermute | solution.py:455
  82.0 2.7 %collective-permute-start.20 = (bf16[96,256]{1,0:T(8,128)(2,1)S(1)}, bf16[96,256]{1,0:T(8,128)(2,1)S(1)}, u32[]{:S(2)}, u32[]{:S(2)}) collective-permute-start(bf16[96,256]{1,0:T(8,128)(2,1)S(1)} %get-tuple-element.79), channel_id=1, source_target_pairs={{0,16},{8,24},{16,0},{24,8},{32,48},{40,56},{48,32},{56,40},{64,80... | collective-permute-start | bytes 147464 | tf_op jit(solution)/shard_map/ppermute | solution.py:455
  84.9 1.9 %collective-permute-done.20.refs_1_ = bf16[96,256]{1,0:T(8,128)(2,1)S(1)} collective-permute-done((bf16[96,256]{1,0:T(8,128)(2,1)S(1)}, bf16[96,256]{1,0:T(8,128)(2,1)S(1)}, u32[]{:S(2)}, u32[]{:S(2)}) %collective-permute-start.20) | collective-permute-done | bytes 49184 | tf_op jit(solution)/shard_map/ppermute | solution.py:455
  87.0 1.1 collective-permute-done.13.refs_3_
  88.2 0.6 shard_map.126.refs_2_.refs_0_
  89.0 1.3 %shard_map.138 = (bf16[64,2048]{1,0:T(8,128)(2,1)S(1)}, bf16[64,2048]{1,0:T(8,128)(2,1)S(1)}, f32[32,8,128]{2,1,0:T(8,128)S(1)}, f32[32,64]{1,0:T(8,128)S(1)}) custom-call(f32[64,2048]{1,0:T(8,128)S(1)} %shard_map.126.refs_2_.refs_0_, f32[64,256]{1,0:T(8,128)S(1)} %shard_map.137.refs_1_, bf16[96,256]{1,0:T(8,128)(2,1)S(1)} %collective-permute-done.21.refs_2_, ...), custom_call_target="tpu_custom_call" | custom-call | flops 134217728 | bytes 2744320 | tf_op jit(solution)/shard_map/pallas_call | solution.py:28
  90.4 12.8 %all_to_all.10.refs_0_ = f32[32,8,128]{2,1,0:T(8,128)S(1)} all-to-all(f32[32,8,128]{2,1,0:T(8,128)S(1)} %get-tuple-element.84), channel_id=1, replica_groups=mesh['px'=32,'py'=8] {'px'}, dimensions={0} | all-to-all | bytes 262144 | tf_op jit(solution)/shard_map/all_to_all | solution.py:622
  103.1 0.6 shard_map.139
  103.8 5.4 %all-to-all-start.1 = ((f32[8,8,128]{2,1,0:T(8,128)}), f32[8,8,128]{2,1,0:T(8,128)S(1)}, u32[]{:S(2)}, u32[]{:S(2)}) async-start(f32[8,8,128]{2,1,0:T(8,128)} %shard_map.139), calls=%async_computation.1 | async-start | bytes 65536 | tf_op jit(solution)/shard_map/all_to_all | solution.py:624
  109.2 1.3 %shard_map.119 = f32[32,32,128]{2,1,0:T(8,128)} custom-call(f32[64,2048]{1,0:T(8,128)S(1)} %copy-done.13), custom_call_target="tpu_custom_call" | custom-call | bytes 524288 | tf_op jit(solution)/shard_map/pallas_call | solution.py:28
  110.5 6.7 %all-to-all-done.1.refs_0_ = f32[8,8,128]{2,1,0:T(8,128)S(1)} async-done(((f32[8,8,128]{2,1,0:T(8,128)}), f32[8,8,128]{2,1,0:T(8,128)S(1)}, u32[]{:S(2)}, u32[]{:S(2)}) %all-to-all-start.1) | async-done | bytes 32800 | tf_op jit(solution)/shard_map/all_to_all | solution.py:624
  117.2 4.3 %shard_map.140 = f32[64,32,128]{2,1,0:T(8,128)} custom-call(f32[8,8,128]{2,1,0:T(8,128)S(1)} %all-to-all-done.1.refs_0_, f32[32,64]{1,0:T(8,128)S(1)} %get-tuple-element.85.refs_1_, bf16[64,2048]{1,0:T(8,128)(2,1)S(1)} %get-tuple-element.86.refs_2_, bf16[64,2048]{1,0:T(8,128)(2,1)S(1)} %get-tuple-element.87.refs_3_, ...), custom_call_target="tpu_custom_call" | custom-call | flops 67108864 | bytes 1089536 | tf_op jit(solution)/shard_map/pallas_call | solution.py:28
  (79 shorter events, 6.9 us)
Async XLA Ops:
  0.6 15.5 %copy-start = (s32[32,8,4,2]{0,3,2,1:T(2,128)S(1)}, s32[32,8,4,2]{0,3,2,1:T(2,128)}, u32[]{:S(2)}) copy-start(s32[32,8,4,2]{0,3,2,1:T(2,128)} %param.9) | copy-start | bytes 24580
  3.1 1.3 %collective-permute-start = (bf16[64,256]{1,0:T(8,128)(2,1)S(1)}, bf16[64,256]{1,0:T(8,128)(2,1)S(1)}, u32[]{:S(2)}, u32[]{:S(2)}) collective-permute-start(bf16[64,256]{1,0:T(8,128)(2,1)S(1)} %get-tuple-element.45.rest_0_.refs_0_), channel_id=1, source_target_pairs={{0,8},{8,0},{16,24},{24,16},{32,40},{40,32},{48,56},{56,48},{64,72... | collective-permute-start | bytes 98312 | tf_op jit(solution)/shard_map/ppermute | solution.py:455
  4.6 4.3 %collective-permute-start.1 = (bf16[64,256]{1,0:T(8,128)(2,1)S(1)}, bf16[64,256]{1,0:T(8,128)(2,1)S(1)}, u32[]{:S(2)}, u32[]{:S(2)}) collective-permute-start(bf16[64,256]{1,0:T(8,128)(2,1)S(1)} %shard_map.98.rest_0_.refs_0_), channel_id=1, source_target_pairs={{0,16},{8,24},{16,0},{24,8},{32,48},{40,56},{48,32},{56,40},{64,80... | collective-permute-start | bytes 98312 | tf_op jit(solution)/shard_map/ppermute | solution.py:455
  8.2 1.0 copy-start.1
  9.3 5.5 %collective-permute-start.2 = (bf16[64,256]{1,0:T(8,128)(2,1)S(1)}, bf16[64,256]{1,0:T(8,128)(2,1)S(1)}, u32[]{:S(2)}, u32[]{:S(2)}) collective-permute-start(bf16[64,256]{1,0:T(8,128)(2,1)S(1)} %shard_map.101.rest_0_.refs_0_), channel_id=1, source_target_pairs={{0,32},{8,40},{16,48},{24,56},{32,0},{40,8},{48,16},{56,24},{64,96... | collective-permute-start | bytes 98312 | tf_op jit(solution)/shard_map/ppermute | solution.py:455
  11.2 2.0 %copy-start.2 = (bf16[2,2,2,256,256]{4,3,2,1,0:T(8,128)(2,1)S(1)}, bf16[2,2,2,256,256]{4,3,2,1,0:T(8,128)(2,1)}, u32[]{:S(2)}) copy-start(bf16[2,2,2,256,256]{4,3,2,1,0:T(8,128)(2,1)} %copy-done.1) | copy-start | bytes 3145732
  13.2 2.9 %copy-start.14 = (s32[4]{0:T(128)S(1)}, s32[4]{0:T(128)}, u32[]{:S(2)}) copy-start(s32[4]{0:T(128)} %constant.40.clone) | copy-start | bytes 52
  15.0 4.0 %collective-permute-start.3 = (bf16[64,256]{1,0:T(8,128)(2,1)S(1)}, bf16[64,256]{1,0:T(8,128)(2,1)S(1)}, u32[]{:S(2)}, u32[]{:S(2)}) collective-permute-start(bf16[64,256]{1,0:T(8,128)(2,1)S(1)} %shard_map.104.refs_2_.refs_0_), channel_id=1, source_target_pairs={{0,64},{8,72},{16,80},{24,88},{32,96},{40,104},{48,112},{56,120},{... | collective-permute-start | bytes 98312 | tf_op jit(solution)/shard_map/ppermute | solution.py:455
  17.2 1.2 %copy-start.7 = (bf16[1,1,2,16,128,128]{5,4,3,2,1,0:T(8,128)(2,1)S(1)}, bf16[1,1,2,16,128,128]{5,4,3,2,1,0:T(8,128)(2,1)}, u32[]{:S(2)}) copy-start(bf16[1,1,2,16,128,128]{5,4,3,2,1,0:T(8,128)(2,1)} %param.10) | copy-start | bytes 3145732
  18.8 3.2 %copy-start.9 = (f32[32,1,1,2,2048]{4,3,2,1,0:T(2,128)S(1)}, f32[32,1,1,2,2048]{4,3,2,1,0:T(2,128)}, u32[]{:S(2)}) copy-start(f32[32,1,1,2,2048]{4,3,2,1,0:T(2,128)} %param.8) | copy-start | bytes 1572868
  19.1 5.5 %collective-permute-start.4 = (bf16[64,256]{1,0:T(8,128)(2,1)S(1)}, bf16[64,256]{1,0:T(8,128)(2,1)S(1)}, u32[]{:S(2)}, u32[]{:S(2)}) collective-permute-start(bf16[64,256]{1,0:T(8,128)(2,1)S(1)} %shard_map.108.refs_1_.refs_0_), channel_id=1, source_target_pairs={{0,128},{8,136},{16,144},{24,152},{32,160},{40,168},{48,176},{56,1... | collective-permute-start | bytes 98312 | tf_op jit(solution)/shard_map/ppermute | solution.py:455
  23.7 1.1 copy-start.10
  24.8 4.4 %collective-permute-start.6 = (bf16[128,256]{1,0:T(8,128)(2,1)S(1)}, bf16[128,256]{1,0:T(8,128)(2,1)S(1)}, u32[]{:S(2)}, u32[]{:S(2)}) collective-permute-start(bf16[128,256]{1,0:T(8,128)(2,1)S(1)} %shard_map.111.refs_0_), channel_id=1, source_target_pairs={{0,1},{1,0},{2,3},{3,2},{4,5},{5,4},{6,7},{7,6},{8,9},{9,8},{10,11... | collective-permute-start | bytes 196616 | tf_op jit(solution)/shard_map/ppermute | solution.py:457
  26.8 1.2 collective-permute-start.5
  29.4 12.4 %copy-start.6 = (bf16[1,1,4,2,256,256]{5,4,3,2,1,0:T(8,128)(2,1)S(1)}, bf16[1,1,4,2,256,256]{5,4,3,2,1,0:T(8,128)(2,1)}, u32[]{:S(2)}) copy-start(bf16[1,1,4,2,256,256]{5,4,3,2,1,0:T(8,128)(2,1)} %param.11) | copy-start | bytes 3145732
  29.4 7.6 %collective-permute-start.7 = (bf16[64,256]{1,0:T(8,128)(2,1)S(1)}, bf16[64,256]{1,0:T(8,128)(2,1)S(1)}, u32[]{:S(2)}, u32[]{:S(2)}) collective-permute-start(bf16[64,256]{1,0:T(8,128)(2,1)S(1)} %shard_map.113.refs_0_), channel_id=1, source_target_pairs={{0,2},{1,3},{2,0},{3,1},{4,6},{5,7},{6,4},{7,5},{8,10},{9,11},{10,... | collective-permute-start | bytes 98312 | tf_op jit(solution)/shard_map/ppermute | solution.py:457
  32.7 9.0 %collective-permute-start.8 = (bf16[64,256]{1,0:T(8,128)(2,1)S(1)}, bf16[64,256]{1,0:T(8,128)(2,1)S(1)}, u32[]{:S(2)}, u32[]{:S(2)}) collective-permute-start(bf16[64,256]{1,0:T(8,128)(2,1)S(1)} %get-tuple-element.48.refs_3_), channel_id=1, source_target_pairs={{8,16},{24,32},{40,48},{56,64},{72,80},{88,96},{104,112},{120,128}... | collective-permute-start | bytes 98312 | tf_op jit(solution)/shard_map/ppermute | solution.py:461
  32.7 9.0 %collective-permute-start.9 = (bf16[64,256]{1,0:T(8,128)(2,1)S(1)}, bf16[64,256]{1,0:T(8,128)(2,1)S(1)}, u32[]{:S(2)}, u32[]{:S(2)}) collective-permute-start(bf16[64,256]{1,0:T(8,128)(2,1)S(1)} %get-tuple-element.50.refs_5_), channel_id=1, source_target_pairs={{1,2},{3,4},{5,6},{7,0},{2,1},{4,3},{6,5},{0,7},{9,10},{11,12},{13... | collective-permute-start | bytes 98312 | tf_op jit(solution)/shard_map/ppermute | solution.py:461
  36.9 6.2 %copy-start.5 = (bf16[1,1,2,256,2048]{4,3,2,1,0:T(8,128)(2,1)S(1)}, bf16[1,1,2,256,2048]{4,3,2,1,0:T(8,128)(2,1)}, u32[]{:S(2)}) copy-start(bf16[1,1,2,256,2048]{4,3,2,1,0:T(8,128)(2,1)} %param.13) | copy-start | bytes 6291460
  37.1 7.9 %collective-permute-start.10 = (bf16[64,256]{1,0:T(8,128)(2,1)S(1)}, bf16[64,256]{1,0:T(8,128)(2,1)S(1)}, u32[]{:S(2)}, u32[]{:S(2)}) collective-permute-start(bf16[64,256]{1,0:T(8,128)(2,1)S(1)} %shard_map.115.refs_7_.refs_0_), channel_id=1, source_target_pairs={{0,4},{1,5},{2,6},{3,7},{4,0},{5,1},{6,2},{7,3},{8,12},{9,13},{10,... | collective-permute-start | bytes 98312 | tf_op jit(solution)/shard_map/ppermute | solution.py:457
  47.0 8.4 %copy-start.12 = (f32[64,2048]{1,0:T(8,128)}, f32[64,2048]{1,0:T(8,128)S(1)}, u32[]{:S(2)}) copy-start(f32[64,2048]{1,0:T(8,128)S(1)} %get-tuple-element.54.refs_0_) | copy-start | bytes 1572868
  47.0 8.2 %collective-permute-start.11 = (bf16[96,256]{1,0:T(8,128)(2,1)S(1)}, bf16[96,256]{1,0:T(8,128)(2,1)S(1)}, u32[]{:S(2)}, u32[]{:S(2)}) collective-permute-start(bf16[96,256]{1,0:T(8,128)(2,1)S(1)} %get-tuple-element.61), channel_id=1, source_target_pairs={{0,4},{1,5},{2,6},{3,7},{4,0},{5,1},{6,2},{7,3},{8,12},{9,13},{10,... | collective-permute-start | bytes 147464 | tf_op jit(solution)/shard_map/ppermute | solution.py:457
  52.7 3.4 %copy-start.8 = (bf16[1,1,2,16,128,128]{5,4,3,2,1,0:T(8,128)(2,1)S(1)}, bf16[1,1,2,16,128,128]{5,4,3,2,1,0:T(8,128)(2,1)}, u32[]{:S(2)}) copy-start(bf16[1,1,2,16,128,128]{5,4,3,2,1,0:T(8,128)(2,1)} %param.10) | copy-start | bytes 3145732
  55.4 5.1 %collective-permute-start.14 = (bf16[96,256]{1,0:T(8,128)(2,1)S(1)}, bf16[96,256]{1,0:T(8,128)(2,1)S(1)}, u32[]{:S(2)}, u32[]{:S(2)}) collective-permute-start(bf16[96,256]{1,0:T(8,128)(2,1)S(1)} %get-tuple-element.63.refs_2_), channel_id=1, source_target_pairs={{0,2},{1,3},{2,0},{3,1},{4,6},{5,7},{6,4},{7,5},{8,10},{9,11},{10,... | collective-permute-start | bytes 147464 | tf_op jit(solution)/shard_map/ppermute | solution.py:457
  60.8 4.5 %collective-permute-start.15 = (bf16[160,256]{1,0:T(8,128)(2,1)S(1)}, bf16[160,256]{1,0:T(8,128)(2,1)S(1)}, u32[]{:S(2)}, u32[]{:S(2)}) collective-permute-start(bf16[160,256]{1,0:T(8,128)(2,1)S(1)} %get-tuple-element.66), channel_id=1, source_target_pairs={{0,1},{1,0},{2,3},{3,2},{4,5},{5,4},{6,7},{7,6},{8,9},{9,8},{10,11... | collective-permute-start | bytes 245768 | tf_op jit(solution)/shard_map/ppermute | solution.py:457
  65.5 5.7 %collective-permute-start.17 = (bf16[96,256]{1,0:T(8,128)(2,1)S(1)}, bf16[96,256]{1,0:T(8,128)(2,1)S(1)}, u32[]{:S(2)}, u32[]{:S(2)}) collective-permute-start(bf16[96,256]{1,0:T(8,128)(2,1)S(1)} %get-tuple-element.70), channel_id=1, source_target_pairs={{0,128},{8,136},{16,144},{24,152},{32,160},{40,168},{48,176},{56,1... | collective-permute-start | bytes 147464 | tf_op jit(solution)/shard_map/ppermute | solution.py:455
  71.2 4.7 %copy-start.3 = (bf16[2,2,2,256,256]{4,3,2,1,0:T(8,128)(2,1)S(1)}, bf16[2,2,2,256,256]{4,3,2,1,0:T(8,128)(2,1)}, u32[]{:S(2)}) copy-start(bf16[2,2,2,256,256]{4,3,2,1,0:T(8,128)(2,1)} %copy-done.1) | copy-start | bytes 3145732
  71.4 4.5 %collective-permute-start.18 = (bf16[96,256]{1,0:T(8,128)(2,1)S(1)}, bf16[96,256]{1,0:T(8,128)(2,1)S(1)}, u32[]{:S(2)}, u32[]{:S(2)}) collective-permute-start(bf16[96,256]{1,0:T(8,128)(2,1)S(1)} %get-tuple-element.73), channel_id=1, source_target_pairs={{0,64},{8,72},{16,80},{24,88},{32,96},{40,104},{48,112},{56,120},{... | collective-permute-start | bytes 147464 | tf_op jit(solution)/shard_map/ppermute | solution.py:455
  72.9 6.2 %collective-permute-start.16 = (bf16[96,256]{1,0:T(8,128)(2,1)S(1)}, bf16[96,256]{1,0:T(8,128)(2,1)S(1)}, u32[]{:S(2)}, u32[]{:S(2)}) collective-permute-start(bf16[96,256]{1,0:T(8,128)(2,1)S(1)} %get-tuple-element.60.refs_5_), channel_id=1, source_target_pairs={{1,2},{3,4},{5,6},{7,0},{2,1},{4,3},{6,5},{0,7},{9,10},{11,12},{13... | collective-permute-start | bytes 147464 | tf_op jit(solution)/shard_map/ppermute | solution.py:461
  75.7 9.0 %copy-start.4 = (bf16[1,1,2,2048,256]{4,3,2,1,0:T(8,128)(2,1)S(1)}, bf16[1,1,2,2048,256]{4,3,2,1,0:T(8,128)(2,1)}, u32[]{:S(2)}) copy-start(bf16[1,1,2,2048,256]{4,3,2,1,0:T(8,128)(2,1)} %param.12) | copy-start | bytes 6291460
  76.1 5.7 %collective-permute-start.19 = (bf16[96,256]{1,0:T(8,128)(2,1)S(1)}, bf16[96,256]{1,0:T(8,128)(2,1)S(1)}, u32[]{:S(2)}, u32[]{:S(2)}) collective-permute-start(bf16[96,256]{1,0:T(8,128)(2,1)S(1)} %get-tuple-element.76), channel_id=1, source_target_pairs={{0,32},{8,40},{16,48},{24,56},{32,0},{40,8},{48,16},{56,24},{64,96... | collective-permute-start | bytes 147464 | tf_op jit(solution)/shard_map/ppermute | solution.py:455
  79.0 5.6 %collective-permute-start.12 = (bf16[96,256]{1,0:T(8,128)(2,1)S(1)}, bf16[96,256]{1,0:T(8,128)(2,1)S(1)}, u32[]{:S(2)}, u32[]{:S(2)}) collective-permute-start(bf16[96,256]{1,0:T(8,128)(2,1)S(1)} %get-tuple-element.57.refs_2_), channel_id=1, source_target_pairs={{0,8},{8,0},{16,24},{24,16},{32,40},{40,32},{48,56},{56,48},{64,72... | collective-permute-start | bytes 147464 | tf_op jit(solution)/shard_map/ppermute | solution.py:455
  82.0 4.7 %collective-permute-start.20 = (bf16[96,256]{1,0:T(8,128)(2,1)S(1)}, bf16[96,256]{1,0:T(8,128)(2,1)S(1)}, u32[]{:S(2)}, u32[]{:S(2)}) collective-permute-start(bf16[96,256]{1,0:T(8,128)(2,1)S(1)} %get-tuple-element.79), channel_id=1, source_target_pairs={{0,16},{8,24},{16,0},{24,8},{32,48},{40,56},{48,32},{56,40},{64,80... | collective-permute-start | bytes 147464 | tf_op jit(solution)/shard_map/ppermute | solution.py:455
  84.7 3.5 %collective-permute-start.13 = (bf16[96,256]{1,0:T(8,128)(2,1)S(1)}, bf16[96,256]{1,0:T(8,128)(2,1)S(1)}, u32[]{:S(2)}, u32[]{:S(2)}) collective-permute-start(bf16[96,256]{1,0:T(8,128)(2,1)S(1)} %get-tuple-element.58.refs_3_), channel_id=1, source_target_pairs={{8,16},{24,32},{40,48},{56,64},{72,80},{88,96},{104,112},{120,128}... | collective-permute-start | bytes 147464 | tf_op jit(solution)/shard_map/ppermute | solution.py:461
  86.9 22.3 %copy-start.13 = (f32[64,2048]{1,0:T(8,128)S(1)}, f32[64,2048]{1,0:T(8,128)}, u32[]{:S(2)}) copy-start(f32[64,2048]{1,0:T(8,128)} %copy-done.12) | copy-start | bytes 1572868
  86.9 2.1 %collective-permute-start.21 = (bf16[96,256]{1,0:T(8,128)(2,1)S(1)}, bf16[96,256]{1,0:T(8,128)(2,1)S(1)}, u32[]{:S(2)}, u32[]{:S(2)}) collective-permute-start(bf16[96,256]{1,0:T(8,128)(2,1)S(1)} %get-tuple-element.82), channel_id=1, source_target_pairs={{0,8},{8,0},{16,24},{24,16},{32,40},{40,32},{48,56},{56,48},{64,72... | collective-permute-start | bytes 147464 | tf_op jit(solution)/shard_map/ppermute | solution.py:455
  88.8 28.4 %copy-start.11 = (bf16[64,2048]{1,0:T(8,128)(2,1)S(1)}, bf16[64,2048]{1,0:T(8,128)(2,1)}, u32[]{:S(2)}) copy-start(bf16[64,2048]{1,0:T(8,128)(2,1)} %copy-done.10) | copy-start | bytes 786436
  103.8 13.5 %all-to-all-start.1 = ((f32[8,8,128]{2,1,0:T(8,128)}), f32[8,8,128]{2,1,0:T(8,128)S(1)}, u32[]{:S(2)}, u32[]{:S(2)}) async-start(f32[8,8,128]{2,1,0:T(8,128)} %shard_map.139), calls=%async_computation.1 | async-start | bytes 65536 | tf_op jit(solution)/shard_map/all_to_all | solution.py:624
